TPU v7x, 32 devices: a whole 2x2x4 slice. The times are simulated.
32 devices in a mesh: ctx: 16 (over z, y, core), head: 2 (over x).
Axes of the slice: x: 2, y: 2, z: 4, core: 2. Of those that a mesh axis runs over, the one named last changes fastest.
Arguments:
- queries: bfloat16 [16384, 8, 128], P('ctx', 'head'), may hold values from -6 to 6
- keys: bfloat16 [16384, 128], P('ctx'), may hold values from -6 to 6
- values: bfloat16 [16384, 128], P('ctx'), may hold values from -6 to 6
- outputs: bfloat16 [16384, 8, 128], P('ctx', 'head'), may hold values from -6 to 6
- out_grad: bfloat16 [16384, 8, 128], P('ctx', 'head'), may hold values from -16 to 16
- log_norm: float32 [8, 16384], P('head', 'ctx'), may hold values from 6 to 8
- span_ids: int32 [32], replicated, may hold values from 0 to 31, as said below
Outputs:
- query_grad: bfloat16 [16384, 8, 128], P('ctx', 'head')
- key_grad: bfloat16 [16384, 128], P(('ctx', 'head'))
- value_grad: bfloat16 [16384, 128], P(('ctx', 'head'))
Inputs may be any that keep to these rules, and one draw needn't show every extreme that they name: `span_ids`: a permutation of 0 to 31 in which blocks 2 k and 2 k + 1 hold two spans that sum to 31.
All inputs are finite; a program needn't handle non-finite values.
Results may differ from a plain program's by a relative error of at most 0.0065.
Values may be sent and summed in bfloat16 or wider, within the bound.
No kernel may reach another device: no remote copies, remote signals or barrier semaphores. Data moves between devices by JAX's collectives and lax.ppermute only.
A program may use at most 128 MiB of HBM per device.

v0:
```python
import functools
import math

import jax
import jax.numpy as jnp
from jax import lax
from jax.experimental import pallas as pl
from jax.experimental.pallas import tpu as pltpu
from jax.sharding import PartitionSpec as P

STEPS = 3
NT = (((1,), (1,)), ((), ()))
NN = (((1,), (0,)), ((), ()))
TN = (((0,), (0,)), ((), ()))


def dot(a, b, dims):
    return lax.dot_general(a, b, dims, preferred_element_type=jnp.float32)


def three_terms(x):
    high = x.astype(jnp.bfloat16)
    rest = x - high.astype(jnp.float32)
    mid = rest.astype(jnp.bfloat16)
    low = (rest - mid.astype(jnp.float32)).astype(jnp.bfloat16)
    return high, mid, low


def row_terms(heads, tile, refs, out, norm_ref):
    grad_ref, outputs_ref = refs
    rows = grad_ref.shape[0]
    toks = tile // heads
    spread = (
        lax.broadcasted_iota(jnp.int32, (toks, tile), 1) // heads
        == lax.broadcasted_iota(jnp.int32, (toks, tile), 0)
    ).astype(jnp.bfloat16)
    mine = (
        lax.broadcasted_iota(jnp.int32, (heads, tile), 1) % heads
        == lax.broadcasted_iota(jnp.int32, (heads, tile), 0)
    )
    ones = jnp.ones((8, grad_ref.shape[1]), jnp.bfloat16)
    for index in range(rows // tile):
        norm = norm_ref[:, pl.ds(index * toks, toks)] * math.log2(math.e)
        wide = sum(dot(part, spread, NN) for part in three_terms(norm))
        out[0:1, pl.ds(index * tile, tile)] = jnp.sum(
            jnp.where(mine, wide, 0.0), axis=0, keepdims=True
        )
        prod = grad_ref[pl.ds(index * tile, tile), :].astype(jnp.float32) * outputs_ref[
            pl.ds(index * tile, tile), :
        ].astype(jnp.float32)
        high = prod.astype(jnp.bfloat16)
        low = (prod - high.astype(jnp.float32)).astype(jnp.bfloat16)
        out[1:2, pl.ds(index * tile, tile)] = (dot(ones, high, NT) + dot(ones, low, NT))[0:1]


def tile_grads(
    refs, accs, row, key, length, scale, triangle=None
):
    query_ref, grad_ref, key_ref, value_ref, terms_ref, tile = refs
    query_acc, key_acc, value_acc = accs
    q = query_ref[pl.ds(row, tile), :]
    g = grad_ref[pl.ds(row, tile), :]
    k = key_ref[pl.ds(key, length), :]
    v = value_ref[pl.ds(key, length), :]
    norm = terms_ref[0:1, pl.ds(row, tile)]
    delta = terms_ref[1:2, pl.ds(row, tile)]
    scores = dot(k, q, NT)
    prob = jnp.exp2(scores * (scale * math.log2(math.e)) - norm)
    if triangle is not None:
        edge = length - triangle.shape[0]
        last = jnp.where(triangle, prob[edge:], 0.0)
        prob = last if edge == 0 else jnp.concatenate([prob[:edge], last], axis=0)
    value_acc[pl.ds(key, length), :] += dot(prob.astype(jnp.bfloat16), g, NN)
    dprob = dot(v, g, NT)
    dscore = (prob * (dprob - delta)).astype(jnp.bfloat16)
    key_acc[pl.ds(key, length), :] += dot(dscore, q, NN)
    query_acc[pl.ds(row, tile), :] += dot(dscore, k, TN)


def own_kernel(heads, tile, scale, parts, places, *refs):
    query_ref, grad_ref, outputs_ref, norm_ref, key_ref, value_ref = refs[:6]
    query_acc, terms_ref, mine_ref = refs[6:9]
    sent = refs[9 : 8 + parts]
    key_acc, value_acc = refs[8 + parts :]
    half = key_ref.shape[0] // 2
    toks = tile // heads
    query_acc[...] = jnp.zeros_like(query_acc)
    key_acc[...] = jnp.zeros_like(key_acc)
    value_acc[...] = jnp.zeros_like(value_acc)
    row_terms(heads, tile, (grad_ref, outputs_ref), terms_ref, norm_ref)
    low = places[0]
    group = (query_ref, grad_ref, key_ref, value_ref, terms_ref, tile)
    accs = (query_acc, key_acc, value_acc)
    triangle = lax.broadcasted_iota(jnp.int32, (toks, tile), 0) <= (
        lax.broadcasted_iota(jnp.int32, (toks, tile), 1) // heads
    )

    @pl.loop(0, 2)
    def _(index):
        key = pl.multiple_of(index * half, half)
        for part in range(half // toks):
            row = pl.multiple_of(index * half * heads + part * tile, tile)
            tile_grads(group, accs, row, key, (part + 1) * toks, scale, triangle)

    @pl.loop(0, half // toks)
    def _(part):
        row = pl.multiple_of((1 - low) * half * heads + part * tile, tile)
        tile_grads(group, accs, row, pl.multiple_of(low * half, half), half, scale)

    share = key_ref.shape[0] // parts
    for away in range(parts):
        start = pl.multiple_of(lax.rem(places[1] + away, parts) * share, share)
        out = mine_ref if away == 0 else sent[away - 1]
        out[0:share, :] = (key_acc[pl.ds(start, share), :] * scale).astype(out.dtype)
        out[share : 2 * share, :] = value_acc[pl.ds(start, share), :].astype(out.dtype)


def far_kernel(heads, tile, scale, parts, last, places, *refs):
    query_ref, grad_ref, key_ref, value_ref, terms_ref, before_ref = refs[:6]
    query_out = refs[6]
    sent = refs[7 : 7 + parts]
    key_acc, value_acc = refs[7 + parts : 9 + parts]
    query_acc = refs[9 + parts] if last else query_out
    half = key_ref.shape[0] // 2
    key_acc[...] = jnp.zeros_like(key_acc)
    value_acc[...] = jnp.zeros_like(value_acc)
    query_acc[...] = before_ref[...]
    group = (query_ref, grad_ref, key_ref, value_ref, terms_ref, tile)
    accs = (query_acc, key_acc, value_acc)
    per = half * heads // tile

    @pl.loop(0, 2 * per)
    def _(index):
        item = index // per
        row_half = jnp.where(places[2] == 1, places[0], item)
        key_half = jnp.where(places[2] == 1, item, places[0])
        row = pl.multiple_of(row_half * half * heads + lax.rem(index, per) * tile, tile)
        tile_grads(group, accs, row, pl.multiple_of(key_half * half, half), half, scale)

    share = key_ref.shape[0] // parts
    for away in range(parts):
        start = pl.multiple_of(lax.rem(places[1] + away, parts) * share, share)
        out = sent[away]
        out[0:share, :] = (key_acc[pl.ds(start, share), :] * scale).astype(out.dtype)
        out[share : 2 * share, :] = value_acc[pl.ds(start, share), :].astype(out.dtype)
    if last:
        query_out[...] = (query_acc[...] * scale).astype(query_out.dtype)


VMEM = pl.BlockSpec(memory_space=pltpu.VMEM)
SMEM = pl.BlockSpec(memory_space=pltpu.SMEM)
PARAMS = pltpu.CompilerParams(vmem_limit_bytes=32 * 1024 * 1024)


def call(kernel, ins, outs, scratch, blocks, name):
    flops = blocks * 10 * 512 * 512 * 128
    return pl.pallas_call(
        kernel,
        out_shape=outs,
        in_specs=[SMEM] + [VMEM] * (len(ins) - 1),
        out_specs=[VMEM] * len(outs),
        scratch_shapes=scratch,
        compiler_params=PARAMS,
        name=name,
        cost_estimate=pl.CostEstimate(flops=int(flops), bytes_accessed=6 << 20, transcendentals=0),
    )(*ins)


def moved(block, back, away):
    holders, parts = lax.axis_size("ctx"), lax.axis_size("head")
    route = [
        (h * parts + x, ((h - back) % holders) * parts + (x + away) % parts)
        for h in range(holders)
        for x in range(parts)
    ]
    return lax.ppermute(block, ("ctx", "head"), route)


def local(queries, keys, values, outputs, out_grad, log_norm, span_ids):
    toks, heads, dim = queries.shape
    rows = toks * heads
    scale = dim ** (-0.5)
    holders, parts = lax.axis_size("ctx"), lax.axis_size("head")
    me, x = lax.axis_index("ctx"), lax.axis_index("head")
    tile = 512
    q = queries.reshape(rows, dim)
    g = out_grad.reshape(rows, dim)
    o = outputs.reshape(rows, dim)
    share = 2 * toks // parts
    f32, bf16 = jnp.float32, jnp.bfloat16

    def pair(holder):
        return lax.dynamic_slice_in_dim(span_ids, holder * 2, 2, 0)

    mine = pair(me)
    low = (mine[0] > mine[1]).astype(jnp.int32)

    def far_places(step):
        theirs = pair((me - step) % holders)
        high_only = jnp.min(mine) < jnp.min(theirs)
        their_low = (theirs[0] > theirs[1]).astype(jnp.int32)
        return jnp.stack(
            [jnp.where(high_only, 1 - low, their_low), x, high_only.astype(jnp.int32)]
        ).astype(jnp.int32)

    accs = [pltpu.VMEM((toks, dim), f32)] * 2
    key_1, value_1 = moved(keys, -1, 0), moved(values, -1, 0)
    key_2, value_2 = moved(key_1, -1, 0), moved(value_1, -1, 0)

    query_sum, terms, total, *sent = call(
        functools.partial(own_kernel, heads, tile, scale, parts),
        (jnp.stack([low, x]).astype(jnp.int32), q, g, o, log_norm, keys, values),
        [
            jax.ShapeDtypeStruct((rows, dim), f32),
            jax.ShapeDtypeStruct((8, rows), f32),
            jax.ShapeDtypeStruct((share, dim), f32),
        ]
        + [jax.ShapeDtypeStruct((share, dim), bf16)] * (parts - 1),
        accs,
        3 * heads,
        "own",
    )
    landed = [moved(block, 0, away + 1) for away, block in enumerate(sent)]
    for step, (key, value) in ((1, (key_1, value_1)), (2, (key_2, value_2))):
        last = step == STEPS - 1
        query_sum, *sent = call(
            functools.partial(far_kernel, heads, tile, scale, parts, last),
            (far_places(step), q, g, key, value, terms, query_sum),
            [jax.ShapeDtypeStruct((rows, dim), bf16 if last else f32)]
            + [jax.ShapeDtypeStruct((share, dim), bf16)] * parts,
            accs + ([pltpu.VMEM((rows, dim), f32)] if last else []),
            2 * heads,
            "far",
        )
        landed += [moved(block, step, away) for away, block in enumerate(sent)]
    for block in landed:
        total = total + block.astype(f32)
    total = total.astype(bf16)
    return query_sum.reshape(toks, heads, dim), total[: share // 2], total[share // 2 :]


def solution(mesh):
    in_specs = (
        P("ctx", "head", None),
        P("ctx", None),
        P("ctx", None),
        P("ctx", "head", None),
        P("ctx", "head", None),
        P("head", "ctx"),
        P(),
    )
    out_specs = (P("ctx", "head", None), P(("ctx", "head"), None), P(("ctx", "head"), None))
    return jax.shard_map(local, mesh=mesh, in_specs=in_specs, out_specs=out_specs, check_vma=False)
```

profile of v0, /device:TPU:0, one launch (start us, length us, event | category | flops | bytes accessed | tf_op | source)
XLA Modules:
  0.0 72.1 jit_solution(13567025888595666411)
XLA Ops:
  0.6 0.5 collective-permute-start
  1.1 2.6 %collective-permute-start.2 = (bf16[1024,128]{1,0:T(8,128)(2,1)}, bf16[1024,128]{1,0:T(8,128)(2,1)S(1)}, u32[]{:S(2)}, u32[]{:S(2)}) collective-permute-start(bf16[1024,128]{1,0:T(8,128)(2,1)} %refs_5_.1), channel_id=1, source_target_pairs={{0,2},{1,3},{2,4},{3,5},{4,6},{5,7},{6,8},{7,9},{8,10},{9,11},{10,... | collective-permute-start | bytes 786440 | tf_op jit(solution)/shard_map/ppermute | solution.py:176
  3.8 1.5 %fusion = (s32[]{:T(128)}, s32[2]{0:T(128)S(1)}, s32[]{:T(128)}, s32[2]{0:T(128)S(1)}, s32[]{:T(128)}, /*index=5*/s32[2]{0:T(128)S(1)}) fusion(s32[32]{0:T(128)} %param.13, s32[]{:T(128)S(6)} %select_n.31, s32[]{:T(128)S(6)} %select_n.26, s32[]{:T(128)S(6)} %select_n.28), kind=kLoop, calls=%fused_computation.4 | loop fusion | flops 3 | bytes 72 | tf_op jit(solution)/shard_map/reduce_min | solution.py:200
  5.3 0.6 fusion.6
  7.1 0.1 pad_add_fusion.1.places
  7.2 0.0 copy-start
  7.2 1.2 %copy-done = bf16[1024,4,128]{2,1,0:T(4,128)(2,1)S(1)} copy-done((bf16[1024,4,128]{2,1,0:T(4,128)(2,1)S(1)}, bf16[1024,4,128]{2,1,0:T(4,128)(2,1)}, u32[]{:S(2)}) %copy-start) | copy-done | bytes 1048600
  8.4 0.0 copy-start.1
  8.4 1.2 %copy-done.1 = bf16[1024,4,128]{2,1,0:T(4,128)(2,1)S(1)} copy-done((bf16[1024,4,128]{2,1,0:T(4,128)(2,1)S(1)}, bf16[1024,4,128]{2,1,0:T(4,128)(2,1)}, u32[]{:S(2)}) %copy-start.1) | copy-done | bytes 1048600
  9.6 0.0 copy-start.3
  9.6 1.2 %copy-done.3 = bf16[1024,4,128]{2,1,0:T(4,128)(2,1)S(1)} copy-done((bf16[1024,4,128]{2,1,0:T(4,128)(2,1)S(1)}, bf16[1024,4,128]{2,1,0:T(4,128)(2,1)}, u32[]{:S(2)}) %copy-start.3) | copy-done | bytes 1048600
  10.9 0.0 copy-start.5
  10.9 0.9 %copy-done.5 = bf16[1024,128]{1,0:T(8,128)(2,1)S(1)} copy-done((bf16[1024,128]{1,0:T(8,128)(2,1)S(1)}, bf16[1024,128]{1,0:T(8,128)(2,1)}, u32[]{:S(2)}) %copy-start.5) | copy-done | bytes 262168
  11.8 0.0 copy-start.6
  11.8 0.9 %copy-done.6 = bf16[1024,128]{1,0:T(8,128)(2,1)S(1)} copy-done((bf16[1024,128]{1,0:T(8,128)(2,1)S(1)}, bf16[1024,128]{1,0:T(8,128)(2,1)}, u32[]{:S(2)}) %copy-start.6) | copy-done | bytes 262168
  12.8 0.0 copy-start.7
  12.8 0.7 copy-done.7
  13.5 0.0 copy-start.2
  13.5 0.0 copy-start.4
  13.5 10.1 %own.1 = (f32[4096,128]{1,0:T(8,128)S(1)}, f32[8,4096]{1,0:T(8,128)S(1)}, f32[1024,128]{1,0:T(8,128)S(1)}, bf16[1024,128]{1,0:T(8,128)(2,1)S(1)}) custom-call(s32[2]{0:T(128)S(1)} %pad_add_fusion.1.places, bf16[4096,128]{1,0:T(8,128)(2,1)S(1)} %bitcast.13, bf16[4096,128]{1,0:T(8,128)(2,1)S(1)} %bitcast.16, bf16[4096,128]{1,0:T(8,128)(2,1)S(1)} %bitcast.12, ...), custom_call_target="tpu_custom_call" | custom-call | flops 4026531840 | bytes 6291456 | tf_op jit(solution)/shard_map/own/pallas_call | solution.py:157
  23.6 0.0 copy-start.8
  23.6 1.3 %copy-done.8 = f32[4096,128]{1,0:T(8,128)} copy-done((f32[4096,128]{1,0:T(8,128)}, f32[4096,128]{1,0:T(8,128)S(1)}, u32[]{:S(2)}) %copy-start.8) | copy-done | bytes 2097176
  25.0 1.5 %collective-permute-start.4 = (bf16[1024,128]{1,0:T(8,128)(2,1)S(1)}, bf16[1024,128]{1,0:T(8,128)(2,1)}, u32[]{:S(2)}, u32[]{:S(2)}) collective-permute-start(bf16[1024,128]{1,0:T(8,128)(2,1)S(1)} %get-tuple-element.18), channel_id=1, source_target_pairs={{0,1},{1,0},{2,3},{3,2},{4,5},{5,4},{6,7},{7,6},{8,9},{9,8},{10,11... | collective-permute-start | bytes 786440 | tf_op jit(solution)/shard_map/ppermute | solution.py:176
  26.5 0.7 fusion.4
  32.4 0.1 pad_add_fusion.2.places
  32.5 0.0 collective-permute-done.refs_2_
  32.5 0.0 collective-permute-start.1
  32.5 0.0 collective-permute-done.2.refs_3_
  32.5 1.6 %collective-permute-start.3 = (bf16[1024,128]{1,0:T(8,128)(2,1)S(1)}, bf16[1024,128]{1,0:T(8,128)(2,1)S(1)}, u32[]{:S(2)}, u32[]{:S(2)}) collective-permute-start(bf16[1024,128]{1,0:T(8,128)(2,1)S(1)} %collective-permute-done.2.refs_3_), channel_id=1, source_target_pairs={{0,2},{1,3},{2,4},{3,5},{4,6},{5,7},{6,8},{7,9},{8,10},{9,11},{10,... | collective-permute-start | bytes 786440 | tf_op jit(solution)/shard_map/ppermute | solution.py:176
  34.1 0.1 pad_add_fusion.places
  34.2 0.0 copy-done.2
  34.2 0.0 copy-done.4
  34.2 0.0 copy-start.9
  34.2 1.6 %copy-done.9 = f32[4096,128]{1,0:T(8,128)S(1)} copy-done((f32[4096,128]{1,0:T(8,128)S(1)}, f32[4096,128]{1,0:T(8,128)}, u32[]{:S(2)}) %copy-start.9) | copy-done | bytes 2097176
  35.8 7.9 %far.2 = (f32[4096,128]{1,0:T(8,128)S(1)}, bf16[1024,128]{1,0:T(8,128)(2,1)S(1)}, bf16[1024,128]{1,0:T(8,128)(2,1)S(1)}) custom-call(s32[3]{0:T(128)S(1)} %pad_add_fusion.2.places, bf16[4096,128]{1,0:T(8,128)(2,1)S(1)} %bitcast.14, bf16[4096,128]{1,0:T(8,128)(2,1)S(1)} %bitcast.17, bf16[1024,128]{1,0:T(8,128)(2,1)S(1)} %collective-permute-done.refs_2_, ...), custom_call_target="tpu_custom_call" | custom-call | flops 2684354560 | bytes 6291456 | tf_op jit(solution)/shard_map/far/pallas_call | solution.py:157
  43.8 2.9 %collective-permute-start.5 = (bf16[1024,128]{1,0:T(8,128)(2,1)S(1)}, bf16[1024,128]{1,0:T(8,128)(2,1)S(1)}, u32[]{:S(2)}, u32[]{:S(2)}) collective-permute-start(bf16[1024,128]{1,0:T(8,128)(2,1)S(1)} %get-tuple-element.19), channel_id=1, source_target_pairs={{0,30},{1,31},{2,0},{3,1},{4,2},{5,3},{6,4},{7,5},{8,6},{9,7},{10,... | collective-permute-start | bytes 786440 | tf_op jit(solution)/shard_map/ppermute | solution.py:176
  46.7 0.4 collective-permute-start.6
  47.1 0.0 collective-permute-done.1.refs_2_
  47.1 0.0 collective-permute-done.3.refs_3_
  47.1 9.0 %far.3 = (bf16[4096,128]{1,0:T(8,128)(2,1)}, bf16[1024,128]{1,0:T(8,128)(2,1)S(1)}, bf16[1024,128]{1,0:T(8,128)(2,1)S(1)}) custom-call(s32[3]{0:T(128)S(1)} %pad_add_fusion.places, bf16[4096,128]{1,0:T(8,128)(2,1)S(1)} %bitcast.15, bf16[4096,128]{1,0:T(8,128)(2,1)S(1)} %bitcast.18, bf16[1024,128]{1,0:T(8,128)(2,1)S(1)} %collective-permute-done.1.refs_2_, ...), custom_call_target="tpu_custom_call" | custom-call | flops 2684354560 | bytes 6291456 | tf_op jit(solution)/shard_map/far/pallas_call | solution.py:157
  56.1 0.4 collective-permute-start.7
  56.5 3.8 %collective-permute-start.8 = (bf16[1024,128]{1,0:T(8,128)(2,1)S(1)}, bf16[1024,128]{1,0:T(8,128)(2,1)S(1)}, u32[]{:S(2)}, u32[]{:S(2)}) collective-permute-start(bf16[1024,128]{1,0:T(8,128)(2,1)S(1)} %get-tuple-element.22), channel_id=1, source_target_pairs={{0,29},{1,28},{2,31},{3,30},{4,1},{5,0},{6,3},{7,2},{8,5},{9,4},{1... | collective-permute-start | bytes 786440 | tf_op jit(solution)/shard_map/ppermute | solution.py:176
  60.3 0.0 collective-permute-done.4
  60.3 0.0 collective-permute-done.5
  60.3 0.0 collective-permute-done.6
  60.3 9.9 %collective-permute-done.7 = bf16[1024,128]{1,0:T(8,128)(2,1)S(1)} collective-permute-done((bf16[1024,128]{1,0:T(8,128)(2,1)S(1)}, bf16[1024,128]{1,0:T(8,128)(2,1)S(1)}, u32[]{:S(2)}, u32[]{:S(2)}) %collective-permute-start.7) | collective-permute-done | bytes 262176 | tf_op jit(solution)/shard_map/ppermute | solution.py:176
  70.2 0.0 collective-permute-done.8
  70.2 1.2 %add_convert_fusion = bf16[1024,128]{1,0:T(8,128)(2,1)S(1)} fusion(bf16[1024,128]{1,0:T(8,128)(2,1)S(1)} %collective-permute-done.8, bf16[1024,128]{1,0:T(8,128)(2,1)S(1)} %collective-permute-done.7, bf16[1024,128]{1,0:T(8,128)(2,1)S(1)} %collective-permute-done.6, bf16[1024,128]{1,0:T(8,128)(2,1)S(1)} %collective-permute-done.5, ...), kind=kLoop, calls=%fused_computation | loop fusion | flops 1441792 | bytes 2097152 | tf_op jit(solution)/shard_map/convert_element_type | solution.py:238
  71.4 0.7 fusion.3
Async XLA Ops:
  0.6 31.9 %collective-permute-start = (bf16[1024,128]{1,0:T(8,128)(2,1)}, bf16[1024,128]{1,0:T(8,128)(2,1)S(1)}, u32[]{:S(2)}, u32[]{:S(2)}) collective-permute-start(bf16[1024,128]{1,0:T(8,128)(2,1)} %refs_4_.1), channel_id=1, source_target_pairs={{0,2},{1,3},{2,4},{3,5},{4,6},{5,7},{6,8},{7,9},{8,10},{9,11},{10,... | collective-permute-start | bytes 786440 | tf_op jit(solution)/shard_map/ppermute | solution.py:176
  1.1 31.4 %collective-permute-start.2 = (bf16[1024,128]{1,0:T(8,128)(2,1)}, bf16[1024,128]{1,0:T(8,128)(2,1)S(1)}, u32[]{:S(2)}, u32[]{:S(2)}) collective-permute-start(bf16[1024,128]{1,0:T(8,128)(2,1)} %refs_5_.1), channel_id=1, source_target_pairs={{0,2},{1,3},{2,4},{3,5},{4,6},{5,7},{6,8},{7,9},{8,10},{9,11},{10,... | collective-permute-start | bytes 786440 | tf_op jit(solution)/shard_map/ppermute | solution.py:176
  7.2 1.2 %copy-start = (bf16[1024,4,128]{2,1,0:T(4,128)(2,1)S(1)}, bf16[1024,4,128]{2,1,0:T(4,128)(2,1)}, u32[]{:S(2)}) copy-start(bf16[1024,4,128]{2,1,0:T(4,128)(2,1)} %param.10) | copy-start | bytes 3145732
  8.4 1.2 %copy-start.1 = (bf16[1024,4,128]{2,1,0:T(4,128)(2,1)S(1)}, bf16[1024,4,128]{2,1,0:T(4,128)(2,1)}, u32[]{:S(2)}) copy-start(bf16[1024,4,128]{2,1,0:T(4,128)(2,1)} %param.7) | copy-start | bytes 3145732
  9.6 1.2 %copy-start.3 = (bf16[1024,4,128]{2,1,0:T(4,128)(2,1)S(1)}, bf16[1024,4,128]{2,1,0:T(4,128)(2,1)}, u32[]{:S(2)}) copy-start(bf16[1024,4,128]{2,1,0:T(4,128)(2,1)} %param.11) | copy-start | bytes 3145732
  10.9 0.9 %copy-start.5 = (bf16[1024,128]{1,0:T(8,128)(2,1)S(1)}, bf16[1024,128]{1,0:T(8,128)(2,1)}, u32[]{:S(2)}) copy-start(bf16[1024,128]{1,0:T(8,128)(2,1)} %refs_4_.1) | copy-start | bytes 786436
  11.8 0.9 %copy-start.6 = (bf16[1024,128]{1,0:T(8,128)(2,1)S(1)}, bf16[1024,128]{1,0:T(8,128)(2,1)}, u32[]{:S(2)}) copy-start(bf16[1024,128]{1,0:T(8,128)(2,1)} %refs_5_.1) | copy-start | bytes 786436
  12.8 0.7 copy-start.7
  13.5 20.7 %copy-start.2 = (bf16[1024,4,128]{2,1,0:T(4,128)(2,1)S(1)}, bf16[1024,4,128]{2,1,0:T(4,128)(2,1)}, u32[]{:S(2)}) copy-start(bf16[1024,4,128]{2,1,0:T(4,128)(2,1)} %param.7) | copy-start | bytes 3145732
  13.5 20.7 %copy-start.4 = (bf16[1024,4,128]{2,1,0:T(4,128)(2,1)S(1)}, bf16[1024,4,128]{2,1,0:T(4,128)(2,1)}, u32[]{:S(2)}) copy-start(bf16[1024,4,128]{2,1,0:T(4,128)(2,1)} %param.11) | copy-start | bytes 3145732
  23.6 1.3 %copy-start.8 = (f32[4096,128]{1,0:T(8,128)}, f32[4096,128]{1,0:T(8,128)S(1)}, u32[]{:S(2)}) copy-start(f32[4096,128]{1,0:T(8,128)S(1)} %get-tuple-element.14.refs_5_) | copy-start | bytes 6291460
  25.0 35.4 %collective-permute-start.4 = (bf16[1024,128]{1,0:T(8,128)(2,1)S(1)}, bf16[1024,128]{1,0:T(8,128)(2,1)}, u32[]{:S(2)}, u32[]{:S(2)}) collective-permute-start(bf16[1024,128]{1,0:T(8,128)(2,1)S(1)} %get-tuple-element.18), channel_id=1, source_target_pairs={{0,1},{1,0},{2,3},{3,2},{4,5},{5,4},{6,7},{7,6},{8,9},{9,8},{10,11... | collective-permute-start | bytes 786440 | tf_op jit(solution)/shard_map/ppermute | solution.py:176
  32.5 14.6 %collective-permute-start.1 = (bf16[1024,128]{1,0:T(8,128)(2,1)S(1)}, bf16[1024,128]{1,0:T(8,128)(2,1)S(1)}, u32[]{:S(2)}, u32[]{:S(2)}) collective-permute-start(bf16[1024,128]{1,0:T(8,128)(2,1)S(1)} %collective-permute-done.refs_2_), channel_id=1, source_target_pairs={{0,2},{1,3},{2,4},{3,5},{4,6},{5,7},{6,8},{7,9},{8,10},{9,11},{10,... | collective-permute-start | bytes 786440 | tf_op jit(solution)/shard_map/ppermute | solution.py:176
  32.5 14.6 %collective-permute-start.3 = (bf16[1024,128]{1,0:T(8,128)(2,1)S(1)}, bf16[1024,128]{1,0:T(8,128)(2,1)S(1)}, u32[]{:S(2)}, u32[]{:S(2)}) collective-permute-start(bf16[1024,128]{1,0:T(8,128)(2,1)S(1)} %collective-permute-done.2.refs_3_), channel_id=1, source_target_pairs={{0,2},{1,3},{2,4},{3,5},{4,6},{5,7},{6,8},{7,9},{8,10},{9,11},{10,... | collective-permute-start | bytes 786440 | tf_op jit(solution)/shard_map/ppermute | solution.py:176
  34.2 1.6 %copy-start.9 = (f32[4096,128]{1,0:T(8,128)S(1)}, f32[4096,128]{1,0:T(8,128)}, u32[]{:S(2)}) copy-start(f32[4096,128]{1,0:T(8,128)} %copy-done.8) | copy-start | bytes 6291460
  43.8 16.6 %collective-permute-start.5 = (bf16[1024,128]{1,0:T(8,128)(2,1)S(1)}, bf16[1024,128]{1,0:T(8,128)(2,1)S(1)}, u32[]{:S(2)}, u32[]{:S(2)}) collective-permute-start(bf16[1024,128]{1,0:T(8,128)(2,1)S(1)} %get-tuple-element.19), channel_id=1, source_target_pairs={{0,30},{1,31},{2,0},{3,1},{4,2},{5,3},{6,4},{7,5},{8,6},{9,7},{10,... | collective-permute-start | bytes 786440 | tf_op jit(solution)/shard_map/ppermute | solution.py:176
  46.7 13.6 %collective-permute-start.6 = (bf16[1024,128]{1,0:T(8,128)(2,1)S(1)}, bf16[1024,128]{1,0:T(8,128)(2,1)S(1)}, u32[]{:S(2)}, u32[]{:S(2)}) collective-permute-start(bf16[1024,128]{1,0:T(8,128)(2,1)S(1)} %get-tuple-element.20), channel_id=1, source_target_pairs={{0,31},{1,30},{2,1},{3,0},{4,3},{5,2},{6,5},{7,4},{8,7},{9,6},{10,... | collective-permute-start | bytes 786440 | tf_op jit(solution)/shard_map/ppermute | solution.py:176
  56.1 14.1 %collective-permute-start.7 = (bf16[1024,128]{1,0:T(8,128)(2,1)S(1)}, bf16[1024,128]{1,0:T(8,128)(2,1)S(1)}, u32[]{:S(2)}, u32[]{:S(2)}) collective-permute-start(bf16[1024,128]{1,0:T(8,128)(2,1)S(1)} %get-tuple-element.21), channel_id=1, source_target_pairs={{0,28},{1,29},{2,30},{3,31},{4,0},{5,1},{6,2},{7,3},{8,4},{9,5},{1... | collective-permute-start | bytes 786440 | tf_op jit(solution)/shard_map/ppermute | solution.py:176
  56.5 13.7 %collective-permute-start.8 = (bf16[1024,128]{1,0:T(8,128)(2,1)S(1)}, bf16[1024,128]{1,0:T(8,128)(2,1)S(1)}, u32[]{:S(2)}, u32[]{:S(2)}) collective-permute-start(bf16[1024,128]{1,0:T(8,128)(2,1)S(1)} %get-tuple-element.22), channel_id=1, source_target_pairs={{0,29},{1,28},{2,31},{3,30},{4,1},{5,0},{6,3},{7,2},{8,5},{9,4},{1... | collective-permute-start | bytes 786440 | tf_op jit(solution)/shard_map/ppermute | solution.py:176
where the time goes:
time: 72.6 us; the launch traced here: 72.1 us
  Pallas kernels  27.1 us (37%)
  starting transfers between devices  13.8 us (19%)
  local copies, waits for them, and re-layouts  11.2 us (15%)
  waiting for transfers between devices  9.88 us (14%)
  between operations  7.22 us (10%)
  other arithmetic  2.9 us (4%)
    pallas_call x3, Pallas kernels, call(): pl.pallas_call(kernel, out_shape=outs, in_specs=[SMEM] + [VMEM] * (len(in...  27.1 us
    ppermute x9, starting transfers between devices, moved(): return lax.ppermute(block, ('ctx', 'head'), route)  13.8 us
    ppermute x9, waiting for transfers between devices, moved(): return lax.ppermute(block, ('ctx', 'head'), route)  9.88 us
    unnamed x20, local copies, waits for them, and re-layouts  9.22 us
    reduce_min x1, other arithmetic, far_places(): high_only = jnp.min(mine) < jnp.min(theirs)  1.51 us
  transfers between devices with their start and end apart: 9, of which 1 were waited for; matrix products, arithmetic and copies ran while one was open for 4% of the time, Pallas kernels for 38%

commit v1 on v0

v1 whole, which is shorter than its diff:
```python
import functools
import math

import jax
import jax.numpy as jnp
from jax import lax
from jax.experimental import pallas as pl
from jax.experimental.pallas import tpu as pltpu
from jax.sharding import PartitionSpec as P

STEPS = 3
NT = (((1,), (1,)), ((), ()))
NN = (((1,), (0,)), ((), ()))
TN = (((0,), (0,)), ((), ()))


def dot(a, b, dims):
    return lax.dot_general(a, b, dims, preferred_element_type=jnp.float32)


def three_terms(x):
    high = x.astype(jnp.bfloat16)
    rest = x - high.astype(jnp.float32)
    mid = rest.astype(jnp.bfloat16)
    low = (rest - mid.astype(jnp.float32)).astype(jnp.bfloat16)
    return high, mid, low


def row_terms(heads, tile, span, refs, out):
    grad_ref, outputs_ref, norm_ref = refs
    rows = grad_ref.shape[0] // 2
    toks = tile // heads
    spread = (
        lax.broadcasted_iota(jnp.int32, (toks, tile), 1) // heads
        == lax.broadcasted_iota(jnp.int32, (toks, tile), 0)
    ).astype(jnp.bfloat16)
    mine = (
        lax.broadcasted_iota(jnp.int32, (heads, tile), 1) % heads
        == lax.broadcasted_iota(jnp.int32, (heads, tile), 0)
    )
    ones = jnp.ones((8, grad_ref.shape[1]), jnp.bfloat16)
    for index in range(rows // tile):
        tok = pl.multiple_of(span * (rows // heads) + index * toks, toks)
        row = pl.multiple_of(span * rows + index * tile, tile)
        norm = norm_ref[:, pl.ds(tok, toks)] * math.log2(math.e)
        wide = sum(dot(part, spread, NN) for part in three_terms(norm))
        out[0:1, pl.ds(row, tile)] = jnp.sum(jnp.where(mine, wide, 0.0), axis=0, keepdims=True)
        prod = grad_ref[pl.ds(row, tile), :].astype(jnp.float32) * outputs_ref[
            pl.ds(row, tile), :
        ].astype(jnp.float32)
        high = prod.astype(jnp.bfloat16)
        low = (prod - high.astype(jnp.float32)).astype(jnp.bfloat16)
        out[1:2, pl.ds(row, tile)] = (dot(ones, high, NT) + dot(ones, low, NT))[0:1]


def tile_grads(
    refs, accs, row, key, length, scale, triangle=None
):
    query_ref, grad_ref, key_ref, value_ref, terms_ref, tile = refs
    query_acc, key_acc, value_acc = accs
    q = query_ref[pl.ds(row, tile), :]
    g = grad_ref[pl.ds(row, tile), :]
    k = key_ref[pl.ds(key, length), :]
    v = value_ref[pl.ds(key, length), :]
    norm = terms_ref[0:1, pl.ds(row, tile)]
    delta = terms_ref[1:2, pl.ds(row, tile)]
    scores = dot(k, q, NT)
    prob = jnp.exp2(scores * (scale * math.log2(math.e)) - norm)
    if triangle is not None:
        edge = length - triangle.shape[0]
        last = jnp.where(triangle, prob[edge:], 0.0)
        prob = last if edge == 0 else jnp.concatenate([prob[:edge], last], axis=0)
    value_acc[pl.ds(key, length), :] += dot(prob.astype(jnp.bfloat16), g, NN)
    dprob = dot(v, g, NT)
    dscore = (prob * (dprob - delta)).astype(jnp.bfloat16)
    key_acc[pl.ds(key, length), :] += dot(dscore, q, NN)
    query_acc[pl.ds(row, tile), :] += dot(dscore, k, TN)


def span_pair(span_ids, holder):
    return span_ids[2 * holder], span_ids[2 * holder + 1]


def put_shares(outs, key_acc, value_acc, scale):
    parts = len(outs)
    share = key_acc.shape[0] // parts
    x = lax.axis_index("head")
    for away, out in enumerate(outs):
        start = pl.multiple_of(lax.rem(x + away, parts) * share, share)
        out[0:share, :] = (key_acc[pl.ds(start, share), :] * scale).astype(out.dtype)
        out[share : 2 * share, :] = value_acc[pl.ds(start, share), :].astype(out.dtype)


def own_kernel(heads, tile, scale, parts, *refs):
    inputs, refs = refs[:7], refs[7:]
    query_acc, terms_ref, both_ref = refs[:3]
    outs, refs = refs[3 : 3 + parts], refs[3 + parts :]
    held, (key_acc, value_acc, sems) = refs[:5], refs[5:]
    query_ref, grad_ref, outputs_ref, norm_ref, span_ids = held
    toks = both_ref.shape[0] // 2
    key_ref, value_ref = both_ref.at[pl.ds(0, toks)], both_ref.at[pl.ds(toks, toks)]
    half = toks // 2
    rows = half * heads
    per = tile // heads
    whole = [
        pltpu.make_async_copy(a, b, sems.at[i, 2])
        for i, (a, b) in enumerate(zip(inputs[3:], (norm_ref, key_ref, value_ref, span_ids)))
    ]

    def halves(index):
        part = pl.ds(pl.multiple_of(index * rows, rows), rows)
        return [
            pltpu.make_async_copy(inputs[i].at[part], held[i].at[part], sems.at[i, index])
            for i in (1, 2, 0)
        ]

    for copy in whole + halves(0) + halves(1):
        copy.start()
    query_acc[...] = jnp.zeros_like(query_acc)
    key_acc[...] = jnp.zeros_like(key_acc)
    value_acc[...] = jnp.zeros_like(value_acc)
    group = (query_ref, grad_ref, key_ref, value_ref, terms_ref, tile)
    accs = (query_acc, key_acc, value_acc)
    triangle = lax.broadcasted_iota(jnp.int32, (per, tile), 0) <= (
        lax.broadcasted_iota(jnp.int32, (per, tile), 1) // heads
    )
    for copy in whole:
        copy.wait()

    @pl.loop(0, 2)
    def _(index):
        for copy in halves(index):
            copy.wait()
        row_terms(heads, tile, index, (grad_ref, outputs_ref, norm_ref), terms_ref)
        key = pl.multiple_of(index * half, half)
        for part in range(half // per):
            row = pl.multiple_of(index * rows + part * tile, tile)
            tile_grads(group, accs, row, key, (part + 1) * per, scale, triangle)

    first, second = span_pair(span_ids, lax.axis_index("ctx"))
    low = jnp.where(first > second, 1, 0)

    @pl.loop(0, rows // tile)
    def _(part):
        row = pl.multiple_of((1 - low) * rows + part * tile, tile)
        tile_grads(group, accs, row, pl.multiple_of(low * half, half), half, scale)

    put_shares(outs, key_acc, value_acc, scale)


def far_kernel(heads, tile, scale, parts, step, count, span_ids, *refs):
    query_ref, grad_ref, terms_ref = refs[:3]
    if count == 1:
        toks = refs[3].shape[0] // 2
        key_ref, value_ref = refs[3].at[pl.ds(0, toks)], refs[3].at[pl.ds(toks, toks)]
    else:
        key_ref, value_ref = refs[3:5]
    query_acc = refs[4 + count]
    outs = refs[5 + count : 5 + count + parts]
    key_acc, value_acc = refs[5 + count + parts :]
    half = key_ref.shape[0] // 2
    key_acc[...] = jnp.zeros_like(key_acc)
    value_acc[...] = jnp.zeros_like(value_acc)
    group = (query_ref, grad_ref, key_ref, value_ref, terms_ref, tile)
    accs = (query_acc, key_acc, value_acc)
    per = half * heads // tile
    me, holders = lax.axis_index("ctx"), lax.axis_size("ctx")
    mine = span_pair(span_ids, me)
    theirs = span_pair(span_ids, lax.rem(me + holders - step, holders))
    high_only = jnp.minimum(*mine) < jnp.minimum(*theirs)
    our_high = jnp.where(mine[0] > mine[1], 0, 1)
    their_low = jnp.where(theirs[0] > theirs[1], 1, 0)

    @pl.loop(0, 2 * per)
    def _(index):
        item = index // per
        row_half = jnp.where(high_only, our_high, item)
        key_half = jnp.where(high_only, item, their_low)
        row = pl.multiple_of(row_half * half * heads + lax.rem(index, per) * tile, tile)
        tile_grads(group, accs, row, pl.multiple_of(key_half * half, half), half, scale)

    put_shares(outs, key_acc, value_acc, scale)


VMEM = pl.BlockSpec(memory_space=pltpu.VMEM)
SMEM = pl.BlockSpec(memory_space=pltpu.SMEM)
HBM = pl.BlockSpec(memory_space=pltpu.HBM)
PARAMS = pltpu.CompilerParams(vmem_limit_bytes=20 * 1024 * 1024)


def call(kernel, ins, where, outs, scratch, blocks, name, aliases=None):
    flops = blocks * 40 * 512 * 512 * 128
    return pl.pallas_call(
        kernel,
        out_shape=outs,
        in_specs=where,
        out_specs=[VMEM] * len(outs),
        scratch_shapes=scratch,
        input_output_aliases=aliases or {},
        compiler_params=PARAMS,
        name=name,
        cost_estimate=pl.CostEstimate(flops=int(flops), bytes_accessed=6 << 20, transcendentals=0),
    )(*ins)


def moved(block, back, away):
    holders, parts = lax.axis_size("ctx"), lax.axis_size("head")
    route = [
        (h * parts + x, ((h - back) % holders) * parts + (x + away) % parts)
        for h in range(holders)
        for x in range(parts)
    ]
    return lax.ppermute(block, ("ctx", "head"), route)


def local(queries, keys, values, outputs, out_grad, log_norm, span_ids):
    toks, heads, dim = queries.shape
    rows = toks * heads
    scale = dim ** (-0.5)
    parts = lax.axis_size("head")
    tile = 512
    q = queries.reshape(rows, dim)
    g = out_grad.reshape(rows, dim)
    o = outputs.reshape(rows, dim)
    share = 2 * toks // parts
    f32, bf16 = jnp.float32, jnp.bfloat16
    shape = jax.ShapeDtypeStruct

    accs = [pltpu.VMEM((toks, dim), f32)] * 2
    far = moved(keys, 1 - STEPS, 0), moved(values, 1 - STEPS, 0)

    inputs = tuple(
        pltpu.with_memory_space_constraint(a, pltpu.HBM)
        for a in (q, g, o, log_norm, keys, values, span_ids)
    )
    query_sum, terms, both, total, *sent = call(
        functools.partial(own_kernel, heads, tile, scale, parts),
        inputs,
        [HBM] * len(inputs),
        [shape((rows, dim), f32), shape((8, rows), f32), shape((2 * toks, dim), bf16)]
        + [shape((share, dim), f32)]
        + [shape((share, dim), bf16)] * (parts - 1),
        [pltpu.VMEM(a.shape, a.dtype) for a in inputs[:4]]
        + [pltpu.SMEM(span_ids.shape, span_ids.dtype)]
        + accs
        + [pltpu.SemaphoreType.DMA((4, 3))],
        3 * heads,
        "own",
    )
    near = (moved(both, -1, 0),)
    landed = [moved(block, 0, away + 1) for away, block in enumerate(sent)]
    for step, held in ((2, far), (1, near)):
        query_sum, *sent = call(
            functools.partial(far_kernel, heads, tile, scale, parts, step, len(held)),
            (span_ids, q, g, terms, *held, query_sum),
            [SMEM] + [VMEM] * (4 + len(held)),
            [shape((rows, dim), f32)] + [shape((share, dim), bf16)] * parts,
            accs,
            2 * heads,
            "far",
            {4 + len(held): 0},
        )
        landed += [moved(block, step, away) for away, block in enumerate(sent)]
    for block in landed:
        total = total + block.astype(f32)
    total = total.astype(bf16)
    query_grad = (query_sum * scale).astype(bf16).reshape(toks, heads, dim)
    return query_grad, total[: share // 2], total[share // 2 :]


def solution(mesh):
    in_specs = (
        P("ctx", "head", None),
        P("ctx", None),
        P("ctx", None),
        P("ctx", "head", None),
        P("ctx", "head", None),
        P("head", "ctx"),
        P(),
    )
    out_specs = (P("ctx", "head", None), P(("ctx", "head"), None), P(("ctx", "head"), None))
    return jax.shard_map(local, mesh=mesh, in_specs=in_specs, out_specs=out_specs, check_vma=False)
```

time: 72.6 us -> 48.6 us (0.67)
  local copies, waits for them, and re-layouts: 11.2 us -> 0.73 us
  between operations: 7.22 us -> 0.68 us
  waiting for transfers between devices: 9.88 us -> 6.02 us
  other arithmetic: 2.9 us -> 1.33 us
  starting transfers between devices: 13.8 us -> 12.7 us
    unnamed x20 -> x6, local copies, waits for them, and re-layouts: 9.22 us -> 0.01 us
    ppermute x9 -> x8, waiting for transfers between devices: 9.88 us -> 6.02 us  [moved(): return lax.ppermute(block, ('ctx', 'head'), route)]
    reduce_min x1 -> x0, other arithmetic: 1.51 us -> none  [far_places(): high_only = jnp.min(mine) < jnp.min(theirs)]
    slice x3 -> x1, local copies, waits for them, and re-layouts: 1.97 us -> 0.72 us  [local(): return (query_grad, total[:share // 2], total[share // 2:])]
    convert_element_type x0 -> x1, other arithmetic: none -> 1.13 us  [local(): query_grad = (query_sum * scale).astype(bf16).reshape(toks, heads, dim)]
    ppermute x9 -> x8, starting transfers between devices: 13.8 us -> 12.7 us  [moved(): return lax.ppermute(block, ('ctx', 'head'), route)]
    convert_element_type x1, other arithmetic: 1.16 us -> 0.2 us  [local(): total = total.astype(bf16)]
  transfers between devices with their start and end apart: 9 -> 8, of which waited for: 1 -> 3; matrix products, arithmetic and copies ran while one was open for 4% -> 2% of each run, Pallas kernels for 38% -> 56%
where the time goes in v1:
time: 48.6 us; the launch traced here: 48.1 us
  Pallas kernels  26.7 us (55%)
  starting transfers between devices  12.7 us (26%)
  waiting for transfers between devices  6.02 us (12%)
  other arithmetic  1.33 us (3%)
  local copies, waits for them, and re-layouts  0.73 us (2%)
  between operations  0.68 us (1%)
    pallas_call x3, Pallas kernels, call(): pl.pallas_call(kernel, out_shape=outs, in_specs=where, out_specs=[VMEM] *...  26.7 us
    ppermute x8, starting transfers between devices, moved(): return lax.ppermute(block, ('ctx', 'head'), route)  12.7 us
    ppermute x8, waiting for transfers between devices, moved(): return lax.ppermute(block, ('ctx', 'head'), route)  6.02 us
    convert_element_type x1, other arithmetic, local(): query_grad = (query_sum * scale).astype(bf16).reshape(toks, heads, dim)  1.13 us
  transfers between devices with their start and end apart: 8, of which 3 were waited for; matrix products, arithmetic and copies ran while one was open for 2% of the time, Pallas kernels for 56%

profile of v1, /device:TPU:0, one launch (start us, length us, event | category | flops | bytes accessed | tf_op | source)
XLA Modules:
  0.0 48.1 jit_solution(15619934691231562912)
XLA Ops:
  0.6 3.0 %collective-permute-start.1 = (bf16[1024,128]{1,0:T(8,128)(2,1)}, bf16[1024,128]{1,0:T(8,128)(2,1)S(1)}, u32[]{:S(2)}, u32[]{:S(2)}) collective-permute-start(bf16[1024,128]{1,0:T(8,128)(2,1)} %refs_4_.1), channel_id=1, source_target_pairs={{0,4},{1,5},{2,6},{3,7},{4,8},{5,9},{6,10},{7,11},{8,12},{9,13},{1... | collective-permute-start | bytes 786440 | tf_op jit(solution)/shard_map/ppermute | solution.py:213
  3.7 1.5 %collective-permute-start.2 = (bf16[1024,128]{1,0:T(8,128)(2,1)}, bf16[1024,128]{1,0:T(8,128)(2,1)S(1)}, u32[]{:S(2)}, u32[]{:S(2)}) collective-permute-start(bf16[1024,128]{1,0:T(8,128)(2,1)} %refs_5_.1), channel_id=1, source_target_pairs={{0,4},{1,5},{2,6},{3,7},{4,8},{5,9},{6,10},{7,11},{8,12},{9,13},{1... | collective-permute-start | bytes 786440 | tf_op jit(solution)/shard_map/ppermute | solution.py:213
  5.2 0.0 copy-start
  5.2 0.0 copy-start.1
  5.2 0.0 copy-start.2
  5.2 11.1 %own.1 = (f32[4096,128]{1,0:T(8,128)S(1)}, f32[8,4096]{1,0:T(8,128)S(1)}, bf16[2048,128]{1,0:T(8,128)(2,1)S(1)}, f32[1024,128]{1,0:T(8,128)S(1)}, bf16[1024,128]{1,0:T(8,128)(2,1)S(1)}) custom-call(bf16[4096,128]{1,0:T(8,128)(2,1)} %bitcast.4, bf16[4096,128]{1,0:T(8,128)(2,1)} %bitcast.7, bf16[4096,128]{1,0:T(8,128)(2,1)} %bitcast.11, f32[4,1024]{1,0:T(4,128)} %refs_3_.1, ...), custom_call_target="tpu_custom_call" | custom-call | flops 16106127360 | bytes 6291456 | tf_op jit(solution)/shard_map/own/pallas_call | solution.py:193
  16.2 1.6 %collective-permute-start.3 = (bf16[1024,128]{1,0:T(8,128)(2,1)S(1)}, bf16[1024,128]{1,0:T(8,128)(2,1)S(1)}, u32[]{:S(2)}, u32[]{:S(2)}) collective-permute-start(bf16[1024,128]{1,0:T(8,128)(2,1)S(1)} %get-tuple-element.20), channel_id=1, source_target_pairs={{0,1},{1,0},{2,3},{3,2},{4,5},{5,4},{6,7},{7,6},{8,9},{9,8},{10,11... | collective-permute-start | bytes 786440 | tf_op jit(solution)/shard_map/ppermute | solution.py:213
  17.8 0.0 collective-permute-start
  17.8 0.0 collective-permute-done.1.refs_3_
  17.8 1.0 %collective-permute-done.2.refs_4_ = bf16[1024,128]{1,0:T(8,128)(2,1)S(1)} collective-permute-done((bf16[1024,128]{1,0:T(8,128)(2,1)}, bf16[1024,128]{1,0:T(8,128)(2,1)S(1)}, u32[]{:S(2)}, u32[]{:S(2)}) %collective-permute-start.2) | collective-permute-done | bytes 262176 | tf_op jit(solution)/shard_map/ppermute | solution.py:213
  18.8 0.0 copy-done
  18.8 0.0 copy-done.1
  18.8 0.0 copy-done.2
  18.8 7.8 %far.2 = (f32[4096,128]{1,0:T(8,128)S(1)}, bf16[1024,128]{1,0:T(8,128)(2,1)S(1)}, bf16[1024,128]{1,0:T(8,128)(2,1)S(1)}) custom-call(s32[32]{0:T(128)S(1)} %copy-done.2, bf16[4096,128]{1,0:T(8,128)(2,1)S(1)} %bitcast.5, bf16[4096,128]{1,0:T(8,128)(2,1)S(1)} %bitcast.8, f32[8,4096]{1,0:T(8,128)S(1)} %get-tuple-element.14.refs_2_, ...), custom_call_target="tpu_custom_call", output_to_operand_aliasing={{0}: (6, {})} | custom-call | flops 10737418240 | bytes 6291456 | tf_op jit(solution)/shard_map/far/pallas_call | solution.py:193
  26.7 2.3 %collective-permute-start.4 = (bf16[1024,128]{1,0:T(8,128)(2,1)S(1)}, bf16[1024,128]{1,0:T(8,128)(2,1)S(1)}, u32[]{:S(2)}, u32[]{:S(2)}) collective-permute-start(bf16[1024,128]{1,0:T(8,128)(2,1)S(1)} %get-tuple-element.21), channel_id=1, source_target_pairs={{0,28},{1,29},{2,30},{3,31},{4,0},{5,1},{6,2},{7,3},{8,4},{9,5},{1... | collective-permute-start | bytes 786440 | tf_op jit(solution)/shard_map/ppermute | solution.py:213
  28.9 1.9 %collective-permute-start.5 = (bf16[1024,128]{1,0:T(8,128)(2,1)S(1)}, bf16[1024,128]{1,0:T(8,128)(2,1)S(1)}, u32[]{:S(2)}, u32[]{:S(2)}) collective-permute-start(bf16[1024,128]{1,0:T(8,128)(2,1)S(1)} %get-tuple-element.22), channel_id=1, source_target_pairs={{0,29},{1,28},{2,31},{3,30},{4,1},{5,0},{6,3},{7,2},{8,5},{9,4},{1... | collective-permute-start | bytes 786440 | tf_op jit(solution)/shard_map/ppermute | solution.py:213
  30.8 0.0 collective-permute-done.refs_3_
  30.8 7.8 %far.3 = (f32[4096,128]{1,0:T(8,128)S(1)}, bf16[1024,128]{1,0:T(8,128)(2,1)S(1)}, bf16[1024,128]{1,0:T(8,128)(2,1)S(1)}) custom-call(s32[32]{0:T(128)S(1)} %copy-done.2, bf16[4096,128]{1,0:T(8,128)(2,1)S(1)} %bitcast.6, bf16[4096,128]{1,0:T(8,128)(2,1)S(1)} %bitcast.9, f32[8,4096]{1,0:T(8,128)S(1)} %get-tuple-element.14.refs_2_, ...), custom_call_target="tpu_custom_call", output_to_operand_aliasing={{0}: (5, {})} | custom-call | flops 10737418240 | bytes 6291456 | tf_op jit(solution)/shard_map/far/pallas_call | solution.py:193
  38.6 0.6 %collective-permute-start.6 = (bf16[1024,128]{1,0:T(8,128)(2,1)S(1)}, bf16[1024,128]{1,0:T(8,128)(2,1)S(1)}, u32[]{:S(2)}, u32[]{:S(2)}) collective-permute-start(bf16[1024,128]{1,0:T(8,128)(2,1)S(1)} %get-tuple-element.23), channel_id=1, source_target_pairs={{0,30},{1,31},{2,0},{3,1},{4,2},{5,3},{6,4},{7,5},{8,6},{9,7},{10,... | collective-permute-start | bytes 786440 | tf_op jit(solution)/shard_map/ppermute | solution.py:213
  39.3 1.8 %collective-permute-start.7 = (bf16[1024,128]{1,0:T(8,128)(2,1)S(1)}, bf16[1024,128]{1,0:T(8,128)(2,1)S(1)}, u32[]{:S(2)}, u32[]{:S(2)}) collective-permute-start(bf16[1024,128]{1,0:T(8,128)(2,1)S(1)} %get-tuple-element.24), channel_id=1, source_target_pairs={{0,31},{1,30},{2,1},{3,0},{4,3},{5,2},{6,5},{7,4},{8,7},{9,6},{10,... | collective-permute-start | bytes 786440 | tf_op jit(solution)/shard_map/ppermute | solution.py:213
  41.1 1.1 %multiply_convert_fusion = bf16[4096,128]{1,0:T(8,128)(2,1)} fusion(f32[4096,128]{1,0:T(8,128)S(1)} %get-tuple-element.18), kind=kLoop, calls=%fused_computation | loop fusion | flops 1048576 | bytes 3145728 | tf_op jit(solution)/shard_map/convert_element_type | solution.py:267
  42.2 0.0 collective-permute-done.3
  42.2 0.0 collective-permute-done.4
  42.2 0.0 collective-permute-done.5
  42.2 1.8 %collective-permute-done.6 = bf16[1024,128]{1,0:T(8,128)(2,1)S(1)} collective-permute-done((bf16[1024,128]{1,0:T(8,128)(2,1)S(1)}, bf16[1024,128]{1,0:T(8,128)(2,1)S(1)}, u32[]{:S(2)}, u32[]{:S(2)}) %collective-permute-start.6) | collective-permute-done | bytes 262176 | tf_op jit(solution)/shard_map/ppermute | solution.py:213
  44.1 3.2 %collective-permute-done.7 = bf16[1024,128]{1,0:T(8,128)(2,1)S(1)} collective-permute-done((bf16[1024,128]{1,0:T(8,128)(2,1)S(1)}, bf16[1024,128]{1,0:T(8,128)(2,1)S(1)}, u32[]{:S(2)}, u32[]{:S(2)}) %collective-permute-start.7) | collective-permute-done | bytes 262176 | tf_op jit(solution)/shard_map/ppermute | solution.py:213
  47.2 0.2 add_convert_fusion
  47.4 0.7 %fusion = (bf16[512,128]{1,0:T(8,128)(2,1)}, bf16[512,128]{1,0:T(8,128)(2,1)}) fusion(bf16[1024,128]{1,0:T(8,128)(2,1)S(1)} %add_convert_fusion), kind=kLoop, calls=%fused_computation.2 | loop fusion | bytes 524288 | tf_op jit(solution)/shard_map/slice | solution.py:268
Async XLA Ops:
  0.6 17.2 %collective-permute-start.1 = (bf16[1024,128]{1,0:T(8,128)(2,1)}, bf16[1024,128]{1,0:T(8,128)(2,1)S(1)}, u32[]{:S(2)}, u32[]{:S(2)}) collective-permute-start(bf16[1024,128]{1,0:T(8,128)(2,1)} %refs_4_.1), channel_id=1, source_target_pairs={{0,4},{1,5},{2,6},{3,7},{4,8},{5,9},{6,10},{7,11},{8,12},{9,13},{1... | collective-permute-start | bytes 786440 | tf_op jit(solution)/shard_map/ppermute | solution.py:213
  3.7 15.2 %collective-permute-start.2 = (bf16[1024,128]{1,0:T(8,128)(2,1)}, bf16[1024,128]{1,0:T(8,128)(2,1)S(1)}, u32[]{:S(2)}, u32[]{:S(2)}) collective-permute-start(bf16[1024,128]{1,0:T(8,128)(2,1)} %refs_5_.1), channel_id=1, source_target_pairs={{0,4},{1,5},{2,6},{3,7},{4,8},{5,9},{6,10},{7,11},{8,12},{9,13},{1... | collective-permute-start | bytes 786440 | tf_op jit(solution)/shard_map/ppermute | solution.py:213
  5.2 13.7 %copy-start = (bf16[1024,4,128]{2,1,0:T(4,128)(2,1)S(1)}, bf16[1024,4,128]{2,1,0:T(4,128)(2,1)}, u32[]{:S(2)}) copy-start(bf16[1024,4,128]{2,1,0:T(4,128)(2,1)} %param.7) | copy-start | bytes 3145732
  5.2 13.7 %copy-start.1 = (bf16[1024,4,128]{2,1,0:T(4,128)(2,1)S(1)}, bf16[1024,4,128]{2,1,0:T(4,128)(2,1)}, u32[]{:S(2)}) copy-start(bf16[1024,4,128]{2,1,0:T(4,128)(2,1)} %param.11) | copy-start | bytes 3145732
  5.2 13.7 %copy-start.2 = (s32[32]{0:T(128)S(1)}, s32[32]{0:T(128)}, u32[]{:S(2)}) copy-start(s32[32]{0:T(128)} %span_ids.3) | copy-start | bytes 388
  16.2 26.0 %collective-permute-start.3 = (bf16[1024,128]{1,0:T(8,128)(2,1)S(1)}, bf16[1024,128]{1,0:T(8,128)(2,1)S(1)}, u32[]{:S(2)}, u32[]{:S(2)}) collective-permute-start(bf16[1024,128]{1,0:T(8,128)(2,1)S(1)} %get-tuple-element.20), channel_id=1, source_target_pairs={{0,1},{1,0},{2,3},{3,2},{4,5},{5,4},{6,7},{7,6},{8,9},{9,8},{10,11... | collective-permute-start | bytes 786440 | tf_op jit(solution)/shard_map/ppermute | solution.py:213
  17.8 13.0 %collective-permute-start = (bf16[2048,128]{1,0:T(8,128)(2,1)S(1)}, bf16[2048,128]{1,0:T(8,128)(2,1)S(1)}, u32[]{:S(2)}, u32[]{:S(2)}) collective-permute-start(bf16[2048,128]{1,0:T(8,128)(2,1)S(1)} %get-tuple-element.15), channel_id=1, source_target_pairs={{0,2},{1,3},{2,4},{3,5},{4,6},{5,7},{6,8},{7,9},{8,10},{9,11},{10,... | collective-permute-start | bytes 1572872 | tf_op jit(solution)/shard_map/ppermute | solution.py:213
  26.7 15.6 %collective-permute-start.4 = (bf16[1024,128]{1,0:T(8,128)(2,1)S(1)}, bf16[1024,128]{1,0:T(8,128)(2,1)S(1)}, u32[]{:S(2)}, u32[]{:S(2)}) collective-permute-start(bf16[1024,128]{1,0:T(8,128)(2,1)S(1)} %get-tuple-element.21), channel_id=1, source_target_pairs={{0,28},{1,29},{2,30},{3,31},{4,0},{5,1},{6,2},{7,3},{8,4},{9,5},{1... | collective-permute-start | bytes 786440 | tf_op jit(solution)/shard_map/ppermute | solution.py:213
  28.9 13.3 %collective-permute-start.5 = (bf16[1024,128]{1,0:T(8,128)(2,1)S(1)}, bf16[1024,128]{1,0:T(8,128)(2,1)S(1)}, u32[]{:S(2)}, u32[]{:S(2)}) collective-permute-start(bf16[1024,128]{1,0:T(8,128)(2,1)S(1)} %get-tuple-element.22), channel_id=1, source_target_pairs={{0,29},{1,28},{2,31},{3,30},{4,1},{5,0},{6,3},{7,2},{8,5},{9,4},{1... | collective-permute-start | bytes 786440 | tf_op jit(solution)/shard_map/ppermute | solution.py:213
  38.6 5.4 %collective-permute-start.6 = (bf16[1024,128]{1,0:T(8,128)(2,1)S(1)}, bf16[1024,128]{1,0:T(8,128)(2,1)S(1)}, u32[]{:S(2)}, u32[]{:S(2)}) collective-permute-start(bf16[1024,128]{1,0:T(8,128)(2,1)S(1)} %get-tuple-element.23), channel_id=1, source_target_pairs={{0,30},{1,31},{2,0},{3,1},{4,2},{5,3},{6,4},{7,5},{8,6},{9,7},{10,... | collective-permute-start | bytes 786440 | tf_op jit(solution)/shard_map/ppermute | solution.py:213
  39.3 8.0 %collective-permute-start.7 = (bf16[1024,128]{1,0:T(8,128)(2,1)S(1)}, bf16[1024,128]{1,0:T(8,128)(2,1)S(1)}, u32[]{:S(2)}, u32[]{:S(2)}) collective-permute-start(bf16[1024,128]{1,0:T(8,128)(2,1)S(1)} %get-tuple-element.24), channel_id=1, source_target_pairs={{0,31},{1,30},{2,1},{3,0},{4,3},{5,2},{6,5},{7,4},{8,7},{9,6},{10,... | collective-permute-start | bytes 786440 | tf_op jit(solution)/shard_map/ppermute | solution.py:213

commit v2 on v1

--- a/solution.py
+++ b/solution.py
@@ -53,28 +53,37 @@
         out[1:2, pl.ds(row, tile)] = (dot(ones, high, NT) + dot(ones, low, NT))[0:1]
 
 
-def tile_grads(
-    refs, accs, row, key, length, scale, triangle=None
-):
-    query_ref, grad_ref, key_ref, value_ref, terms_ref, tile = refs
+def tile_grads(group, accs, scale, tiles):
+    query_ref, grad_ref, key_ref, value_ref, terms_ref, tile = group
     query_acc, key_acc, value_acc = accs
-    q = query_ref[pl.ds(row, tile), :]
-    g = grad_ref[pl.ds(row, tile), :]
-    k = key_ref[pl.ds(key, length), :]
-    v = value_ref[pl.ds(key, length), :]
-    norm = terms_ref[0:1, pl.ds(row, tile)]
-    delta = terms_ref[1:2, pl.ds(row, tile)]
-    scores = dot(k, q, NT)
-    prob = jnp.exp2(scores * (scale * math.log2(math.e)) - norm)
-    if triangle is not None:
-        edge = length - triangle.shape[0]
-        last = jnp.where(triangle, prob[edge:], 0.0)
-        prob = last if edge == 0 else jnp.concatenate([prob[:edge], last], axis=0)
-    value_acc[pl.ds(key, length), :] += dot(prob.astype(jnp.bfloat16), g, NN)
-    dprob = dot(v, g, NT)
-    dscore = (prob * (dprob - delta)).astype(jnp.bfloat16)
-    key_acc[pl.ds(key, length), :] += dot(dscore, q, NN)
-    query_acc[pl.ds(row, tile), :] += dot(dscore, k, TN)
+
+    def opened(row, key, length, _):
+        k = key_ref[pl.ds(key, length), :]
+        v = value_ref[pl.ds(key, length), :]
+        scores = dot(k, query_ref[pl.ds(row, tile), :], NT)
+        return scores, dot(v, grad_ref[pl.ds(row, tile), :], NT)
+
+    def closed(row, key, length, triangle, scores, dprob):
+        norm = terms_ref[0:1, pl.ds(row, tile)]
+        delta = terms_ref[1:2, pl.ds(row, tile)]
+        prob = jnp.exp2(scores * (scale * math.log2(math.e)) - norm)
+        if triangle is not None:
+            edge = length - triangle.shape[0]
+            last = jnp.where(triangle, prob[edge:], 0.0)
+            prob = last if edge == 0 else jnp.concatenate([prob[:edge], last], axis=0)
+        dscore = (prob * (dprob - delta)).astype(jnp.bfloat16)
+        value_acc[pl.ds(key, length), :] += dot(
+            prob.astype(jnp.bfloat16), grad_ref[pl.ds(row, tile), :], NN
+        )
+        key_acc[pl.ds(key, length), :] += dot(dscore, query_ref[pl.ds(row, tile), :], NN)
+        query_acc[pl.ds(row, tile), :] += dot(dscore, key_ref[pl.ds(key, length), :], TN)
+
+    ahead = opened(*tiles[0])
+    for index, this in enumerate(tiles):
+        now = ahead
+        if index + 1 < len(tiles):
+            ahead = opened(*tiles[index + 1])
+        closed(*this, *now)
 
 
 def span_pair(span_ids, holder):
@@ -133,18 +142,21 @@
             copy.wait()
         row_terms(heads, tile, index, (grad_ref, outputs_ref, norm_ref), terms_ref)
         key = pl.multiple_of(index * half, half)
-        for part in range(half // per):
-            row = pl.multiple_of(index * rows + part * tile, tile)
-            tile_grads(group, accs, row, key, (part + 1) * per, scale, triangle)
+        tiles = [
+            (pl.multiple_of(index * rows + part * tile, tile), key, (part + 1) * per, triangle)
+            for part in range(half // per)
+        ]
+        tile_grads(group, accs, scale, tiles)
 
     first, second = span_pair(span_ids, lax.axis_index("ctx"))
     low = jnp.where(first > second, 1, 0)
 
-    @pl.loop(0, rows // tile)
-    def _(part):
-        row = pl.multiple_of((1 - low) * rows + part * tile, tile)
-        tile_grads(group, accs, row, pl.multiple_of(low * half, half), half, scale)
-
+    key = pl.multiple_of(low * half, half)
+    tiles = [
+        (pl.multiple_of((1 - low) * rows + part * tile, tile), key, half, None)
+        for part in range(rows // tile)
+    ]
+    tile_grads(group, accs, scale, tiles)
     put_shares(outs, key_acc, value_acc, scale)
 
 
@@ -171,13 +183,14 @@
     our_high = jnp.where(mine[0] > mine[1], 0, 1)
     their_low = jnp.where(theirs[0] > theirs[1], 1, 0)
 
-    @pl.loop(0, 2 * per)
-    def _(index):
-        item = index // per
+    @pl.loop(0, 2)
+    def _(item):
         row_half = jnp.where(high_only, our_high, item)
         key_half = jnp.where(high_only, item, their_low)
-        row = pl.multiple_of(row_half * half * heads + lax.rem(index, per) * tile, tile)
-        tile_grads(group, accs, row, pl.multiple_of(key_half * half, half), half, scale)
+        row = pl.multiple_of(row_half * half * heads, half * heads)
+        key = pl.multiple_of(key_half * half, half)
+        tiles = [(pl.multiple_of(row + part * tile, tile), key, half, None) for part in range(per)]
+        tile_grads(group, accs, scale, tiles)
 
     put_shares(outs, key_acc, value_acc, scale)
 

time: 48.6 us -> 46.1 us (0.949)
  Pallas kernels: 26.7 us -> 23 us
  waiting for transfers between devices: 6.02 us -> 8.86 us
  starting transfers between devices: 12.7 us -> 11.3 us
    pallas_call x3, Pallas kernels: 26.7 us -> 23 us  [call(): pl.pallas_call(kernel, out_shape=outs, in_specs=where, out_specs=[VMEM] *...]
    ppermute x8, waiting for transfers between devices: 6.02 us -> 8.86 us  [moved(): return lax.ppermute(block, ('ctx', 'head'), route)]
    ppermute x8, starting transfers between devices: 12.7 us -> 11.3 us  [moved(): return lax.ppermute(block, ('ctx', 'head'), route)]
  transfers between devices with their start and end apart: 8 -> 8, of which waited for: 3 -> 5; matrix products, arithmetic and copies ran while one was open for 2% -> 2% of each run, Pallas kernels for 56% -> 50%
where the time goes in v2:
time: 46.1 us; the launch traced here: 45.9 us
  Pallas kernels  23 us (50%)
  starting transfers between devices  11.3 us (25%)
  waiting for transfers between devices  8.86 us (19%)
  other arithmetic  1.33 us (3%)
  local copies, waits for them, and re-layouts  0.73 us (2%)
  between operations  0.68 us (1%)
    pallas_call x3, Pallas kernels, call(): pl.pallas_call(kernel, out_shape=outs, in_specs=where, out_specs=[VMEM] *...  23 us
    ppermute x8, starting transfers between devices, moved(): return lax.ppermute(block, ('ctx', 'head'), route)  11.3 us
    ppermute x8, waiting for transfers between devices, moved(): return lax.ppermute(block, ('ctx', 'head'), route)  8.86 us
    convert_element_type x1, other arithmetic, local(): query_grad = (query_sum * scale).astype(bf16).reshape(toks, heads, dim)  1.13 us
  transfers between devices with their start and end apart: 8, of which 5 were waited for; matrix products, arithmetic and copies ran while one was open for 2% of the time, Pallas kernels for 50%

profile of v2, /device:TPU:0, one launch (start us, length us, event | category | flops | bytes accessed | tf_op | source)
XLA Modules:
  0.0 45.9 jit_solution(8158405644944391774)
XLA Ops:
  0.6 3.0 %collective-permute-start.1 = (bf16[1024,128]{1,0:T(8,128)(2,1)}, bf16[1024,128]{1,0:T(8,128)(2,1)S(1)}, u32[]{:S(2)}, u32[]{:S(2)}) collective-permute-start(bf16[1024,128]{1,0:T(8,128)(2,1)} %refs_4_.1), channel_id=1, source_target_pairs={{0,4},{1,5},{2,6},{3,7},{4,8},{5,9},{6,10},{7,11},{8,12},{9,13},{1... | collective-permute-start | bytes 786440 | tf_op jit(solution)/shard_map/ppermute | solution.py:226
  3.7 1.5 %collective-permute-start.2 = (bf16[1024,128]{1,0:T(8,128)(2,1)}, bf16[1024,128]{1,0:T(8,128)(2,1)S(1)}, u32[]{:S(2)}, u32[]{:S(2)}) collective-permute-start(bf16[1024,128]{1,0:T(8,128)(2,1)} %refs_5_.1), channel_id=1, source_target_pairs={{0,4},{1,5},{2,6},{3,7},{4,8},{5,9},{6,10},{7,11},{8,12},{9,13},{1... | collective-permute-start | bytes 786440 | tf_op jit(solution)/shard_map/ppermute | solution.py:226
  5.2 0.0 copy-start
  5.2 0.0 copy-start.1
  5.2 0.0 copy-start.2
  5.2 9.7 %own.1 = (f32[4096,128]{1,0:T(8,128)S(1)}, f32[8,4096]{1,0:T(8,128)S(1)}, bf16[2048,128]{1,0:T(8,128)(2,1)S(1)}, f32[1024,128]{1,0:T(8,128)S(1)}, bf16[1024,128]{1,0:T(8,128)(2,1)S(1)}) custom-call(bf16[4096,128]{1,0:T(8,128)(2,1)} %bitcast.4, bf16[4096,128]{1,0:T(8,128)(2,1)} %bitcast.7, bf16[4096,128]{1,0:T(8,128)(2,1)} %bitcast.11, f32[4,1024]{1,0:T(4,128)} %refs_3_.1, ...), custom_call_target="tpu_custom_call" | custom-call | flops 16106127360 | bytes 6291456 | tf_op jit(solution)/shard_map/own/pallas_call | solution.py:206
  14.9 1.6 %collective-permute-start.3 = (bf16[1024,128]{1,0:T(8,128)(2,1)S(1)}, bf16[1024,128]{1,0:T(8,128)(2,1)S(1)}, u32[]{:S(2)}, u32[]{:S(2)}) collective-permute-start(bf16[1024,128]{1,0:T(8,128)(2,1)S(1)} %get-tuple-element.20), channel_id=1, source_target_pairs={{0,1},{1,0},{2,3},{3,2},{4,5},{5,4},{6,7},{7,6},{8,9},{9,8},{10,11... | collective-permute-start | bytes 786440 | tf_op jit(solution)/shard_map/ppermute | solution.py:226
  16.4 0.0 collective-permute-start
  16.5 0.0 collective-permute-done.1.refs_3_
  16.5 2.4 %collective-permute-done.2.refs_4_ = bf16[1024,128]{1,0:T(8,128)(2,1)S(1)} collective-permute-done((bf16[1024,128]{1,0:T(8,128)(2,1)}, bf16[1024,128]{1,0:T(8,128)(2,1)S(1)}, u32[]{:S(2)}, u32[]{:S(2)}) %collective-permute-start.2) | collective-permute-done | bytes 262176 | tf_op jit(solution)/shard_map/ppermute | solution.py:226
  18.8 0.0 copy-done
  18.8 0.0 copy-done.1
  18.8 0.0 copy-done.2
  18.8 6.6 %far.2 = (f32[4096,128]{1,0:T(8,128)S(1)}, bf16[1024,128]{1,0:T(8,128)(2,1)S(1)}, bf16[1024,128]{1,0:T(8,128)(2,1)S(1)}) custom-call(s32[32]{0:T(128)S(1)} %copy-done.2, bf16[4096,128]{1,0:T(8,128)(2,1)S(1)} %bitcast.5, bf16[4096,128]{1,0:T(8,128)(2,1)S(1)} %bitcast.8, f32[8,4096]{1,0:T(8,128)S(1)} %get-tuple-element.14.refs_2_, ...), custom_call_target="tpu_custom_call", output_to_operand_aliasing={{0}: (6, {})} | custom-call | flops 10737418240 | bytes 6291456 | tf_op jit(solution)/shard_map/far/pallas_call | solution.py:206
  25.5 1.8 %collective-permute-start.4 = (bf16[1024,128]{1,0:T(8,128)(2,1)S(1)}, bf16[1024,128]{1,0:T(8,128)(2,1)S(1)}, u32[]{:S(2)}, u32[]{:S(2)}) collective-permute-start(bf16[1024,128]{1,0:T(8,128)(2,1)S(1)} %get-tuple-element.21), channel_id=1, source_target_pairs={{0,28},{1,29},{2,30},{3,31},{4,0},{5,1},{6,2},{7,3},{8,4},{9,5},{1... | collective-permute-start | bytes 786440 | tf_op jit(solution)/shard_map/ppermute | solution.py:226
  27.3 2.3 %collective-permute-start.5 = (bf16[1024,128]{1,0:T(8,128)(2,1)S(1)}, bf16[1024,128]{1,0:T(8,128)(2,1)S(1)}, u32[]{:S(2)}, u32[]{:S(2)}) collective-permute-start(bf16[1024,128]{1,0:T(8,128)(2,1)S(1)} %get-tuple-element.22), channel_id=1, source_target_pairs={{0,29},{1,28},{2,31},{3,30},{4,1},{5,0},{6,3},{7,2},{8,5},{9,4},{1... | collective-permute-start | bytes 786440 | tf_op jit(solution)/shard_map/ppermute | solution.py:226
  29.6 0.0 collective-permute-done.refs_3_
  29.6 6.6 %far.3 = (f32[4096,128]{1,0:T(8,128)S(1)}, bf16[1024,128]{1,0:T(8,128)(2,1)S(1)}, bf16[1024,128]{1,0:T(8,128)(2,1)S(1)}) custom-call(s32[32]{0:T(128)S(1)} %copy-done.2, bf16[4096,128]{1,0:T(8,128)(2,1)S(1)} %bitcast.6, bf16[4096,128]{1,0:T(8,128)(2,1)S(1)} %bitcast.9, f32[8,4096]{1,0:T(8,128)S(1)} %get-tuple-element.14.refs_2_, ...), custom_call_target="tpu_custom_call", output_to_operand_aliasing={{0}: (5, {})} | custom-call | flops 10737418240 | bytes 6291456 | tf_op jit(solution)/shard_map/far/pallas_call | solution.py:206
  36.2 0.1 collective-permute-start.6
  36.3 1.0 %collective-permute-start.7 = (bf16[1024,128]{1,0:T(8,128)(2,1)S(1)}, bf16[1024,128]{1,0:T(8,128)(2,1)S(1)}, u32[]{:S(2)}, u32[]{:S(2)}) collective-permute-start(bf16[1024,128]{1,0:T(8,128)(2,1)S(1)} %get-tuple-element.24), channel_id=1, source_target_pairs={{0,31},{1,30},{2,1},{3,0},{4,3},{5,2},{6,5},{7,4},{8,7},{9,6},{10,... | collective-permute-start | bytes 786440 | tf_op jit(solution)/shard_map/ppermute | solution.py:226
  37.3 1.1 %multiply_convert_fusion = bf16[4096,128]{1,0:T(8,128)(2,1)} fusion(f32[4096,128]{1,0:T(8,128)S(1)} %get-tuple-element.18), kind=kLoop, calls=%fused_computation | loop fusion | flops 1048576 | bytes 3145728 | tf_op jit(solution)/shard_map/convert_element_type | solution.py:280
  38.5 0.0 collective-permute-done.3
  38.5 0.5 %collective-permute-done.4 = bf16[1024,128]{1,0:T(8,128)(2,1)S(1)} collective-permute-done((bf16[1024,128]{1,0:T(8,128)(2,1)S(1)}, bf16[1024,128]{1,0:T(8,128)(2,1)S(1)}, u32[]{:S(2)}, u32[]{:S(2)}) %collective-permute-start.4) | collective-permute-done | bytes 262176 | tf_op jit(solution)/shard_map/ppermute | solution.py:226
  39.0 0.4 collective-permute-done.5
  39.4 2.8 %collective-permute-done.6 = bf16[1024,128]{1,0:T(8,128)(2,1)S(1)} collective-permute-done((bf16[1024,128]{1,0:T(8,128)(2,1)S(1)}, bf16[1024,128]{1,0:T(8,128)(2,1)S(1)}, u32[]{:S(2)}, u32[]{:S(2)}) %collective-permute-start.6) | collective-permute-done | bytes 262176 | tf_op jit(solution)/shard_map/ppermute | solution.py:226
  42.2 2.8 %collective-permute-done.7 = bf16[1024,128]{1,0:T(8,128)(2,1)S(1)} collective-permute-done((bf16[1024,128]{1,0:T(8,128)(2,1)S(1)}, bf16[1024,128]{1,0:T(8,128)(2,1)S(1)}, u32[]{:S(2)}, u32[]{:S(2)}) %collective-permute-start.7) | collective-permute-done | bytes 262176 | tf_op jit(solution)/shard_map/ppermute | solution.py:226
  45.0 0.2 add_convert_fusion
  45.2 0.7 %fusion = (bf16[512,128]{1,0:T(8,128)(2,1)}, bf16[512,128]{1,0:T(8,128)(2,1)}) fusion(bf16[1024,128]{1,0:T(8,128)(2,1)S(1)} %add_convert_fusion), kind=kLoop, calls=%fused_computation.2 | loop fusion | bytes 524288 | tf_op jit(solution)/shard_map/slice | solution.py:281
Async XLA Ops:
  0.6 15.8 %collective-permute-start.1 = (bf16[1024,128]{1,0:T(8,128)(2,1)}, bf16[1024,128]{1,0:T(8,128)(2,1)S(1)}, u32[]{:S(2)}, u32[]{:S(2)}) collective-permute-start(bf16[1024,128]{1,0:T(8,128)(2,1)} %refs_4_.1), channel_id=1, source_target_pairs={{0,4},{1,5},{2,6},{3,7},{4,8},{5,9},{6,10},{7,11},{8,12},{9,13},{1... | collective-permute-start | bytes 786440 | tf_op jit(solution)/shard_map/ppermute | solution.py:226
  3.7 15.2 %collective-permute-start.2 = (bf16[1024,128]{1,0:T(8,128)(2,1)}, bf16[1024,128]{1,0:T(8,128)(2,1)S(1)}, u32[]{:S(2)}, u32[]{:S(2)}) collective-permute-start(bf16[1024,128]{1,0:T(8,128)(2,1)} %refs_5_.1), channel_id=1, source_target_pairs={{0,4},{1,5},{2,6},{3,7},{4,8},{5,9},{6,10},{7,11},{8,12},{9,13},{1... | collective-permute-start | bytes 786440 | tf_op jit(solution)/shard_map/ppermute | solution.py:226
  5.2 13.7 %copy-start = (bf16[1024,4,128]{2,1,0:T(4,128)(2,1)S(1)}, bf16[1024,4,128]{2,1,0:T(4,128)(2,1)}, u32[]{:S(2)}) copy-start(bf16[1024,4,128]{2,1,0:T(4,128)(2,1)} %param.7) | copy-start | bytes 3145732
  5.2 13.7 %copy-start.1 = (bf16[1024,4,128]{2,1,0:T(4,128)(2,1)S(1)}, bf16[1024,4,128]{2,1,0:T(4,128)(2,1)}, u32[]{:S(2)}) copy-start(bf16[1024,4,128]{2,1,0:T(4,128)(2,1)} %param.11) | copy-start | bytes 3145732
  5.2 13.7 %copy-start.2 = (s32[32]{0:T(128)S(1)}, s32[32]{0:T(128)}, u32[]{:S(2)}) copy-start(s32[32]{0:T(128)} %span_ids.3) | copy-start | bytes 388
  14.9 23.6 %collective-permute-start.3 = (bf16[1024,128]{1,0:T(8,128)(2,1)S(1)}, bf16[1024,128]{1,0:T(8,128)(2,1)S(1)}, u32[]{:S(2)}, u32[]{:S(2)}) collective-permute-start(bf16[1024,128]{1,0:T(8,128)(2,1)S(1)} %get-tuple-element.20), channel_id=1, source_target_pairs={{0,1},{1,0},{2,3},{3,2},{4,5},{5,4},{6,7},{7,6},{8,9},{9,8},{10,11... | collective-permute-start | bytes 786440 | tf_op jit(solution)/shard_map/ppermute | solution.py:226
  16.4 13.2 %collective-permute-start = (bf16[2048,128]{1,0:T(8,128)(2,1)S(1)}, bf16[2048,128]{1,0:T(8,128)(2,1)S(1)}, u32[]{:S(2)}, u32[]{:S(2)}) collective-permute-start(bf16[2048,128]{1,0:T(8,128)(2,1)S(1)} %get-tuple-element.15), channel_id=1, source_target_pairs={{0,2},{1,3},{2,4},{3,5},{4,6},{5,7},{6,8},{7,9},{8,10},{9,11},{10,... | collective-permute-start | bytes 1572872 | tf_op jit(solution)/shard_map/ppermute | solution.py:226
  25.5 13.5 %collective-permute-start.4 = (bf16[1024,128]{1,0:T(8,128)(2,1)S(1)}, bf16[1024,128]{1,0:T(8,128)(2,1)S(1)}, u32[]{:S(2)}, u32[]{:S(2)}) collective-permute-start(bf16[1024,128]{1,0:T(8,128)(2,1)S(1)} %get-tuple-element.21), channel_id=1, source_target_pairs={{0,28},{1,29},{2,30},{3,31},{4,0},{5,1},{6,2},{7,3},{8,4},{9,5},{1... | collective-permute-start | bytes 786440 | tf_op jit(solution)/shard_map/ppermute | solution.py:226
  27.3 12.1 %collective-permute-start.5 = (bf16[1024,128]{1,0:T(8,128)(2,1)S(1)}, bf16[1024,128]{1,0:T(8,128)(2,1)S(1)}, u32[]{:S(2)}, u32[]{:S(2)}) collective-permute-start(bf16[1024,128]{1,0:T(8,128)(2,1)S(1)} %get-tuple-element.22), channel_id=1, source_target_pairs={{0,29},{1,28},{2,31},{3,30},{4,1},{5,0},{6,3},{7,2},{8,5},{9,4},{1... | collective-permute-start | bytes 786440 | tf_op jit(solution)/shard_map/ppermute | solution.py:226
  36.2 5.9 %collective-permute-start.6 = (bf16[1024,128]{1,0:T(8,128)(2,1)S(1)}, bf16[1024,128]{1,0:T(8,128)(2,1)S(1)}, u32[]{:S(2)}, u32[]{:S(2)}) collective-permute-start(bf16[1024,128]{1,0:T(8,128)(2,1)S(1)} %get-tuple-element.23), channel_id=1, source_target_pairs={{0,30},{1,31},{2,0},{3,1},{4,2},{5,3},{6,4},{7,5},{8,6},{9,7},{10,... | collective-permute-start | bytes 786440 | tf_op jit(solution)/shard_map/ppermute | solution.py:226
  36.3 8.7 %collective-permute-start.7 = (bf16[1024,128]{1,0:T(8,128)(2,1)S(1)}, bf16[1024,128]{1,0:T(8,128)(2,1)S(1)}, u32[]{:S(2)}, u32[]{:S(2)}) collective-permute-start(bf16[1024,128]{1,0:T(8,128)(2,1)S(1)} %get-tuple-element.24), channel_id=1, source_target_pairs={{0,31},{1,30},{2,1},{3,0},{4,3},{5,2},{6,5},{7,4},{8,7},{9,6},{10,... | collective-permute-start | bytes 786440 | tf_op jit(solution)/shard_map/ppermute | solution.py:226

commit v3 on v2

--- a/solution.py
+++ b/solution.py
@@ -90,22 +90,25 @@
     return span_ids[2 * holder], span_ids[2 * holder + 1]
 
 
-def put_shares(outs, key_acc, value_acc, scale):
+def put_shares(outs, key_acc, value_acc, scale, more=None):
     parts = len(outs)
     share = key_acc.shape[0] // parts
     x = lax.axis_index("head")
     for away, out in enumerate(outs):
         start = pl.multiple_of(lax.rem(x + away, parts) * share, share)
-        out[0:share, :] = (key_acc[pl.ds(start, share), :] * scale).astype(out.dtype)
-        out[share : 2 * share, :] = value_acc[pl.ds(start, share), :].astype(out.dtype)
-
-
-def own_kernel(heads, tile, scale, parts, *refs):
-    inputs, refs = refs[:7], refs[7:]
-    query_acc, terms_ref, both_ref = refs[:3]
-    outs, refs = refs[3 : 3 + parts], refs[3 + parts :]
-    held, (key_acc, value_acc, sems) = refs[:5], refs[5:]
-    query_ref, grad_ref, outputs_ref, norm_ref, span_ids = held
+        for low, part in (
+            (0, key_acc[pl.ds(start, share), :] * scale),
+            (share, value_acc[pl.ds(start, share), :]),
+        ):
+            if more is not None:
+                part = part + more[away, low : low + share, :].astype(jnp.float32)
+            out[low : low + share, :] = part.astype(out.dtype)
+
+
+def first_kernel(heads, tile, scale, *refs):
+    inputs, refs = refs[:6], refs[6:]
+    query_ref, grad_ref, both_ref, terms_ref, query_acc, key_acc, value_acc = refs[:7]
+    outputs_ref, norm_ref, sems = refs[7:]
     toks = both_ref.shape[0] // 2
     key_ref, value_ref = both_ref.at[pl.ds(0, toks)], both_ref.at[pl.ds(toks, toks)]
     half = toks // 2
@@ -113,14 +116,14 @@
     per = tile // heads
     whole = [
         pltpu.make_async_copy(a, b, sems.at[i, 2])
-        for i, (a, b) in enumerate(zip(inputs[3:], (norm_ref, key_ref, value_ref, span_ids)))
+        for i, (a, b) in enumerate(zip(inputs[3:], (norm_ref, key_ref, value_ref)))
     ]
 
     def halves(index):
         part = pl.ds(pl.multiple_of(index * rows, rows), rows)
         return [
-            pltpu.make_async_copy(inputs[i].at[part], held[i].at[part], sems.at[i, index])
-            for i in (1, 2, 0)
+            pltpu.make_async_copy(a.at[part], b.at[part], sems.at[i, index])
+            for i, (a, b) in enumerate(zip(inputs, (grad_ref, outputs_ref, query_ref)))
         ]
 
     for copy in whole + halves(0) + halves(1):
@@ -148,28 +151,42 @@
         ]
         tile_grads(group, accs, scale, tiles)
 
-    first, second = span_pair(span_ids, lax.axis_index("ctx"))
+
+def last_kernel(heads, tile, scale, parts, span_ids, *refs):
+    query_ref, grad_ref, terms_ref, both_ref, joined_ref = refs[:5]
+    query_acc, key_acc, value_acc = refs[8:11]
+    outs, more = refs[11 : 11 + parts], refs[11 + parts]
+    toks = both_ref.shape[0] // 2
+    key_ref, value_ref = both_ref.at[pl.ds(0, toks)], both_ref.at[pl.ds(toks, toks)]
+    half = toks // 2
+    me = lax.axis_index("ctx")
+    even = lax.rem(me, 2) == 0
+
+    @pl.when(even)
+    def _():
+        more[...] = joined_ref[...]
+
+    @pl.when(jnp.logical_not(even))
+    def _():
+        more[...] = jnp.zeros_like(more)
+
+    first, second = span_pair(span_ids, me)
     low = jnp.where(first > second, 1, 0)
-
     key = pl.multiple_of(low * half, half)
+    rows = half * heads
     tiles = [
         (pl.multiple_of((1 - low) * rows + part * tile, tile), key, half, None)
         for part in range(rows // tile)
     ]
-    tile_grads(group, accs, scale, tiles)
-    put_shares(outs, key_acc, value_acc, scale)
-
-
-def far_kernel(heads, tile, scale, parts, step, count, span_ids, *refs):
-    query_ref, grad_ref, terms_ref = refs[:3]
-    if count == 1:
-        toks = refs[3].shape[0] // 2
-        key_ref, value_ref = refs[3].at[pl.ds(0, toks)], refs[3].at[pl.ds(toks, toks)]
-    else:
-        key_ref, value_ref = refs[3:5]
-    query_acc = refs[4 + count]
-    outs = refs[5 + count : 5 + count + parts]
-    key_acc, value_acc = refs[5 + count + parts :]
+    group = (query_ref, grad_ref, key_ref, value_ref, terms_ref, tile)
+    tile_grads(group, (query_acc, key_acc, value_acc), scale, tiles)
+    put_shares(outs, key_acc, value_acc, scale, more)
+
+
+def far_kernel(heads, tile, scale, parts, step, span_ids, *refs):
+    query_ref, grad_ref, terms_ref, key_ref, value_ref = refs[:5]
+    query_acc, outs = refs[6], refs[7:-2]
+    key_acc, value_acc = refs[-2:]
     half = key_ref.shape[0] // 2
     key_acc[...] = jnp.zeros_like(key_acc)
     value_acc[...] = jnp.zeros_like(value_acc)
@@ -192,6 +209,8 @@
         tiles = [(pl.multiple_of(row + part * tile, tile), key, half, None) for part in range(per)]
         tile_grads(group, accs, scale, tiles)
 
+    if len(outs) == 1:
+        outs = [outs[0].at[away] for away in range(parts)]
     put_shares(outs, key_acc, value_acc, scale)
 
 
@@ -219,7 +238,7 @@
 def moved(block, back, away):
     holders, parts = lax.axis_size("ctx"), lax.axis_size("head")
     route = [
-        (h * parts + x, ((h - back) % holders) * parts + (x + away) % parts)
+        (h * parts + x, ((h - back[h % 2]) % holders) * parts + (x + away) % parts)
         for h in range(holders)
         for x in range(parts)
     ]
@@ -238,42 +257,58 @@
     share = 2 * toks // parts
     f32, bf16 = jnp.float32, jnp.bfloat16
     shape = jax.ShapeDtypeStruct
-
-    accs = [pltpu.VMEM((toks, dim), f32)] * 2
-    far = moved(keys, 1 - STEPS, 0), moved(values, 1 - STEPS, 0)
-
+    grads = [shape((share, dim), bf16)] * parts
+    sums = [shape((rows, dim), f32), shape((toks, dim), f32), shape((toks, dim), f32)]
+
+    key_1, value_1 = moved(keys, (-1, -1), 0), moved(values, (-1, -1), 0)
     inputs = tuple(
-        pltpu.with_memory_space_constraint(a, pltpu.HBM)
-        for a in (q, g, o, log_norm, keys, values, span_ids)
-    )
-    query_sum, terms, both, total, *sent = call(
-        functools.partial(own_kernel, heads, tile, scale, parts),
+        pltpu.with_memory_space_constraint(a, pltpu.HBM) for a in (g, o, q, log_norm, keys, values)
+    )
+    q, g, both, terms, query_sum, key_sum, value_sum = call(
+        functools.partial(first_kernel, heads, tile, scale),
         inputs,
         [HBM] * len(inputs),
-        [shape((rows, dim), f32), shape((8, rows), f32), shape((2 * toks, dim), bf16)]
-        + [shape((share, dim), f32)]
-        + [shape((share, dim), bf16)] * (parts - 1),
-        [pltpu.VMEM(a.shape, a.dtype) for a in inputs[:4]]
-        + [pltpu.SMEM(span_ids.shape, span_ids.dtype)]
-        + accs
-        + [pltpu.SemaphoreType.DMA((4, 3))],
-        3 * heads,
-        "own",
-    )
-    near = (moved(both, -1, 0),)
-    landed = [moved(block, 0, away + 1) for away, block in enumerate(sent)]
-    for step, held in ((2, far), (1, near)):
-        query_sum, *sent = call(
-            functools.partial(far_kernel, heads, tile, scale, parts, step, len(held)),
-            (span_ids, q, g, terms, *held, query_sum),
-            [SMEM] + [VMEM] * (4 + len(held)),
-            [shape((rows, dim), f32)] + [shape((share, dim), bf16)] * parts,
-            accs,
+        [shape((rows, dim), bf16), shape((rows, dim), bf16), shape((2 * toks, dim), bf16)]
+        + [shape((8, rows), f32)]
+        + sums,
+        [pltpu.VMEM(a.shape, a.dtype) for a in (o, log_norm)] + [pltpu.SemaphoreType.DMA((3, 3))],
+        1.25 * heads,
+        "first",
+    )
+    key_2, value_2 = moved(key_1, (-1, -1), 0), moved(value_1, (-1, -1), 0)
+
+    def far(step, key, value, query_sum, grads):
+        return call(
+            functools.partial(far_kernel, heads, tile, scale, parts, step),
+            (span_ids, q, g, terms, key, value, query_sum),
+            [SMEM] + [VMEM] * 6,
+            [shape((rows, dim), f32)] + grads,
+            [pltpu.VMEM((toks, dim), f32)] * 2,
             2 * heads,
             "far",
-            {4 + len(held): 0},
+            {6: 0},
         )
-        landed += [moved(block, step, away) for away, block in enumerate(sent)]
+
+    query_sum, near = far(1, key_1, value_1, query_sum, [shape((parts, share, dim), bf16)])
+    joined = moved(near, (-1, 1), 0)
+    query_sum, *sent = far(2, key_2, value_2, query_sum, grads)
+    odd = lax.axis_index("ctx") % 2 == 1
+    landed = []
+    for away, block in enumerate(sent):
+        more = jnp.where(odd, joined[away], jnp.zeros_like(block))
+        block = (block.astype(f32) + more.astype(f32)).astype(bf16)
+        landed.append(moved(block, (2, 2), away))
+    query_sum, _, _, total, *sent = call(
+        functools.partial(last_kernel, heads, tile, scale, parts),
+        (span_ids, q, g, terms, both, joined, query_sum, key_sum, value_sum),
+        [SMEM] + [VMEM] * 8,
+        sums + [shape((share, dim), f32)] + grads[1:],
+        [pltpu.VMEM((parts, share, dim), bf16)],
+        heads,
+        "last",
+        {6: 0, 7: 1, 8: 2},
+    )
+    landed += [moved(block, (0, 0), away + 1) for away, block in enumerate(sent)]
     for block in landed:
         total = total + block.astype(f32)
     total = total.astype(bf16)

time: 46.1 us -> 54.4 us (1.18)
  local copies, waits for them, and re-layouts: 0.73 us -> 6.74 us
  waiting for transfers between devices: 8.86 us -> 11.9 us
  starting transfers between devices: 11.3 us -> 9.74 us
  Pallas kernels: 23 us -> 23.7 us
    unnamed x6 -> x18, local copies, waits for them, and re-layouts: 0.01 us -> 6.03 us
    ppermute x8, waiting for transfers between devices: 8.86 us -> 11.9 us  [moved(): return lax.ppermute(block, ('ctx', 'head'), route)]
    ppermute x8, starting transfers between devices: 11.3 us -> 9.74 us  [moved(): return lax.ppermute(block, ('ctx', 'head'), route)]
    pallas_call x3 -> x4, Pallas kernels: 23 us -> 23.7 us  [call(): pl.pallas_call(kernel, out_shape=outs, in_specs=where, out_specs=[VMEM] *...]
  transfers between devices with their start and end apart: 8 -> 8, of which waited for: 5 -> 4; matrix products, arithmetic and copies ran while one was open for 2% -> 2% of each run, Pallas kernels for 50% -> 44%
where the time goes in v3:
time: 54.4 us; the launch traced here: 54.2 us
  Pallas kernels  23.7 us (44%)
  waiting for transfers between devices  11.9 us (22%)
  starting transfers between devices  9.74 us (18%)
  local copies, waits for them, and re-layouts  6.74 us (12%)
  other arithmetic  1.44 us (3%)
  between operations  0.71 us (1%)
    pallas_call x4, Pallas kernels, call(): pl.pallas_call(kernel, out_shape=outs, in_specs=where, out_specs=[VMEM] *...  23.7 us
    ppermute x8, waiting for transfers between devices, moved(): return lax.ppermute(block, ('ctx', 'head'), route)  11.9 us
    ppermute x8, starting transfers between devices, moved(): return lax.ppermute(block, ('ctx', 'head'), route)  9.74 us
    unnamed x18, local copies, waits for them, and re-layouts  6.03 us
    convert_element_type x1, other arithmetic, local(): query_grad = (query_sum * scale).astype(bf16).reshape(toks, heads, dim)  1.13 us
  transfers between devices with their start and end apart: 8, of which 4 were waited for; matrix products, arithmetic and copies ran while one was open for 2% of the time, Pallas kernels for 44%

profile of v3, /device:TPU:0, one launch (start us, length us, event | category | flops | bytes accessed | tf_op | source)
XLA Modules:
  0.0 54.2 jit_solution(5897847708910962713)
XLA Ops:
  0.6 0.5 collective-permute-start
  1.1 2.6 %collective-permute-start.1 = (bf16[1024,128]{1,0:T(8,128)(2,1)}, bf16[1024,128]{1,0:T(8,128)(2,1)S(1)}, u32[]{:S(2)}, u32[]{:S(2)}) collective-permute-start(bf16[1024,128]{1,0:T(8,128)(2,1)} %refs_5_.1), channel_id=1, source_target_pairs={{0,2},{1,3},{2,4},{3,5},{4,6},{5,7},{6,8},{7,9},{8,10},{9,11},{10,... | collective-permute-start | bytes 786440 | tf_op jit(solution)/shard_map/ppermute | solution.py:245
  3.8 0.0 copy-start
  3.8 6.5 %first.1 = (bf16[4096,128]{1,0:T(8,128)(2,1)S(1)}, bf16[4096,128]{1,0:T(8,128)(2,1)S(1)}, bf16[2048,128]{1,0:T(8,128)(2,1)S(1)}, f32[8,4096]{1,0:T(8,128)S(1)}, ...) custom-call(bf16[4096,128]{1,0:T(8,128)(2,1)} %bitcast.15, bf16[4096,128]{1,0:T(8,128)(2,1)} %bitcast.16, ...), custom_call_target="tpu_custom_call" | custom-call | flops 6710886400 | bytes 6291456 | tf_op jit(solution)/shard_map/first/pallas_call | solution.py:225
  10.2 0.0 copy-start.1
  10.3 1.0 %copy-done.1 = bf16[4096,128]{1,0:T(8,128)(2,1)} copy-done((bf16[4096,128]{1,0:T(8,128)(2,1)}, bf16[4096,128]{1,0:T(8,128)(2,1)S(1)}, u32[]{:S(2)}) %copy-start.1) | copy-done | bytes 1048600
  11.2 0.0 copy-start.3
  11.2 1.0 %copy-done.3 = bf16[4096,128]{1,0:T(8,128)(2,1)} copy-done((bf16[4096,128]{1,0:T(8,128)(2,1)}, bf16[4096,128]{1,0:T(8,128)(2,1)S(1)}, u32[]{:S(2)}) %copy-start.3) | copy-done | bytes 1048600
  12.2 0.0 copy-start.5
  12.2 0.8 %copy-done.5 = f32[1024,128]{1,0:T(8,128)} copy-done((f32[1024,128]{1,0:T(8,128)}, f32[1024,128]{1,0:T(8,128)S(1)}, u32[]{:S(2)}) %copy-start.5) | copy-done | bytes 524312
  13.0 0.0 copy-start.7
  13.0 0.8 %copy-done.7 = f32[1024,128]{1,0:T(8,128)} copy-done((f32[1024,128]{1,0:T(8,128)}, f32[1024,128]{1,0:T(8,128)S(1)}, u32[]{:S(2)}) %copy-start.7) | copy-done | bytes 524312
  13.8 0.0 collective-permute-done.refs_3_
  13.8 0.1 collective-permute-start.3
  13.9 0.0 collective-permute-done.1.refs_4_
  13.9 1.6 %collective-permute-start.4 = (bf16[1024,128]{1,0:T(8,128)(2,1)S(1)}, bf16[1024,128]{1,0:T(8,128)(2,1)S(1)}, u32[]{:S(2)}, u32[]{:S(2)}) collective-permute-start(bf16[1024,128]{1,0:T(8,128)(2,1)S(1)} %collective-permute-done.1.refs_4_), channel_id=1, source_target_pairs={{0,2},{1,3},{2,4},{3,5},{4,6},{5,7},{6,8},{7,9},{8,10},{9,11},{10,... | collective-permute-start | bytes 786440 | tf_op jit(solution)/shard_map/ppermute | solution.py:245
  15.5 0.0 copy-done
  15.5 0.0 copy-start.2
  15.5 1.2 %copy-done.2 = bf16[4096,128]{1,0:T(8,128)(2,1)S(1)} copy-done((bf16[4096,128]{1,0:T(8,128)(2,1)S(1)}, bf16[4096,128]{1,0:T(8,128)(2,1)}, u32[]{:S(2)}) %copy-start.2) | copy-done | bytes 1048600
  16.7 0.0 copy-start.4
  16.7 1.2 %copy-done.4 = bf16[4096,128]{1,0:T(8,128)(2,1)S(1)} copy-done((bf16[4096,128]{1,0:T(8,128)(2,1)S(1)}, bf16[4096,128]{1,0:T(8,128)(2,1)}, u32[]{:S(2)}) %copy-start.4) | copy-done | bytes 1048600
  17.9 6.6 %far.2 = (f32[4096,128]{1,0:T(8,128)S(1)}, bf16[2,1024,128]{2,1,0:T(8,128)(2,1)S(1)}) custom-call(s32[32]{0:T(128)S(1)} %copy-done, bf16[4096,128]{1,0:T(8,128)(2,1)S(1)} %copy-done.2, bf16[4096,128]{1,0:T(8,128)(2,1)S(1)} %copy-done.4, f32[8,4096]{1,0:T(8,128)S(1)} %get-tuple-element.20.refs_2_, ...), custom_call_target="tpu_custom_call", output_to_operand_aliasing={{0}: (6, {})} | custom-call | flops 10737418240 | bytes 6291456 | tf_op jit(solution)/shard_map/far/pallas_call | solution.py:225
  24.5 0.1 collective-permute-start.2
  24.7 0.0 collective-permute-done.3.refs_3_
  24.7 0.5 collective-permute-done.4.refs_4_
  25.1 0.0 copy-start.6
  25.1 0.0 copy-start.8
  25.1 6.6 %far.3 = (f32[4096,128]{1,0:T(8,128)S(1)}, bf16[1024,128]{1,0:T(8,128)(2,1)S(1)}, bf16[1024,128]{1,0:T(8,128)(2,1)S(1)}) custom-call(s32[32]{0:T(128)S(1)} %copy-done, bf16[4096,128]{1,0:T(8,128)(2,1)S(1)} %copy-done.2, bf16[4096,128]{1,0:T(8,128)(2,1)S(1)} %copy-done.4, f32[8,4096]{1,0:T(8,128)S(1)} %get-tuple-element.20.refs_2_, ...), custom_call_target="tpu_custom_call", output_to_operand_aliasing={{0}: (6, {})} | custom-call | flops 10737418240 | bytes 6291456 | tf_op jit(solution)/shard_map/far/pallas_call | solution.py:225
  31.8 0.0 collective-permute-done.2.refs_4_
  31.8 0.2 fusion.1
  32.0 2.8 %collective-permute-start.5 = (bf16[1024,128]{1,0:T(8,128)(2,1)S(1)}, bf16[1024,128]{1,0:T(8,128)(2,1)S(1)}, u32[]{:S(2)}, u32[]{:S(2)}) collective-permute-start(bf16[1024,128]{1,0:T(8,128)(2,1)S(1)} %get-tuple-element.33), channel_id=1, source_target_pairs={{0,28},{1,29},{2,30},{3,31},{4,0},{5,1},{6,2},{7,3},{8,4},{9,5},{1... | collective-permute-start | bytes 786440 | tf_op jit(solution)/shard_map/ppermute | solution.py:245
  34.8 1.4 %collective-permute-start.6 = (bf16[1024,128]{1,0:T(8,128)(2,1)S(1)}, bf16[1024,128]{1,0:T(8,128)(2,1)S(1)}, u32[]{:S(2)}, u32[]{:S(2)}) collective-permute-start(bf16[1024,128]{1,0:T(8,128)(2,1)S(1)} %get-tuple-element.34), channel_id=1, source_target_pairs={{0,29},{1,28},{2,31},{3,30},{4,1},{5,0},{6,3},{7,2},{8,5},{9,4},{1... | collective-permute-start | bytes 786440 | tf_op jit(solution)/shard_map/ppermute | solution.py:245
  36.2 0.0 copy-done.6
  36.2 0.0 copy-done.8
  36.2 3.9 %last.1 = (f32[4096,128]{1,0:T(8,128)S(1)}, f32[1024,128]{1,0:T(8,128)S(1)}, f32[1024,128]{1,0:T(8,128)S(1)}, f32[1024,128]{1,0:T(8,128)S(1)}, bf16[1024,128]{1,0:T(8,128)(2,1)S(1)}) custom-call(s32[32]{0:T(128)S(1)} %copy-done, bf16[4096,128]{1,0:T(8,128)(2,1)S(1)} %copy-done.2, ...), custom_call_target="tpu_custom_call", output_to_operand_aliasing={{0}: (6, {}), {1}: (7, {}), {2}: (8, {})} | custom-call | flops 5368709120 | bytes 6291456 | tf_op jit(solution)/shard_map/last/pallas_call | solution.py:225
  40.2 0.6 %collective-permute-start.7 = (bf16[1024,128]{1,0:T(8,128)(2,1)S(1)}, bf16[1024,128]{1,0:T(8,128)(2,1)S(1)}, u32[]{:S(2)}, u32[]{:S(2)}) collective-permute-start(bf16[1024,128]{1,0:T(8,128)(2,1)S(1)} %get-tuple-element.32), channel_id=1, source_target_pairs={{0,1},{1,0},{2,3},{3,2},{4,5},{5,4},{6,7},{7,6},{8,9},{9,8},{10,11... | collective-permute-start | bytes 786440 | tf_op jit(solution)/shard_map/ppermute | solution.py:245
  40.8 1.1 %multiply_convert_fusion = bf16[4096,128]{1,0:T(8,128)(2,1)} fusion(f32[4096,128]{1,0:T(8,128)S(1)} %get-tuple-element.28), kind=kLoop, calls=%fused_computation | loop fusion | flops 1048576 | bytes 3145728 | tf_op jit(solution)/shard_map/convert_element_type | solution.py:315
  41.9 4.0 %collective-permute-done.5 = bf16[1024,128]{1,0:T(8,128)(2,1)S(1)} collective-permute-done((bf16[1024,128]{1,0:T(8,128)(2,1)S(1)}, bf16[1024,128]{1,0:T(8,128)(2,1)S(1)}, u32[]{:S(2)}, u32[]{:S(2)}) %collective-permute-start.5) | collective-permute-done | bytes 262176 | tf_op jit(solution)/shard_map/ppermute | solution.py:245
  45.9 0.7 %collective-permute-done.6 = bf16[1024,128]{1,0:T(8,128)(2,1)S(1)} collective-permute-done((bf16[1024,128]{1,0:T(8,128)(2,1)S(1)}, bf16[1024,128]{1,0:T(8,128)(2,1)S(1)}, u32[]{:S(2)}, u32[]{:S(2)}) %collective-permute-start.6) | collective-permute-done | bytes 262176 | tf_op jit(solution)/shard_map/ppermute | solution.py:245
  46.6 6.8 %collective-permute-done.7 = bf16[1024,128]{1,0:T(8,128)(2,1)S(1)} collective-permute-done((bf16[1024,128]{1,0:T(8,128)(2,1)S(1)}, bf16[1024,128]{1,0:T(8,128)(2,1)S(1)}, u32[]{:S(2)}, u32[]{:S(2)}) %collective-permute-start.7) | collective-permute-done | bytes 262176 | tf_op jit(solution)/shard_map/ppermute | solution.py:245
  53.4 0.1 add_convert_fusion
  53.5 0.7 %fusion.4 = (bf16[512,128]{1,0:T(8,128)(2,1)}, bf16[512,128]{1,0:T(8,128)(2,1)}) fusion(bf16[1024,128]{1,0:T(8,128)(2,1)S(1)} %add_convert_fusion), kind=kLoop, calls=%fused_computation.10 | loop fusion | bytes 524288 | tf_op jit(solution)/shard_map/slice | solution.py:316
Async XLA Ops:
  0.6 13.2 %collective-permute-start = (bf16[1024,128]{1,0:T(8,128)(2,1)}, bf16[1024,128]{1,0:T(8,128)(2,1)S(1)}, u32[]{:S(2)}, u32[]{:S(2)}) collective-permute-start(bf16[1024,128]{1,0:T(8,128)(2,1)} %refs_4_.1), channel_id=1, source_target_pairs={{0,2},{1,3},{2,4},{3,5},{4,6},{5,7},{6,8},{7,9},{8,10},{9,11},{10,... | collective-permute-start | bytes 786440 | tf_op jit(solution)/shard_map/ppermute | solution.py:245
  1.1 12.8 %collective-permute-start.1 = (bf16[1024,128]{1,0:T(8,128)(2,1)}, bf16[1024,128]{1,0:T(8,128)(2,1)S(1)}, u32[]{:S(2)}, u32[]{:S(2)}) collective-permute-start(bf16[1024,128]{1,0:T(8,128)(2,1)} %refs_5_.1), channel_id=1, source_target_pairs={{0,2},{1,3},{2,4},{3,5},{4,6},{5,7},{6,8},{7,9},{8,10},{9,11},{10,... | collective-permute-start | bytes 786440 | tf_op jit(solution)/shard_map/ppermute | solution.py:245
  3.8 11.7 %copy-start = (s32[32]{0:T(128)S(1)}, s32[32]{0:T(128)}, u32[]{:S(2)}) copy-start(s32[32]{0:T(128)} %span_ids.5) | copy-start | bytes 388
  10.2 1.0 %copy-start.1 = (bf16[4096,128]{1,0:T(8,128)(2,1)}, bf16[4096,128]{1,0:T(8,128)(2,1)S(1)}, u32[]{:S(2)}) copy-start(bf16[4096,128]{1,0:T(8,128)(2,1)S(1)} %get-tuple-element.18.refs_0_) | copy-start | bytes 3145732
  11.2 1.0 %copy-start.3 = (bf16[4096,128]{1,0:T(8,128)(2,1)}, bf16[4096,128]{1,0:T(8,128)(2,1)S(1)}, u32[]{:S(2)}) copy-start(bf16[4096,128]{1,0:T(8,128)(2,1)S(1)} %get-tuple-element.19.refs_1_) | copy-start | bytes 3145732
  12.2 0.8 %copy-start.5 = (f32[1024,128]{1,0:T(8,128)}, f32[1024,128]{1,0:T(8,128)S(1)}, u32[]{:S(2)}) copy-start(f32[1024,128]{1,0:T(8,128)S(1)} %get-tuple-element.26.refs_6_) | copy-start | bytes 1572868
  13.0 0.8 %copy-start.7 = (f32[1024,128]{1,0:T(8,128)}, f32[1024,128]{1,0:T(8,128)S(1)}, u32[]{:S(2)}) copy-start(f32[1024,128]{1,0:T(8,128)S(1)} %get-tuple-element.27.refs_7_) | copy-start | bytes 1572868
  13.8 10.9 %collective-permute-start.3 = (bf16[1024,128]{1,0:T(8,128)(2,1)S(1)}, bf16[1024,128]{1,0:T(8,128)(2,1)S(1)}, u32[]{:S(2)}, u32[]{:S(2)}) collective-permute-start(bf16[1024,128]{1,0:T(8,128)(2,1)S(1)} %collective-permute-done.refs_3_), channel_id=1, source_target_pairs={{0,2},{1,3},{2,4},{3,5},{4,6},{5,7},{6,8},{7,9},{8,10},{9,11},{10,... | collective-permute-start | bytes 786440 | tf_op jit(solution)/shard_map/ppermute | solution.py:245
  13.9 11.2 %collective-permute-start.4 = (bf16[1024,128]{1,0:T(8,128)(2,1)S(1)}, bf16[1024,128]{1,0:T(8,128)(2,1)S(1)}, u32[]{:S(2)}, u32[]{:S(2)}) collective-permute-start(bf16[1024,128]{1,0:T(8,128)(2,1)S(1)} %collective-permute-done.1.refs_4_), channel_id=1, source_target_pairs={{0,2},{1,3},{2,4},{3,5},{4,6},{5,7},{6,8},{7,9},{8,10},{9,11},{10,... | collective-permute-start | bytes 786440 | tf_op jit(solution)/shard_map/ppermute | solution.py:245
  15.5 1.2 %copy-start.2 = (bf16[4096,128]{1,0:T(8,128)(2,1)S(1)}, bf16[4096,128]{1,0:T(8,128)(2,1)}, u32[]{:S(2)}) copy-start(bf16[4096,128]{1,0:T(8,128)(2,1)} %copy-done.1) | copy-start | bytes 3145732
  16.7 1.2 %copy-start.4 = (bf16[4096,128]{1,0:T(8,128)(2,1)S(1)}, bf16[4096,128]{1,0:T(8,128)(2,1)}, u32[]{:S(2)}) copy-start(bf16[4096,128]{1,0:T(8,128)(2,1)} %copy-done.3) | copy-start | bytes 3145732
  24.5 7.2 %collective-permute-start.2 = (bf16[2,1024,128]{2,1,0:T(8,128)(2,1)S(1)}, bf16[2,1024,128]{2,1,0:T(8,128)(2,1)S(1)}, u32[]{:S(2)}, u32[]{:S(2)}) collective-permute-start(bf16[2,1024,128]{2,1,0:T(8,128)(2,1)S(1)} %get-tuple-element.23), channel_id=1, source_target_pairs={{0,2},{1,3},{2,0},{3,1},{4,6},{5,7},{6,4},{7,5},{8,10},{9,11},{10,... | collective-permute-start | bytes 1572872 | tf_op jit(solution)/shard_map/ppermute | solution.py:245
  25.1 11.1 %copy-start.6 = (f32[1024,128]{1,0:T(8,128)S(1)}, f32[1024,128]{1,0:T(8,128)}, u32[]{:S(2)}) copy-start(f32[1024,128]{1,0:T(8,128)} %copy-done.5) | copy-start | bytes 1572868
  25.1 11.1 %copy-start.8 = (f32[1024,128]{1,0:T(8,128)S(1)}, f32[1024,128]{1,0:T(8,128)}, u32[]{:S(2)}) copy-start(f32[1024,128]{1,0:T(8,128)} %copy-done.7) | copy-start | bytes 1572868
  32.0 13.9 %collective-permute-start.5 = (bf16[1024,128]{1,0:T(8,128)(2,1)S(1)}, bf16[1024,128]{1,0:T(8,128)(2,1)S(1)}, u32[]{:S(2)}, u32[]{:S(2)}) collective-permute-start(bf16[1024,128]{1,0:T(8,128)(2,1)S(1)} %get-tuple-element.33), channel_id=1, source_target_pairs={{0,28},{1,29},{2,30},{3,31},{4,0},{5,1},{6,2},{7,3},{8,4},{9,5},{1... | collective-permute-start | bytes 786440 | tf_op jit(solution)/shard_map/ppermute | solution.py:245
  34.8 11.8 %collective-permute-start.6 = (bf16[1024,128]{1,0:T(8,128)(2,1)S(1)}, bf16[1024,128]{1,0:T(8,128)(2,1)S(1)}, u32[]{:S(2)}, u32[]{:S(2)}) collective-permute-start(bf16[1024,128]{1,0:T(8,128)(2,1)S(1)} %get-tuple-element.34), channel_id=1, source_target_pairs={{0,29},{1,28},{2,31},{3,30},{4,1},{5,0},{6,3},{7,2},{8,5},{9,4},{1... | collective-permute-start | bytes 786440 | tf_op jit(solution)/shard_map/ppermute | solution.py:245
  40.2 13.2 %collective-permute-start.7 = (bf16[1024,128]{1,0:T(8,128)(2,1)S(1)}, bf16[1024,128]{1,0:T(8,128)(2,1)S(1)}, u32[]{:S(2)}, u32[]{:S(2)}) collective-permute-start(bf16[1024,128]{1,0:T(8,128)(2,1)S(1)} %get-tuple-element.32), channel_id=1, source_target_pairs={{0,1},{1,0},{2,3},{3,2},{4,5},{5,4},{6,7},{7,6},{8,9},{9,8},{10,11... | collective-permute-start | bytes 786440 | tf_op jit(solution)/shard_map/ppermute | solution.py:245

commit v4 on v2

--- a/solution.py
+++ b/solution.py
@@ -55,15 +55,15 @@
 
 def tile_grads(group, accs, scale, tiles):
     query_ref, grad_ref, key_ref, value_ref, terms_ref, tile = group
-    query_acc, key_acc, value_acc = accs
-
-    def opened(row, key, length, _):
+    key_acc, value_acc = accs
+
+    def opened(row, key, length, *_):
         k = key_ref[pl.ds(key, length), :]
         v = value_ref[pl.ds(key, length), :]
         scores = dot(k, query_ref[pl.ds(row, tile), :], NT)
         return scores, dot(v, grad_ref[pl.ds(row, tile), :], NT)
 
-    def closed(row, key, length, triangle, scores, dprob):
+    def closed(row, key, length, triangle, kept, scores, dprob):
         norm = terms_ref[0:1, pl.ds(row, tile)]
         delta = terms_ref[1:2, pl.ds(row, tile)]
         prob = jnp.exp2(scores * (scale * math.log2(math.e)) - norm)
@@ -72,11 +72,11 @@
             last = jnp.where(triangle, prob[edge:], 0.0)
             prob = last if edge == 0 else jnp.concatenate([prob[:edge], last], axis=0)
         dscore = (prob * (dprob - delta)).astype(jnp.bfloat16)
+        kept[...] = dscore
         value_acc[pl.ds(key, length), :] += dot(
             prob.astype(jnp.bfloat16), grad_ref[pl.ds(row, tile), :], NN
         )
         key_acc[pl.ds(key, length), :] += dot(dscore, query_ref[pl.ds(row, tile), :], NN)
-        query_acc[pl.ds(row, tile), :] += dot(dscore, key_ref[pl.ds(key, length), :], TN)
 
     ahead = opened(*tiles[0])
     for index, this in enumerate(tiles):
@@ -88,6 +88,19 @@
 
 def span_pair(span_ids, holder):
     return span_ids[2 * holder], span_ids[2 * holder + 1]
+
+
+def far_halves(span_ids, step):
+    me, holders = lax.axis_index("ctx"), lax.axis_size("ctx")
+    mine = span_pair(span_ids, me)
+    theirs = span_pair(span_ids, lax.rem(me + holders - step, holders))
+    high_only = jnp.minimum(*mine) < jnp.minimum(*theirs)
+    our_high = jnp.where(mine[0] > mine[1], 0, 1)
+    their_low = jnp.where(theirs[0] > theirs[1], 1, 0)
+    return lambda item: (
+        jnp.where(high_only, our_high, item),
+        jnp.where(high_only, item, their_low),
+    )
 
 
 def put_shares(outs, key_acc, value_acc, scale):
@@ -102,7 +115,7 @@
 
 def own_kernel(heads, tile, scale, parts, *refs):
     inputs, refs = refs[:7], refs[7:]
-    query_acc, terms_ref, both_ref = refs[:3]
+    terms_ref, both_ref, kept_ref = refs[:3]
     outs, refs = refs[3 : 3 + parts], refs[3 + parts :]
     held, (key_acc, value_acc, sems) = refs[:5], refs[5:]
     query_ref, grad_ref, outputs_ref, norm_ref, span_ids = held
@@ -125,14 +138,17 @@
 
     for copy in whole + halves(0) + halves(1):
         copy.start()
-    query_acc[...] = jnp.zeros_like(query_acc)
     key_acc[...] = jnp.zeros_like(key_acc)
     value_acc[...] = jnp.zeros_like(value_acc)
     group = (query_ref, grad_ref, key_ref, value_ref, terms_ref, tile)
-    accs = (query_acc, key_acc, value_acc)
+    accs = (key_acc, value_acc)
     triangle = lax.broadcasted_iota(jnp.int32, (per, tile), 0) <= (
         lax.broadcasted_iota(jnp.int32, (per, tile), 1) // heads
     )
+
+    def placed(row, key, length, triangle):
+        return row, key, length, triangle, kept_ref.at[pl.ds(key, length), pl.ds(row, tile)]
+
     for copy in whole:
         copy.wait()
 
@@ -143,65 +159,102 @@
         row_terms(heads, tile, index, (grad_ref, outputs_ref, norm_ref), terms_ref)
         key = pl.multiple_of(index * half, half)
         tiles = [
-            (pl.multiple_of(index * rows + part * tile, tile), key, (part + 1) * per, triangle)
-            for part in range(half // per)
+            placed(pl.multiple_of(index * rows + p * tile, tile), key, (p + 1) * per, triangle)
+            for p in range(half // per)
         ]
         tile_grads(group, accs, scale, tiles)
 
     first, second = span_pair(span_ids, lax.axis_index("ctx"))
     low = jnp.where(first > second, 1, 0)
-
     key = pl.multiple_of(low * half, half)
     tiles = [
-        (pl.multiple_of((1 - low) * rows + part * tile, tile), key, half, None)
-        for part in range(rows // tile)
+        placed(pl.multiple_of((1 - low) * rows + p * tile, tile), key, half, None)
+        for p in range(rows // tile)
     ]
     tile_grads(group, accs, scale, tiles)
     put_shares(outs, key_acc, value_acc, scale)
 
 
-def far_kernel(heads, tile, scale, parts, step, count, span_ids, *refs):
-    query_ref, grad_ref, terms_ref = refs[:3]
-    if count == 1:
-        toks = refs[3].shape[0] // 2
-        key_ref, value_ref = refs[3].at[pl.ds(0, toks)], refs[3].at[pl.ds(toks, toks)]
-    else:
-        key_ref, value_ref = refs[3:5]
-    query_acc = refs[4 + count]
-    outs = refs[5 + count : 5 + count + parts]
-    key_acc, value_acc = refs[5 + count + parts :]
+def far_kernel(heads, tile, scale, parts, step, span_ids, *refs):
+    query_ref, grad_ref, terms_ref, key_ref, value_ref, kept_ref = refs[:6]
+    outs = refs[6:-2]
+    key_acc, value_acc = refs[-2:]
     half = key_ref.shape[0] // 2
+    rows = half * heads
     key_acc[...] = jnp.zeros_like(key_acc)
     value_acc[...] = jnp.zeros_like(value_acc)
     group = (query_ref, grad_ref, key_ref, value_ref, terms_ref, tile)
-    accs = (query_acc, key_acc, value_acc)
-    per = half * heads // tile
-    me, holders = lax.axis_index("ctx"), lax.axis_size("ctx")
-    mine = span_pair(span_ids, me)
-    theirs = span_pair(span_ids, lax.rem(me + holders - step, holders))
-    high_only = jnp.minimum(*mine) < jnp.minimum(*theirs)
-    our_high = jnp.where(mine[0] > mine[1], 0, 1)
-    their_low = jnp.where(theirs[0] > theirs[1], 1, 0)
+    halves = far_halves(span_ids, step)
 
     @pl.loop(0, 2)
     def _(item):
-        row_half = jnp.where(high_only, our_high, item)
-        key_half = jnp.where(high_only, item, their_low)
-        row = pl.multiple_of(row_half * half * heads, half * heads)
+        row_half, key_half = halves(item)
+        row = pl.multiple_of(row_half * rows, rows)
         key = pl.multiple_of(key_half * half, half)
-        tiles = [(pl.multiple_of(row + part * tile, tile), key, half, None) for part in range(per)]
-        tile_grads(group, accs, scale, tiles)
+        tiles = [
+            (
+                pl.multiple_of(row + p * tile, tile),
+                key,
+                half,
+                None,
+                kept_ref.at[item, :, pl.ds(p * tile, tile)],
+            )
+            for p in range(rows // tile)
+        ]
+        tile_grads(group, (key_acc, value_acc), scale, tiles)
 
     put_shares(outs, key_acc, value_acc, scale)
+
+
+def query_kernel(heads, tile, scale, span_ids, both_ref, own_ref, *refs):
+    far_refs, (out_ref, acc) = refs[:-2], refs[-2:]
+    toks = both_ref.shape[0] // 2
+    half = toks // 2
+    rows = half * heads
+    per = tile // heads
+
+    @pl.loop(0, 2)
+    def _(index):
+        key = pl.multiple_of(index * half, half)
+        for p in range(half // per):
+            row = pl.multiple_of(index * rows + p * tile, tile)
+            length = (p + 1) * per
+            acc[pl.ds(row, tile), :] = dot(
+                own_ref[pl.ds(key, length), pl.ds(row, tile)], both_ref[pl.ds(key, length), :], TN
+            )
+
+    first, second = span_pair(span_ids, lax.axis_index("ctx"))
+    low = jnp.where(first > second, 1, 0)
+    key = pl.multiple_of(low * half, half)
+    for p in range(rows // tile):
+        row = pl.multiple_of((1 - low) * rows + p * tile, tile)
+        acc[pl.ds(row, tile), :] += dot(
+            own_ref[pl.ds(key, half), pl.ds(row, tile)], both_ref[pl.ds(key, half), :], TN
+        )
+    for step in range(1, STEPS):
+        key_ref, kept_ref = far_refs[2 * step - 2 : 2 * step]
+        halves = far_halves(span_ids, step)
+
+        @pl.loop(0, 2)
+        def _(item):
+            row_half, key_half = halves(item)
+            key = pl.multiple_of(key_half * half, half)
+            for p in range(rows // tile):
+                row = pl.multiple_of(row_half * rows + p * tile, tile)
+                acc[pl.ds(row, tile), :] += dot(
+                    kept_ref[item, :, p * tile : (p + 1) * tile], key_ref[pl.ds(key, half), :], TN
+                )
+
+    out_ref[...] = (acc[...] * scale).astype(out_ref.dtype)
 
 
 VMEM = pl.BlockSpec(memory_space=pltpu.VMEM)
 SMEM = pl.BlockSpec(memory_space=pltpu.SMEM)
 HBM = pl.BlockSpec(memory_space=pltpu.HBM)
-PARAMS = pltpu.CompilerParams(vmem_limit_bytes=20 * 1024 * 1024)
-
-
-def call(kernel, ins, where, outs, scratch, blocks, name, aliases=None):
+MIB = 1024 * 1024
+
+
+def call(kernel, ins, where, outs, scratch, blocks, limit, name):
     flops = blocks * 40 * 512 * 512 * 128
     return pl.pallas_call(
         kernel,
@@ -209,8 +262,7 @@
         in_specs=where,
         out_specs=[VMEM] * len(outs),
         scratch_shapes=scratch,
-        input_output_aliases=aliases or {},
-        compiler_params=PARAMS,
+        compiler_params=pltpu.CompilerParams(vmem_limit_bytes=limit * MIB),
         name=name,
         cost_estimate=pl.CostEstimate(flops=int(flops), bytes_accessed=6 << 20, transcendentals=0),
     )(*ins)
@@ -219,7 +271,7 @@
 def moved(block, back, away):
     holders, parts = lax.axis_size("ctx"), lax.axis_size("head")
     route = [
-        (h * parts + x, ((h - back) % holders) * parts + (x + away) % parts)
+        (h * parts + x, ((h - back[h % 2]) % holders) * parts + (x + away) % parts)
         for h in range(holders)
         for x in range(parts)
     ]
@@ -238,47 +290,67 @@
     share = 2 * toks // parts
     f32, bf16 = jnp.float32, jnp.bfloat16
     shape = jax.ShapeDtypeStruct
-
+    grads = [shape((share, dim), bf16)] * parts
     accs = [pltpu.VMEM((toks, dim), f32)] * 2
-    far = moved(keys, 1 - STEPS, 0), moved(values, 1 - STEPS, 0)
-
+
+    key_1, value_1 = moved(keys, (-1, -1), 0), moved(values, (-1, -1), 0)
     inputs = tuple(
         pltpu.with_memory_space_constraint(a, pltpu.HBM)
         for a in (q, g, o, log_norm, keys, values, span_ids)
     )
-    query_sum, terms, both, total, *sent = call(
+    terms, both, kept, total, *sent = call(
         functools.partial(own_kernel, heads, tile, scale, parts),
         inputs,
         [HBM] * len(inputs),
-        [shape((rows, dim), f32), shape((8, rows), f32), shape((2 * toks, dim), bf16)]
+        [shape((8, rows), f32), shape((2 * toks, dim), bf16), shape((toks, rows), bf16)]
         + [shape((share, dim), f32)]
-        + [shape((share, dim), bf16)] * (parts - 1),
+        + grads[1:],
         [pltpu.VMEM(a.shape, a.dtype) for a in inputs[:4]]
         + [pltpu.SMEM(span_ids.shape, span_ids.dtype)]
         + accs
         + [pltpu.SemaphoreType.DMA((4, 3))],
-        3 * heads,
+        2.25 * heads,
+        20,
         "own",
     )
-    near = (moved(both, -1, 0),)
-    landed = [moved(block, 0, away + 1) for away, block in enumerate(sent)]
-    for step, held in ((2, far), (1, near)):
-        query_sum, *sent = call(
-            functools.partial(far_kernel, heads, tile, scale, parts, step, len(held)),
-            (span_ids, q, g, terms, *held, query_sum),
-            [SMEM] + [VMEM] * (4 + len(held)),
-            [shape((rows, dim), f32)] + [shape((share, dim), bf16)] * parts,
+    landed = [moved(block, (0, 0), away + 1) for away, block in enumerate(sent)]
+    key_2, value_2 = moved(key_1, (-1, -1), 0), moved(value_1, (-1, -1), 0)
+
+    def far(step, key, value):
+        return call(
+            functools.partial(far_kernel, heads, tile, scale, parts, step),
+            (span_ids, q, g, terms, key, value),
+            [SMEM] + [VMEM] * 5,
+            [shape((2, toks // 2, rows // 2), bf16)] + grads,
             accs,
             2 * heads,
+            14,
             "far",
-            {4 + len(held): 0},
         )
-        landed += [moved(block, step, away) for away, block in enumerate(sent)]
+
+    kept_1, *sent = far(1, key_1, value_1)
+    joined = [moved(block, (-1, 1), away) for away, block in enumerate(sent)]
+    kept_2, *sent = far(2, key_2, value_2)
+    odd = lax.axis_index("ctx") % 2 == 1
+    joined = sum(block.astype(f32) for block in joined)
+    straight = sent[0].astype(f32) + jnp.where(odd, joined, 0.0)
+    total = total + jnp.where(odd, 0.0, joined)
+    for away, block in enumerate([straight.astype(bf16)] + sent[1:]):
+        landed.append(moved(block, (2, 2), away))
+    (query_grad,) = call(
+        functools.partial(query_kernel, heads, tile, scale),
+        (span_ids, both, kept, key_1, kept_1, key_2, kept_2),
+        [SMEM] + [VMEM] * 6,
+        [shape((rows, dim), bf16)],
+        [pltpu.VMEM((rows, dim), f32)],
+        1.25 * heads,
+        28,
+        "queries",
+    )
     for block in landed:
         total = total + block.astype(f32)
     total = total.astype(bf16)
-    query_grad = (query_sum * scale).astype(bf16).reshape(toks, heads, dim)
-    return query_grad, total[: share // 2], total[share // 2 :]
+    return query_grad.reshape(toks, heads, dim), total[: share // 2], total[share // 2 :]
 
 
 def solution(mesh):

time: 46.1 us -> 50.5 us (1.095)
  local copies, waits for them, and re-layouts: 0.73 us -> 4.78 us
  Pallas kernels: 23 us -> 26.7 us
  waiting for transfers between devices: 8.86 us -> 6.53 us
  starting transfers between devices: 11.3 us -> 10.3 us
    unnamed x6 -> x16, local copies, waits for them, and re-layouts: 0.01 us -> 4.06 us
    pallas_call x3 -> x4, Pallas kernels: 23 us -> 26.7 us  [call(): pl.pallas_call(kernel, out_shape=outs, in_specs=where, out_specs=[VMEM] *...]
    ppermute x8 -> x9, waiting for transfers between devices: 8.86 us -> 6.53 us  [moved(): return lax.ppermute(block, ('ctx', 'head'), route)]
    ppermute x8 -> x9, starting transfers between devices: 11.3 us -> 10.3 us  [moved(): return lax.ppermute(block, ('ctx', 'head'), route)]
    convert_element_type x1, other arithmetic: 1.13 us -> 0.12 us  [local(): straight.astype(bf16)]
    convert_element_type x1, other arithmetic: 0.2 us -> 1.16 us  [local(): total = total.astype(bf16)]
  transfers between devices with their start and end apart: 8 -> 9, of which waited for: 5 -> 4; matrix products, arithmetic and copies ran while one was open for 2% -> 0% of each run, Pallas kernels for 50% -> 53%
where the time goes in v4:
time: 50.5 us; the launch traced here: 50.3 us
  Pallas kernels  26.7 us (53%)
  starting transfers between devices  10.3 us (20%)
  waiting for transfers between devices  6.53 us (13%)
  local copies, waits for them, and re-layouts  4.78 us (9%)
  other arithmetic  1.28 us (3%)
  between operations  0.71 us (1%)
    pallas_call x4, Pallas kernels, call(): pl.pallas_call(kernel, out_shape=outs, in_specs=where, out_specs=[VMEM] *...  26.7 us
    ppermute x9, starting transfers between devices, moved(): return lax.ppermute(block, ('ctx', 'head'), route)  10.3 us
    ppermute x9, waiting for transfers between devices, moved(): return lax.ppermute(block, ('ctx', 'head'), route)  6.53 us
    unnamed x16, local copies, waits for them, and re-layouts  4.06 us
    convert_element_type x1, other arithmetic, local(): total = total.astype(bf16)  1.16 us
  transfers between devices with their start and end apart: 9, of which 4 were waited for; matrix products, arithmetic and copies ran while one was open for 0% of the time, Pallas kernels for 53%

profile of v4, /device:TPU:0, one launch (start us, length us, event | category | flops | bytes accessed | tf_op | source)
XLA Modules:
  0.0 50.3 jit_solution(2221722329508482607)
XLA Ops:
  0.6 0.5 %collective-permute-start = (bf16[1024,128]{1,0:T(8,128)(2,1)}, bf16[1024,128]{1,0:T(8,128)(2,1)S(1)}, u32[]{:S(2)}, u32[]{:S(2)}) collective-permute-start(bf16[1024,128]{1,0:T(8,128)(2,1)} %refs_4_.1), channel_id=1, source_target_pairs={{0,2},{1,3},{2,4},{3,5},{4,6},{5,7},{6,8},{7,9},{8,10},{9,11},{10,... | collective-permute-start | bytes 786440 | tf_op jit(solution)/shard_map/ppermute | solution.py:278
  1.1 2.6 %collective-permute-start.1 = (bf16[1024,128]{1,0:T(8,128)(2,1)}, bf16[1024,128]{1,0:T(8,128)(2,1)S(1)}, u32[]{:S(2)}, u32[]{:S(2)}) collective-permute-start(bf16[1024,128]{1,0:T(8,128)(2,1)} %refs_5_.1), channel_id=1, source_target_pairs={{0,2},{1,3},{2,4},{3,5},{4,6},{5,7},{6,8},{7,9},{8,10},{9,11},{10,... | collective-permute-start | bytes 786440 | tf_op jit(solution)/shard_map/ppermute | solution.py:278
  3.8 0.0 copy-start
  3.8 0.0 copy-start.1
  3.8 0.0 copy-start.2
  3.8 8.6 %own.1 = (f32[8,4096]{1,0:T(8,128)S(1)}, bf16[2048,128]{1,0:T(8,128)(2,1)S(1)}, bf16[1024,4096]{1,0:T(8,128)(2,1)S(1)}, f32[1024,128]{1,0:T(8,128)S(1)}, bf16[1024,128]{1,0:T(8,128)(2,1)S(1)}) custom-call(bf16[4096,128]{1,0:T(8,128)(2,1)} %bitcast.4, bf16[4096,128]{1,0:T(8,128)(2,1)} %bitcast.7, bf16[4096,128]{1,0:T(8,128)(2,1)} %bitcast.12, ...), custom_call_target="tpu_custom_call" | custom-call | flops 12079595520 | bytes 6291456 | tf_op jit(solution)/shard_map/own/pallas_call | solution.py:259
  12.3 0.0 copy-start.3
  12.4 3.2 %copy-done.3 = bf16[1024,4096]{1,0:T(8,128)(2,1)} copy-done((bf16[1024,4096]{1,0:T(8,128)(2,1)}, bf16[1024,4096]{1,0:T(8,128)(2,1)S(1)}, u32[]{:S(2)}) %copy-start.3) | copy-done | bytes 8388632
  15.6 0.0 copy-start.4
  15.6 0.8 %copy-done.4 = bf16[2048,128]{1,0:T(8,128)(2,1)} copy-done((bf16[2048,128]{1,0:T(8,128)(2,1)}, bf16[2048,128]{1,0:T(8,128)(2,1)S(1)}, u32[]{:S(2)}) %copy-start.4) | copy-done | bytes 524312
  16.4 1.5 %collective-permute-start.6 = (bf16[1024,128]{1,0:T(8,128)(2,1)S(1)}, bf16[1024,128]{1,0:T(8,128)(2,1)}, u32[]{:S(2)}, u32[]{:S(2)}) collective-permute-start(bf16[1024,128]{1,0:T(8,128)(2,1)S(1)} %get-tuple-element.22), channel_id=1, source_target_pairs={{0,1},{1,0},{2,3},{3,2},{4,5},{5,4},{6,7},{7,6},{8,9},{9,8},{10,11... | collective-permute-start | bytes 786440 | tf_op jit(solution)/shard_map/ppermute | solution.py:278
  17.9 0.0 collective-permute-done.refs_3_.refs_0_
  17.9 0.0 collective-permute-start.2
  17.9 0.0 collective-permute-done.1.refs_4_
  17.9 1.6 %collective-permute-start.3 = (bf16[1024,128]{1,0:T(8,128)(2,1)S(1)}, bf16[1024,128]{1,0:T(8,128)(2,1)S(1)}, u32[]{:S(2)}, u32[]{:S(2)}) collective-permute-start(bf16[1024,128]{1,0:T(8,128)(2,1)S(1)} %collective-permute-done.1.refs_4_), channel_id=1, source_target_pairs={{0,2},{1,3},{2,4},{3,5},{4,6},{5,7},{6,8},{7,9},{8,10},{9,11},{10,... | collective-permute-start | bytes 786440 | tf_op jit(solution)/shard_map/ppermute | solution.py:278
  19.5 0.0 copy-done
  19.5 0.0 copy-done.1
  19.5 0.0 copy-done.2
  19.5 5.6 %far.2 = (bf16[2,512,2048]{2,1,0:T(8,128)(2,1)S(1)}, bf16[1024,128]{1,0:T(8,128)(2,1)S(1)}, bf16[1024,128]{1,0:T(8,128)(2,1)S(1)}) custom-call(s32[32]{0:T(128)S(1)} %copy-done.2, bf16[4096,128]{1,0:T(8,128)(2,1)S(1)} %bitcast.5, bf16[4096,128]{1,0:T(8,128)(2,1)S(1)} %bitcast.8, f32[8,4096]{1,0:T(8,128)S(1)} %get-tuple-element.16.refs_2_, ...), custom_call_target="tpu_custom_call" | custom-call | flops 10737418240 | bytes 6291456 | tf_op jit(solution)/shard_map/far/pallas_call | solution.py:259
  25.1 0.1 collective-permute-start.4
  25.2 0.0 slice-start
  25.2 0.0 slice-start.1
  25.2 0.0 copy-start.5
  25.2 0.6 %collective-permute-start.5 = (bf16[1024,128]{1,0:T(8,128)(2,1)S(1)}, bf16[1024,128]{1,0:T(8,128)(2,1)S(1)}, u32[]{:S(2)}, u32[]{:S(2)}) collective-permute-start(bf16[1024,128]{1,0:T(8,128)(2,1)S(1)} %get-tuple-element.21), channel_id=1, source_target_pairs={{0,3},{1,2},{2,1},{3,0},{4,7},{5,6},{6,5},{7,4},{8,11},{9,10},{10,... | collective-permute-start | bytes 786440 | tf_op jit(solution)/shard_map/ppermute | solution.py:278
  25.9 0.5 %collective-permute-done.2.refs_3_.refs_2_ = bf16[1024,128]{1,0:T(8,128)(2,1)S(1)} collective-permute-done((bf16[1024,128]{1,0:T(8,128)(2,1)S(1)}, bf16[1024,128]{1,0:T(8,128)(2,1)S(1)}, u32[]{:S(2)}, u32[]{:S(2)}) %collective-permute-start.2) | collective-permute-done | bytes 262176 | tf_op jit(solution)/shard_map/ppermute | solution.py:278
  26.4 2.8 %collective-permute-done.3.refs_4_ = bf16[1024,128]{1,0:T(8,128)(2,1)S(1)} collective-permute-done((bf16[1024,128]{1,0:T(8,128)(2,1)S(1)}, bf16[1024,128]{1,0:T(8,128)(2,1)S(1)}, u32[]{:S(2)}, u32[]{:S(2)}) %collective-permute-start.3) | collective-permute-done | bytes 262176 | tf_op jit(solution)/shard_map/ppermute | solution.py:278
  29.2 5.6 %far.3 = (bf16[2,512,2048]{2,1,0:T(8,128)(2,1)S(1)}, bf16[1024,128]{1,0:T(8,128)(2,1)S(1)}, bf16[1024,128]{1,0:T(8,128)(2,1)S(1)}) custom-call(s32[32]{0:T(128)S(1)} %copy-done.2, bf16[4096,128]{1,0:T(8,128)(2,1)S(1)} %bitcast.6, bf16[4096,128]{1,0:T(8,128)(2,1)S(1)} %bitcast.9, f32[8,4096]{1,0:T(8,128)S(1)} %get-tuple-element.16.refs_2_, ...), custom_call_target="tpu_custom_call" | custom-call | flops 10737418240 | bytes 6291456 | tf_op jit(solution)/shard_map/far/pallas_call | solution.py:259
  34.8 0.0 collective-permute-done.4
  34.8 0.0 collective-permute-done.5
  34.8 0.1 add_convert_fusion.1
  34.9 1.8 %collective-permute-start.7 = (bf16[1024,128]{1,0:T(8,128)(2,1)S(1)}, bf16[1024,128]{1,0:T(8,128)(2,1)S(1)}, u32[]{:S(2)}, u32[]{:S(2)}) collective-permute-start(bf16[1024,128]{1,0:T(8,128)(2,1)S(1)} %add_convert_fusion.1), channel_id=1, source_target_pairs={{0,28},{1,29},{2,30},{3,31},{4,0},{5,1},{6,2},{7,3},{8,4},{9,5},{1... | collective-permute-start | bytes 786440 | tf_op jit(solution)/shard_map/ppermute | solution.py:278
  36.7 1.5 %collective-permute-start.8 = (bf16[1024,128]{1,0:T(8,128)(2,1)S(1)}, bf16[1024,128]{1,0:T(8,128)(2,1)S(1)}, u32[]{:S(2)}, u32[]{:S(2)}) collective-permute-start(bf16[1024,128]{1,0:T(8,128)(2,1)S(1)} %get-tuple-element.24), channel_id=1, source_target_pairs={{0,29},{1,28},{2,31},{3,30},{4,1},{5,0},{6,3},{7,2},{8,5},{9,4},{1... | collective-permute-start | bytes 786440 | tf_op jit(solution)/shard_map/ppermute | solution.py:278
  38.2 0.0 slice-done
  38.2 0.0 slice-done.1
  38.2 0.0 copy-done.5
  38.2 7.0 %queries.1 = bf16[4096,128]{1,0:T(8,128)(2,1)} custom-call(s32[32]{0:T(128)S(1)} %copy-done.2, bf16[2048,128]{1,0:T(8,128)(2,1)S(1)} %copy-done.5, bf16[1024,4096]{1,0:T(8,128)(2,1)S(1)} %bitcast.11, bf16[1024,128]{1,0:T(8,128)(2,1)S(1)} %collective-permute-done.refs_3_.refs_0_, bf16[2,512,2048]{2,1,0:T(8,128)(2,1)S(1)} %get-tuple-element.17.refs_1_, ...), custom_call_target="tpu_custom_call" | custom-call | flops 6710886400 | bytes 6291456 | tf_op jit(solution)/shard_map/queries/pallas_call | solution.py:259
  45.3 0.0 collective-permute-done.6
  45.3 2.5 %collective-permute-done.7 = bf16[1024,128]{1,0:T(8,128)(2,1)S(1)} collective-permute-done((bf16[1024,128]{1,0:T(8,128)(2,1)S(1)}, bf16[1024,128]{1,0:T(8,128)(2,1)S(1)}, u32[]{:S(2)}, u32[]{:S(2)}) %collective-permute-start.7) | collective-permute-done | bytes 262176 | tf_op jit(solution)/shard_map/ppermute | solution.py:278
  47.7 0.7 %collective-permute-done.8 = bf16[1024,128]{1,0:T(8,128)(2,1)S(1)} collective-permute-done((bf16[1024,128]{1,0:T(8,128)(2,1)S(1)}, bf16[1024,128]{1,0:T(8,128)(2,1)S(1)}, u32[]{:S(2)}, u32[]{:S(2)}) %collective-permute-start.8) | collective-permute-done | bytes 262176 | tf_op jit(solution)/shard_map/ppermute | solution.py:278
  48.4 1.2 %add_convert_fusion = bf16[1024,128]{1,0:T(8,128)(2,1)S(1)} fusion(bf16[1024,128]{1,0:T(8,128)(2,1)S(1)} %collective-permute-done.8, bf16[1024,128]{1,0:T(8,128)(2,1)S(1)} %collective-permute-done.7, bf16[1024,128]{1,0:T(8,128)(2,1)} %collective-permute-done.6, f32[1024,128]{1,0:T(8,128)S(1)} %get-tuple-element.19, ...), kind=kLoop, calls=%fused_computation | loop fusion | flops 1572864 | bytes 2097153 | tf_op jit(solution)/shard_map/convert_element_type | solution.py:352
  49.6 0.7 %fusion = (bf16[512,128]{1,0:T(8,128)(2,1)}, bf16[512,128]{1,0:T(8,128)(2,1)}) fusion(bf16[1024,128]{1,0:T(8,128)(2,1)S(1)} %add_convert_fusion), kind=kLoop, calls=%fused_computation.3 | loop fusion | bytes 524288 | tf_op jit(solution)/shard_map/slice | solution.py:353
  (1 shorter events, 0.0 us)
Async XLA Ops:
  0.6 17.3 %collective-permute-start = (bf16[1024,128]{1,0:T(8,128)(2,1)}, bf16[1024,128]{1,0:T(8,128)(2,1)S(1)}, u32[]{:S(2)}, u32[]{:S(2)}) collective-permute-start(bf16[1024,128]{1,0:T(8,128)(2,1)} %refs_4_.1), channel_id=1, source_target_pairs={{0,2},{1,3},{2,4},{3,5},{4,6},{5,7},{6,8},{7,9},{8,10},{9,11},{10,... | collective-permute-start | bytes 786440 | tf_op jit(solution)/shard_map/ppermute | solution.py:278
  1.1 16.8 %collective-permute-start.1 = (bf16[1024,128]{1,0:T(8,128)(2,1)}, bf16[1024,128]{1,0:T(8,128)(2,1)S(1)}, u32[]{:S(2)}, u32[]{:S(2)}) collective-permute-start(bf16[1024,128]{1,0:T(8,128)(2,1)} %refs_5_.1), channel_id=1, source_target_pairs={{0,2},{1,3},{2,4},{3,5},{4,6},{5,7},{6,8},{7,9},{8,10},{9,11},{10,... | collective-permute-start | bytes 786440 | tf_op jit(solution)/shard_map/ppermute | solution.py:278
  3.8 15.8 %copy-start = (bf16[1024,4,128]{2,1,0:T(4,128)(2,1)S(1)}, bf16[1024,4,128]{2,1,0:T(4,128)(2,1)}, u32[]{:S(2)}) copy-start(bf16[1024,4,128]{2,1,0:T(4,128)(2,1)} %param.7) | copy-start | bytes 3145732
  3.8 15.8 %copy-start.1 = (bf16[1024,4,128]{2,1,0:T(4,128)(2,1)S(1)}, bf16[1024,4,128]{2,1,0:T(4,128)(2,1)}, u32[]{:S(2)}) copy-start(bf16[1024,4,128]{2,1,0:T(4,128)(2,1)} %param.11) | copy-start | bytes 3145732
  3.8 15.8 %copy-start.2 = (s32[32]{0:T(128)S(1)}, s32[32]{0:T(128)}, u32[]{:S(2)}) copy-start(s32[32]{0:T(128)} %span_ids.5) | copy-start | bytes 388
  12.3 3.3 %copy-start.3 = (bf16[1024,4096]{1,0:T(8,128)(2,1)}, bf16[1024,4096]{1,0:T(8,128)(2,1)S(1)}, u32[]{:S(2)}) copy-start(bf16[1024,4096]{1,0:T(8,128)(2,1)S(1)} %get-tuple-element.15.own_ref) | copy-start | bytes 25165828
  15.6 0.8 %copy-start.4 = (bf16[2048,128]{1,0:T(8,128)(2,1)}, bf16[2048,128]{1,0:T(8,128)(2,1)S(1)}, u32[]{:S(2)}) copy-start(bf16[2048,128]{1,0:T(8,128)(2,1)S(1)} %get-tuple-element.14.both_ref) | copy-start | bytes 1572868
  16.4 28.9 %collective-permute-start.6 = (bf16[1024,128]{1,0:T(8,128)(2,1)S(1)}, bf16[1024,128]{1,0:T(8,128)(2,1)}, u32[]{:S(2)}, u32[]{:S(2)}) collective-permute-start(bf16[1024,128]{1,0:T(8,128)(2,1)S(1)} %get-tuple-element.22), channel_id=1, source_target_pairs={{0,1},{1,0},{2,3},{3,2},{4,5},{5,4},{6,7},{7,6},{8,9},{9,8},{10,11... | collective-permute-start | bytes 786440 | tf_op jit(solution)/shard_map/ppermute | solution.py:278
  17.9 8.5 %collective-permute-start.2 = (bf16[1024,128]{1,0:T(8,128)(2,1)S(1)}, bf16[1024,128]{1,0:T(8,128)(2,1)S(1)}, u32[]{:S(2)}, u32[]{:S(2)}) collective-permute-start(bf16[1024,128]{1,0:T(8,128)(2,1)S(1)} %collective-permute-done.refs_3_.refs_0_), channel_id=1, source_target_pairs={{0,2},{1,3},{2,4},{3,5},{4,6},{5,7},{6,8},{7,9},{8,10},{9,11},{10,... | collective-permute-start | bytes 786440 | tf_op jit(solution)/shard_map/ppermute | solution.py:278
  17.9 11.3 %collective-permute-start.3 = (bf16[1024,128]{1,0:T(8,128)(2,1)S(1)}, bf16[1024,128]{1,0:T(8,128)(2,1)S(1)}, u32[]{:S(2)}, u32[]{:S(2)}) collective-permute-start(bf16[1024,128]{1,0:T(8,128)(2,1)S(1)} %collective-permute-done.1.refs_4_), channel_id=1, source_target_pairs={{0,2},{1,3},{2,4},{3,5},{4,6},{5,7},{6,8},{7,9},{8,10},{9,11},{10,... | collective-permute-start | bytes 786440 | tf_op jit(solution)/shard_map/ppermute | solution.py:278
  25.1 9.7 %collective-permute-start.4 = (bf16[1024,128]{1,0:T(8,128)(2,1)S(1)}, bf16[1024,128]{1,0:T(8,128)(2,1)S(1)}, u32[]{:S(2)}, u32[]{:S(2)}) collective-permute-start(bf16[1024,128]{1,0:T(8,128)(2,1)S(1)} %get-tuple-element.20), channel_id=1, source_target_pairs={{0,2},{1,3},{2,0},{3,1},{4,6},{5,7},{6,4},{7,5},{8,10},{9,11},{10,... | collective-permute-start | bytes 786440 | tf_op jit(solution)/shard_map/ppermute | solution.py:278
  25.2 13.0 %slice-start = ((s8[8388608]{0:T(1024)(128)(4,1)}), s8[4194304]{0:T(1024)(128)(4,1)S(1)}, s32[]{:S(2)}) async-start(s8[8388608]{0:T(1024)(128)(4,1)} %bitcast.10), calls=%async_computation | async-start | bytes 8388608
  25.2 13.0 %slice-start.1 = ((s8[8388608]{0:T(1024)(128)(4,1)}), s8[4194304]{0:T(1024)(128)(4,1)S(1)}, s32[]{:S(2)}) async-start(s8[8388608]{0:T(1024)(128)(4,1)} %bitcast.10), calls=%async_computation.1 | async-start | bytes 8388608
  25.2 13.0 %copy-start.5 = (bf16[2048,128]{1,0:T(8,128)(2,1)S(1)}, bf16[2048,128]{1,0:T(8,128)(2,1)}, u32[]{:S(2)}) copy-start(bf16[2048,128]{1,0:T(8,128)(2,1)} %copy-done.4) | copy-start | bytes 1572868
  25.2 9.6 %collective-permute-start.5 = (bf16[1024,128]{1,0:T(8,128)(2,1)S(1)}, bf16[1024,128]{1,0:T(8,128)(2,1)S(1)}, u32[]{:S(2)}, u32[]{:S(2)}) collective-permute-start(bf16[1024,128]{1,0:T(8,128)(2,1)S(1)} %get-tuple-element.21), channel_id=1, source_target_pairs={{0,3},{1,2},{2,1},{3,0},{4,7},{5,6},{6,5},{7,4},{8,11},{9,10},{10,... | collective-permute-start | bytes 786440 | tf_op jit(solution)/shard_map/ppermute | solution.py:278
  34.9 12.8 %collective-permute-start.7 = (bf16[1024,128]{1,0:T(8,128)(2,1)S(1)}, bf16[1024,128]{1,0:T(8,128)(2,1)S(1)}, u32[]{:S(2)}, u32[]{:S(2)}) collective-permute-start(bf16[1024,128]{1,0:T(8,128)(2,1)S(1)} %add_convert_fusion.1), channel_id=1, source_target_pairs={{0,28},{1,29},{2,30},{3,31},{4,0},{5,1},{6,2},{7,3},{8,4},{9,5},{1... | collective-permute-start | bytes 786440 | tf_op jit(solution)/shard_map/ppermute | solution.py:278
  36.7 11.7 %collective-permute-start.8 = (bf16[1024,128]{1,0:T(8,128)(2,1)S(1)}, bf16[1024,128]{1,0:T(8,128)(2,1)S(1)}, u32[]{:S(2)}, u32[]{:S(2)}) collective-permute-start(bf16[1024,128]{1,0:T(8,128)(2,1)S(1)} %get-tuple-element.24), channel_id=1, source_target_pairs={{0,29},{1,28},{2,31},{3,30},{4,1},{5,0},{6,3},{7,2},{8,5},{9,4},{1... | collective-permute-start | bytes 786440 | tf_op jit(solution)/shard_map/ppermute | solution.py:278

commit v5 on v4

--- a/solution.py
+++ b/solution.py
@@ -103,22 +103,26 @@
     )
 
 
-def put_shares(outs, key_acc, value_acc, scale):
+def put_shares(outs, key_acc, value_acc, scale, more=None):
     parts = len(outs)
     share = key_acc.shape[0] // parts
     x = lax.axis_index("head")
     for away, out in enumerate(outs):
         start = pl.multiple_of(lax.rem(x + away, parts) * share, share)
-        out[0:share, :] = (key_acc[pl.ds(start, share), :] * scale).astype(out.dtype)
-        out[share : 2 * share, :] = value_acc[pl.ds(start, share), :].astype(out.dtype)
-
-
-def own_kernel(heads, tile, scale, parts, *refs):
-    inputs, refs = refs[:7], refs[7:]
-    terms_ref, both_ref, kept_ref = refs[:3]
-    outs, refs = refs[3 : 3 + parts], refs[3 + parts :]
-    held, (key_acc, value_acc, sems) = refs[:5], refs[5:]
-    query_ref, grad_ref, outputs_ref, norm_ref, span_ids = held
+        for low, part in (
+            (0, key_acc[pl.ds(start, share), :] * scale),
+            (share, value_acc[pl.ds(start, share), :]),
+        ):
+            if more is not None:
+                part = part + more(away, low, share)
+            out[low : low + share, :] = part.astype(out.dtype)
+
+
+def first_kernel(heads, tile, scale, *refs):
+    inputs, refs = refs[:6], refs[6:]
+    terms_ref, both_ref, kept_ref, key_acc, value_acc = refs[:5]
+    held, sems = refs[5:-1], refs[-1]
+    grad_ref, outputs_ref, query_ref, norm_ref = held
     toks = both_ref.shape[0] // 2
     key_ref, value_ref = both_ref.at[pl.ds(0, toks)], both_ref.at[pl.ds(toks, toks)]
     half = toks // 2
@@ -126,14 +130,14 @@
     per = tile // heads
     whole = [
         pltpu.make_async_copy(a, b, sems.at[i, 2])
-        for i, (a, b) in enumerate(zip(inputs[3:], (norm_ref, key_ref, value_ref, span_ids)))
+        for i, (a, b) in enumerate(zip(inputs[3:], (norm_ref, key_ref, value_ref)))
     ]
 
     def halves(index):
         part = pl.ds(pl.multiple_of(index * rows, rows), rows)
         return [
             pltpu.make_async_copy(inputs[i].at[part], held[i].at[part], sems.at[i, index])
-            for i in (1, 2, 0)
+            for i in range(3)
         ]
 
     for copy in whole + halves(0) + halves(1):
@@ -141,14 +145,9 @@
     key_acc[...] = jnp.zeros_like(key_acc)
     value_acc[...] = jnp.zeros_like(value_acc)
     group = (query_ref, grad_ref, key_ref, value_ref, terms_ref, tile)
-    accs = (key_acc, value_acc)
     triangle = lax.broadcasted_iota(jnp.int32, (per, tile), 0) <= (
         lax.broadcasted_iota(jnp.int32, (per, tile), 1) // heads
     )
-
-    def placed(row, key, length, triangle):
-        return row, key, length, triangle, kept_ref.at[pl.ds(key, length), pl.ds(row, tile)]
-
     for copy in whole:
         copy.wait()
 
@@ -158,21 +157,12 @@
             copy.wait()
         row_terms(heads, tile, index, (grad_ref, outputs_ref, norm_ref), terms_ref)
         key = pl.multiple_of(index * half, half)
-        tiles = [
-            placed(pl.multiple_of(index * rows + p * tile, tile), key, (p + 1) * per, triangle)
-            for p in range(half // per)
-        ]
-        tile_grads(group, accs, scale, tiles)
-
-    first, second = span_pair(span_ids, lax.axis_index("ctx"))
-    low = jnp.where(first > second, 1, 0)
-    key = pl.multiple_of(low * half, half)
-    tiles = [
-        placed(pl.multiple_of((1 - low) * rows + p * tile, tile), key, half, None)
-        for p in range(rows // tile)
-    ]
-    tile_grads(group, accs, scale, tiles)
-    put_shares(outs, key_acc, value_acc, scale)
+        tiles = []
+        for p in range(half // per):
+            row, length = pl.multiple_of(index * rows + p * tile, tile), (p + 1) * per
+            kept = kept_ref.at[pl.ds(key, length), pl.ds(row, tile)]
+            tiles.append((row, key, length, triangle, kept))
+        tile_grads(group, (key_acc, value_acc), scale, tiles)
 
 
 def far_kernel(heads, tile, scale, parts, step, span_ids, *refs):
@@ -203,7 +193,53 @@
         ]
         tile_grads(group, (key_acc, value_acc), scale, tiles)
 
+    if len(outs) == 1:
+        outs = [outs[0].at[away] for away in range(parts)]
     put_shares(outs, key_acc, value_acc, scale)
+
+
+def join_kernel(swapped_ref, *refs):
+    ins, outs = refs[: len(refs) // 2], refs[len(refs) // 2 :]
+    odd = lax.rem(lax.axis_index("ctx"), 2).astype(jnp.float32)
+    for away, (this, out) in enumerate(zip(ins, outs)):
+        more = swapped_ref[away].astype(jnp.float32) * odd
+        out[...] = (this[...].astype(jnp.float32) + more).astype(out.dtype)
+
+
+def last_kernel(heads, tile, scale, parts, span_ids, *refs):
+    query_ref, grad_ref, terms_ref, both_ref, swapped_ref = refs[:5]
+    kept_ref, key_acc, value_acc = refs[8:11]
+    outs = refs[11:]
+    toks = both_ref.shape[0] // 2
+    key_ref, value_ref = both_ref.at[pl.ds(0, toks)], both_ref.at[pl.ds(toks, toks)]
+    half = toks // 2
+    rows = half * heads
+    me = lax.axis_index("ctx")
+    first, second = span_pair(span_ids, me)
+    low = jnp.where(first > second, 1, 0)
+    key = pl.multiple_of(low * half, half)
+    tiles = []
+    for p in range(rows // tile):
+        row = pl.multiple_of((1 - low) * rows + p * tile, tile)
+        tiles.append((row, key, half, None, kept_ref.at[pl.ds(key, half), pl.ds(row, tile)]))
+    group = (query_ref, grad_ref, key_ref, value_ref, terms_ref, tile)
+    tile_grads(group, (key_acc, value_acc), scale, tiles)
+    even = 1.0 - lax.rem(me, 2).astype(jnp.float32)
+
+    def more(away, start, count):
+        return swapped_ref[away, start : start + count, :].astype(jnp.float32) * even
+
+    put_shares(outs, key_acc, value_acc, scale, more)
+
+
+def total_kernel(total_ref, *refs):
+    ins, (key_out, value_out) = refs[:-2], refs[-2:]
+    share = key_out.shape[0]
+    for low, out in ((0, key_out), (share, value_out)):
+        part = total_ref[low : low + share, :]
+        for ref in ins:
+            part = part + ref[low : low + share, :].astype(jnp.float32)
+        out[...] = part.astype(out.dtype)
 
 
 def query_kernel(heads, tile, scale, span_ids, both_ref, own_ref, *refs):
@@ -254,7 +290,7 @@
 MIB = 1024 * 1024
 
 
-def call(kernel, ins, where, outs, scratch, blocks, limit, name):
+def call(kernel, ins, where, outs, scratch, blocks, limit, name, aliases=None):
     flops = blocks * 40 * 512 * 512 * 128
     return pl.pallas_call(
         kernel,
@@ -262,6 +298,7 @@
         in_specs=where,
         out_specs=[VMEM] * len(outs),
         scratch_shapes=scratch,
+        input_output_aliases=aliases or {},
         compiler_params=pltpu.CompilerParams(vmem_limit_bytes=limit * MIB),
         name=name,
         cost_estimate=pl.CostEstimate(flops=int(flops), bytes_accessed=6 << 20, transcendentals=0),
@@ -291,32 +328,27 @@
     f32, bf16 = jnp.float32, jnp.bfloat16
     shape = jax.ShapeDtypeStruct
     grads = [shape((share, dim), bf16)] * parts
+    packed = [shape((parts, share, dim), bf16)]
     accs = [pltpu.VMEM((toks, dim), f32)] * 2
 
     key_1, value_1 = moved(keys, (-1, -1), 0), moved(values, (-1, -1), 0)
     inputs = tuple(
-        pltpu.with_memory_space_constraint(a, pltpu.HBM)
-        for a in (q, g, o, log_norm, keys, values, span_ids)
-    )
-    terms, both, kept, total, *sent = call(
-        functools.partial(own_kernel, heads, tile, scale, parts),
+        pltpu.with_memory_space_constraint(a, pltpu.HBM) for a in (g, o, q, log_norm, keys, values)
+    )
+    sums = [shape((toks, rows), bf16), shape((toks, dim), f32), shape((toks, dim), f32)]
+    terms, both, kept, key_sum, value_sum = call(
+        functools.partial(first_kernel, heads, tile, scale),
         inputs,
         [HBM] * len(inputs),
-        [shape((8, rows), f32), shape((2 * toks, dim), bf16), shape((toks, rows), bf16)]
-        + [shape((share, dim), f32)]
-        + grads[1:],
-        [pltpu.VMEM(a.shape, a.dtype) for a in inputs[:4]]
-        + [pltpu.SMEM(span_ids.shape, span_ids.dtype)]
-        + accs
-        + [pltpu.SemaphoreType.DMA((4, 3))],
-        2.25 * heads,
+        [shape((8, rows), f32), shape((2 * toks, dim), bf16)] + sums,
+        [pltpu.VMEM(a.shape, a.dtype) for a in inputs[:4]] + [pltpu.SemaphoreType.DMA((3, 3))],
+        1.25 * heads,
         20,
-        "own",
-    )
-    landed = [moved(block, (0, 0), away + 1) for away, block in enumerate(sent)]
+        "first",
+    )
     key_2, value_2 = moved(key_1, (-1, -1), 0), moved(value_1, (-1, -1), 0)
 
-    def far(step, key, value):
+    def far(step, key, value, grads):
         return call(
             functools.partial(far_kernel, heads, tile, scale, parts, step),
             (span_ids, q, g, terms, key, value),
@@ -328,15 +360,23 @@
             "far",
         )
 
-    kept_1, *sent = far(1, key_1, value_1)
-    joined = [moved(block, (-1, 1), away) for away, block in enumerate(sent)]
-    kept_2, *sent = far(2, key_2, value_2)
-    odd = lax.axis_index("ctx") % 2 == 1
-    joined = sum(block.astype(f32) for block in joined)
-    straight = sent[0].astype(f32) + jnp.where(odd, joined, 0.0)
-    total = total + jnp.where(odd, 0.0, joined)
-    for away, block in enumerate([straight.astype(bf16)] + sent[1:]):
-        landed.append(moved(block, (2, 2), away))
+    kept_1, near = far(1, key_1, value_1, packed)
+    swapped = moved(near, (-1, 1), 0)
+    kept_2, *sent = far(2, key_2, value_2, grads)
+    sent = call(join_kernel, (swapped, *sent), [VMEM] * (1 + parts), grads, [], 0.01, 4, "join")
+    landed = [moved(block, (2, 2), away) for away, block in enumerate(sent)]
+    kept, _, _, total, *sent = call(
+        functools.partial(last_kernel, heads, tile, scale, parts),
+        (span_ids, q, g, terms, both, swapped, kept, key_sum, value_sum),
+        [SMEM] + [VMEM] * 8,
+        sums + [shape((share, dim), f32)] + grads[1:],
+        [],
+        heads,
+        20,
+        "last",
+        {6: 0, 7: 1, 8: 2},
+    )
+    landed += [moved(block, (0, 0), away + 1) for away, block in enumerate(sent)]
     (query_grad,) = call(
         functools.partial(query_kernel, heads, tile, scale),
         (span_ids, both, kept, key_1, kept_1, key_2, kept_2),
@@ -347,10 +387,17 @@
         28,
         "queries",
     )
-    for block in landed:
-        total = total + block.astype(f32)
-    total = total.astype(bf16)
-    return query_grad.reshape(toks, heads, dim), total[: share // 2], total[share // 2 :]
+    key_grad, value_grad = call(
+        total_kernel,
+        (total, *landed),
+        [VMEM] * (1 + len(landed)),
+        [shape((share // 2, dim), bf16)] * 2,
+        [],
+        0.01,
+        8,
+        "total",
+    )
+    return query_grad.reshape(toks, heads, dim), key_grad, value_grad
 
 
 def solution(mesh):

time: 50.5 us -> 47.3 us (0.937)
  local copies, waits for them, and re-layouts: 4.78 us -> 0.01 us
  waiting for transfers between devices: 6.53 us -> 10.7 us
  starting transfers between devices: 10.3 us -> 7.43 us
  Pallas kernels: 26.7 us -> 28.3 us
  other arithmetic: 1.28 us -> 0 us
    ppermute x9 -> x8, waiting for transfers between devices: 6.53 us -> 10.7 us  [moved(): return lax.ppermute(block, ('ctx', 'head'), route)]
    unnamed x16 -> x6, local copies, waits for them, and re-layouts: 4.06 us -> 0.01 us
    ppermute x9 -> x8, starting transfers between devices: 10.3 us -> 7.43 us  [moved(): return lax.ppermute(block, ('ctx', 'head'), route)]
    pallas_call x4 -> x7, Pallas kernels: 26.7 us -> 28.3 us  [call(): pl.pallas_call(kernel, out_shape=outs, in_specs=where, out_specs=[VMEM] *...]
    convert_element_type x2 -> x0, other arithmetic: 1.28 us -> none  [the longest x1 1.16 us: local(): total = total.astype(bf16)]
    slice x1 -> x0, local copies, waits for them, and re-layouts: 0.72 us -> none  [local(): total[share // 2:]]
  transfers between devices with their start and end apart: 9 -> 8, of which waited for: 4 -> 4; matrix products, arithmetic and copies ran while one was open for 0% -> 0% of each run, Pallas kernels for 53% -> 58%
where the time goes in v5:
time: 47.3 us; the launch traced here: 47.2 us
  Pallas kernels  28.3 us (60%)
  waiting for transfers between devices  10.7 us (23%)
  starting transfers between devices  7.43 us (16%)
  between operations  0.71 us (2%)
    pallas_call x7, Pallas kernels, call(): pl.pallas_call(kernel, out_shape=outs, in_specs=where, out_specs=[VMEM] *...  28.3 us
    ppermute x8, waiting for transfers between devices, moved(): return lax.ppermute(block, ('ctx', 'head'), route)  10.7 us
    ppermute x8, starting transfers between devices, moved(): return lax.ppermute(block, ('ctx', 'head'), route)  7.43 us
  transfers between devices with their start and end apart: 8, of which 4 were waited for; matrix products, arithmetic and copies ran while one was open for 0% of the time, Pallas kernels for 58%

profile of v5, /device:TPU:0, one launch (start us, length us, event | category | flops | bytes accessed | tf_op | source)
XLA Modules:
  0.0 47.2 jit_solution(5167045136436014372)
XLA Ops:
  0.6 0.5 %collective-permute-start = (bf16[1024,128]{1,0:T(8,128)(2,1)}, bf16[1024,128]{1,0:T(8,128)(2,1)S(1)}, u32[]{:S(2)}, u32[]{:S(2)}) collective-permute-start(bf16[1024,128]{1,0:T(8,128)(2,1)} %refs_4_.1), channel_id=1, source_target_pairs={{0,2},{1,3},{2,4},{3,5},{4,6},{5,7},{6,8},{7,9},{8,10},{9,11},{10,... | collective-permute-start | bytes 786440 | tf_op jit(solution)/shard_map/ppermute | solution.py:315
  1.1 2.6 %collective-permute-start.1 = (bf16[1024,128]{1,0:T(8,128)(2,1)}, bf16[1024,128]{1,0:T(8,128)(2,1)S(1)}, u32[]{:S(2)}, u32[]{:S(2)}) collective-permute-start(bf16[1024,128]{1,0:T(8,128)(2,1)} %refs_5_.1), channel_id=1, source_target_pairs={{0,2},{1,3},{2,4},{3,5},{4,6},{5,7},{6,8},{7,9},{8,10},{9,11},{10,... | collective-permute-start | bytes 786440 | tf_op jit(solution)/shard_map/ppermute | solution.py:315
  3.8 0.0 copy-start
  3.8 0.0 copy-start.1
  3.8 0.0 copy-start.2
  3.8 5.9 %first.1 = (f32[8,4096]{1,0:T(8,128)S(1)}, bf16[2048,128]{1,0:T(8,128)(2,1)S(1)}, bf16[1024,4096]{1,0:T(8,128)(2,1)S(1)}, f32[1024,128]{1,0:T(8,128)S(1)}, f32[1024,128]{1,0:T(8,128)S(1)}) custom-call(bf16[4096,128]{1,0:T(8,128)(2,1)} %bitcast.4, bf16[4096,128]{1,0:T(8,128)(2,1)} %bitcast.12, bf16[4096,128]{1,0:T(8,128)(2,1)} %bitcast.8, f32[4,1024]{1,0:T(4,128)} %refs_3_.1, ...), custom_call_target="tpu_custom_call" | custom-call | flops 6710886400 | bytes 6291456 | tf_op jit(solution)/shard_map/first/pallas_call | solution.py:295
  9.7 0.7 %collective-permute-done.refs_3_.refs_0_ = bf16[1024,128]{1,0:T(8,128)(2,1)S(1)} collective-permute-done((bf16[1024,128]{1,0:T(8,128)(2,1)}, bf16[1024,128]{1,0:T(8,128)(2,1)S(1)}, u32[]{:S(2)}, u32[]{:S(2)}) %collective-permute-start) | collective-permute-done | bytes 262176 | tf_op jit(solution)/shard_map/ppermute | solution.py:315
  10.4 0.0 collective-permute-start.3
  10.4 2.8 %collective-permute-done.1.refs_4_ = bf16[1024,128]{1,0:T(8,128)(2,1)S(1)} collective-permute-done((bf16[1024,128]{1,0:T(8,128)(2,1)}, bf16[1024,128]{1,0:T(8,128)(2,1)S(1)}, u32[]{:S(2)}, u32[]{:S(2)}) %collective-permute-start.1) | collective-permute-done | bytes 262176 | tf_op jit(solution)/shard_map/ppermute | solution.py:315
  13.2 0.0 collective-permute-start.4
  13.2 0.0 copy-done
  13.2 0.0 copy-done.1
  13.2 0.0 copy-done.2
  13.2 5.6 %far.2 = (bf16[2,512,2048]{2,1,0:T(8,128)(2,1)S(1)}, bf16[2,1024,128]{2,1,0:T(8,128)(2,1)S(1)}) custom-call(s32[32]{0:T(128)S(1)} %copy-done.2, bf16[4096,128]{1,0:T(8,128)(2,1)S(1)} %bitcast.9, bf16[4096,128]{1,0:T(8,128)(2,1)S(1)} %bitcast.5, f32[8,4096]{1,0:T(8,128)S(1)} %get-tuple-element.21.refs_2_, ...), custom_call_target="tpu_custom_call" | custom-call | flops 10737418240 | bytes 6291456 | tf_op jit(solution)/shard_map/far/pallas_call | solution.py:295
  18.9 0.1 collective-permute-start.2
  18.9 0.0 collective-permute-done.3.refs_3_.refs_2_
  18.9 2.8 %collective-permute-done.4.refs_4_ = bf16[1024,128]{1,0:T(8,128)(2,1)S(1)} collective-permute-done((bf16[1024,128]{1,0:T(8,128)(2,1)S(1)}, bf16[1024,128]{1,0:T(8,128)(2,1)S(1)}, u32[]{:S(2)}, u32[]{:S(2)}) %collective-permute-start.4) | collective-permute-done | bytes 262176 | tf_op jit(solution)/shard_map/ppermute | solution.py:315
  21.7 5.6 %far.3 = (bf16[2,512,2048]{2,1,0:T(8,128)(2,1)S(1)}, bf16[1024,128]{1,0:T(8,128)(2,1)S(1)}, bf16[1024,128]{1,0:T(8,128)(2,1)S(1)}) custom-call(s32[32]{0:T(128)S(1)} %copy-done.2, bf16[4096,128]{1,0:T(8,128)(2,1)S(1)} %bitcast.10, bf16[4096,128]{1,0:T(8,128)(2,1)S(1)} %bitcast.6, f32[8,4096]{1,0:T(8,128)S(1)} %get-tuple-element.21.refs_2_, ...), custom_call_target="tpu_custom_call" | custom-call | flops 10737418240 | bytes 6291456 | tf_op jit(solution)/shard_map/far/pallas_call | solution.py:295
  27.3 0.0 collective-permute-done.2.refs_4_.swapped_ref
  27.3 0.2 join.1
  27.5 2.1 %collective-permute-start.5 = (bf16[1024,128]{1,0:T(8,128)(2,1)S(1)}, bf16[1024,128]{1,0:T(8,128)(2,1)S(1)}, u32[]{:S(2)}, u32[]{:S(2)}) collective-permute-start(bf16[1024,128]{1,0:T(8,128)(2,1)S(1)} %get-tuple-element.32), channel_id=1, source_target_pairs={{0,28},{1,29},{2,30},{3,31},{4,0},{5,1},{6,2},{7,3},{8,4},{9,5},{1... | collective-permute-start | bytes 786440 | tf_op jit(solution)/shard_map/ppermute | solution.py:315
  29.6 1.6 %collective-permute-start.6 = (bf16[1024,128]{1,0:T(8,128)(2,1)S(1)}, bf16[1024,128]{1,0:T(8,128)(2,1)S(1)}, u32[]{:S(2)}, u32[]{:S(2)}) collective-permute-start(bf16[1024,128]{1,0:T(8,128)(2,1)S(1)} %get-tuple-element.33), channel_id=1, source_target_pairs={{0,29},{1,28},{2,31},{3,30},{4,1},{5,0},{6,3},{7,2},{8,5},{9,4},{1... | collective-permute-start | bytes 786440 | tf_op jit(solution)/shard_map/ppermute | solution.py:315
  31.2 3.2 %last.1 = (bf16[1024,4096]{1,0:T(8,128)(2,1)S(1)}, f32[1024,128]{1,0:T(8,128)S(1)}, f32[1024,128]{1,0:T(8,128)S(1)}, f32[1024,128]{1,0:T(8,128)S(1)}, bf16[1024,128]{1,0:T(8,128)(2,1)S(1)}) custom-call(s32[32]{0:T(128)S(1)} %copy-done.2, bf16[4096,128]{1,0:T(8,128)(2,1)S(1)} %bitcast.11, ...), custom_call_target="tpu_custom_call", output_to_operand_aliasing={{0}: (6, {}), {1}: (7, {}), {2}: (8, {})} | custom-call | flops 5368709120 | bytes 6291456 | tf_op jit(solution)/shard_map/last/pallas_call | solution.py:295
  34.4 0.5 %collective-permute-start.7 = (bf16[1024,128]{1,0:T(8,128)(2,1)S(1)}, bf16[1024,128]{1,0:T(8,128)(2,1)S(1)}, u32[]{:S(2)}, u32[]{:S(2)}) collective-permute-start(bf16[1024,128]{1,0:T(8,128)(2,1)S(1)} %get-tuple-element.34), channel_id=1, source_target_pairs={{0,1},{1,0},{2,3},{3,2},{4,5},{5,4},{6,7},{7,6},{8,9},{9,8},{10,11... | collective-permute-start | bytes 786440 | tf_op jit(solution)/shard_map/ppermute | solution.py:315
  34.9 7.0 %queries.1 = bf16[4096,128]{1,0:T(8,128)(2,1)} custom-call(s32[32]{0:T(128)S(1)} %copy-done.2, bf16[2048,128]{1,0:T(8,128)(2,1)S(1)} %get-tuple-element.20.refs_3_.both_ref, bf16[1024,4096]{1,0:T(8,128)(2,1)S(1)} %get-tuple-element.26.own_ref, bf16[1024,128]{1,0:T(8,128)(2,1)S(1)} %collective-permute-done.refs_3_.refs_0_, ...), custom_call_target="tpu_custom_call" | custom-call | flops 6710886400 | bytes 6291456 | tf_op jit(solution)/shard_map/queries/pallas_call | solution.py:295
  41.9 0.0 collective-permute-done.5.refs_0_
  41.9 0.0 collective-permute-done.6.refs_1_
  41.9 4.5 %collective-permute-done.7.refs_2_ = bf16[1024,128]{1,0:T(8,128)(2,1)S(1)} collective-permute-done((bf16[1024,128]{1,0:T(8,128)(2,1)S(1)}, bf16[1024,128]{1,0:T(8,128)(2,1)S(1)}, u32[]{:S(2)}, u32[]{:S(2)}) %collective-permute-start.7) | collective-permute-done | bytes 262176 | tf_op jit(solution)/shard_map/ppermute | solution.py:315
  46.4 0.8 %total.1 = (bf16[512,128]{1,0:T(8,128)(2,1)}, bf16[512,128]{1,0:T(8,128)(2,1)}) custom-call(f32[1024,128]{1,0:T(8,128)S(1)} %get-tuple-element.29.total_ref, bf16[1024,128]{1,0:T(8,128)(2,1)S(1)} %collective-permute-done.5.refs_0_, bf16[1024,128]{1,0:T(8,128)(2,1)S(1)} %collective-permute-done.6.refs_1_, bf16[1024,128]{1,0:T(8,128)(2,1)S(1)} %collective-permute-done.7.refs_2_), custom_call_target="tpu_custom_call" | custom-call | flops 13421772 | bytes 6291456 | tf_op jit(solution)/shard_map/total/pallas_call | solution.py:295
Async XLA Ops:
  0.6 9.8 %collective-permute-start = (bf16[1024,128]{1,0:T(8,128)(2,1)}, bf16[1024,128]{1,0:T(8,128)(2,1)S(1)}, u32[]{:S(2)}, u32[]{:S(2)}) collective-permute-start(bf16[1024,128]{1,0:T(8,128)(2,1)} %refs_4_.1), channel_id=1, source_target_pairs={{0,2},{1,3},{2,4},{3,5},{4,6},{5,7},{6,8},{7,9},{8,10},{9,11},{10,... | collective-permute-start | bytes 786440 | tf_op jit(solution)/shard_map/ppermute | solution.py:315
  1.1 12.1 %collective-permute-start.1 = (bf16[1024,128]{1,0:T(8,128)(2,1)}, bf16[1024,128]{1,0:T(8,128)(2,1)S(1)}, u32[]{:S(2)}, u32[]{:S(2)}) collective-permute-start(bf16[1024,128]{1,0:T(8,128)(2,1)} %refs_5_.1), channel_id=1, source_target_pairs={{0,2},{1,3},{2,4},{3,5},{4,6},{5,7},{6,8},{7,9},{8,10},{9,11},{10,... | collective-permute-start | bytes 786440 | tf_op jit(solution)/shard_map/ppermute | solution.py:315
  3.8 9.4 %copy-start = (bf16[1024,4,128]{2,1,0:T(4,128)(2,1)S(1)}, bf16[1024,4,128]{2,1,0:T(4,128)(2,1)}, u32[]{:S(2)}) copy-start(bf16[1024,4,128]{2,1,0:T(4,128)(2,1)} %param.11) | copy-start | bytes 3145732
  3.8 9.4 %copy-start.1 = (bf16[1024,4,128]{2,1,0:T(4,128)(2,1)S(1)}, bf16[1024,4,128]{2,1,0:T(4,128)(2,1)}, u32[]{:S(2)}) copy-start(bf16[1024,4,128]{2,1,0:T(4,128)(2,1)} %param.7) | copy-start | bytes 3145732
  3.8 9.4 %copy-start.2 = (s32[32]{0:T(128)S(1)}, s32[32]{0:T(128)}, u32[]{:S(2)}) copy-start(s32[32]{0:T(128)} %span_ids.7) | copy-start | bytes 388
  10.4 8.5 %collective-permute-start.3 = (bf16[1024,128]{1,0:T(8,128)(2,1)S(1)}, bf16[1024,128]{1,0:T(8,128)(2,1)S(1)}, u32[]{:S(2)}, u32[]{:S(2)}) collective-permute-start(bf16[1024,128]{1,0:T(8,128)(2,1)S(1)} %collective-permute-done.refs_3_.refs_0_), channel_id=1, source_target_pairs={{0,2},{1,3},{2,4},{3,5},{4,6},{5,7},{6,8},{7,9},{8,10},{9,11},{10,... | collective-permute-start | bytes 786440 | tf_op jit(solution)/shard_map/ppermute | solution.py:315
  13.2 8.5 %collective-permute-start.4 = (bf16[1024,128]{1,0:T(8,128)(2,1)S(1)}, bf16[1024,128]{1,0:T(8,128)(2,1)S(1)}, u32[]{:S(2)}, u32[]{:S(2)}) collective-permute-start(bf16[1024,128]{1,0:T(8,128)(2,1)S(1)} %collective-permute-done.1.refs_4_), channel_id=1, source_target_pairs={{0,2},{1,3},{2,4},{3,5},{4,6},{5,7},{6,8},{7,9},{8,10},{9,11},{10,... | collective-permute-start | bytes 786440 | tf_op jit(solution)/shard_map/ppermute | solution.py:315
  18.9 8.5 %collective-permute-start.2 = (bf16[2,1024,128]{2,1,0:T(8,128)(2,1)S(1)}, bf16[2,1024,128]{2,1,0:T(8,128)(2,1)S(1)}, u32[]{:S(2)}, u32[]{:S(2)}) collective-permute-start(bf16[2,1024,128]{2,1,0:T(8,128)(2,1)S(1)} %get-tuple-element.22), channel_id=1, source_target_pairs={{0,2},{1,3},{2,0},{3,1},{4,6},{5,7},{6,4},{7,5},{8,10},{9,11},{10,... | collective-permute-start | bytes 1572872 | tf_op jit(solution)/shard_map/ppermute | solution.py:315
  27.5 14.4 %collective-permute-start.5 = (bf16[1024,128]{1,0:T(8,128)(2,1)S(1)}, bf16[1024,128]{1,0:T(8,128)(2,1)S(1)}, u32[]{:S(2)}, u32[]{:S(2)}) collective-permute-start(bf16[1024,128]{1,0:T(8,128)(2,1)S(1)} %get-tuple-element.32), channel_id=1, source_target_pairs={{0,28},{1,29},{2,30},{3,31},{4,0},{5,1},{6,2},{7,3},{8,4},{9,5},{1... | collective-permute-start | bytes 786440 | tf_op jit(solution)/shard_map/ppermute | solution.py:315
  29.6 12.3 %collective-permute-start.6 = (bf16[1024,128]{1,0:T(8,128)(2,1)S(1)}, bf16[1024,128]{1,0:T(8,128)(2,1)S(1)}, u32[]{:S(2)}, u32[]{:S(2)}) collective-permute-start(bf16[1024,128]{1,0:T(8,128)(2,1)S(1)} %get-tuple-element.33), channel_id=1, source_target_pairs={{0,29},{1,28},{2,31},{3,30},{4,1},{5,0},{6,3},{7,2},{8,5},{9,4},{1... | collective-permute-start | bytes 786440 | tf_op jit(solution)/shard_map/ppermute | solution.py:315
  34.4 12.0 %collective-permute-start.7 = (bf16[1024,128]{1,0:T(8,128)(2,1)S(1)}, bf16[1024,128]{1,0:T(8,128)(2,1)S(1)}, u32[]{:S(2)}, u32[]{:S(2)}) collective-permute-start(bf16[1024,128]{1,0:T(8,128)(2,1)S(1)} %get-tuple-element.34), channel_id=1, source_target_pairs={{0,1},{1,0},{2,3},{3,2},{4,5},{5,4},{6,7},{7,6},{8,9},{9,8},{10,11... | collective-permute-start | bytes 786440 | tf_op jit(solution)/shard_map/ppermute | solution.py:315

commit v6 on v5

--- a/solution.py
+++ b/solution.py
@@ -103,66 +103,110 @@
     )
 
 
-def put_shares(outs, key_acc, value_acc, scale, more=None):
-    parts = len(outs)
+def put_shares(outs, key_acc, value_acc, scale, first=0, parts=None):
+    parts = parts or len(outs) + first
     share = key_acc.shape[0] // parts
     x = lax.axis_index("head")
-    for away, out in enumerate(outs):
+    for away, out in enumerate(outs, first):
         start = pl.multiple_of(lax.rem(x + away, parts) * share, share)
-        for low, part in (
-            (0, key_acc[pl.ds(start, share), :] * scale),
-            (share, value_acc[pl.ds(start, share), :]),
-        ):
-            if more is not None:
-                part = part + more(away, low, share)
-            out[low : low + share, :] = part.astype(out.dtype)
-
-
-def first_kernel(heads, tile, scale, *refs):
-    inputs, refs = refs[:6], refs[6:]
+        out[0:share, :] = (key_acc[pl.ds(start, share), :] * scale).astype(out.dtype)
+        out[share : 2 * share, :] = value_acc[pl.ds(start, share), :].astype(out.dtype)
+
+
+def own_tiles(group, accs, scale, span_ids, kept_ref, heads, halves):
+    tile = group[-1]
+    toks, rows = kept_ref.shape
+    half, span_rows, per = toks // 2, rows // 2, tile // heads
+    first, second = span_pair(span_ids, lax.axis_index("ctx"))
+    low = jnp.where(first > second, 1, 0)
+    triangle = lax.broadcasted_iota(jnp.int32, (per, tile), 0) <= (
+        lax.broadcasted_iota(jnp.int32, (per, tile), 1) // heads
+    )
+
+    def placed(row, key, length, triangle):
+        return row, key, length, triangle, kept_ref.at[pl.ds(key, length), pl.ds(row, tile)]
+
+    for before, which in halves:
+        before()
+        key = pl.multiple_of(which * half, half)
+        tiles = []
+        for p in range(span_rows // tile):
+            row = pl.multiple_of(which * span_rows + p * tile, tile)
+            tiles.append(placed(row, key, (p + 1) * per, triangle))
+        tile_grads(group, accs, scale, tiles)
+
+    def square():
+        key = pl.multiple_of(low * half, half)
+        tiles = []
+        for p in range(span_rows // tile):
+            row = pl.multiple_of((1 - low) * span_rows + p * tile, tile)
+            tiles.append(placed(row, key, half, None))
+        tile_grads(group, accs, scale, tiles)
+
+    return low, square
+
+
+def first_kernel(heads, tile, scale, parts, *refs):
+    inputs, refs = refs[:7], refs[7:]
     terms_ref, both_ref, kept_ref, key_acc, value_acc = refs[:5]
-    held, sems = refs[5:-1], refs[-1]
+    outs, refs = refs[5 : 4 + parts], refs[4 + parts :]
+    held, span_ids, sems = refs[:-2], refs[-2], refs[-1]
     grad_ref, outputs_ref, query_ref, norm_ref = held
     toks = both_ref.shape[0] // 2
     key_ref, value_ref = both_ref.at[pl.ds(0, toks)], both_ref.at[pl.ds(toks, toks)]
-    half = toks // 2
-    rows = half * heads
-    per = tile // heads
+    rows = toks * heads // 2
     whole = [
         pltpu.make_async_copy(a, b, sems.at[i, 2])
-        for i, (a, b) in enumerate(zip(inputs[3:], (norm_ref, key_ref, value_ref)))
+        for i, (a, b) in enumerate(zip(inputs[3:], (norm_ref, key_ref, value_ref, span_ids)))
     ]
 
-    def halves(index):
+    def halves(slot, index):
         part = pl.ds(pl.multiple_of(index * rows, rows), rows)
         return [
-            pltpu.make_async_copy(inputs[i].at[part], held[i].at[part], sems.at[i, index])
+            pltpu.make_async_copy(inputs[i].at[part], held[i].at[part], sems.at[i, slot])
             for i in range(3)
         ]
 
-    for copy in whole + halves(0) + halves(1):
+    x = lax.axis_index("head")
+    order = (1 - x, x) if parts == 2 else (0, 1)
+    for copy in whole + halves(0, order[0]) + halves(1, order[1]):
         copy.start()
     key_acc[...] = jnp.zeros_like(key_acc)
     value_acc[...] = jnp.zeros_like(value_acc)
-    group = (query_ref, grad_ref, key_ref, value_ref, terms_ref, tile)
-    triangle = lax.broadcasted_iota(jnp.int32, (per, tile), 0) <= (
-        lax.broadcasted_iota(jnp.int32, (per, tile), 1) // heads
-    )
     for copy in whole:
         copy.wait()
 
-    @pl.loop(0, 2)
-    def _(index):
-        for copy in halves(index):
+    def arrive(slot):
+        for copy in halves(slot, order[slot]):
             copy.wait()
-        row_terms(heads, tile, index, (grad_ref, outputs_ref, norm_ref), terms_ref)
-        key = pl.multiple_of(index * half, half)
-        tiles = []
-        for p in range(half // per):
-            row, length = pl.multiple_of(index * rows + p * tile, tile), (p + 1) * per
-            kept = kept_ref.at[pl.ds(key, length), pl.ds(row, tile)]
-            tiles.append((row, key, length, triangle, kept))
-        tile_grads(group, (key_acc, value_acc), scale, tiles)
+        row_terms(heads, tile, order[slot], (grad_ref, outputs_ref, norm_ref), terms_ref)
+
+    group = (query_ref, grad_ref, key_ref, value_ref, terms_ref, tile)
+    accs = (key_acc, value_acc)
+    todo = [(functools.partial(arrive, slot), order[slot]) for slot in range(2)]
+    if parts == 2:
+        low, square = own_tiles(group, accs, scale, span_ids, kept_ref, heads, todo[:1])
+        arrive(1)
+        pl.when(low == order[0])(square)
+    else:
+        _, square = own_tiles(group, accs, scale, span_ids, kept_ref, heads, todo)
+        square()
+    put_shares(outs, key_acc, value_acc, scale, 1)
+
+
+def last_kernel(heads, tile, scale, parts, span_ids, *refs):
+    query_ref, grad_ref, terms_ref, both_ref = refs[:4]
+    kept_ref, key_acc, value_acc, total_ref = refs[8:]
+    if parts == 2:
+        toks = both_ref.shape[0] // 2
+        key_ref, value_ref = both_ref.at[pl.ds(0, toks)], both_ref.at[pl.ds(toks, toks)]
+        group = (query_ref, grad_ref, key_ref, value_ref, terms_ref, tile)
+        x = lax.axis_index("head")
+        low, square = own_tiles(
+            group, (key_acc, value_acc), scale, span_ids, kept_ref, heads, [(lambda: None, x)]
+        )
+        pl.when(low == x)(square)
+    put_shares([total_ref], key_acc, value_acc, scale, 0, parts)
 
 
 def far_kernel(heads, tile, scale, parts, step, span_ids, *refs):
@@ -193,53 +237,26 @@
         ]
         tile_grads(group, (key_acc, value_acc), scale, tiles)
 
-    if len(outs) == 1:
-        outs = [outs[0].at[away] for away in range(parts)]
     put_shares(outs, key_acc, value_acc, scale)
 
 
-def join_kernel(swapped_ref, *refs):
-    ins, outs = refs[: len(refs) // 2], refs[len(refs) // 2 :]
+def join_kernel(*refs):
+    this_ref, out_ref = refs[0], refs[-1]
     odd = lax.rem(lax.axis_index("ctx"), 2).astype(jnp.float32)
-    for away, (this, out) in enumerate(zip(ins, outs)):
-        more = swapped_ref[away].astype(jnp.float32) * odd
-        out[...] = (this[...].astype(jnp.float32) + more).astype(out.dtype)
-
-
-def last_kernel(heads, tile, scale, parts, span_ids, *refs):
-    query_ref, grad_ref, terms_ref, both_ref, swapped_ref = refs[:5]
-    kept_ref, key_acc, value_acc = refs[8:11]
-    outs = refs[11:]
-    toks = both_ref.shape[0] // 2
-    key_ref, value_ref = both_ref.at[pl.ds(0, toks)], both_ref.at[pl.ds(toks, toks)]
-    half = toks // 2
-    rows = half * heads
-    me = lax.axis_index("ctx")
-    first, second = span_pair(span_ids, me)
-    low = jnp.where(first > second, 1, 0)
-    key = pl.multiple_of(low * half, half)
-    tiles = []
-    for p in range(rows // tile):
-        row = pl.multiple_of((1 - low) * rows + p * tile, tile)
-        tiles.append((row, key, half, None, kept_ref.at[pl.ds(key, half), pl.ds(row, tile)]))
-    group = (query_ref, grad_ref, key_ref, value_ref, terms_ref, tile)
-    tile_grads(group, (key_acc, value_acc), scale, tiles)
-    even = 1.0 - lax.rem(me, 2).astype(jnp.float32)
-
-    def more(away, start, count):
-        return swapped_ref[away, start : start + count, :].astype(jnp.float32) * even
-
-    put_shares(outs, key_acc, value_acc, scale, more)
-
-
-def total_kernel(total_ref, *refs):
+    more = sum(ref[...].astype(jnp.float32) for ref in refs[1:-1])
+    out_ref[...] = (this_ref[...].astype(jnp.float32) + more * odd).astype(out_ref.dtype)
+
+
+def total_kernel(parts, total_ref, *refs):
     ins, (key_out, value_out) = refs[:-2], refs[-2:]
     share = key_out.shape[0]
+    even = 1.0 - lax.rem(lax.axis_index("ctx"), 2).astype(jnp.float32)
     for low, out in ((0, key_out), (share, value_out)):
-        part = total_ref[low : low + share, :]
-        for ref in ins:
-            part = part + ref[low : low + share, :].astype(jnp.float32)
-        out[...] = part.astype(out.dtype)
+        joined, landed = (
+            sum(ref[low : low + share, :].astype(jnp.float32) for ref in some)
+            for some in (ins[:parts], ins[parts:])
+        )
+        out[...] = (total_ref[low : low + share, :] + joined * even + landed).astype(out.dtype)
 
 
 def query_kernel(heads, tile, scale, span_ids, both_ref, own_ref, *refs):
@@ -287,6 +304,7 @@
 VMEM = pl.BlockSpec(memory_space=pltpu.VMEM)
 SMEM = pl.BlockSpec(memory_space=pltpu.SMEM)
 HBM = pl.BlockSpec(memory_space=pltpu.HBM)
+ANY = pl.BlockSpec(memory_space=pl.ANY)
 MIB = 1024 * 1024
 
 
@@ -301,7 +319,7 @@
         input_output_aliases=aliases or {},
         compiler_params=pltpu.CompilerParams(vmem_limit_bytes=limit * MIB),
         name=name,
-        cost_estimate=pl.CostEstimate(flops=int(flops), bytes_accessed=6 << 20, transcendentals=0),
+        cost_estimate=pl.CostEstimate(flops=int(flops), bytes_accessed=int(blocks * (1 << 20)), transcendentals=0),
     )(*ins)
 
 
@@ -328,27 +346,29 @@
     f32, bf16 = jnp.float32, jnp.bfloat16
     shape = jax.ShapeDtypeStruct
     grads = [shape((share, dim), bf16)] * parts
-    packed = [shape((parts, share, dim), bf16)]
     accs = [pltpu.VMEM((toks, dim), f32)] * 2
 
     key_1, value_1 = moved(keys, (-1, -1), 0), moved(values, (-1, -1), 0)
     inputs = tuple(
-        pltpu.with_memory_space_constraint(a, pltpu.HBM) for a in (g, o, q, log_norm, keys, values)
+        pltpu.with_memory_space_constraint(a, pltpu.HBM)
+        for a in (g, o, q, log_norm, keys, values, span_ids)
     )
     sums = [shape((toks, rows), bf16), shape((toks, dim), f32), shape((toks, dim), f32)]
-    terms, both, kept, key_sum, value_sum = call(
-        functools.partial(first_kernel, heads, tile, scale),
+    terms, both, kept, key_sum, value_sum, *sent = call(
+        functools.partial(first_kernel, heads, tile, scale, parts),
         inputs,
         [HBM] * len(inputs),
-        [shape((8, rows), f32), shape((2 * toks, dim), bf16)] + sums,
-        [pltpu.VMEM(a.shape, a.dtype) for a in inputs[:4]] + [pltpu.SemaphoreType.DMA((3, 3))],
-        1.25 * heads,
+        [shape((8, rows), f32), shape((2 * toks, dim), bf16)] + sums + grads[1:],
+        [pltpu.VMEM(a.shape, a.dtype) for a in inputs[:4]]
+        + [pltpu.SMEM(span_ids.shape, span_ids.dtype), pltpu.SemaphoreType.DMA((4, 3))],
+        1.625 * heads,
         20,
         "first",
     )
+    landed = [moved(block, (0, 0), away + 1) for away, block in enumerate(sent)]
     key_2, value_2 = moved(key_1, (-1, -1), 0), moved(value_1, (-1, -1), 0)
 
-    def far(step, key, value, grads):
+    def far(step, key, value):
         return call(
             functools.partial(far_kernel, heads, tile, scale, parts, step),
             (span_ids, q, g, terms, key, value),
@@ -360,23 +380,24 @@
             "far",
         )
 
-    kept_1, near = far(1, key_1, value_1, packed)
-    swapped = moved(near, (-1, 1), 0)
-    kept_2, *sent = far(2, key_2, value_2, grads)
-    sent = call(join_kernel, (swapped, *sent), [VMEM] * (1 + parts), grads, [], 0.01, 4, "join")
-    landed = [moved(block, (2, 2), away) for away, block in enumerate(sent)]
-    kept, _, _, total, *sent = call(
+    kept_1, *sent = far(1, key_1, value_1)
+    joined = [moved(block, (-1, 1), away) for away, block in enumerate(sent)]
+    kept_2, *sent = far(2, key_2, value_2)
+    sent[:1] = call(
+        join_kernel, (sent[0], *joined), [VMEM] * (1 + parts), grads[:1], [], 0.01, 4, "join"
+    )
+    landed += [moved(block, (2, 2), away) for away, block in enumerate(sent)]
+    kept, _, _, total = call(
         functools.partial(last_kernel, heads, tile, scale, parts),
-        (span_ids, q, g, terms, both, swapped, kept, key_sum, value_sum),
-        [SMEM] + [VMEM] * 8,
-        sums + [shape((share, dim), f32)] + grads[1:],
+        (span_ids, q, g, terms, both, kept, key_sum, value_sum, sent[0]),
+        [SMEM] + [VMEM] * 7 + [ANY],
+        sums + [shape((share, dim), f32)],
         [],
-        heads,
+        1.625 * heads,
         20,
         "last",
-        {6: 0, 7: 1, 8: 2},
-    )
-    landed += [moved(block, (0, 0), away + 1) for away, block in enumerate(sent)]
+        {5: 0, 6: 1, 7: 2},
+    )
     (query_grad,) = call(
         functools.partial(query_kernel, heads, tile, scale),
         (span_ids, both, kept, key_1, kept_1, key_2, kept_2),
@@ -388,9 +409,9 @@
         "queries",
     )
     key_grad, value_grad = call(
-        total_kernel,
-        (total, *landed),
-        [VMEM] * (1 + len(landed)),
+        functools.partial(total_kernel, parts),
+        (total, *joined, *landed),
+        [VMEM] * (1 + len(joined) + len(landed)),
         [shape((share // 2, dim), bf16)] * 2,
         [],
         0.01,

time: 47.3 us -> 46.6 us (0.985)
  waiting for transfers between devices: 10.7 us -> 3.55 us
  starting transfers between devices: 7.43 us -> 13.6 us
    ppermute x8 -> x9, waiting for transfers between devices: 10.7 us -> 3.55 us  [moved(): return lax.ppermute(block, ('ctx', 'head'), route)]
    ppermute x8 -> x9, starting transfers between devices: 7.43 us -> 13.6 us  [moved(): return lax.ppermute(block, ('ctx', 'head'), route)]
  transfers between devices with their start and end apart: 8 -> 9, of which waited for: 4 -> 2; matrix products, arithmetic and copies ran while one was open for 0% -> 0% of each run, Pallas kernels for 58% -> 60%
where the time goes in v6:
time: 46.6 us; the launch traced here: 46.4 us
  Pallas kernels  28.6 us (61%)
  starting transfers between devices  13.6 us (29%)
  waiting for transfers between devices  3.55 us (8%)
  between operations  0.7 us (2%)
    pallas_call x7, Pallas kernels, call(): pl.pallas_call(kernel, out_shape=outs, in_specs=where, out_specs=[VMEM] *...  28.6 us
    ppermute x9, starting transfers between devices, moved(): return lax.ppermute(block, ('ctx', 'head'), route)  13.6 us
    ppermute x9, waiting for transfers between devices, moved(): return lax.ppermute(block, ('ctx', 'head'), route)  3.55 us
  transfers between devices with their start and end apart: 9, of which 2 were waited for; matrix products, arithmetic and copies ran while one was open for 0% of the time, Pallas kernels for 60%

profile of v6, /device:TPU:0, one launch (start us, length us, event | category | flops | bytes accessed | tf_op | source)
XLA Modules:
  0.0 46.4 jit_solution(7862776424728510689)
XLA Ops:
  0.6 0.5 %collective-permute-start = (bf16[1024,128]{1,0:T(8,128)(2,1)}, bf16[1024,128]{1,0:T(8,128)(2,1)S(1)}, u32[]{:S(2)}, u32[]{:S(2)}) collective-permute-start(bf16[1024,128]{1,0:T(8,128)(2,1)} %refs_4_.1), channel_id=1, source_target_pairs={{0,2},{1,3},{2,4},{3,5},{4,6},{5,7},{6,8},{7,9},{8,10},{9,11},{10,... | collective-permute-start | bytes 786440 | tf_op jit(solution)/shard_map/ppermute | solution.py:333
  1.1 2.6 %collective-permute-start.2 = (bf16[1024,128]{1,0:T(8,128)(2,1)}, bf16[1024,128]{1,0:T(8,128)(2,1)S(1)}, u32[]{:S(2)}, u32[]{:S(2)}) collective-permute-start(bf16[1024,128]{1,0:T(8,128)(2,1)} %refs_5_.1), channel_id=1, source_target_pairs={{0,2},{1,3},{2,4},{3,5},{4,6},{5,7},{6,8},{7,9},{8,10},{9,11},{10,... | collective-permute-start | bytes 786440 | tf_op jit(solution)/shard_map/ppermute | solution.py:333
  3.8 0.0 copy-start
  3.8 0.0 copy-start.1
  3.8 0.0 copy-start.2
  3.8 4.5 %first.1 = (f32[8,4096]{1,0:T(8,128)S(1)}, bf16[2048,128]{1,0:T(8,128)(2,1)S(1)}, bf16[1024,4096]{1,0:T(8,128)(2,1)S(1)}, f32[1024,128]{1,0:T(8,128)S(1)}, f32[1...) custom-call(bf16[4096,128]{1,0:T(8,128)(2,1)} %bitcast.4, bf16[4096,128]{1,0:T(8,128)(2,1)} %bitcast.12, ...), custom_call_target="tpu_custom_call" | custom-call | flops 8724152320 | bytes 6815744 | tf_op jit(solution)/shard_map/first/pallas_call | solution.py:313
  8.3 4.0 %collective-permute-start.6 = (bf16[1024,128]{1,0:T(8,128)(2,1)S(1)}, bf16[1024,128]{1,0:T(8,128)(2,1)S(1)}, u32[]{:S(2)}, u32[]{:S(2)}) collective-permute-start(bf16[1024,128]{1,0:T(8,128)(2,1)S(1)} %get-tuple-element.31), channel_id=1, source_target_pairs={{0,1},{1,0},{2,3},{3,2},{4,5},{5,4},{6,7},{7,6},{8,9},{9,8},{10,11... | collective-permute-start | bytes 786440 | tf_op jit(solution)/shard_map/ppermute | solution.py:333
  12.3 0.0 collective-permute-done.refs_3_.refs_0_
  12.3 0.0 collective-permute-start.1
  12.3 0.9 %collective-permute-done.2.refs_4_ = bf16[1024,128]{1,0:T(8,128)(2,1)S(1)} collective-permute-done((bf16[1024,128]{1,0:T(8,128)(2,1)}, bf16[1024,128]{1,0:T(8,128)(2,1)S(1)}, u32[]{:S(2)}, u32[]{:S(2)}) %collective-permute-start.2) | collective-permute-done | bytes 262176 | tf_op jit(solution)/shard_map/ppermute | solution.py:333
  13.2 0.7 %collective-permute-start.3 = (bf16[1024,128]{1,0:T(8,128)(2,1)S(1)}, bf16[1024,128]{1,0:T(8,128)(2,1)S(1)}, u32[]{:S(2)}, u32[]{:S(2)}) collective-permute-start(bf16[1024,128]{1,0:T(8,128)(2,1)S(1)} %collective-permute-done.2.refs_4_), channel_id=1, source_target_pairs={{0,2},{1,3},{2,4},{3,5},{4,6},{5,7},{6,8},{7,9},{8,10},{9,11},{10,... | collective-permute-start | bytes 786440 | tf_op jit(solution)/shard_map/ppermute | solution.py:333
  13.9 0.0 copy-done
  13.9 0.0 copy-done.1
  13.9 0.0 copy-done.2
  13.9 5.6 %far.3 = (bf16[2,512,2048]{2,1,0:T(8,128)(2,1)S(1)}, bf16[1024,128]{1,0:T(8,128)(2,1)S(1)}, bf16[1024,128]{1,0:T(8,128)(2,1)S(1)}) custom-call(s32[32]{0:T(128)S(1)} %copy-done.2, bf16[4096,128]{1,0:T(8,128)(2,1)S(1)} %bitcast.9, bf16[4096,128]{1,0:T(8,128)(2,1)S(1)} %bitcast.5, f32[8,4096]{1,0:T(8,128)S(1)} %get-tuple-element.20.refs_2_, ...), custom_call_target="tpu_custom_call" | custom-call | flops 10737418240 | bytes 8388608 | tf_op jit(solution)/shard_map/far/pallas_call | solution.py:313
  19.6 0.1 collective-permute-start.4
  19.7 1.3 %collective-permute-start.5 = (bf16[1024,128]{1,0:T(8,128)(2,1)S(1)}, bf16[1024,128]{1,0:T(8,128)(2,1)S(1)}, u32[]{:S(2)}, u32[]{:S(2)}) collective-permute-start(bf16[1024,128]{1,0:T(8,128)(2,1)S(1)} %get-tuple-element.26), channel_id=1, source_target_pairs={{0,3},{1,2},{2,1},{3,0},{4,7},{5,6},{6,5},{7,4},{8,11},{9,10},{10,... | collective-permute-start | bytes 786440 | tf_op jit(solution)/shard_map/ppermute | solution.py:333
  21.0 0.0 collective-permute-done.1.refs_3_.refs_2_
  21.0 2.6 %collective-permute-done.3.refs_4_ = bf16[1024,128]{1,0:T(8,128)(2,1)S(1)} collective-permute-done((bf16[1024,128]{1,0:T(8,128)(2,1)S(1)}, bf16[1024,128]{1,0:T(8,128)(2,1)S(1)}, u32[]{:S(2)}, u32[]{:S(2)}) %collective-permute-start.3) | collective-permute-done | bytes 262176 | tf_op jit(solution)/shard_map/ppermute | solution.py:333
  23.6 5.6 %far.2 = (bf16[2,512,2048]{2,1,0:T(8,128)(2,1)S(1)}, bf16[1024,128]{1,0:T(8,128)(2,1)S(1)}, bf16[1024,128]{1,0:T(8,128)(2,1)S(1)}) custom-call(s32[32]{0:T(128)S(1)} %copy-done.2, bf16[4096,128]{1,0:T(8,128)(2,1)S(1)} %bitcast.10, bf16[4096,128]{1,0:T(8,128)(2,1)S(1)} %bitcast.6, f32[8,4096]{1,0:T(8,128)S(1)} %get-tuple-element.20.refs_2_, ...), custom_call_target="tpu_custom_call" | custom-call | flops 10737418240 | bytes 8388608 | tf_op jit(solution)/shard_map/far/pallas_call | solution.py:313
  29.2 0.0 collective-permute-done.4.refs_1_.refs_0_
  29.2 0.0 collective-permute-done.5.refs_2_.refs_1_
  29.2 0.1 join.1.refs_7_
  29.4 2.7 %collective-permute-start.7 = (bf16[1024,128]{1,0:T(8,128)(2,1)S(1)}, bf16[1024,128]{1,0:T(8,128)(2,1)S(1)}, u32[]{:S(2)}, u32[]{:S(2)}) collective-permute-start(bf16[1024,128]{1,0:T(8,128)(2,1)S(1)} %join.1.refs_7_), channel_id=1, source_target_pairs={{0,28},{1,29},{2,30},{3,31},{4,0},{5,1},{6,2},{7,3},{8,4},{9,5},{1... | collective-permute-start | bytes 786440 | tf_op jit(solution)/shard_map/ppermute | solution.py:333
  32.1 1.6 %collective-permute-start.8 = (bf16[1024,128]{1,0:T(8,128)(2,1)S(1)}, bf16[1024,128]{1,0:T(8,128)(2,1)S(1)}, u32[]{:S(2)}, u32[]{:S(2)}) collective-permute-start(bf16[1024,128]{1,0:T(8,128)(2,1)S(1)} %get-tuple-element.32), channel_id=1, source_target_pairs={{0,29},{1,28},{2,31},{3,30},{4,1},{5,0},{6,3},{7,2},{8,5},{9,4},{1... | collective-permute-start | bytes 786440 | tf_op jit(solution)/shard_map/ppermute | solution.py:333
  33.7 4.9 %last.1 = (bf16[1024,4096]{1,0:T(8,128)(2,1)S(1)}, f32[1024,128]{1,0:T(8,128)S(1)}, f32[1024,128]{1,0:T(8,128)S(1)}, f32[1024,128]{1,0:T(8,128)S(1)}) custom-call(s32[32]{0:T(128)S(1)} %copy-done.2, bf16[4096,128]{1,0:T(8,128)(2,1)S(1)} %bitcast.11, bf16[4096,128]{1,0:T(8,128)(2,1)S(1)} %bitcast.7, ...), custom_call_target="tpu_custom_call", output_to_operand_aliasing={{0}: (5, {}), {1}: (6, {}), {2}: (7, {})} | custom-call | flops 8724152320 | bytes 6815744 | tf_op jit(solution)/shard_map/last/pallas_call | solution.py:313
  38.6 7.0 %queries.1 = bf16[4096,128]{1,0:T(8,128)(2,1)} custom-call(s32[32]{0:T(128)S(1)} %copy-done.2, bf16[2048,128]{1,0:T(8,128)(2,1)S(1)} %get-tuple-element.19.refs_3_.both_ref, bf16[1024,4096]{1,0:T(8,128)(2,1)S(1)} %get-tuple-element.27.own_ref, bf16[1024,128]{1,0:T(8,128)(2,1)S(1)} %collective-permute-done.refs_3_.refs_0_, ...), custom_call_target="tpu_custom_call" | custom-call | flops 6710886400 | bytes 5242880 | tf_op jit(solution)/shard_map/queries/pallas_call | solution.py:313
  45.6 0.0 collective-permute-done.6.refs_2_
  45.6 0.0 collective-permute-done.7.refs_3_
  45.6 0.0 collective-permute-done.8.refs_4_
  45.6 0.9 %total.1 = (bf16[512,128]{1,0:T(8,128)(2,1)}, bf16[512,128]{1,0:T(8,128)(2,1)}) custom-call(f32[1024,128]{1,0:T(8,128)S(1)} %get-tuple-element.30.total_ref, bf16[1024,128]{1,0:T(8,128)(2,1)S(1)} %collective-permute-done.4.refs_1_.refs_0_, bf16[1024,128]{1,0:T(8,128)(2,1)S(1)} %collective-permute-done.5.refs_2_.refs_1_, ...), custom_call_target="tpu_custom_call" | custom-call | flops 13421772 | bytes 10485 | tf_op jit(solution)/shard_map/total/pallas_call | solution.py:313
Async XLA Ops:
  0.6 11.7 %collective-permute-start = (bf16[1024,128]{1,0:T(8,128)(2,1)}, bf16[1024,128]{1,0:T(8,128)(2,1)S(1)}, u32[]{:S(2)}, u32[]{:S(2)}) collective-permute-start(bf16[1024,128]{1,0:T(8,128)(2,1)} %refs_4_.1), channel_id=1, source_target_pairs={{0,2},{1,3},{2,4},{3,5},{4,6},{5,7},{6,8},{7,9},{8,10},{9,11},{10,... | collective-permute-start | bytes 786440 | tf_op jit(solution)/shard_map/ppermute | solution.py:333
  1.1 12.1 %collective-permute-start.2 = (bf16[1024,128]{1,0:T(8,128)(2,1)}, bf16[1024,128]{1,0:T(8,128)(2,1)S(1)}, u32[]{:S(2)}, u32[]{:S(2)}) collective-permute-start(bf16[1024,128]{1,0:T(8,128)(2,1)} %refs_5_.1), channel_id=1, source_target_pairs={{0,2},{1,3},{2,4},{3,5},{4,6},{5,7},{6,8},{7,9},{8,10},{9,11},{10,... | collective-permute-start | bytes 786440 | tf_op jit(solution)/shard_map/ppermute | solution.py:333
  3.8 10.2 %copy-start = (bf16[1024,4,128]{2,1,0:T(4,128)(2,1)S(1)}, bf16[1024,4,128]{2,1,0:T(4,128)(2,1)}, u32[]{:S(2)}) copy-start(bf16[1024,4,128]{2,1,0:T(4,128)(2,1)} %param.11) | copy-start | bytes 3145732
  3.8 10.2 %copy-start.1 = (bf16[1024,4,128]{2,1,0:T(4,128)(2,1)S(1)}, bf16[1024,4,128]{2,1,0:T(4,128)(2,1)}, u32[]{:S(2)}) copy-start(bf16[1024,4,128]{2,1,0:T(4,128)(2,1)} %param.7) | copy-start | bytes 3145732
  3.8 10.2 %copy-start.2 = (s32[32]{0:T(128)S(1)}, s32[32]{0:T(128)}, u32[]{:S(2)}) copy-start(s32[32]{0:T(128)} %span_ids.7) | copy-start | bytes 388
  8.3 37.3 %collective-permute-start.6 = (bf16[1024,128]{1,0:T(8,128)(2,1)S(1)}, bf16[1024,128]{1,0:T(8,128)(2,1)S(1)}, u32[]{:S(2)}, u32[]{:S(2)}) collective-permute-start(bf16[1024,128]{1,0:T(8,128)(2,1)S(1)} %get-tuple-element.31), channel_id=1, source_target_pairs={{0,1},{1,0},{2,3},{3,2},{4,5},{5,4},{6,7},{7,6},{8,9},{9,8},{10,11... | collective-permute-start | bytes 786440 | tf_op jit(solution)/shard_map/ppermute | solution.py:333
  12.3 8.7 %collective-permute-start.1 = (bf16[1024,128]{1,0:T(8,128)(2,1)S(1)}, bf16[1024,128]{1,0:T(8,128)(2,1)S(1)}, u32[]{:S(2)}, u32[]{:S(2)}) collective-permute-start(bf16[1024,128]{1,0:T(8,128)(2,1)S(1)} %collective-permute-done.refs_3_.refs_0_), channel_id=1, source_target_pairs={{0,2},{1,3},{2,4},{3,5},{4,6},{5,7},{6,8},{7,9},{8,10},{9,11},{10,... | collective-permute-start | bytes 786440 | tf_op jit(solution)/shard_map/ppermute | solution.py:333
  13.2 10.4 %collective-permute-start.3 = (bf16[1024,128]{1,0:T(8,128)(2,1)S(1)}, bf16[1024,128]{1,0:T(8,128)(2,1)S(1)}, u32[]{:S(2)}, u32[]{:S(2)}) collective-permute-start(bf16[1024,128]{1,0:T(8,128)(2,1)S(1)} %collective-permute-done.2.refs_4_), channel_id=1, source_target_pairs={{0,2},{1,3},{2,4},{3,5},{4,6},{5,7},{6,8},{7,9},{8,10},{9,11},{10,... | collective-permute-start | bytes 786440 | tf_op jit(solution)/shard_map/ppermute | solution.py:333
  19.6 9.7 %collective-permute-start.4 = (bf16[1024,128]{1,0:T(8,128)(2,1)S(1)}, bf16[1024,128]{1,0:T(8,128)(2,1)S(1)}, u32[]{:S(2)}, u32[]{:S(2)}) collective-permute-start(bf16[1024,128]{1,0:T(8,128)(2,1)S(1)} %get-tuple-element.25), channel_id=1, source_target_pairs={{0,2},{1,3},{2,0},{3,1},{4,6},{5,7},{6,4},{7,5},{8,10},{9,11},{10,... | collective-permute-start | bytes 786440 | tf_op jit(solution)/shard_map/ppermute | solution.py:333
  19.7 9.6 %collective-permute-start.5 = (bf16[1024,128]{1,0:T(8,128)(2,1)S(1)}, bf16[1024,128]{1,0:T(8,128)(2,1)S(1)}, u32[]{:S(2)}, u32[]{:S(2)}) collective-permute-start(bf16[1024,128]{1,0:T(8,128)(2,1)S(1)} %get-tuple-element.26), channel_id=1, source_target_pairs={{0,3},{1,2},{2,1},{3,0},{4,7},{5,6},{6,5},{7,4},{8,11},{9,10},{10,... | collective-permute-start | bytes 786440 | tf_op jit(solution)/shard_map/ppermute | solution.py:333
  29.4 16.2 %collective-permute-start.7 = (bf16[1024,128]{1,0:T(8,128)(2,1)S(1)}, bf16[1024,128]{1,0:T(8,128)(2,1)S(1)}, u32[]{:S(2)}, u32[]{:S(2)}) collective-permute-start(bf16[1024,128]{1,0:T(8,128)(2,1)S(1)} %join.1.refs_7_), channel_id=1, source_target_pairs={{0,28},{1,29},{2,30},{3,31},{4,0},{5,1},{6,2},{7,3},{8,4},{9,5},{1... | collective-permute-start | bytes 786440 | tf_op jit(solution)/shard_map/ppermute | solution.py:333
  32.1 13.5 %collective-permute-start.8 = (bf16[1024,128]{1,0:T(8,128)(2,1)S(1)}, bf16[1024,128]{1,0:T(8,128)(2,1)S(1)}, u32[]{:S(2)}, u32[]{:S(2)}) collective-permute-start(bf16[1024,128]{1,0:T(8,128)(2,1)S(1)} %get-tuple-element.32), channel_id=1, source_target_pairs={{0,29},{1,28},{2,31},{3,30},{4,1},{5,0},{6,3},{7,2},{8,5},{9,4},{1... | collective-permute-start | bytes 786440 | tf_op jit(solution)/shard_map/ppermute | solution.py:333

commit v7 on v6

--- a/solution.py
+++ b/solution.py
@@ -149,8 +149,7 @@
 def first_kernel(heads, tile, scale, parts, *refs):
     inputs, refs = refs[:7], refs[7:]
     terms_ref, both_ref, kept_ref, key_acc, value_acc = refs[:5]
-    outs, refs = refs[5 : 4 + parts], refs[4 + parts :]
-    held, span_ids, sems = refs[:-2], refs[-2], refs[-1]
+    held, span_ids, sems = refs[5:-2], refs[-2], refs[-1]
     grad_ref, outputs_ref, query_ref, norm_ref = held
     toks = both_ref.shape[0] // 2
     key_ref, value_ref = both_ref.at[pl.ds(0, toks)], both_ref.at[pl.ds(toks, toks)]
@@ -191,7 +190,6 @@
     else:
         _, square = own_tiles(group, accs, scale, span_ids, kept_ref, heads, todo)
         square()
-    put_shares(outs, key_acc, value_acc, scale, 1)
 
 
 def last_kernel(heads, tile, scale, parts, span_ids, *refs):
@@ -210,9 +208,12 @@
 
 
 def far_kernel(heads, tile, scale, parts, step, span_ids, *refs):
-    query_ref, grad_ref, terms_ref, key_ref, value_ref, kept_ref = refs[:6]
-    outs = refs[6:-2]
+    query_ref, grad_ref, terms_ref, key_ref, value_ref = refs[:5]
+    own, refs = (refs[5:7], refs[7:]) if step == 1 else (None, refs[5:])
+    kept_ref, outs, own_outs = refs[0], refs[1 : 1 + parts], refs[1 + parts : -2]
     key_acc, value_acc = refs[-2:]
+    if own:
+        put_shares(own_outs, *own, scale, 1)
     half = key_ref.shape[0] // 2
     rows = half * heads
     key_acc[...] = jnp.zeros_like(key_acc)
@@ -260,11 +261,14 @@
 
 
 def query_kernel(heads, tile, scale, span_ids, both_ref, own_ref, *refs):
-    far_refs, (out_ref, acc) = refs[:-2], refs[-2:]
+    far_refs, (out_ref, acc, turned) = refs[:-3], refs[-3:]
     toks = both_ref.shape[0] // 2
     half = toks // 2
     rows = half * heads
     per = tile // heads
+    for index, key_ref in enumerate([both_ref] + list(far_refs[::2])):
+        for low in range(0, toks, half):
+            turned[index, :, low : low + half] = key_ref[low : low + half, :].T
 
     @pl.loop(0, 2)
     def _(index):
@@ -272,8 +276,8 @@
         for p in range(half // per):
             row = pl.multiple_of(index * rows + p * tile, tile)
             length = (p + 1) * per
-            acc[pl.ds(row, tile), :] = dot(
-                own_ref[pl.ds(key, length), pl.ds(row, tile)], both_ref[pl.ds(key, length), :], TN
+            acc[:, pl.ds(row, tile)] = dot(
+                turned[0, :, pl.ds(key, length)], own_ref[pl.ds(key, length), pl.ds(row, tile)], NN
             )
 
     first, second = span_pair(span_ids, lax.axis_index("ctx"))
@@ -281,11 +285,11 @@
     key = pl.multiple_of(low * half, half)
     for p in range(rows // tile):
         row = pl.multiple_of((1 - low) * rows + p * tile, tile)
-        acc[pl.ds(row, tile), :] += dot(
-            own_ref[pl.ds(key, half), pl.ds(row, tile)], both_ref[pl.ds(key, half), :], TN
+        acc[:, pl.ds(row, tile)] += dot(
+            turned[0, :, pl.ds(key, half)], own_ref[pl.ds(key, half), pl.ds(row, tile)], NN
         )
     for step in range(1, STEPS):
-        key_ref, kept_ref = far_refs[2 * step - 2 : 2 * step]
+        kept_ref = far_refs[2 * step - 1]
         halves = far_halves(span_ids, step)
 
         @pl.loop(0, 2)
@@ -294,11 +298,14 @@
             key = pl.multiple_of(key_half * half, half)
             for p in range(rows // tile):
                 row = pl.multiple_of(row_half * rows + p * tile, tile)
-                acc[pl.ds(row, tile), :] += dot(
-                    kept_ref[item, :, p * tile : (p + 1) * tile], key_ref[pl.ds(key, half), :], TN
+                acc[:, pl.ds(row, tile)] += dot(
+                    turned[step, :, pl.ds(key, half)],
+                    kept_ref[item, :, p * tile : (p + 1) * tile],
+                    NN,
                 )
 
-    out_ref[...] = (acc[...] * scale).astype(out_ref.dtype)
+    for row in range(0, 2 * rows, tile):
+        out_ref[row : row + tile, :] = (acc[:, row : row + tile] * scale).T.astype(out_ref.dtype)
 
 
 VMEM = pl.BlockSpec(memory_space=pltpu.VMEM)
@@ -354,34 +361,34 @@
         for a in (g, o, q, log_norm, keys, values, span_ids)
     )
     sums = [shape((toks, rows), bf16), shape((toks, dim), f32), shape((toks, dim), f32)]
-    terms, both, kept, key_sum, value_sum, *sent = call(
+    terms, both, kept, key_sum, value_sum = call(
         functools.partial(first_kernel, heads, tile, scale, parts),
         inputs,
         [HBM] * len(inputs),
-        [shape((8, rows), f32), shape((2 * toks, dim), bf16)] + sums + grads[1:],
+        [shape((8, rows), f32), shape((2 * toks, dim), bf16)] + sums,
         [pltpu.VMEM(a.shape, a.dtype) for a in inputs[:4]]
         + [pltpu.SMEM(span_ids.shape, span_ids.dtype), pltpu.SemaphoreType.DMA((4, 3))],
         1.625 * heads,
         20,
         "first",
     )
-    landed = [moved(block, (0, 0), away + 1) for away, block in enumerate(sent)]
     key_2, value_2 = moved(key_1, (-1, -1), 0), moved(value_1, (-1, -1), 0)
 
-    def far(step, key, value):
+    def far(step, key, value, *own):
         return call(
             functools.partial(far_kernel, heads, tile, scale, parts, step),
-            (span_ids, q, g, terms, key, value),
-            [SMEM] + [VMEM] * 5,
-            [shape((2, toks // 2, rows // 2), bf16)] + grads,
+            (span_ids, q, g, terms, key, value, *own),
+            [SMEM] + [VMEM] * (5 + len(own)),
+            [shape((2, toks // 2, rows // 2), bf16)] + grads + (grads[1:] if own else []),
             accs,
             2 * heads,
             14,
             "far",
         )
 
-    kept_1, *sent = far(1, key_1, value_1)
-    joined = [moved(block, (-1, 1), away) for away, block in enumerate(sent)]
+    kept_1, *sent = far(1, key_1, value_1, key_sum, value_sum)
+    joined = [moved(block, (-1, 1), away) for away, block in enumerate(sent[:parts])]
+    landed = [moved(block, (0, 0), away + 1) for away, block in enumerate(sent[parts:])]
     kept_2, *sent = far(2, key_2, value_2)
     sent[:1] = call(
         join_kernel, (sent[0], *joined), [VMEM] * (1 + parts), grads[:1], [], 0.01, 4, "join"
@@ -403,7 +410,7 @@
         (span_ids, both, kept, key_1, kept_1, key_2, kept_2),
         [SMEM] + [VMEM] * 6,
         [shape((rows, dim), bf16)],
-        [pltpu.VMEM((rows, dim), f32)],
+        [pltpu.VMEM((dim, rows), f32), pltpu.VMEM((STEPS, dim, toks), bf16)],
         1.25 * heads,
         28,
         "queries",

time: 46.6 us -> 45.5 us (0.976)
  waiting for transfers between devices: 3.55 us -> 6.26 us
  starting transfers between devices: 13.6 us -> 11.3 us
  Pallas kernels: 28.6 us -> 26.8 us
    ppermute x9, waiting for transfers between devices: 3.55 us -> 6.26 us  [moved(): return lax.ppermute(block, ('ctx', 'head'), route)]
    ppermute x9, starting transfers between devices: 13.6 us -> 11.3 us  [moved(): return lax.ppermute(block, ('ctx', 'head'), route)]
    pallas_call x7, Pallas kernels: 28.6 us -> 26.8 us  [call(): pl.pallas_call(kernel, out_shape=outs, in_specs=where, out_specs=[VMEM] *...]
  transfers between devices with their start and end apart: 9 -> 9, of which waited for: 2 -> 5; matrix products, arithmetic and copies ran while one was open for 0% -> 0% of each run, Pallas kernels for 60% -> 58%
where the time goes in v7:
time: 45.5 us; the launch traced here: 45.1 us
  Pallas kernels  26.8 us (59%)
  starting transfers between devices  11.3 us (25%)
  waiting for transfers between devices  6.26 us (14%)
  between operations  0.7 us (2%)
    pallas_call x7, Pallas kernels, call(): pl.pallas_call(kernel, out_shape=outs, in_specs=where, out_specs=[VMEM] *...  26.8 us
    ppermute x9, starting transfers between devices, moved(): return lax.ppermute(block, ('ctx', 'head'), route)  11.3 us
    ppermute x9, waiting for transfers between devices, moved(): return lax.ppermute(block, ('ctx', 'head'), route)  6.26 us
  transfers between devices with their start and end apart: 9, of which 5 were waited for; matrix products, arithmetic and copies ran while one was open for 0% of the time, Pallas kernels for 58%

profile of v7, /device:TPU:0, one launch (start us, length us, event | category | flops | bytes accessed | tf_op | source)
XLA Modules:
  0.0 45.1 jit_solution(14055903074623730998)
XLA Ops:
  0.6 0.5 %collective-permute-start = (bf16[1024,128]{1,0:T(8,128)(2,1)}, bf16[1024,128]{1,0:T(8,128)(2,1)S(1)}, u32[]{:S(2)}, u32[]{:S(2)}) collective-permute-start(bf16[1024,128]{1,0:T(8,128)(2,1)} %refs_4_.1), channel_id=1, source_target_pairs={{0,2},{1,3},{2,4},{3,5},{4,6},{5,7},{6,8},{7,9},{8,10},{9,11},{10,... | collective-permute-start | bytes 786440 | tf_op jit(solution)/shard_map/ppermute | solution.py:340
  1.1 2.6 %collective-permute-start.2 = (bf16[1024,128]{1,0:T(8,128)(2,1)}, bf16[1024,128]{1,0:T(8,128)(2,1)S(1)}, u32[]{:S(2)}, u32[]{:S(2)}) collective-permute-start(bf16[1024,128]{1,0:T(8,128)(2,1)} %refs_5_.1), channel_id=1, source_target_pairs={{0,2},{1,3},{2,4},{3,5},{4,6},{5,7},{6,8},{7,9},{8,10},{9,11},{10,... | collective-permute-start | bytes 786440 | tf_op jit(solution)/shard_map/ppermute | solution.py:340
  3.8 0.0 copy-start
  3.8 0.0 copy-start.1
  3.8 0.0 copy-start.2
  3.8 4.5 %first.1 = (f32[8,4096]{1,0:T(8,128)S(1)}, bf16[2048,128]{1,0:T(8,128)(2,1)S(1)}, bf16[1024,4096]{1,0:T(8,128)(2,1)S(1)}, f32[1024,128]{1,0:T(8,128)S(1)}, f32[1024,128]{1,0:T(8,128)S(1)}) custom-call(bf16[4096,128]{1,0:T(8,128)(2,1)} %bitcast.4, bf16[4096,128]{1,0:T(8,128)(2,1)} %bitcast.12, bf16[4096,128]{1,0:T(8,128)(2,1)} %bitcast.8, f32[4,1024]{1,0:T(4,128)} %refs_3_.1, ...), custom_call_target="tpu_custom_call" | custom-call | flops 8724152320 | bytes 6815744 | tf_op jit(solution)/shard_map/first/pallas_call | solution.py:320
  8.3 2.1 %collective-permute-done.refs_3_.refs_0_ = bf16[1024,128]{1,0:T(8,128)(2,1)S(1)} collective-permute-done((bf16[1024,128]{1,0:T(8,128)(2,1)}, bf16[1024,128]{1,0:T(8,128)(2,1)S(1)}, u32[]{:S(2)}, u32[]{:S(2)}) %collective-permute-start) | collective-permute-done | bytes 262176 | tf_op jit(solution)/shard_map/ppermute | solution.py:340
  10.4 0.0 collective-permute-start.1
  10.4 2.8 %collective-permute-done.2.refs_4_ = bf16[1024,128]{1,0:T(8,128)(2,1)S(1)} collective-permute-done((bf16[1024,128]{1,0:T(8,128)(2,1)}, bf16[1024,128]{1,0:T(8,128)(2,1)S(1)}, u32[]{:S(2)}, u32[]{:S(2)}) %collective-permute-start.2) | collective-permute-done | bytes 262176 | tf_op jit(solution)/shard_map/ppermute | solution.py:340
  13.2 0.0 collective-permute-start.3
  13.2 0.0 copy-done
  13.2 0.0 copy-done.1
  13.2 0.0 copy-done.2
  13.2 5.6 %far.3 = (bf16[2,512,2048]{2,1,0:T(8,128)(2,1)S(1)}, bf16[1024,128]{1,0:T(8,128)(2,1)S(1)}, bf16[1024,128]{1,0:T(8,128)(2,1)S(1)}, bf16[1024,128]{1,0:T(8,128)(2,1)S(1)}) custom-call(s32[32]{0:T(128)S(1)} %copy-done.2, bf16[4096,128]{1,0:T(8,128)(2,1)S(1)} %bitcast.9, bf16[4096,128]{1,0:T(8,128)(2,1)S(1)} %bitcast.5, ...), custom_call_target="tpu_custom_call" | custom-call | flops 10737418240 | bytes 8388608 | tf_op jit(solution)/shard_map/far/pallas_call | solution.py:320
  18.9 0.1 collective-permute-start.4
  18.9 2.0 %collective-permute-start.5 = (bf16[1024,128]{1,0:T(8,128)(2,1)S(1)}, bf16[1024,128]{1,0:T(8,128)(2,1)S(1)}, u32[]{:S(2)}, u32[]{:S(2)}) collective-permute-start(bf16[1024,128]{1,0:T(8,128)(2,1)S(1)} %get-tuple-element.26), channel_id=1, source_target_pairs={{0,3},{1,2},{2,1},{3,0},{4,7},{5,6},{6,5},{7,4},{8,11},{9,10},{10,... | collective-permute-start | bytes 786440 | tf_op jit(solution)/shard_map/ppermute | solution.py:340
  21.0 0.1 collective-permute-start.6
  21.1 0.0 collective-permute-done.1.refs_3_.refs_2_
  21.1 0.6 %collective-permute-done.3.refs_4_ = bf16[1024,128]{1,0:T(8,128)(2,1)S(1)} collective-permute-done((bf16[1024,128]{1,0:T(8,128)(2,1)S(1)}, bf16[1024,128]{1,0:T(8,128)(2,1)S(1)}, u32[]{:S(2)}, u32[]{:S(2)}) %collective-permute-start.3) | collective-permute-done | bytes 262176 | tf_op jit(solution)/shard_map/ppermute | solution.py:340
  21.7 5.6 %far.2 = (bf16[2,512,2048]{2,1,0:T(8,128)(2,1)S(1)}, bf16[1024,128]{1,0:T(8,128)(2,1)S(1)}, bf16[1024,128]{1,0:T(8,128)(2,1)S(1)}) custom-call(s32[32]{0:T(128)S(1)} %copy-done.2, bf16[4096,128]{1,0:T(8,128)(2,1)S(1)} %bitcast.10, bf16[4096,128]{1,0:T(8,128)(2,1)S(1)} %bitcast.6, f32[8,4096]{1,0:T(8,128)S(1)} %get-tuple-element.20.refs_2_, ...), custom_call_target="tpu_custom_call" | custom-call | flops 10737418240 | bytes 8388608 | tf_op jit(solution)/shard_map/far/pallas_call | solution.py:320
  27.3 0.0 collective-permute-done.4.refs_1_.refs_0_
  27.3 0.3 collective-permute-done.5.refs_2_.refs_1_
  27.6 0.1 join.1.refs_7_
  27.8 4.5 %collective-permute-start.7 = (bf16[1024,128]{1,0:T(8,128)(2,1)S(1)}, bf16[1024,128]{1,0:T(8,128)(2,1)S(1)}, u32[]{:S(2)}, u32[]{:S(2)}) collective-permute-start(bf16[1024,128]{1,0:T(8,128)(2,1)S(1)} %join.1.refs_7_), channel_id=1, source_target_pairs={{0,28},{1,29},{2,30},{3,31},{4,0},{5,1},{6,2},{7,3},{8,4},{9,5},{1... | collective-permute-start | bytes 786440 | tf_op jit(solution)/shard_map/ppermute | solution.py:340
  32.2 1.5 %collective-permute-start.8 = (bf16[1024,128]{1,0:T(8,128)(2,1)S(1)}, bf16[1024,128]{1,0:T(8,128)(2,1)S(1)}, u32[]{:S(2)}, u32[]{:S(2)}) collective-permute-start(bf16[1024,128]{1,0:T(8,128)(2,1)S(1)} %get-tuple-element.32), channel_id=1, source_target_pairs={{0,29},{1,28},{2,31},{3,30},{4,1},{5,0},{6,3},{7,2},{8,5},{9,4},{1... | collective-permute-start | bytes 786440 | tf_op jit(solution)/shard_map/ppermute | solution.py:340
  33.7 4.9 %last.1 = (bf16[1024,4096]{1,0:T(8,128)(2,1)S(1)}, f32[1024,128]{1,0:T(8,128)S(1)}, f32[1024,128]{1,0:T(8,128)S(1)}, f32[1024,128]{1,0:T(8,128)S(1)}) custom-call(s32[32]{0:T(128)S(1)} %copy-done.2, bf16[4096,128]{1,0:T(8,128)(2,1)S(1)} %bitcast.11, bf16[4096,128]{1,0:T(8,128)(2,1)S(1)} %bitcast.7, ...), custom_call_target="tpu_custom_call", output_to_operand_aliasing={{0}: (5, {}), {1}: (6, {}), {2}: (7, {})} | custom-call | flops 8724152320 | bytes 6815744 | tf_op jit(solution)/shard_map/last/pallas_call | solution.py:320
  38.6 5.2 %queries.1 = bf16[4096,128]{1,0:T(8,128)(2,1)} custom-call(s32[32]{0:T(128)S(1)} %copy-done.2, bf16[2048,128]{1,0:T(8,128)(2,1)S(1)} %get-tuple-element.19.refs_3_.both_ref, bf16[1024,4096]{1,0:T(8,128)(2,1)S(1)} %get-tuple-element.27.own_ref, bf16[1024,128]{1,0:T(8,128)(2,1)S(1)} %collective-permute-done.refs_3_.refs_0_, ...), custom_call_target="tpu_custom_call" | custom-call | flops 6710886400 | bytes 5242880 | tf_op jit(solution)/shard_map/queries/pallas_call | solution.py:320
  43.8 0.0 collective-permute-done.6.refs_2_
  43.8 0.0 collective-permute-done.7.refs_3_
  43.8 0.4 collective-permute-done.8.refs_4_
  44.2 0.9 %total.1 = (bf16[512,128]{1,0:T(8,128)(2,1)}, bf16[512,128]{1,0:T(8,128)(2,1)}) custom-call(f32[1024,128]{1,0:T(8,128)S(1)} %get-tuple-element.30.total_ref, bf16[1024,128]{1,0:T(8,128)(2,1)S(1)} %collective-permute-done.4.refs_1_.refs_0_, bf16[1024,128]{1,0:T(8,128)(2,1)S(1)} %collective-permute-done.5.refs_2_.refs_1_, ...), custom_call_target="tpu_custom_call" | custom-call | flops 13421772 | bytes 10485 | tf_op jit(solution)/shard_map/total/pallas_call | solution.py:320
Async XLA Ops:
  0.6 9.8 %collective-permute-start = (bf16[1024,128]{1,0:T(8,128)(2,1)}, bf16[1024,128]{1,0:T(8,128)(2,1)S(1)}, u32[]{:S(2)}, u32[]{:S(2)}) collective-permute-start(bf16[1024,128]{1,0:T(8,128)(2,1)} %refs_4_.1), channel_id=1, source_target_pairs={{0,2},{1,3},{2,4},{3,5},{4,6},{5,7},{6,8},{7,9},{8,10},{9,11},{10,... | collective-permute-start | bytes 786440 | tf_op jit(solution)/shard_map/ppermute | solution.py:340
  1.1 12.1 %collective-permute-start.2 = (bf16[1024,128]{1,0:T(8,128)(2,1)}, bf16[1024,128]{1,0:T(8,128)(2,1)S(1)}, u32[]{:S(2)}, u32[]{:S(2)}) collective-permute-start(bf16[1024,128]{1,0:T(8,128)(2,1)} %refs_5_.1), channel_id=1, source_target_pairs={{0,2},{1,3},{2,4},{3,5},{4,6},{5,7},{6,8},{7,9},{8,10},{9,11},{10,... | collective-permute-start | bytes 786440 | tf_op jit(solution)/shard_map/ppermute | solution.py:340
  3.8 9.4 %copy-start = (bf16[1024,4,128]{2,1,0:T(4,128)(2,1)S(1)}, bf16[1024,4,128]{2,1,0:T(4,128)(2,1)}, u32[]{:S(2)}) copy-start(bf16[1024,4,128]{2,1,0:T(4,128)(2,1)} %param.11) | copy-start | bytes 3145732
  3.8 9.4 %copy-start.1 = (bf16[1024,4,128]{2,1,0:T(4,128)(2,1)S(1)}, bf16[1024,4,128]{2,1,0:T(4,128)(2,1)}, u32[]{:S(2)}) copy-start(bf16[1024,4,128]{2,1,0:T(4,128)(2,1)} %param.7) | copy-start | bytes 3145732
  3.8 9.4 %copy-start.2 = (s32[32]{0:T(128)S(1)}, s32[32]{0:T(128)}, u32[]{:S(2)}) copy-start(s32[32]{0:T(128)} %span_ids.7) | copy-start | bytes 388
  10.4 10.7 %collective-permute-start.1 = (bf16[1024,128]{1,0:T(8,128)(2,1)S(1)}, bf16[1024,128]{1,0:T(8,128)(2,1)S(1)}, u32[]{:S(2)}, u32[]{:S(2)}) collective-permute-start(bf16[1024,128]{1,0:T(8,128)(2,1)S(1)} %collective-permute-done.refs_3_.refs_0_), channel_id=1, source_target_pairs={{0,2},{1,3},{2,4},{3,5},{4,6},{5,7},{6,8},{7,9},{8,10},{9,11},{10,... | collective-permute-start | bytes 786440 | tf_op jit(solution)/shard_map/ppermute | solution.py:340
  13.2 8.5 %collective-permute-start.3 = (bf16[1024,128]{1,0:T(8,128)(2,1)S(1)}, bf16[1024,128]{1,0:T(8,128)(2,1)S(1)}, u32[]{:S(2)}, u32[]{:S(2)}) collective-permute-start(bf16[1024,128]{1,0:T(8,128)(2,1)S(1)} %collective-permute-done.2.refs_4_), channel_id=1, source_target_pairs={{0,2},{1,3},{2,4},{3,5},{4,6},{5,7},{6,8},{7,9},{8,10},{9,11},{10,... | collective-permute-start | bytes 786440 | tf_op jit(solution)/shard_map/ppermute | solution.py:340
  18.9 8.5 %collective-permute-start.4 = (bf16[1024,128]{1,0:T(8,128)(2,1)S(1)}, bf16[1024,128]{1,0:T(8,128)(2,1)S(1)}, u32[]{:S(2)}, u32[]{:S(2)}) collective-permute-start(bf16[1024,128]{1,0:T(8,128)(2,1)S(1)} %get-tuple-element.25), channel_id=1, source_target_pairs={{0,2},{1,3},{2,0},{3,1},{4,6},{5,7},{6,4},{7,5},{8,10},{9,11},{10,... | collective-permute-start | bytes 786440 | tf_op jit(solution)/shard_map/ppermute | solution.py:340
  18.9 8.7 %collective-permute-start.5 = (bf16[1024,128]{1,0:T(8,128)(2,1)S(1)}, bf16[1024,128]{1,0:T(8,128)(2,1)S(1)}, u32[]{:S(2)}, u32[]{:S(2)}) collective-permute-start(bf16[1024,128]{1,0:T(8,128)(2,1)S(1)} %get-tuple-element.26), channel_id=1, source_target_pairs={{0,3},{1,2},{2,1},{3,0},{4,7},{5,6},{6,5},{7,4},{8,11},{9,10},{10,... | collective-permute-start | bytes 786440 | tf_op jit(solution)/shard_map/ppermute | solution.py:340
  21.0 22.8 %collective-permute-start.6 = (bf16[1024,128]{1,0:T(8,128)(2,1)S(1)}, bf16[1024,128]{1,0:T(8,128)(2,1)S(1)}, u32[]{:S(2)}, u32[]{:S(2)}) collective-permute-start(bf16[1024,128]{1,0:T(8,128)(2,1)S(1)} %get-tuple-element.31), channel_id=1, source_target_pairs={{0,1},{1,0},{2,3},{3,2},{4,5},{5,4},{6,7},{7,6},{8,9},{9,8},{10,11... | collective-permute-start | bytes 786440 | tf_op jit(solution)/shard_map/ppermute | solution.py:340
  27.8 16.1 %collective-permute-start.7 = (bf16[1024,128]{1,0:T(8,128)(2,1)S(1)}, bf16[1024,128]{1,0:T(8,128)(2,1)S(1)}, u32[]{:S(2)}, u32[]{:S(2)}) collective-permute-start(bf16[1024,128]{1,0:T(8,128)(2,1)S(1)} %join.1.refs_7_), channel_id=1, source_target_pairs={{0,28},{1,29},{2,30},{3,31},{4,0},{5,1},{6,2},{7,3},{8,4},{9,5},{1... | collective-permute-start | bytes 786440 | tf_op jit(solution)/shard_map/ppermute | solution.py:340
  32.2 12.0 %collective-permute-start.8 = (bf16[1024,128]{1,0:T(8,128)(2,1)S(1)}, bf16[1024,128]{1,0:T(8,128)(2,1)S(1)}, u32[]{:S(2)}, u32[]{:S(2)}) collective-permute-start(bf16[1024,128]{1,0:T(8,128)(2,1)S(1)} %get-tuple-element.32), channel_id=1, source_target_pairs={{0,29},{1,28},{2,31},{3,30},{4,1},{5,0},{6,3},{7,2},{8,5},{9,4},{1... | collective-permute-start | bytes 786440 | tf_op jit(solution)/shard_map/ppermute | solution.py:340

commit v8 on v7

--- a/solution.py
+++ b/solution.py
@@ -53,37 +53,64 @@
         out[1:2, pl.ds(row, tile)] = (dot(ones, high, NT) + dot(ones, low, NT))[0:1]
 
 
-def tile_grads(group, accs, scale, tiles):
-    query_ref, grad_ref, key_ref, value_ref, terms_ref, tile = group
+def opened(group, row, key, length):
+    query_ref, grad_ref, key_ref, value_ref, _, tile = group
+    k = key_ref[pl.ds(key, length), :]
+    v = value_ref[pl.ds(key, length), :]
+    scores = dot(k, query_ref[pl.ds(row, tile), :], NT)
+    return scores, dot(v, grad_ref[pl.ds(row, tile), :], NT)
+
+
+def closed(group, scale, row, triangle, scores, dprob):
+    terms_ref, tile = group[4:]
+    norm = terms_ref[0:1, pl.ds(row, tile)]
+    delta = terms_ref[1:2, pl.ds(row, tile)]
+    prob = jnp.exp2(scores * (scale * math.log2(math.e)) - norm)
+    if triangle is not None:
+        edge = prob.shape[0] - triangle.shape[0]
+        last = jnp.where(triangle, prob[edge:], 0.0)
+        prob = last if edge == 0 else jnp.concatenate([prob[:edge], last], axis=0)
+    return prob.astype(jnp.bfloat16), (prob * (dprob - delta)).astype(jnp.bfloat16)
+
+
+def triangle_grads(group, accs, scale, row, key, half, triangle, kept_ref):
+    query_ref, grad_ref, tile = group[0], group[1], group[-1]
     key_acc, value_acc = accs
-
-    def opened(row, key, length, *_):
-        k = key_ref[pl.ds(key, length), :]
-        v = value_ref[pl.ds(key, length), :]
-        scores = dot(k, query_ref[pl.ds(row, tile), :], NT)
-        return scores, dot(v, grad_ref[pl.ds(row, tile), :], NT)
-
-    def closed(row, key, length, triangle, kept, scores, dprob):
-        norm = terms_ref[0:1, pl.ds(row, tile)]
-        delta = terms_ref[1:2, pl.ds(row, tile)]
-        prob = jnp.exp2(scores * (scale * math.log2(math.e)) - norm)
-        if triangle is not None:
-            edge = length - triangle.shape[0]
-            last = jnp.where(triangle, prob[edge:], 0.0)
-            prob = last if edge == 0 else jnp.concatenate([prob[:edge], last], axis=0)
-        dscore = (prob * (dprob - delta)).astype(jnp.bfloat16)
-        kept[...] = dscore
-        value_acc[pl.ds(key, length), :] += dot(
-            prob.astype(jnp.bfloat16), grad_ref[pl.ds(row, tile), :], NN
-        )
-        key_acc[pl.ds(key, length), :] += dot(dscore, query_ref[pl.ds(row, tile), :], NN)
-
-    ahead = opened(*tiles[0])
-    for index, this in enumerate(tiles):
+    per = triangle.shape[0]
+    tiles = [(pl.multiple_of(row + p * tile, tile), (p + 1) * per) for p in range(half // per)]
+    ahead = opened(group, tiles[0][0], key, tiles[0][1])
+    for index, (row, length) in enumerate(tiles):
         now = ahead
         if index + 1 < len(tiles):
-            ahead = opened(*tiles[index + 1])
-        closed(*this, *now)
+            ahead = opened(group, tiles[index + 1][0], key, tiles[index + 1][1])
+        prob, dscore = closed(group, scale, row, triangle, *now)
+        kept_ref[pl.ds(key, length), pl.ds(row, tile)] = dscore
+        value_acc[pl.ds(key, length), :] += dot(prob, grad_ref[pl.ds(row, tile), :], NN)
+        key_acc[pl.ds(key, length), :] += dot(dscore, query_ref[pl.ds(row, tile), :], NN)
+
+
+def block_grads(group, accs, scale, rows, blocks):
+    query_ref, grad_ref, tile = group[0], group[1], group[-1]
+    key_acc, value_acc = accs
+    count = rows // tile
+    tiles = [(block, p) for block in blocks for p in range(count)]
+
+    def start(block, p):
+        row, key, length = block[:3]
+        return opened(group, pl.multiple_of(row + p * tile, tile), key, length)
+
+    ahead = start(*tiles[0])
+    for index, (block, p) in enumerate(tiles):
+        now = ahead
+        if index + 1 < len(tiles):
+            ahead = start(*tiles[index + 1])
+        row, key, length, kept, probs = block
+        prob, dscore = closed(group, scale, pl.multiple_of(row + p * tile, tile), None, *now)
+        probs[:, p * tile : (p + 1) * tile] = prob
+        kept[:, p * tile : (p + 1) * tile] = dscore
+        if p == count - 1:
+            value_acc[pl.ds(key, length), :] += dot(probs[...], grad_ref[pl.ds(row, rows), :], NN)
+            key_acc[pl.ds(key, length), :] += dot(kept[...], query_ref[pl.ds(row, rows), :], NN)
 
 
 def span_pair(span_ids, holder):
@@ -113,7 +140,7 @@
         out[share : 2 * share, :] = value_acc[pl.ds(start, share), :].astype(out.dtype)
 
 
-def own_tiles(group, accs, scale, span_ids, kept_ref, heads, halves):
+def own_work(group, accs, scale, span_ids, kept_ref, probs_ref, heads):
     tile = group[-1]
     toks, rows = kept_ref.shape
     half, span_rows, per = toks // 2, rows // 2, tile // heads
@@ -123,33 +150,24 @@
         lax.broadcasted_iota(jnp.int32, (per, tile), 1) // heads
     )
 
-    def placed(row, key, length, triangle):
-        return row, key, length, triangle, kept_ref.at[pl.ds(key, length), pl.ds(row, tile)]
-
-    for before, which in halves:
-        before()
+    def corner(which):
         key = pl.multiple_of(which * half, half)
-        tiles = []
-        for p in range(span_rows // tile):
-            row = pl.multiple_of(which * span_rows + p * tile, tile)
-            tiles.append(placed(row, key, (p + 1) * per, triangle))
-        tile_grads(group, accs, scale, tiles)
+        row = pl.multiple_of(which * span_rows, span_rows)
+        triangle_grads(group, accs, scale, row, key, half, triangle, kept_ref)
 
     def square():
         key = pl.multiple_of(low * half, half)
-        tiles = []
-        for p in range(span_rows // tile):
-            row = pl.multiple_of((1 - low) * span_rows + p * tile, tile)
-            tiles.append(placed(row, key, half, None))
-        tile_grads(group, accs, scale, tiles)
-
-    return low, square
+        row = pl.multiple_of((1 - low) * span_rows, span_rows)
+        kept = kept_ref.at[pl.ds(key, half), pl.ds(row, span_rows)]
+        block_grads(group, accs, scale, span_rows, [(row, key, half, kept, probs_ref)])
+
+    return low, corner, square
 
 
 def first_kernel(heads, tile, scale, parts, *refs):
     inputs, refs = refs[:7], refs[7:]
     terms_ref, both_ref, kept_ref, key_acc, value_acc = refs[:5]
-    held, span_ids, sems = refs[5:-2], refs[-2], refs[-1]
+    held, (probs_ref, span_ids, sems) = refs[5:-3], refs[-3:]
     grad_ref, outputs_ref, query_ref, norm_ref = held
     toks = both_ref.shape[0] // 2
     key_ref, value_ref = both_ref.at[pl.ds(0, toks)], both_ref.at[pl.ds(toks, toks)]
@@ -182,36 +200,38 @@
 
     group = (query_ref, grad_ref, key_ref, value_ref, terms_ref, tile)
     accs = (key_acc, value_acc)
-    todo = [(functools.partial(arrive, slot), order[slot]) for slot in range(2)]
+    low, corner, square = own_work(group, accs, scale, span_ids, kept_ref, probs_ref, heads)
+    arrive(0)
+    corner(order[0])
+    arrive(1)
     if parts == 2:
-        low, square = own_tiles(group, accs, scale, span_ids, kept_ref, heads, todo[:1])
-        arrive(1)
         pl.when(low == order[0])(square)
+        pl.when(low == order[1])(lambda: corner(order[1]))
     else:
-        _, square = own_tiles(group, accs, scale, span_ids, kept_ref, heads, todo)
+        corner(order[1])
         square()
 
 
 def last_kernel(heads, tile, scale, parts, span_ids, *refs):
     query_ref, grad_ref, terms_ref, both_ref = refs[:4]
-    kept_ref, key_acc, value_acc, total_ref = refs[8:]
+    kept_ref, key_acc, value_acc, total_ref, probs_ref = refs[8:]
     if parts == 2:
         toks = both_ref.shape[0] // 2
         key_ref, value_ref = both_ref.at[pl.ds(0, toks)], both_ref.at[pl.ds(toks, toks)]
         group = (query_ref, grad_ref, key_ref, value_ref, terms_ref, tile)
+        accs = (key_acc, value_acc)
         x = lax.axis_index("head")
-        low, square = own_tiles(
-            group, (key_acc, value_acc), scale, span_ids, kept_ref, heads, [(lambda: None, x)]
-        )
+        low, corner, square = own_work(group, accs, scale, span_ids, kept_ref, probs_ref, heads)
         pl.when(low == x)(square)
+        pl.when(low != x)(lambda: corner(x))
     put_shares([total_ref], key_acc, value_acc, scale, 0, parts)
 
 
 def far_kernel(heads, tile, scale, parts, step, span_ids, *refs):
     query_ref, grad_ref, terms_ref, key_ref, value_ref = refs[:5]
     own, refs = (refs[5:7], refs[7:]) if step == 1 else (None, refs[5:])
-    kept_ref, outs, own_outs = refs[0], refs[1 : 1 + parts], refs[1 + parts : -2]
-    key_acc, value_acc = refs[-2:]
+    kept_ref, outs, own_outs = refs[0], refs[1 : 1 + parts], refs[1 + parts : -3]
+    key_acc, value_acc, probs_ref = refs[-3:]
     if own:
         put_shares(own_outs, *own, scale, 1)
     half = key_ref.shape[0] // 2
@@ -221,23 +241,13 @@
     group = (query_ref, grad_ref, key_ref, value_ref, terms_ref, tile)
     halves = far_halves(span_ids, step)
 
-    @pl.loop(0, 2)
-    def _(item):
+    blocks = []
+    for item in range(2):
         row_half, key_half = halves(item)
         row = pl.multiple_of(row_half * rows, rows)
         key = pl.multiple_of(key_half * half, half)
-        tiles = [
-            (
-                pl.multiple_of(row + p * tile, tile),
-                key,
-                half,
-                None,
-                kept_ref.at[item, :, pl.ds(p * tile, tile)],
-            )
-            for p in range(rows // tile)
-        ]
-        tile_grads(group, (key_acc, value_acc), scale, tiles)
-
+        blocks.append((row, key, half, kept_ref.at[item], probs_ref.at[item]))
+    block_grads(group, (key_acc, value_acc), scale, rows, blocks)
     put_shares(outs, key_acc, value_acc, scale)
 
 
@@ -354,6 +364,7 @@
     shape = jax.ShapeDtypeStruct
     grads = [shape((share, dim), bf16)] * parts
     accs = [pltpu.VMEM((toks, dim), f32)] * 2
+    probs = pltpu.VMEM((toks // 2, rows // 2), bf16)
 
     key_1, value_1 = moved(keys, (-1, -1), 0), moved(values, (-1, -1), 0)
     inputs = tuple(
@@ -367,7 +378,7 @@
         [HBM] * len(inputs),
         [shape((8, rows), f32), shape((2 * toks, dim), bf16)] + sums,
         [pltpu.VMEM(a.shape, a.dtype) for a in inputs[:4]]
-        + [pltpu.SMEM(span_ids.shape, span_ids.dtype), pltpu.SemaphoreType.DMA((4, 3))],
+        + [probs, pltpu.SMEM(span_ids.shape, span_ids.dtype), pltpu.SemaphoreType.DMA((4, 3))],
         1.625 * heads,
         20,
         "first",
@@ -380,9 +391,9 @@
             (span_ids, q, g, terms, key, value, *own),
             [SMEM] + [VMEM] * (5 + len(own)),
             [shape((2, toks // 2, rows // 2), bf16)] + grads + (grads[1:] if own else []),
-            accs,
+            accs + [pltpu.VMEM((2, toks // 2, rows // 2), bf16)],
             2 * heads,
-            14,
+            18,
             "far",
         )
 
@@ -399,7 +410,7 @@
         (span_ids, q, g, terms, both, kept, key_sum, value_sum, sent[0]),
         [SMEM] + [VMEM] * 7 + [ANY],
         sums + [shape((share, dim), f32)],
-        [],
+        [probs],
         1.625 * heads,
         20,
         "last",

time: 45.5 us -> 45.4 us (level)
  transfers between devices with their start and end apart: 9 -> 9, of which waited for: 5 -> 5; matrix products, arithmetic and copies ran while one was open for 0% -> 0% of each run, Pallas kernels for 58% -> 57%
where the time goes in v8:
time: 45.4 us; the launch traced here: 45 us
  Pallas kernels  26.5 us (58%)
  starting transfers between devices  11.3 us (25%)
  waiting for transfers between devices  6.4 us (14%)
  between operations  0.7 us (2%)
    pallas_call x7, Pallas kernels, call(): pl.pallas_call(kernel, out_shape=outs, in_specs=where, out_specs=[VMEM] *...  26.5 us
    ppermute x9, starting transfers between devices, moved(): return lax.ppermute(block, ('ctx', 'head'), route)  11.3 us
    ppermute x9, waiting for transfers between devices, moved(): return lax.ppermute(block, ('ctx', 'head'), route)  6.4 us
  transfers between devices with their start and end apart: 9, of which 5 were waited for; matrix products, arithmetic and copies ran while one was open for 0% of the time, Pallas kernels for 57%

profile of v8, /device:TPU:0, one launch (start us, length us, event | category | flops | bytes accessed | tf_op | source)
XLA Modules:
  0.0 45.0 jit_solution(8419410446900424427)
XLA Ops:
  0.6 0.5 %collective-permute-start = (bf16[1024,128]{1,0:T(8,128)(2,1)}, bf16[1024,128]{1,0:T(8,128)(2,1)S(1)}, u32[]{:S(2)}, u32[]{:S(2)}) collective-permute-start(bf16[1024,128]{1,0:T(8,128)(2,1)} %refs_4_.1), channel_id=1, source_target_pairs={{0,2},{1,3},{2,4},{3,5},{4,6},{5,7},{6,8},{7,9},{8,10},{9,11},{10,... | collective-permute-start | bytes 786440 | tf_op jit(solution)/shard_map/ppermute | solution.py:350
  1.1 2.6 %collective-permute-start.2 = (bf16[1024,128]{1,0:T(8,128)(2,1)}, bf16[1024,128]{1,0:T(8,128)(2,1)S(1)}, u32[]{:S(2)}, u32[]{:S(2)}) collective-permute-start(bf16[1024,128]{1,0:T(8,128)(2,1)} %refs_5_.1), channel_id=1, source_target_pairs={{0,2},{1,3},{2,4},{3,5},{4,6},{5,7},{6,8},{7,9},{8,10},{9,11},{10,... | collective-permute-start | bytes 786440 | tf_op jit(solution)/shard_map/ppermute | solution.py:350
  3.8 0.0 copy-start
  3.8 0.0 copy-start.1
  3.8 0.0 copy-start.2
  3.8 6.1 %first.1 = (f32[8,4096]{1,0:T(8,128)S(1)}, bf16[2048,128]{1,0:T(8,128)(2,1)S(1)}, bf16[1024,4096]{1,0:T(8,128)(2,1)S(1)}, f32[1024,128]{1,0:T(8,128)S(1)}, f32[1024,128]{1,0:T(8,128)S(1)}) custom-call(bf16[4096,128]{1,0:T(8,128)(2,1)} %bitcast.4, bf16[4096,128]{1,0:T(8,128)(2,1)} %bitcast.12, bf16[4096,128]{1,0:T(8,128)(2,1)} %bitcast.8, f32[4,1024]{1,0:T(4,128)} %refs_3_.1, ...), custom_call_target="tpu_custom_call" | custom-call | flops 8724152320 | bytes 6815744 | tf_op jit(solution)/shard_map/first/pallas_call | solution.py:330
  9.9 0.5 %collective-permute-done.refs_3_.refs_0_ = bf16[1024,128]{1,0:T(8,128)(2,1)S(1)} collective-permute-done((bf16[1024,128]{1,0:T(8,128)(2,1)}, bf16[1024,128]{1,0:T(8,128)(2,1)S(1)}, u32[]{:S(2)}, u32[]{:S(2)}) %collective-permute-start) | collective-permute-done | bytes 262176 | tf_op jit(solution)/shard_map/ppermute | solution.py:350
  10.4 0.0 collective-permute-start.1
  10.4 2.8 %collective-permute-done.2.refs_4_ = bf16[1024,128]{1,0:T(8,128)(2,1)S(1)} collective-permute-done((bf16[1024,128]{1,0:T(8,128)(2,1)}, bf16[1024,128]{1,0:T(8,128)(2,1)S(1)}, u32[]{:S(2)}, u32[]{:S(2)}) %collective-permute-start.2) | collective-permute-done | bytes 262176 | tf_op jit(solution)/shard_map/ppermute | solution.py:350
  13.2 0.0 collective-permute-start.3
  13.2 0.0 copy-done
  13.2 0.0 copy-done.1
  13.2 0.0 copy-done.2
  13.2 5.5 %far.3 = (bf16[2,512,2048]{2,1,0:T(8,128)(2,1)S(1)}, bf16[1024,128]{1,0:T(8,128)(2,1)S(1)}, bf16[1024,128]{1,0:T(8,128)(2,1)S(1)}, bf16[1024,128]{1,0:T(8,128)(2,1)S(1)}) custom-call(s32[32]{0:T(128)S(1)} %copy-done.2, bf16[4096,128]{1,0:T(8,128)(2,1)S(1)} %bitcast.9, bf16[4096,128]{1,0:T(8,128)(2,1)S(1)} %bitcast.5, ...), custom_call_target="tpu_custom_call" | custom-call | flops 10737418240 | bytes 8388608 | tf_op jit(solution)/shard_map/far/pallas_call | solution.py:330
  18.8 0.1 collective-permute-start.4
  18.9 2.0 %collective-permute-start.5 = (bf16[1024,128]{1,0:T(8,128)(2,1)S(1)}, bf16[1024,128]{1,0:T(8,128)(2,1)S(1)}, u32[]{:S(2)}, u32[]{:S(2)}) collective-permute-start(bf16[1024,128]{1,0:T(8,128)(2,1)S(1)} %get-tuple-element.26), channel_id=1, source_target_pairs={{0,3},{1,2},{2,1},{3,0},{4,7},{5,6},{6,5},{7,4},{8,11},{9,10},{10,... | collective-permute-start | bytes 786440 | tf_op jit(solution)/shard_map/ppermute | solution.py:350
  20.9 0.1 collective-permute-start.6
  21.0 0.0 collective-permute-done.1.refs_3_.refs_2_
  21.0 0.7 %collective-permute-done.3.refs_4_ = bf16[1024,128]{1,0:T(8,128)(2,1)S(1)} collective-permute-done((bf16[1024,128]{1,0:T(8,128)(2,1)S(1)}, bf16[1024,128]{1,0:T(8,128)(2,1)S(1)}, u32[]{:S(2)}, u32[]{:S(2)}) %collective-permute-start.3) | collective-permute-done | bytes 262176 | tf_op jit(solution)/shard_map/ppermute | solution.py:350
  21.7 5.5 %far.2 = (bf16[2,512,2048]{2,1,0:T(8,128)(2,1)S(1)}, bf16[1024,128]{1,0:T(8,128)(2,1)S(1)}, bf16[1024,128]{1,0:T(8,128)(2,1)S(1)}) custom-call(s32[32]{0:T(128)S(1)} %copy-done.2, bf16[4096,128]{1,0:T(8,128)(2,1)S(1)} %bitcast.10, bf16[4096,128]{1,0:T(8,128)(2,1)S(1)} %bitcast.6, f32[8,4096]{1,0:T(8,128)S(1)} %get-tuple-element.20.refs_2_, ...), custom_call_target="tpu_custom_call" | custom-call | flops 10737418240 | bytes 8388608 | tf_op jit(solution)/shard_map/far/pallas_call | solution.py:330
  27.2 0.0 collective-permute-done.4.refs_1_.refs_0_
  27.2 0.3 collective-permute-done.5.refs_2_.refs_1_
  27.5 0.1 join.1.refs_7_
  27.7 4.5 %collective-permute-start.7 = (bf16[1024,128]{1,0:T(8,128)(2,1)S(1)}, bf16[1024,128]{1,0:T(8,128)(2,1)S(1)}, u32[]{:S(2)}, u32[]{:S(2)}) collective-permute-start(bf16[1024,128]{1,0:T(8,128)(2,1)S(1)} %join.1.refs_7_), channel_id=1, source_target_pairs={{0,28},{1,29},{2,30},{3,31},{4,0},{5,1},{6,2},{7,3},{8,4},{9,5},{1... | collective-permute-start | bytes 786440 | tf_op jit(solution)/shard_map/ppermute | solution.py:350
  32.1 1.5 %collective-permute-start.8 = (bf16[1024,128]{1,0:T(8,128)(2,1)S(1)}, bf16[1024,128]{1,0:T(8,128)(2,1)S(1)}, u32[]{:S(2)}, u32[]{:S(2)}) collective-permute-start(bf16[1024,128]{1,0:T(8,128)(2,1)S(1)} %get-tuple-element.32), channel_id=1, source_target_pairs={{0,29},{1,28},{2,31},{3,30},{4,1},{5,0},{6,3},{7,2},{8,5},{9,4},{1... | collective-permute-start | bytes 786440 | tf_op jit(solution)/shard_map/ppermute | solution.py:350
  33.6 3.2 %last.1 = (bf16[1024,4096]{1,0:T(8,128)(2,1)S(1)}, f32[1024,128]{1,0:T(8,128)S(1)}, f32[1024,128]{1,0:T(8,128)S(1)}, f32[1024,128]{1,0:T(8,128)S(1)}) custom-call(s32[32]{0:T(128)S(1)} %copy-done.2, bf16[4096,128]{1,0:T(8,128)(2,1)S(1)} %bitcast.11, bf16[4096,128]{1,0:T(8,128)(2,1)S(1)} %bitcast.7, ...), custom_call_target="tpu_custom_call", output_to_operand_aliasing={{0}: (5, {}), {1}: (6, {}), {2}: (7, {})} | custom-call | flops 8724152320 | bytes 6815744 | tf_op jit(solution)/shard_map/last/pallas_call | solution.py:330
  36.9 5.2 %queries.1 = bf16[4096,128]{1,0:T(8,128)(2,1)} custom-call(s32[32]{0:T(128)S(1)} %copy-done.2, bf16[2048,128]{1,0:T(8,128)(2,1)S(1)} %get-tuple-element.19.refs_3_.both_ref, bf16[1024,4096]{1,0:T(8,128)(2,1)S(1)} %get-tuple-element.27.own_ref, bf16[1024,128]{1,0:T(8,128)(2,1)S(1)} %collective-permute-done.refs_3_.refs_0_, ...), custom_call_target="tpu_custom_call" | custom-call | flops 6710886400 | bytes 5242880 | tf_op jit(solution)/shard_map/queries/pallas_call | solution.py:330
  42.1 0.0 collective-permute-done.6.refs_2_
  42.1 0.0 collective-permute-done.7.refs_3_
  42.1 2.0 %collective-permute-done.8.refs_4_ = bf16[1024,128]{1,0:T(8,128)(2,1)S(1)} collective-permute-done((bf16[1024,128]{1,0:T(8,128)(2,1)S(1)}, bf16[1024,128]{1,0:T(8,128)(2,1)S(1)}, u32[]{:S(2)}, u32[]{:S(2)}) %collective-permute-start.8) | collective-permute-done | bytes 262176 | tf_op jit(solution)/shard_map/ppermute | solution.py:350
  44.1 0.9 %total.1 = (bf16[512,128]{1,0:T(8,128)(2,1)}, bf16[512,128]{1,0:T(8,128)(2,1)}) custom-call(f32[1024,128]{1,0:T(8,128)S(1)} %get-tuple-element.30.total_ref, bf16[1024,128]{1,0:T(8,128)(2,1)S(1)} %collective-permute-done.4.refs_1_.refs_0_, bf16[1024,128]{1,0:T(8,128)(2,1)S(1)} %collective-permute-done.5.refs_2_.refs_1_, ...), custom_call_target="tpu_custom_call" | custom-call | flops 13421772 | bytes 10485 | tf_op jit(solution)/shard_map/total/pallas_call | solution.py:330
Async XLA Ops:
  0.6 9.8 %collective-permute-start = (bf16[1024,128]{1,0:T(8,128)(2,1)}, bf16[1024,128]{1,0:T(8,128)(2,1)S(1)}, u32[]{:S(2)}, u32[]{:S(2)}) collective-permute-start(bf16[1024,128]{1,0:T(8,128)(2,1)} %refs_4_.1), channel_id=1, source_target_pairs={{0,2},{1,3},{2,4},{3,5},{4,6},{5,7},{6,8},{7,9},{8,10},{9,11},{10,... | collective-permute-start | bytes 786440 | tf_op jit(solution)/shard_map/ppermute | solution.py:350
  1.1 12.1 %collective-permute-start.2 = (bf16[1024,128]{1,0:T(8,128)(2,1)}, bf16[1024,128]{1,0:T(8,128)(2,1)S(1)}, u32[]{:S(2)}, u32[]{:S(2)}) collective-permute-start(bf16[1024,128]{1,0:T(8,128)(2,1)} %refs_5_.1), channel_id=1, source_target_pairs={{0,2},{1,3},{2,4},{3,5},{4,6},{5,7},{6,8},{7,9},{8,10},{9,11},{10,... | collective-permute-start | bytes 786440 | tf_op jit(solution)/shard_map/ppermute | solution.py:350
  3.8 9.4 %copy-start = (bf16[1024,4,128]{2,1,0:T(4,128)(2,1)S(1)}, bf16[1024,4,128]{2,1,0:T(4,128)(2,1)}, u32[]{:S(2)}) copy-start(bf16[1024,4,128]{2,1,0:T(4,128)(2,1)} %param.11) | copy-start | bytes 3145732
  3.8 9.4 %copy-start.1 = (bf16[1024,4,128]{2,1,0:T(4,128)(2,1)S(1)}, bf16[1024,4,128]{2,1,0:T(4,128)(2,1)}, u32[]{:S(2)}) copy-start(bf16[1024,4,128]{2,1,0:T(4,128)(2,1)} %param.7) | copy-start | bytes 3145732
  3.8 9.4 %copy-start.2 = (s32[32]{0:T(128)S(1)}, s32[32]{0:T(128)}, u32[]{:S(2)}) copy-start(s32[32]{0:T(128)} %span_ids.7) | copy-start | bytes 388
  10.4 10.6 %collective-permute-start.1 = (bf16[1024,128]{1,0:T(8,128)(2,1)S(1)}, bf16[1024,128]{1,0:T(8,128)(2,1)S(1)}, u32[]{:S(2)}, u32[]{:S(2)}) collective-permute-start(bf16[1024,128]{1,0:T(8,128)(2,1)S(1)} %collective-permute-done.refs_3_.refs_0_), channel_id=1, source_target_pairs={{0,2},{1,3},{2,4},{3,5},{4,6},{5,7},{6,8},{7,9},{8,10},{9,11},{10,... | collective-permute-start | bytes 786440 | tf_op jit(solution)/shard_map/ppermute | solution.py:350
  13.2 8.5 %collective-permute-start.3 = (bf16[1024,128]{1,0:T(8,128)(2,1)S(1)}, bf16[1024,128]{1,0:T(8,128)(2,1)S(1)}, u32[]{:S(2)}, u32[]{:S(2)}) collective-permute-start(bf16[1024,128]{1,0:T(8,128)(2,1)S(1)} %collective-permute-done.2.refs_4_), channel_id=1, source_target_pairs={{0,2},{1,3},{2,4},{3,5},{4,6},{5,7},{6,8},{7,9},{8,10},{9,11},{10,... | collective-permute-start | bytes 786440 | tf_op jit(solution)/shard_map/ppermute | solution.py:350
  18.8 8.4 %collective-permute-start.4 = (bf16[1024,128]{1,0:T(8,128)(2,1)S(1)}, bf16[1024,128]{1,0:T(8,128)(2,1)S(1)}, u32[]{:S(2)}, u32[]{:S(2)}) collective-permute-start(bf16[1024,128]{1,0:T(8,128)(2,1)S(1)} %get-tuple-element.25), channel_id=1, source_target_pairs={{0,2},{1,3},{2,0},{3,1},{4,6},{5,7},{6,4},{7,5},{8,10},{9,11},{10,... | collective-permute-start | bytes 786440 | tf_op jit(solution)/shard_map/ppermute | solution.py:350
  18.9 8.7 %collective-permute-start.5 = (bf16[1024,128]{1,0:T(8,128)(2,1)S(1)}, bf16[1024,128]{1,0:T(8,128)(2,1)S(1)}, u32[]{:S(2)}, u32[]{:S(2)}) collective-permute-start(bf16[1024,128]{1,0:T(8,128)(2,1)S(1)} %get-tuple-element.26), channel_id=1, source_target_pairs={{0,3},{1,2},{2,1},{3,0},{4,7},{5,6},{6,5},{7,4},{8,11},{9,10},{10,... | collective-permute-start | bytes 786440 | tf_op jit(solution)/shard_map/ppermute | solution.py:350
  20.9 21.2 %collective-permute-start.6 = (bf16[1024,128]{1,0:T(8,128)(2,1)S(1)}, bf16[1024,128]{1,0:T(8,128)(2,1)S(1)}, u32[]{:S(2)}, u32[]{:S(2)}) collective-permute-start(bf16[1024,128]{1,0:T(8,128)(2,1)S(1)} %get-tuple-element.31), channel_id=1, source_target_pairs={{0,1},{1,0},{2,3},{3,2},{4,5},{5,4},{6,7},{7,6},{8,9},{9,8},{10,11... | collective-permute-start | bytes 786440 | tf_op jit(solution)/shard_map/ppermute | solution.py:350
  27.7 14.4 %collective-permute-start.7 = (bf16[1024,128]{1,0:T(8,128)(2,1)S(1)}, bf16[1024,128]{1,0:T(8,128)(2,1)S(1)}, u32[]{:S(2)}, u32[]{:S(2)}) collective-permute-start(bf16[1024,128]{1,0:T(8,128)(2,1)S(1)} %join.1.refs_7_), channel_id=1, source_target_pairs={{0,28},{1,29},{2,30},{3,31},{4,0},{5,1},{6,2},{7,3},{8,4},{9,5},{1... | collective-permute-start | bytes 786440 | tf_op jit(solution)/shard_map/ppermute | solution.py:350
  32.1 12.0 %collective-permute-start.8 = (bf16[1024,128]{1,0:T(8,128)(2,1)S(1)}, bf16[1024,128]{1,0:T(8,128)(2,1)S(1)}, u32[]{:S(2)}, u32[]{:S(2)}) collective-permute-start(bf16[1024,128]{1,0:T(8,128)(2,1)S(1)} %get-tuple-element.32), channel_id=1, source_target_pairs={{0,29},{1,28},{2,31},{3,30},{4,1},{5,0},{6,3},{7,2},{8,5},{9,4},{1... | collective-permute-start | bytes 786440 | tf_op jit(solution)/shard_map/ppermute | solution.py:350

commit v9 on v8

--- a/solution.py
+++ b/solution.py
@@ -104,13 +104,13 @@
         now = ahead
         if index + 1 < len(tiles):
             ahead = start(*tiles[index + 1])
-        row, key, length, kept, probs = block
+        row, _, length, kept, probs, place = block
         prob, dscore = closed(group, scale, pl.multiple_of(row + p * tile, tile), None, *now)
         probs[:, p * tile : (p + 1) * tile] = prob
         kept[:, p * tile : (p + 1) * tile] = dscore
         if p == count - 1:
-            value_acc[pl.ds(key, length), :] += dot(probs[...], grad_ref[pl.ds(row, rows), :], NN)
-            key_acc[pl.ds(key, length), :] += dot(kept[...], query_ref[pl.ds(row, rows), :], NN)
+            value_acc[pl.ds(place, length), :] += dot(probs[...], grad_ref[pl.ds(row, rows), :], NN)
+            key_acc[pl.ds(place, length), :] += dot(kept[...], query_ref[pl.ds(row, rows), :], NN)
 
 
 def span_pair(span_ids, holder):
@@ -130,14 +130,19 @@
     )
 
 
-def put_shares(outs, key_acc, value_acc, scale, first=0, parts=None):
+def put_shares(outs, key_acc, value_acc, scale, first=0, parts=None, more=None):
     parts = parts or len(outs) + first
     share = key_acc.shape[0] // parts
     x = lax.axis_index("head")
     for away, out in enumerate(outs, first):
         start = pl.multiple_of(lax.rem(x + away, parts) * share, share)
-        out[0:share, :] = (key_acc[pl.ds(start, share), :] * scale).astype(out.dtype)
-        out[share : 2 * share, :] = value_acc[pl.ds(start, share), :].astype(out.dtype)
+        for low, part in (
+            (0, key_acc[pl.ds(start, share), :] * scale),
+            (share, value_acc[pl.ds(start, share), :]),
+        ):
+            if more is not None:
+                part = part + more(away, low, share)
+            out[low : low + share, :] = part.astype(out.dtype)
 
 
 def own_work(group, accs, scale, span_ids, kept_ref, probs_ref, heads):
@@ -159,7 +164,7 @@
         key = pl.multiple_of(low * half, half)
         row = pl.multiple_of((1 - low) * span_rows, span_rows)
         kept = kept_ref.at[pl.ds(key, half), pl.ds(row, span_rows)]
-        block_grads(group, accs, scale, span_rows, [(row, key, half, kept, probs_ref)])
+        block_grads(group, accs, scale, span_rows, [(row, key, half, kept, probs_ref, key)])
 
     return low, corner, square
 
@@ -227,56 +232,93 @@
     put_shares([total_ref], key_acc, value_acc, scale, 0, parts)
 
 
-def far_kernel(heads, tile, scale, parts, step, span_ids, *refs):
-    query_ref, grad_ref, terms_ref, key_ref, value_ref = refs[:5]
-    own, refs = (refs[5:7], refs[7:]) if step == 1 else (None, refs[5:])
-    kept_ref, outs, own_outs = refs[0], refs[1 : 1 + parts], refs[1 + parts : -3]
-    key_acc, value_acc, probs_ref = refs[-3:]
-    if own:
-        put_shares(own_outs, *own, scale, 1)
-    half = key_ref.shape[0] // 2
-    rows = half * heads
+def near_kernel(heads, tile, scale, parts, span_ids, *refs):
+    query_ref, grad_ref, terms_ref, key_ref, value_ref, own_keys, own_values, _, kept_ref = refs[:9]
+    outs, own_outs, (key_acc, value_acc, probs_ref) = refs[9 : 9 + parts], refs[9 + parts : -3], refs[-3:]
+    put_shares(own_outs, own_keys, own_values, scale, 1)
+    group = (query_ref, grad_ref, key_ref, value_ref, terms_ref, tile)
+    far_work(group, (key_acc, value_acc), scale, span_ids, kept_ref, probs_ref, heads, 1, 0, 1)
+    put_shares(outs, key_acc, value_acc, scale)
+
+
+def pack_kernel(key_ref, value_ref, out_ref):
+    toks = key_ref.shape[0]
+    out_ref[0:toks, :] = key_ref[...]
+    out_ref[toks : 2 * toks, :] = value_ref[...]
+
+
+def far_kernel(heads, tile, scale, piece, pieces, span_ids, *refs):
+    query_ref, grad_ref, terms_ref, both_ref, _ = refs[:5]
+    parts = (len(refs) - 9) // 2
+    swapped, kept_ref = refs[5 : 5 + parts], refs[5 + parts]
+    outs, (key_acc, value_acc, probs_ref) = refs[6 + parts : -3], refs[-3:]
+    toks = both_ref.shape[0] // 2
+    key_ref, value_ref = both_ref.at[pl.ds(0, toks)], both_ref.at[pl.ds(toks, toks)]
+    group = (query_ref, grad_ref, key_ref, value_ref, terms_ref, tile)
+    far_work(
+        group, (key_acc, value_acc), scale, span_ids, kept_ref, probs_ref, heads, 2, piece, pieces
+    )
+    odd = lax.rem(lax.axis_index("ctx"), 2).astype(jnp.float32)
+
+    def more(away, low, share):
+        start = low * pieces + piece * share
+        return swapped[away][start : start + share, :].astype(jnp.float32) * odd
+
+    put_shares(outs, key_acc, value_acc, scale, more=more)
+
+
+def far_work(group, accs, scale, span_ids, kept_ref, probs_ref, heads, step, piece, pieces):
+    key_acc, value_acc = accs
     key_acc[...] = jnp.zeros_like(key_acc)
     value_acc[...] = jnp.zeros_like(value_acc)
-    group = (query_ref, grad_ref, key_ref, value_ref, terms_ref, tile)
+    half = group[2].shape[0] // 2
+    rows, length = half * heads, half // pieces
     halves = far_halves(span_ids, step)
-
     blocks = []
     for item in range(2):
         row_half, key_half = halves(item)
         row = pl.multiple_of(row_half * rows, rows)
-        key = pl.multiple_of(key_half * half, half)
-        blocks.append((row, key, half, kept_ref.at[item], probs_ref.at[item]))
-    block_grads(group, (key_acc, value_acc), scale, rows, blocks)
-    put_shares(outs, key_acc, value_acc, scale)
+        key = pl.multiple_of(key_half * half + piece * length, length)
+        place = pl.multiple_of(key_half * length, length)
+        blocks.append((row, key, length, kept_ref.at[item], probs_ref.at[item], place))
+    block_grads(group, accs, scale, rows, blocks)
 
 
 def join_kernel(*refs):
-    this_ref, out_ref = refs[0], refs[-1]
-    odd = lax.rem(lax.axis_index("ctx"), 2).astype(jnp.float32)
-    more = sum(ref[...].astype(jnp.float32) for ref in refs[1:-1])
-    out_ref[...] = (this_ref[...].astype(jnp.float32) + more * odd).astype(out_ref.dtype)
-
-
-def total_kernel(parts, total_ref, *refs):
+    count = len(refs) // 3
+    even = 1.0 - lax.rem(lax.axis_index("ctx"), 2).astype(jnp.float32)
+    for swapped, this, out in zip(refs, refs[count:], refs[2 * count :]):
+        more = swapped[...].astype(jnp.float32) * even
+        out[...] = (this[...].astype(jnp.float32) + more).astype(out.dtype)
+
+
+def total_kernel(pieces, total_ref, swapped_ref, *refs):
     ins, (key_out, value_out) = refs[:-2], refs[-2:]
     share = key_out.shape[0]
     even = 1.0 - lax.rem(lax.axis_index("ctx"), 2).astype(jnp.float32)
-    for low, out in ((0, key_out), (share, value_out)):
-        joined, landed = (
-            sum(ref[low : low + share, :].astype(jnp.float32) for ref in some)
-            for some in (ins[:parts], ins[parts:])
-        )
-        out[...] = (total_ref[low : low + share, :] + joined * even + landed).astype(out.dtype)
-
-
-def query_kernel(heads, tile, scale, span_ids, both_ref, own_ref, *refs):
-    far_refs, (out_ref, acc, turned) = refs[:-3], refs[-3:]
+    length = share // pieces
+    whole = [ref for ref in ins if ref.shape[0] == 2 * share]
+    cut = [ref for ref in ins if ref.shape[0] != 2 * share]
+    for which, out in enumerate((key_out, value_out)):
+        for piece in range(pieces):
+            here = piece * length
+            low = which * share + here
+            part = total_ref[low : low + length, :]
+            part = part + swapped_ref[low : low + length, :].astype(jnp.float32) * even
+            for ref in whole:
+                part = part + ref[low : low + length, :].astype(jnp.float32)
+            for ref in cut[piece * len(cut) // pieces : (piece + 1) * len(cut) // pieces]:
+                part = part + ref[which * length : (which + 1) * length, :].astype(jnp.float32)
+            out[here : here + length, :] = part.astype(out.dtype)
+
+
+def query_kernel(heads, tile, scale, pieces, span_ids, both_ref, own_ref, *refs):
+    (key_1, both_2), kept_refs, (out_ref, acc, turned) = refs[:2], refs[2:-3], refs[-3:]
     toks = both_ref.shape[0] // 2
     half = toks // 2
     rows = half * heads
     per = tile // heads
-    for index, key_ref in enumerate([both_ref] + list(far_refs[::2])):
+    for index, key_ref in enumerate((both_ref, key_1, both_2)):
         for low in range(0, toks, half):
             turned[index, :, low : low + half] = key_ref[low : low + half, :].T
 
@@ -298,18 +340,19 @@
         acc[:, pl.ds(row, tile)] += dot(
             turned[0, :, pl.ds(key, half)], own_ref[pl.ds(key, half), pl.ds(row, tile)], NN
         )
-    for step in range(1, STEPS):
-        kept_ref = far_refs[2 * step - 1]
+    for index, kept_ref in enumerate(kept_refs):
+        step, piece = (1, 0) if index == 0 else (2, index - 1)
+        length = kept_ref.shape[1]
         halves = far_halves(span_ids, step)
 
         @pl.loop(0, 2)
         def _(item):
             row_half, key_half = halves(item)
-            key = pl.multiple_of(key_half * half, half)
+            key = pl.multiple_of(key_half * half + piece * length, length)
             for p in range(rows // tile):
                 row = pl.multiple_of(row_half * rows + p * tile, tile)
                 acc[:, pl.ds(row, tile)] += dot(
-                    turned[step, :, pl.ds(key, half)],
+                    turned[step, :, pl.ds(key, length)],
                     kept_ref[item, :, p * tile : (p + 1) * tile],
                     NN,
                 )
@@ -383,31 +426,54 @@
         20,
         "first",
     )
-    key_2, value_2 = moved(key_1, (-1, -1), 0), moved(value_1, (-1, -1), 0)
-
-    def far(step, key, value, *own):
-        return call(
-            functools.partial(far_kernel, heads, tile, scale, parts, step),
-            (span_ids, q, g, terms, key, value, *own),
-            [SMEM] + [VMEM] * (5 + len(own)),
-            [shape((2, toks // 2, rows // 2), bf16)] + grads + (grads[1:] if own else []),
-            accs + [pltpu.VMEM((2, toks // 2, rows // 2), bf16)],
-            2 * heads,
+    (both_1,) = call(
+        pack_kernel, (key_1, value_1), [VMEM] * 2, [shape((2 * toks, dim), bf16)], [], 0.01, 4, "pack"
+    )
+    both_2 = moved(both_1, (-1, -1), 0)
+
+    block = (toks // 2, rows // 2)
+    kept_1, *sent = call(
+        functools.partial(near_kernel, heads, tile, scale, parts),
+        (span_ids, q, g, terms, key_1, value_1, key_sum, value_sum, both_1),
+        [SMEM] + [VMEM] * 7 + [ANY],
+        [shape((2,) + block, bf16)] + grads + grads[1:],
+        accs + [pltpu.VMEM((2,) + block, bf16)],
+        2 * heads,
+        18,
+        "near",
+    )
+    swapped = [moved(part, (-1, 1), 0) for part in sent[:parts]]
+    sent = call(
+        join_kernel,
+        (*swapped[1:], *sent[parts:]),
+        [VMEM] * (2 * parts - 2),
+        grads[1:],
+        [],
+        0.01,
+        4,
+        "join",
+    )
+    whole = [moved(part, (0, 0), away) for away, part in enumerate(sent, 1)]
+    pieces = 2 if parts == 2 else 1
+    small = (2, toks // 2 // pieces, rows // 2)
+    kept_2, cut, last = [], [], sent[0]
+    for piece in range(pieces):
+        kept_piece, *sent = call(
+            functools.partial(far_kernel, heads, tile, scale, piece, pieces),
+            (span_ids, q, g, terms, both_2, last, *swapped),
+            [SMEM] + [VMEM] * 4 + [ANY] + [VMEM] * parts,
+            [shape(small, bf16)] + [shape((share // pieces, dim), bf16)] * parts,
+            [pltpu.VMEM((toks // pieces, dim), f32)] * 2 + [pltpu.VMEM(small, bf16)],
+            2 * heads / pieces,
             18,
             "far",
         )
-
-    kept_1, *sent = far(1, key_1, value_1, key_sum, value_sum)
-    joined = [moved(block, (-1, 1), away) for away, block in enumerate(sent[:parts])]
-    landed = [moved(block, (0, 0), away + 1) for away, block in enumerate(sent[parts:])]
-    kept_2, *sent = far(2, key_2, value_2)
-    sent[:1] = call(
-        join_kernel, (sent[0], *joined), [VMEM] * (1 + parts), grads[:1], [], 0.01, 4, "join"
-    )
-    landed += [moved(block, (2, 2), away) for away, block in enumerate(sent)]
+        kept_2.append(kept_piece)
+        cut += [moved(part, (2, 2), away) for away, part in enumerate(sent)]
+        last = sent[0]
     kept, _, _, total = call(
         functools.partial(last_kernel, heads, tile, scale, parts),
-        (span_ids, q, g, terms, both, kept, key_sum, value_sum, sent[0]),
+        (span_ids, q, g, terms, both, kept, key_sum, value_sum, last),
         [SMEM] + [VMEM] * 7 + [ANY],
         sums + [shape((share, dim), f32)],
         [probs],
@@ -417,9 +483,9 @@
         {5: 0, 6: 1, 7: 2},
     )
     (query_grad,) = call(
-        functools.partial(query_kernel, heads, tile, scale),
-        (span_ids, both, kept, key_1, kept_1, key_2, kept_2),
-        [SMEM] + [VMEM] * 6,
+        functools.partial(query_kernel, heads, tile, scale, pieces),
+        (span_ids, both, kept, key_1, both_2, kept_1, *kept_2),
+        [SMEM] + [VMEM] * (5 + pieces),
         [shape((rows, dim), bf16)],
         [pltpu.VMEM((dim, rows), f32), pltpu.VMEM((STEPS, dim, toks), bf16)],
         1.25 * heads,
@@ -427,9 +493,9 @@
         "queries",
     )
     key_grad, value_grad = call(
-        functools.partial(total_kernel, parts),
-        (total, *joined, *landed),
-        [VMEM] * (1 + len(joined) + len(landed)),
+        functools.partial(total_kernel, pieces),
+        (total, swapped[0], *whole, *cut),
+        [VMEM] * (2 + len(whole) + len(cut)),
         [shape((share // 2, dim), bf16)] * 2,
         [],
         0.01,

time: 45.4 us -> 46 us (1.013)
  Pallas kernels: 26.5 us -> 27.8 us
    pallas_call x7 -> x9, Pallas kernels: 26.5 us -> 27.8 us  [call(): pl.pallas_call(kernel, out_shape=outs, in_specs=where, out_specs=[VMEM] *...]
    ppermute x9 -> x10, starting transfers between devices: 11.3 us -> 10.9 us  [moved(): return lax.ppermute(block, ('ctx', 'head'), route)]
    ppermute x9 -> x10, waiting for transfers between devices: 6.4 us -> 6.41 us  [moved(): return lax.ppermute(block, ('ctx', 'head'), route)]
  transfers between devices with their start and end apart: 9 -> 10, of which waited for: 5 -> 4; matrix products, arithmetic and copies ran while one was open for 0% -> 0% of each run, Pallas kernels for 57% -> 59%
where the time goes in v9:
time: 46 us; the launch traced here: 45.8 us
  Pallas kernels  27.8 us (60%)
  starting transfers between devices  10.9 us (24%)
  waiting for transfers between devices  6.41 us (14%)
  between operations  0.75 us (2%)
    pallas_call x9, Pallas kernels, call(): pl.pallas_call(kernel, out_shape=outs, in_specs=where, out_specs=[VMEM] *...  27.8 us
    ppermute x10, starting transfers between devices, moved(): return lax.ppermute(block, ('ctx', 'head'), route)  10.9 us
    ppermute x10, waiting for transfers between devices, moved(): return lax.ppermute(block, ('ctx', 'head'), route)  6.41 us
  transfers between devices with their start and end apart: 10, of which 4 were waited for; matrix products, arithmetic and copies ran while one was open for 0% of the time, Pallas kernels for 59%

profile of v9, /device:TPU:0, one launch (start us, length us, event | category | flops | bytes accessed | tf_op | source)
XLA Modules:
  0.0 45.8 jit_solution(663343043461153605)
XLA Ops:
  0.6 0.5 %collective-permute-start = (bf16[1024,128]{1,0:T(8,128)(2,1)}, bf16[1024,128]{1,0:T(8,128)(2,1)S(1)}, u32[]{:S(2)}, u32[]{:S(2)}) collective-permute-start(bf16[1024,128]{1,0:T(8,128)(2,1)} %refs_4_.1), channel_id=1, source_target_pairs={{0,2},{1,3},{2,4},{3,5},{4,6},{5,7},{6,8},{7,9},{8,10},{9,11},{10,... | collective-permute-start | bytes 786440 | tf_op jit(solution)/shard_map/ppermute | solution.py:393
  1.1 2.6 %collective-permute-start.1 = (bf16[1024,128]{1,0:T(8,128)(2,1)}, bf16[1024,128]{1,0:T(8,128)(2,1)S(1)}, u32[]{:S(2)}, u32[]{:S(2)}) collective-permute-start(bf16[1024,128]{1,0:T(8,128)(2,1)} %refs_5_.1), channel_id=1, source_target_pairs={{0,2},{1,3},{2,4},{3,5},{4,6},{5,7},{6,8},{7,9},{8,10},{9,11},{10,... | collective-permute-start | bytes 786440 | tf_op jit(solution)/shard_map/ppermute | solution.py:393
  3.8 0.0 copy-start
  3.8 0.0 copy-start.1
  3.8 0.0 copy-start.2
  3.8 6.1 %first.1 = (f32[8,4096]{1,0:T(8,128)S(1)}, bf16[2048,128]{1,0:T(8,128)(2,1)S(1)}, bf16[1024,4096]{1,0:T(8,128)(2,1)S(1)}, f32[1024,128]{1,0:T(8,128)S(1)}, f32[1024,128]{1,0:T(8,128)S(1)}) custom-call(bf16[4096,128]{1,0:T(8,128)(2,1)} %bitcast.4, bf16[4096,128]{1,0:T(8,128)(2,1)} %bitcast.14, bf16[4096,128]{1,0:T(8,128)(2,1)} %bitcast.9, f32[4,1024]{1,0:T(4,128)} %refs_3_.1, ...), custom_call_target="tpu_custom_call" | custom-call | flops 8724152320 | bytes 6815744 | tf_op jit(solution)/shard_map/first/pallas_call | solution.py:373
  9.9 0.5 %collective-permute-done.key_ref.refs_3_.refs_0_ = bf16[1024,128]{1,0:T(8,128)(2,1)S(1)} collective-permute-done((bf16[1024,128]{1,0:T(8,128)(2,1)}, bf16[1024,128]{1,0:T(8,128)(2,1)S(1)}, u32[]{:S(2)}, u32[]{:S(2)}) %collective-permute-start) | collective-permute-done | bytes 262176 | tf_op jit(solution)/shard_map/ppermute | solution.py:393
  10.4 2.8 %collective-permute-done.1.value_ref.refs_4_ = bf16[1024,128]{1,0:T(8,128)(2,1)S(1)} collective-permute-done((bf16[1024,128]{1,0:T(8,128)(2,1)}, bf16[1024,128]{1,0:T(8,128)(2,1)S(1)}, u32[]{:S(2)}, u32[]{:S(2)}) %collective-permute-start.1) | collective-permute-done | bytes 262176 | tf_op jit(solution)/shard_map/ppermute | solution.py:393
  13.2 0.2 collective-permute-start.2
  13.5 0.0 copy-done
  13.5 0.0 copy-done.1
  13.5 0.0 copy-done.2
  13.5 5.5 %near.1 = (bf16[2,512,2048]{2,1,0:T(8,128)(2,1)S(1)}, bf16[1024,128]{1,0:T(8,128)(2,1)S(1)}, bf16[1024,128]{1,0:T(8,128)(2,1)S(1)}, bf16[1024,128]{1,0:T(8,128)(2,1)S(1)}) custom-call(s32[32]{0:T(128)S(1)} %copy-done.2, bf16[4096,128]{1,0:T(8,128)(2,1)S(1)} %bitcast.10, bf16[4096,128]{1,0:T(8,128)(2,1)S(1)} %bitcast.5, ...), custom_call_target="tpu_custom_call" | custom-call | flops 10737418240 | bytes 8388608 | tf_op jit(solution)/shard_map/near/pallas_call | solution.py:373
  19.1 0.1 collective-permute-start.3
  19.1 0.5 %collective-permute-start.4 = (bf16[1024,128]{1,0:T(8,128)(2,1)S(1)}, bf16[1024,128]{1,0:T(8,128)(2,1)S(1)}, u32[]{:S(2)}, u32[]{:S(2)}) collective-permute-start(bf16[1024,128]{1,0:T(8,128)(2,1)S(1)} %get-tuple-element.29), channel_id=1, source_target_pairs={{0,2},{1,3},{2,0},{3,1},{4,6},{5,7},{6,4},{7,5},{8,10},{9,11},{10,... | collective-permute-start | bytes 786440 | tf_op jit(solution)/shard_map/ppermute | solution.py:393
  19.6 1.0 %collective-permute-done.3.refs_0_.refs_6_ = bf16[1024,128]{1,0:T(8,128)(2,1)S(1)} collective-permute-done((bf16[1024,128]{1,0:T(8,128)(2,1)S(1)}, bf16[1024,128]{1,0:T(8,128)(2,1)S(1)}, u32[]{:S(2)}, u32[]{:S(2)}) %collective-permute-start.3) | collective-permute-done | bytes 262176 | tf_op jit(solution)/shard_map/ppermute | solution.py:393
  20.7 0.1 join.1.refs_4_
  20.8 2.0 %collective-permute-start.5 = (bf16[1024,128]{1,0:T(8,128)(2,1)S(1)}, bf16[1024,128]{1,0:T(8,128)(2,1)S(1)}, u32[]{:S(2)}, u32[]{:S(2)}) collective-permute-start(bf16[1024,128]{1,0:T(8,128)(2,1)S(1)} %join.1.refs_4_), channel_id=1, source_target_pairs={{0,1},{1,0},{2,3},{3,2},{4,5},{5,4},{6,7},{7,6},{8,9},{9,8},{10,11... | collective-permute-start | bytes 786440 | tf_op jit(solution)/shard_map/ppermute | solution.py:393
  22.8 0.0 collective-permute-done.4.refs_5_.swapped_ref
  22.8 2.0 %collective-permute-done.2.refs_3_.refs_1_ = bf16[2048,128]{1,0:T(8,128)(2,1)S(1)} collective-permute-done((bf16[2048,128]{1,0:T(8,128)(2,1)S(1)}, bf16[2048,128]{1,0:T(8,128)(2,1)S(1)}, u32[]{:S(2)}, u32[]{:S(2)}) %collective-permute-start.2) | collective-permute-done | bytes 524320 | tf_op jit(solution)/shard_map/ppermute | solution.py:393
  24.8 3.2 %far.2 = (bf16[2,256,2048]{2,1,0:T(8,128)(2,1)S(1)}, bf16[512,128]{1,0:T(8,128)(2,1)S(1)}, bf16[512,128]{1,0:T(8,128)(2,1)S(1)}) custom-call(s32[32]{0:T(128)S(1)} %copy-done.2, bf16[4096,128]{1,0:T(8,128)(2,1)S(1)} %bitcast.11, bf16[4096,128]{1,0:T(8,128)(2,1)S(1)} %bitcast.6, f32[8,4096]{1,0:T(8,128)S(1)} %get-tuple-element.23.refs_2_, ...), custom_call_target="tpu_custom_call" | custom-call | flops 5368709120 | bytes 4194304 | tf_op jit(solution)/shard_map/far/pallas_call | solution.py:373
  28.0 2.5 %collective-permute-start.6 = (bf16[512,128]{1,0:T(8,128)(2,1)S(1)}, bf16[512,128]{1,0:T(8,128)(2,1)S(1)}, u32[]{:S(2)}, u32[]{:S(2)}) collective-permute-start(bf16[512,128]{1,0:T(8,128)(2,1)S(1)} %get-tuple-element.30.refs_4_), channel_id=1, source_target_pairs={{0,28},{1,29},{2,30},{3,31},{4,0},{5,1},{6,2},{7,3},{8,4},{9,5},{1... | collective-permute-start | bytes 393224 | tf_op jit(solution)/shard_map/ppermute | solution.py:393
  30.5 3.2 %far.3 = (bf16[2,256,2048]{2,1,0:T(8,128)(2,1)S(1)}, bf16[512,128]{1,0:T(8,128)(2,1)S(1)}, bf16[512,128]{1,0:T(8,128)(2,1)S(1)}) custom-call(s32[32]{0:T(128)S(1)} %copy-done.2, bf16[4096,128]{1,0:T(8,128)(2,1)S(1)} %bitcast.12, bf16[4096,128]{1,0:T(8,128)(2,1)S(1)} %bitcast.7, f32[8,4096]{1,0:T(8,128)S(1)} %get-tuple-element.23.refs_2_, ...), custom_call_target="tpu_custom_call" | custom-call | flops 5368709120 | bytes 4194304 | tf_op jit(solution)/shard_map/far/pallas_call | solution.py:373
  33.7 0.1 collective-permute-start.8
  33.8 1.4 %collective-permute-start.9 = (bf16[512,128]{1,0:T(8,128)(2,1)S(1)}, bf16[512,128]{1,0:T(8,128)(2,1)S(1)}, u32[]{:S(2)}, u32[]{:S(2)}) collective-permute-start(bf16[512,128]{1,0:T(8,128)(2,1)S(1)} %get-tuple-element.38), channel_id=1, source_target_pairs={{0,29},{1,28},{2,31},{3,30},{4,1},{5,0},{6,3},{7,2},{8,5},{9,4},{1... | collective-permute-start | bytes 393224 | tf_op jit(solution)/shard_map/ppermute | solution.py:393
  35.2 1.0 %collective-permute-start.7 = (bf16[512,128]{1,0:T(8,128)(2,1)S(1)}, bf16[512,128]{1,0:T(8,128)(2,1)S(1)}, u32[]{:S(2)}, u32[]{:S(2)}) collective-permute-start(bf16[512,128]{1,0:T(8,128)(2,1)S(1)} %get-tuple-element.37), channel_id=1, source_target_pairs={{0,29},{1,28},{2,31},{3,30},{4,1},{5,0},{6,3},{7,2},{8,5},{9,4},{1... | collective-permute-start | bytes 393224 | tf_op jit(solution)/shard_map/ppermute | solution.py:393
  36.2 3.3 %last.1 = (bf16[1024,4096]{1,0:T(8,128)(2,1)S(1)}, f32[1024,128]{1,0:T(8,128)S(1)}, f32[1024,128]{1,0:T(8,128)S(1)}, f32[1024,128]{1,0:T(8,128)S(1)}) custom-call(s32[32]{0:T(128)S(1)} %copy-done.2, bf16[4096,128]{1,0:T(8,128)(2,1)S(1)} %bitcast.13, bf16[4096,128]{1,0:T(8,128)(2,1)S(1)} %bitcast.8, ...), custom_call_target="tpu_custom_call", output_to_operand_aliasing={{0}: (5, {}), {1}: (6, {}), {2}: (7, {})} | custom-call | flops 8724152320 | bytes 6815744 | tf_op jit(solution)/shard_map/last/pallas_call | solution.py:373
  39.4 5.5 %queries.1 = bf16[4096,128]{1,0:T(8,128)(2,1)} custom-call(s32[32]{0:T(128)S(1)} %copy-done.2, bf16[2048,128]{1,0:T(8,128)(2,1)S(1)} %get-tuple-element.22.refs_3_.both_ref, bf16[1024,4096]{1,0:T(8,128)(2,1)S(1)} %get-tuple-element.32.own_ref, bf16[1024,128]{1,0:T(8,128)(2,1)S(1)} %collective-permute-done.key_ref.refs_3_.refs_0_, ...), custom_call_target="tpu_custom_call" | custom-call | flops 6710886400 | bytes 5242880 | tf_op jit(solution)/shard_map/queries/pallas_call | solution.py:373
  45.0 0.0 collective-permute-done.5.refs_0_
  45.0 0.0 collective-permute-done.8.refs_3_
  45.0 0.0 collective-permute-done.9.refs_4_
  45.0 0.0 collective-permute-done.6.refs_1_
  45.0 0.0 collective-permute-done.7.refs_2_
  45.0 0.8 %total.1 = (bf16[512,128]{1,0:T(8,128)(2,1)}, bf16[512,128]{1,0:T(8,128)(2,1)}) custom-call(f32[1024,128]{1,0:T(8,128)S(1)} %get-tuple-element.36.total_ref, bf16[1024,128]{1,0:T(8,128)(2,1)S(1)} %collective-permute-done.4.refs_5_.swapped_ref, bf16[1024,128]{1,0:T(8,128)(2,1)S(1)} %collective-permute-done.5.refs_0_, ...), custom_call_target="tpu_custom_call" | custom-call | flops 13421772 | bytes 10485 | tf_op jit(solution)/shard_map/total/pallas_call | solution.py:373
  (1 shorter events, 0.0 us)
Async XLA Ops:
  0.6 9.8 %collective-permute-start = (bf16[1024,128]{1,0:T(8,128)(2,1)}, bf16[1024,128]{1,0:T(8,128)(2,1)S(1)}, u32[]{:S(2)}, u32[]{:S(2)}) collective-permute-start(bf16[1024,128]{1,0:T(8,128)(2,1)} %refs_4_.1), channel_id=1, source_target_pairs={{0,2},{1,3},{2,4},{3,5},{4,6},{5,7},{6,8},{7,9},{8,10},{9,11},{10,... | collective-permute-start | bytes 786440 | tf_op jit(solution)/shard_map/ppermute | solution.py:393
  1.1 12.1 %collective-permute-start.1 = (bf16[1024,128]{1,0:T(8,128)(2,1)}, bf16[1024,128]{1,0:T(8,128)(2,1)S(1)}, u32[]{:S(2)}, u32[]{:S(2)}) collective-permute-start(bf16[1024,128]{1,0:T(8,128)(2,1)} %refs_5_.1), channel_id=1, source_target_pairs={{0,2},{1,3},{2,4},{3,5},{4,6},{5,7},{6,8},{7,9},{8,10},{9,11},{10,... | collective-permute-start | bytes 786440 | tf_op jit(solution)/shard_map/ppermute | solution.py:393
  3.8 9.7 %copy-start = (bf16[1024,4,128]{2,1,0:T(4,128)(2,1)S(1)}, bf16[1024,4,128]{2,1,0:T(4,128)(2,1)}, u32[]{:S(2)}) copy-start(bf16[1024,4,128]{2,1,0:T(4,128)(2,1)} %param.11) | copy-start | bytes 3145732
  3.8 9.7 %copy-start.1 = (bf16[1024,4,128]{2,1,0:T(4,128)(2,1)S(1)}, bf16[1024,4,128]{2,1,0:T(4,128)(2,1)}, u32[]{:S(2)}) copy-start(bf16[1024,4,128]{2,1,0:T(4,128)(2,1)} %param.7) | copy-start | bytes 3145732
  3.8 9.7 %copy-start.2 = (s32[32]{0:T(128)S(1)}, s32[32]{0:T(128)}, u32[]{:S(2)}) copy-start(s32[32]{0:T(128)} %span_ids.9) | copy-start | bytes 388
  13.2 11.5 %collective-permute-start.2 = (bf16[2048,128]{1,0:T(8,128)(2,1)S(1)}, bf16[2048,128]{1,0:T(8,128)(2,1)S(1)}, u32[]{:S(2)}, u32[]{:S(2)}) collective-permute-start(bf16[2048,128]{1,0:T(8,128)(2,1)S(1)} %pack.1.refs_7_), channel_id=1, source_target_pairs={{0,2},{1,3},{2,4},{3,5},{4,6},{5,7},{6,8},{7,9},{8,10},{9,11},{10,... | collective-permute-start | bytes 1572872 | tf_op jit(solution)/shard_map/ppermute | solution.py:393
  19.1 1.6 %collective-permute-start.3 = (bf16[1024,128]{1,0:T(8,128)(2,1)S(1)}, bf16[1024,128]{1,0:T(8,128)(2,1)S(1)}, u32[]{:S(2)}, u32[]{:S(2)}) collective-permute-start(bf16[1024,128]{1,0:T(8,128)(2,1)S(1)} %get-tuple-element.27), channel_id=1, source_target_pairs={{0,2},{1,3},{2,0},{3,1},{4,6},{5,7},{6,4},{7,5},{8,10},{9,11},{10,... | collective-permute-start | bytes 786440 | tf_op jit(solution)/shard_map/ppermute | solution.py:393
  19.1 3.6 %collective-permute-start.4 = (bf16[1024,128]{1,0:T(8,128)(2,1)S(1)}, bf16[1024,128]{1,0:T(8,128)(2,1)S(1)}, u32[]{:S(2)}, u32[]{:S(2)}) collective-permute-start(bf16[1024,128]{1,0:T(8,128)(2,1)S(1)} %get-tuple-element.29), channel_id=1, source_target_pairs={{0,2},{1,3},{2,0},{3,1},{4,6},{5,7},{6,4},{7,5},{8,10},{9,11},{10,... | collective-permute-start | bytes 786440 | tf_op jit(solution)/shard_map/ppermute | solution.py:393
  20.8 24.2 %collective-permute-start.5 = (bf16[1024,128]{1,0:T(8,128)(2,1)S(1)}, bf16[1024,128]{1,0:T(8,128)(2,1)S(1)}, u32[]{:S(2)}, u32[]{:S(2)}) collective-permute-start(bf16[1024,128]{1,0:T(8,128)(2,1)S(1)} %join.1.refs_4_), channel_id=1, source_target_pairs={{0,1},{1,0},{2,3},{3,2},{4,5},{5,4},{6,7},{7,6},{8,9},{9,8},{10,11... | collective-permute-start | bytes 786440 | tf_op jit(solution)/shard_map/ppermute | solution.py:393
  28.0 17.0 %collective-permute-start.6 = (bf16[512,128]{1,0:T(8,128)(2,1)S(1)}, bf16[512,128]{1,0:T(8,128)(2,1)S(1)}, u32[]{:S(2)}, u32[]{:S(2)}) collective-permute-start(bf16[512,128]{1,0:T(8,128)(2,1)S(1)} %get-tuple-element.30.refs_4_), channel_id=1, source_target_pairs={{0,28},{1,29},{2,30},{3,31},{4,0},{5,1},{6,2},{7,3},{8,4},{9,5},{1... | collective-permute-start | bytes 393224 | tf_op jit(solution)/shard_map/ppermute | solution.py:393
  33.7 11.3 %collective-permute-start.8 = (bf16[512,128]{1,0:T(8,128)(2,1)S(1)}, bf16[512,128]{1,0:T(8,128)(2,1)S(1)}, u32[]{:S(2)}, u32[]{:S(2)}) collective-permute-start(bf16[512,128]{1,0:T(8,128)(2,1)S(1)} %get-tuple-element.31.refs_7_), channel_id=1, source_target_pairs={{0,28},{1,29},{2,30},{3,31},{4,0},{5,1},{6,2},{7,3},{8,4},{9,5},{1... | collective-permute-start | bytes 393224 | tf_op jit(solution)/shard_map/ppermute | solution.py:393
  33.8 11.2 %collective-permute-start.9 = (bf16[512,128]{1,0:T(8,128)(2,1)S(1)}, bf16[512,128]{1,0:T(8,128)(2,1)S(1)}, u32[]{:S(2)}, u32[]{:S(2)}) collective-permute-start(bf16[512,128]{1,0:T(8,128)(2,1)S(1)} %get-tuple-element.38), channel_id=1, source_target_pairs={{0,29},{1,28},{2,31},{3,30},{4,1},{5,0},{6,3},{7,2},{8,5},{9,4},{1... | collective-permute-start | bytes 393224 | tf_op jit(solution)/shard_map/ppermute | solution.py:393
  35.2 9.8 %collective-permute-start.7 = (bf16[512,128]{1,0:T(8,128)(2,1)S(1)}, bf16[512,128]{1,0:T(8,128)(2,1)S(1)}, u32[]{:S(2)}, u32[]{:S(2)}) collective-permute-start(bf16[512,128]{1,0:T(8,128)(2,1)S(1)} %get-tuple-element.37), channel_id=1, source_target_pairs={{0,29},{1,28},{2,31},{3,30},{4,1},{5,0},{6,3},{7,2},{8,5},{9,4},{1... | collective-permute-start | bytes 393224 | tf_op jit(solution)/shard_map/ppermute | solution.py:393

commit v10 on v9

--- a/solution.py
+++ b/solution.py
@@ -454,7 +454,7 @@
         "join",
     )
     whole = [moved(part, (0, 0), away) for away, part in enumerate(sent, 1)]
-    pieces = 2 if parts == 2 else 1
+    pieces = 1
     small = (2, toks // 2 // pieces, rows // 2)
     kept_2, cut, last = [], [], sent[0]
     for piece in range(pieces):

time: 46 us -> 45.3 us (0.985)
  waiting for transfers between devices: 6.41 us -> 8.88 us
  starting transfers between devices: 10.9 us -> 8.84 us
  Pallas kernels: 27.8 us -> 26.7 us
    ppermute x10 -> x8, waiting for transfers between devices: 6.41 us -> 8.88 us  [moved(): return lax.ppermute(block, ('ctx', 'head'), route)]
    ppermute x10 -> x8, starting transfers between devices: 10.9 us -> 8.84 us  [moved(): return lax.ppermute(block, ('ctx', 'head'), route)]
    pallas_call x9 -> x8, Pallas kernels: 27.8 us -> 26.7 us  [call(): pl.pallas_call(kernel, out_shape=outs, in_specs=where, out_specs=[VMEM] *...]
  transfers between devices with their start and end apart: 10 -> 8, of which waited for: 4 -> 6; matrix products, arithmetic and copies ran while one was open for 0% -> 0% of each run, Pallas kernels for 59% -> 57%
where the time goes in v10:
time: 45.3 us; the launch traced here: 45.1 us
  Pallas kernels  26.7 us (59%)
  waiting for transfers between devices  8.88 us (20%)
  starting transfers between devices  8.84 us (20%)
  between operations  0.72 us (2%)
    pallas_call x8, Pallas kernels, call(): pl.pallas_call(kernel, out_shape=outs, in_specs=where, out_specs=[VMEM] *...  26.7 us
    ppermute x8, waiting for transfers between devices, moved(): return lax.ppermute(block, ('ctx', 'head'), route)  8.88 us
    ppermute x8, starting transfers between devices, moved(): return lax.ppermute(block, ('ctx', 'head'), route)  8.84 us
  transfers between devices with their start and end apart: 8, of which 6 were waited for; matrix products, arithmetic and copies ran while one was open for 0% of the time, Pallas kernels for 57%

profile of v10, /device:TPU:0, one launch (start us, length us, event | category | flops | bytes accessed | tf_op | source)
XLA Modules:
  0.0 45.1 jit_solution(8083333900991033314)
XLA Ops:
  0.6 0.5 %collective-permute-start = (bf16[1024,128]{1,0:T(8,128)(2,1)}, bf16[1024,128]{1,0:T(8,128)(2,1)S(1)}, u32[]{:S(2)}, u32[]{:S(2)}) collective-permute-start(bf16[1024,128]{1,0:T(8,128)(2,1)} %refs_4_.1), channel_id=1, source_target_pairs={{0,2},{1,3},{2,4},{3,5},{4,6},{5,7},{6,8},{7,9},{8,10},{9,11},{10,... | collective-permute-start | bytes 786440 | tf_op jit(solution)/shard_map/ppermute | solution.py:393
  1.1 2.6 %collective-permute-start.1 = (bf16[1024,128]{1,0:T(8,128)(2,1)}, bf16[1024,128]{1,0:T(8,128)(2,1)S(1)}, u32[]{:S(2)}, u32[]{:S(2)}) collective-permute-start(bf16[1024,128]{1,0:T(8,128)(2,1)} %refs_5_.1), channel_id=1, source_target_pairs={{0,2},{1,3},{2,4},{3,5},{4,6},{5,7},{6,8},{7,9},{8,10},{9,11},{10,... | collective-permute-start | bytes 786440 | tf_op jit(solution)/shard_map/ppermute | solution.py:393
  3.8 0.0 copy-start
  3.8 0.0 copy-start.1
  3.8 0.0 copy-start.2
  3.8 6.1 %first.1 = (f32[8,4096]{1,0:T(8,128)S(1)}, bf16[2048,128]{1,0:T(8,128)(2,1)S(1)}, bf16[1024,4096]{1,0:T(8,128)(2,1)S(1)}, f32[1024,128]{1,0:T(8,128)S(1)}, f32[1024,128]{1,0:T(8,128)S(1)}) custom-call(bf16[4096,128]{1,0:T(8,128)(2,1)} %bitcast.4, bf16[4096,128]{1,0:T(8,128)(2,1)} %bitcast.12, bf16[4096,128]{1,0:T(8,128)(2,1)} %bitcast.8, f32[4,1024]{1,0:T(4,128)} %refs_3_.1, ...), custom_call_target="tpu_custom_call" | custom-call | flops 8724152320 | bytes 6815744 | tf_op jit(solution)/shard_map/first/pallas_call | solution.py:373
  9.9 0.5 %collective-permute-done.key_ref.refs_3_.refs_0_ = bf16[1024,128]{1,0:T(8,128)(2,1)S(1)} collective-permute-done((bf16[1024,128]{1,0:T(8,128)(2,1)}, bf16[1024,128]{1,0:T(8,128)(2,1)S(1)}, u32[]{:S(2)}, u32[]{:S(2)}) %collective-permute-start) | collective-permute-done | bytes 262176 | tf_op jit(solution)/shard_map/ppermute | solution.py:393
  10.4 2.8 %collective-permute-done.1.value_ref.refs_4_ = bf16[1024,128]{1,0:T(8,128)(2,1)S(1)} collective-permute-done((bf16[1024,128]{1,0:T(8,128)(2,1)}, bf16[1024,128]{1,0:T(8,128)(2,1)S(1)}, u32[]{:S(2)}, u32[]{:S(2)}) %collective-permute-start.1) | collective-permute-done | bytes 262176 | tf_op jit(solution)/shard_map/ppermute | solution.py:393
  13.2 0.2 collective-permute-start.2
  13.5 0.0 copy-done
  13.5 0.0 copy-done.1
  13.5 0.0 copy-done.2
  13.5 5.6 %near.1 = (bf16[2,512,2048]{2,1,0:T(8,128)(2,1)S(1)}, bf16[1024,128]{1,0:T(8,128)(2,1)S(1)}, bf16[1024,128]{1,0:T(8,128)(2,1)S(1)}, bf16[1024,128]{1,0:T(8,128)(2,1)S(1)}) custom-call(s32[32]{0:T(128)S(1)} %copy-done.2, bf16[4096,128]{1,0:T(8,128)(2,1)S(1)} %bitcast.9, bf16[4096,128]{1,0:T(8,128)(2,1)S(1)} %bitcast.5, ...), custom_call_target="tpu_custom_call" | custom-call | flops 10737418240 | bytes 8388608 | tf_op jit(solution)/shard_map/near/pallas_call | solution.py:373
  19.1 0.1 collective-permute-start.3
  19.2 0.5 %collective-permute-start.4 = (bf16[1024,128]{1,0:T(8,128)(2,1)S(1)}, bf16[1024,128]{1,0:T(8,128)(2,1)S(1)}, u32[]{:S(2)}, u32[]{:S(2)}) collective-permute-start(bf16[1024,128]{1,0:T(8,128)(2,1)S(1)} %get-tuple-element.26), channel_id=1, source_target_pairs={{0,2},{1,3},{2,0},{3,1},{4,6},{5,7},{6,4},{7,5},{8,10},{9,11},{10,... | collective-permute-start | bytes 786440 | tf_op jit(solution)/shard_map/ppermute | solution.py:393
  19.7 1.0 %collective-permute-done.3.refs_0_.refs_6_ = bf16[1024,128]{1,0:T(8,128)(2,1)S(1)} collective-permute-done((bf16[1024,128]{1,0:T(8,128)(2,1)S(1)}, bf16[1024,128]{1,0:T(8,128)(2,1)S(1)}, u32[]{:S(2)}, u32[]{:S(2)}) %collective-permute-start.3) | collective-permute-done | bytes 262176 | tf_op jit(solution)/shard_map/ppermute | solution.py:393
  20.7 0.1 join.1.refs_4_
  20.8 2.0 %collective-permute-start.5 = (bf16[1024,128]{1,0:T(8,128)(2,1)S(1)}, bf16[1024,128]{1,0:T(8,128)(2,1)S(1)}, u32[]{:S(2)}, u32[]{:S(2)}) collective-permute-start(bf16[1024,128]{1,0:T(8,128)(2,1)S(1)} %join.1.refs_4_), channel_id=1, source_target_pairs={{0,1},{1,0},{2,3},{3,2},{4,5},{5,4},{6,7},{7,6},{8,9},{9,8},{10,11... | collective-permute-start | bytes 786440 | tf_op jit(solution)/shard_map/ppermute | solution.py:393
  22.8 0.0 collective-permute-done.4.refs_5_.swapped_ref
  22.8 2.0 %collective-permute-done.2.refs_3_.refs_1_ = bf16[2048,128]{1,0:T(8,128)(2,1)S(1)} collective-permute-done((bf16[2048,128]{1,0:T(8,128)(2,1)S(1)}, bf16[2048,128]{1,0:T(8,128)(2,1)S(1)}, u32[]{:S(2)}, u32[]{:S(2)}) %collective-permute-start.2) | collective-permute-done | bytes 524320 | tf_op jit(solution)/shard_map/ppermute | solution.py:393
  24.8 5.6 %far.1 = (bf16[2,512,2048]{2,1,0:T(8,128)(2,1)S(1)}, bf16[1024,128]{1,0:T(8,128)(2,1)S(1)}, bf16[1024,128]{1,0:T(8,128)(2,1)S(1)}) custom-call(s32[32]{0:T(128)S(1)} %copy-done.2, bf16[4096,128]{1,0:T(8,128)(2,1)S(1)} %bitcast.10, bf16[4096,128]{1,0:T(8,128)(2,1)S(1)} %bitcast.6, f32[8,4096]{1,0:T(8,128)S(1)} %get-tuple-element.20.refs_2_, ...), custom_call_target="tpu_custom_call" | custom-call | flops 10737418240 | bytes 8388608 | tf_op jit(solution)/shard_map/far/pallas_call | solution.py:373
  30.4 2.5 %collective-permute-start.6 = (bf16[1024,128]{1,0:T(8,128)(2,1)S(1)}, bf16[1024,128]{1,0:T(8,128)(2,1)S(1)}, u32[]{:S(2)}, u32[]{:S(2)}) collective-permute-start(bf16[1024,128]{1,0:T(8,128)(2,1)S(1)} %get-tuple-element.27.refs_7_), channel_id=1, source_target_pairs={{0,28},{1,29},{2,30},{3,31},{4,0},{5,1},{6,2},{7,3},{8,4},{9,5},{1... | collective-permute-start | bytes 786440 | tf_op jit(solution)/shard_map/ppermute | solution.py:393
  32.8 0.4 collective-permute-start.7
  33.3 3.3 %last.1 = (bf16[1024,4096]{1,0:T(8,128)(2,1)S(1)}, f32[1024,128]{1,0:T(8,128)S(1)}, f32[1024,128]{1,0:T(8,128)S(1)}, f32[1024,128]{1,0:T(8,128)S(1)}) custom-call(s32[32]{0:T(128)S(1)} %copy-done.2, bf16[4096,128]{1,0:T(8,128)(2,1)S(1)} %bitcast.11, bf16[4096,128]{1,0:T(8,128)(2,1)S(1)} %bitcast.7, ...), custom_call_target="tpu_custom_call", output_to_operand_aliasing={{0}: (5, {}), {1}: (6, {}), {2}: (7, {})} | custom-call | flops 8724152320 | bytes 6815744 | tf_op jit(solution)/shard_map/last/pallas_call | solution.py:373
  36.5 5.2 %queries.1 = bf16[4096,128]{1,0:T(8,128)(2,1)} custom-call(s32[32]{0:T(128)S(1)} %copy-done.2, bf16[2048,128]{1,0:T(8,128)(2,1)S(1)} %get-tuple-element.19.refs_3_.both_ref, bf16[1024,4096]{1,0:T(8,128)(2,1)S(1)} %get-tuple-element.28.own_ref, bf16[1024,128]{1,0:T(8,128)(2,1)S(1)} %collective-permute-done.key_ref.refs_3_.refs_0_, ...), custom_call_target="tpu_custom_call" | custom-call | flops 6710886400 | bytes 5242880 | tf_op jit(solution)/shard_map/queries/pallas_call | solution.py:373
  41.7 0.0 collective-permute-done.5.refs_0_
  41.7 0.7 %collective-permute-done.6.refs_1_ = bf16[1024,128]{1,0:T(8,128)(2,1)S(1)} collective-permute-done((bf16[1024,128]{1,0:T(8,128)(2,1)S(1)}, bf16[1024,128]{1,0:T(8,128)(2,1)S(1)}, u32[]{:S(2)}, u32[]{:S(2)}) %collective-permute-start.6) | collective-permute-done | bytes 262176 | tf_op jit(solution)/shard_map/ppermute | solution.py:393
  42.4 1.9 %collective-permute-done.7.refs_2_ = bf16[1024,128]{1,0:T(8,128)(2,1)S(1)} collective-permute-done((bf16[1024,128]{1,0:T(8,128)(2,1)S(1)}, bf16[1024,128]{1,0:T(8,128)(2,1)S(1)}, u32[]{:S(2)}, u32[]{:S(2)}) %collective-permute-start.7) | collective-permute-done | bytes 262176 | tf_op jit(solution)/shard_map/ppermute | solution.py:393
  44.3 0.8 %total.1 = (bf16[512,128]{1,0:T(8,128)(2,1)}, bf16[512,128]{1,0:T(8,128)(2,1)}) custom-call(f32[1024,128]{1,0:T(8,128)S(1)} %get-tuple-element.31.total_ref, bf16[1024,128]{1,0:T(8,128)(2,1)S(1)} %collective-permute-done.4.refs_5_.swapped_ref, bf16[1024,128]{1,0:T(8,128)(2,1)S(1)} %collective-permute-done.5.refs_0_, ...), custom_call_target="tpu_custom_call" | custom-call | flops 13421772 | bytes 10485 | tf_op jit(solution)/shard_map/total/pallas_call | solution.py:373
  (1 shorter events, 0.0 us)
Async XLA Ops:
  0.6 9.8 %collective-permute-start = (bf16[1024,128]{1,0:T(8,128)(2,1)}, bf16[1024,128]{1,0:T(8,128)(2,1)S(1)}, u32[]{:S(2)}, u32[]{:S(2)}) collective-permute-start(bf16[1024,128]{1,0:T(8,128)(2,1)} %refs_4_.1), channel_id=1, source_target_pairs={{0,2},{1,3},{2,4},{3,5},{4,6},{5,7},{6,8},{7,9},{8,10},{9,11},{10,... | collective-permute-start | bytes 786440 | tf_op jit(solution)/shard_map/ppermute | solution.py:393
  1.1 12.1 %collective-permute-start.1 = (bf16[1024,128]{1,0:T(8,128)(2,1)}, bf16[1024,128]{1,0:T(8,128)(2,1)S(1)}, u32[]{:S(2)}, u32[]{:S(2)}) collective-permute-start(bf16[1024,128]{1,0:T(8,128)(2,1)} %refs_5_.1), channel_id=1, source_target_pairs={{0,2},{1,3},{2,4},{3,5},{4,6},{5,7},{6,8},{7,9},{8,10},{9,11},{10,... | collective-permute-start | bytes 786440 | tf_op jit(solution)/shard_map/ppermute | solution.py:393
  3.8 9.7 %copy-start = (bf16[1024,4,128]{2,1,0:T(4,128)(2,1)S(1)}, bf16[1024,4,128]{2,1,0:T(4,128)(2,1)}, u32[]{:S(2)}) copy-start(bf16[1024,4,128]{2,1,0:T(4,128)(2,1)} %param.11) | copy-start | bytes 3145732
  3.8 9.7 %copy-start.1 = (bf16[1024,4,128]{2,1,0:T(4,128)(2,1)S(1)}, bf16[1024,4,128]{2,1,0:T(4,128)(2,1)}, u32[]{:S(2)}) copy-start(bf16[1024,4,128]{2,1,0:T(4,128)(2,1)} %param.7) | copy-start | bytes 3145732
  3.8 9.7 %copy-start.2 = (s32[32]{0:T(128)S(1)}, s32[32]{0:T(128)}, u32[]{:S(2)}) copy-start(s32[32]{0:T(128)} %span_ids.7) | copy-start | bytes 388
  13.2 11.5 %collective-permute-start.2 = (bf16[2048,128]{1,0:T(8,128)(2,1)S(1)}, bf16[2048,128]{1,0:T(8,128)(2,1)S(1)}, u32[]{:S(2)}, u32[]{:S(2)}) collective-permute-start(bf16[2048,128]{1,0:T(8,128)(2,1)S(1)} %pack.1.refs_7_), channel_id=1, source_target_pairs={{0,2},{1,3},{2,4},{3,5},{4,6},{5,7},{6,8},{7,9},{8,10},{9,11},{10,... | collective-permute-start | bytes 1572872 | tf_op jit(solution)/shard_map/ppermute | solution.py:393
  19.1 1.6 %collective-permute-start.3 = (bf16[1024,128]{1,0:T(8,128)(2,1)S(1)}, bf16[1024,128]{1,0:T(8,128)(2,1)S(1)}, u32[]{:S(2)}, u32[]{:S(2)}) collective-permute-start(bf16[1024,128]{1,0:T(8,128)(2,1)S(1)} %get-tuple-element.24), channel_id=1, source_target_pairs={{0,2},{1,3},{2,0},{3,1},{4,6},{5,7},{6,4},{7,5},{8,10},{9,11},{10,... | collective-permute-start | bytes 786440 | tf_op jit(solution)/shard_map/ppermute | solution.py:393
  19.2 3.6 %collective-permute-start.4 = (bf16[1024,128]{1,0:T(8,128)(2,1)S(1)}, bf16[1024,128]{1,0:T(8,128)(2,1)S(1)}, u32[]{:S(2)}, u32[]{:S(2)}) collective-permute-start(bf16[1024,128]{1,0:T(8,128)(2,1)S(1)} %get-tuple-element.26), channel_id=1, source_target_pairs={{0,2},{1,3},{2,0},{3,1},{4,6},{5,7},{6,4},{7,5},{8,10},{9,11},{10,... | collective-permute-start | bytes 786440 | tf_op jit(solution)/shard_map/ppermute | solution.py:393
  20.8 21.0 %collective-permute-start.5 = (bf16[1024,128]{1,0:T(8,128)(2,1)S(1)}, bf16[1024,128]{1,0:T(8,128)(2,1)S(1)}, u32[]{:S(2)}, u32[]{:S(2)}) collective-permute-start(bf16[1024,128]{1,0:T(8,128)(2,1)S(1)} %join.1.refs_4_), channel_id=1, source_target_pairs={{0,1},{1,0},{2,3},{3,2},{4,5},{5,4},{6,7},{7,6},{8,9},{9,8},{10,11... | collective-permute-start | bytes 786440 | tf_op jit(solution)/shard_map/ppermute | solution.py:393
  30.4 12.0 %collective-permute-start.6 = (bf16[1024,128]{1,0:T(8,128)(2,1)S(1)}, bf16[1024,128]{1,0:T(8,128)(2,1)S(1)}, u32[]{:S(2)}, u32[]{:S(2)}) collective-permute-start(bf16[1024,128]{1,0:T(8,128)(2,1)S(1)} %get-tuple-element.27.refs_7_), channel_id=1, source_target_pairs={{0,28},{1,29},{2,30},{3,31},{4,0},{5,1},{6,2},{7,3},{8,4},{9,5},{1... | collective-permute-start | bytes 786440 | tf_op jit(solution)/shard_map/ppermute | solution.py:393
  32.8 11.4 %collective-permute-start.7 = (bf16[1024,128]{1,0:T(8,128)(2,1)S(1)}, bf16[1024,128]{1,0:T(8,128)(2,1)S(1)}, u32[]{:S(2)}, u32[]{:S(2)}) collective-permute-start(bf16[1024,128]{1,0:T(8,128)(2,1)S(1)} %get-tuple-element.32), channel_id=1, source_target_pairs={{0,29},{1,28},{2,31},{3,30},{4,1},{5,0},{6,3},{7,2},{8,5},{9,4},{1... | collective-permute-start | bytes 786440 | tf_op jit(solution)/shard_map/ppermute | solution.py:393

commit v11 on v10

--- a/solution.py
+++ b/solution.py
@@ -104,13 +104,13 @@
         now = ahead
         if index + 1 < len(tiles):
             ahead = start(*tiles[index + 1])
-        row, _, length, kept, probs, place = block
+        row, key, length, kept, probs = block
         prob, dscore = closed(group, scale, pl.multiple_of(row + p * tile, tile), None, *now)
         probs[:, p * tile : (p + 1) * tile] = prob
         kept[:, p * tile : (p + 1) * tile] = dscore
         if p == count - 1:
-            value_acc[pl.ds(place, length), :] += dot(probs[...], grad_ref[pl.ds(row, rows), :], NN)
-            key_acc[pl.ds(place, length), :] += dot(kept[...], query_ref[pl.ds(row, rows), :], NN)
+            value_acc[pl.ds(key, length), :] += dot(probs[...], grad_ref[pl.ds(row, rows), :], NN)
+            key_acc[pl.ds(key, length), :] += dot(kept[...], query_ref[pl.ds(row, rows), :], NN)
 
 
 def span_pair(span_ids, holder):
@@ -164,7 +164,7 @@
         key = pl.multiple_of(low * half, half)
         row = pl.multiple_of((1 - low) * span_rows, span_rows)
         kept = kept_ref.at[pl.ds(key, half), pl.ds(row, span_rows)]
-        block_grads(group, accs, scale, span_rows, [(row, key, half, kept, probs_ref, key)])
+        block_grads(group, accs, scale, span_rows, [(row, key, half, kept, probs_ref)])
 
     return low, corner, square
 
@@ -237,7 +237,7 @@
     outs, own_outs, (key_acc, value_acc, probs_ref) = refs[9 : 9 + parts], refs[9 + parts : -3], refs[-3:]
     put_shares(own_outs, own_keys, own_values, scale, 1)
     group = (query_ref, grad_ref, key_ref, value_ref, terms_ref, tile)
-    far_work(group, (key_acc, value_acc), scale, span_ids, kept_ref, probs_ref, heads, 1, 0, 1)
+    far_work(group, (key_acc, value_acc), scale, span_ids, kept_ref, probs_ref, heads, 1)
     put_shares(outs, key_acc, value_acc, scale)
 
 
@@ -247,40 +247,46 @@
     out_ref[toks : 2 * toks, :] = value_ref[...]
 
 
-def far_kernel(heads, tile, scale, piece, pieces, span_ids, *refs):
-    query_ref, grad_ref, terms_ref, both_ref, _ = refs[:5]
-    parts = (len(refs) - 9) // 2
-    swapped, kept_ref = refs[5 : 5 + parts], refs[5 + parts]
-    outs, (key_acc, value_acc, probs_ref) = refs[6 + parts : -3], refs[-3:]
+def far_kernel(heads, tile, scale, span_ids, *refs):
+    query_ref, grad_ref, terms_ref, over_ref, beside_ref, _ = refs[:6]
+    parts = (len(refs) - 11) // 2
+    swapped, both_ref, kept_ref = refs[6 : 6 + parts], refs[6 + parts], refs[7 + parts]
+    outs, (key_acc, value_acc, probs_ref) = refs[8 + parts : -3], refs[-3:]
     toks = both_ref.shape[0] // 2
+    is_odd = lax.rem(lax.axis_index("ctx"), 2) == 1
+
+    @pl.when(is_odd)
+    def _():
+        both_ref[...] = beside_ref[...]
+
+    @pl.when(jnp.logical_not(is_odd))
+    def _():
+        both_ref[...] = over_ref[...]
+
     key_ref, value_ref = both_ref.at[pl.ds(0, toks)], both_ref.at[pl.ds(toks, toks)]
     group = (query_ref, grad_ref, key_ref, value_ref, terms_ref, tile)
-    far_work(
-        group, (key_acc, value_acc), scale, span_ids, kept_ref, probs_ref, heads, 2, piece, pieces
-    )
-    odd = lax.rem(lax.axis_index("ctx"), 2).astype(jnp.float32)
+    far_work(group, (key_acc, value_acc), scale, span_ids, kept_ref, probs_ref, heads, 2)
+    odd = is_odd.astype(jnp.float32)
 
     def more(away, low, share):
-        start = low * pieces + piece * share
-        return swapped[away][start : start + share, :].astype(jnp.float32) * odd
+        return swapped[away][low : low + share, :].astype(jnp.float32) * odd
 
     put_shares(outs, key_acc, value_acc, scale, more=more)
 
 
-def far_work(group, accs, scale, span_ids, kept_ref, probs_ref, heads, step, piece, pieces):
+def far_work(group, accs, scale, span_ids, kept_ref, probs_ref, heads, step):
     key_acc, value_acc = accs
     key_acc[...] = jnp.zeros_like(key_acc)
     value_acc[...] = jnp.zeros_like(value_acc)
     half = group[2].shape[0] // 2
-    rows, length = half * heads, half // pieces
+    rows = half * heads
     halves = far_halves(span_ids, step)
     blocks = []
     for item in range(2):
         row_half, key_half = halves(item)
         row = pl.multiple_of(row_half * rows, rows)
-        key = pl.multiple_of(key_half * half + piece * length, length)
-        place = pl.multiple_of(key_half * length, length)
-        blocks.append((row, key, length, kept_ref.at[item], probs_ref.at[item], place))
+        key = pl.multiple_of(key_half * half, half)
+        blocks.append((row, key, half, kept_ref.at[item], probs_ref.at[item]))
     block_grads(group, accs, scale, rows, blocks)
 
 
@@ -292,27 +298,19 @@
         out[...] = (this[...].astype(jnp.float32) + more).astype(out.dtype)
 
 
-def total_kernel(pieces, total_ref, swapped_ref, *refs):
+def total_kernel(total_ref, swapped_ref, *refs):
     ins, (key_out, value_out) = refs[:-2], refs[-2:]
     share = key_out.shape[0]
     even = 1.0 - lax.rem(lax.axis_index("ctx"), 2).astype(jnp.float32)
-    length = share // pieces
-    whole = [ref for ref in ins if ref.shape[0] == 2 * share]
-    cut = [ref for ref in ins if ref.shape[0] != 2 * share]
-    for which, out in enumerate((key_out, value_out)):
-        for piece in range(pieces):
-            here = piece * length
-            low = which * share + here
-            part = total_ref[low : low + length, :]
-            part = part + swapped_ref[low : low + length, :].astype(jnp.float32) * even
-            for ref in whole:
-                part = part + ref[low : low + length, :].astype(jnp.float32)
-            for ref in cut[piece * len(cut) // pieces : (piece + 1) * len(cut) // pieces]:
-                part = part + ref[which * length : (which + 1) * length, :].astype(jnp.float32)
-            out[here : here + length, :] = part.astype(out.dtype)
-
-
-def query_kernel(heads, tile, scale, pieces, span_ids, both_ref, own_ref, *refs):
+    for low, out in ((0, key_out), (share, value_out)):
+        part = total_ref[low : low + share, :]
+        part = part + swapped_ref[low : low + share, :].astype(jnp.float32) * even
+        for ref in ins:
+            part = part + ref[low : low + share, :].astype(jnp.float32)
+        out[...] = part.astype(out.dtype)
+
+
+def query_kernel(heads, tile, scale, span_ids, both_ref, own_ref, *refs):
     (key_1, both_2), kept_refs, (out_ref, acc, turned) = refs[:2], refs[2:-3], refs[-3:]
     toks = both_ref.shape[0] // 2
     half = toks // 2
@@ -340,25 +338,23 @@
         acc[:, pl.ds(row, tile)] += dot(
             turned[0, :, pl.ds(key, half)], own_ref[pl.ds(key, half), pl.ds(row, tile)], NN
         )
-    for index, kept_ref in enumerate(kept_refs):
-        step, piece = (1, 0) if index == 0 else (2, index - 1)
-        length = kept_ref.shape[1]
+    for step, kept_ref in enumerate(kept_refs, 1):
         halves = far_halves(span_ids, step)
 
         @pl.loop(0, 2)
         def _(item):
             row_half, key_half = halves(item)
-            key = pl.multiple_of(key_half * half + piece * length, length)
+            key = pl.multiple_of(key_half * half, half)
             for p in range(rows // tile):
                 row = pl.multiple_of(row_half * rows + p * tile, tile)
                 acc[:, pl.ds(row, tile)] += dot(
-                    turned[step, :, pl.ds(key, length)],
+                    turned[step, :, pl.ds(key, half)],
                     kept_ref[item, :, p * tile : (p + 1) * tile],
                     NN,
                 )
 
     for row in range(0, 2 * rows, tile):
-        out_ref[row : row + tile, :] = (acc[:, row : row + tile] * scale).T.astype(out_ref.dtype)
+        out_ref[row : row + tile, :] = (acc[:, row : row + tile] * scale).astype(out_ref.dtype).T
 
 
 VMEM = pl.BlockSpec(memory_space=pltpu.VMEM)
@@ -429,7 +425,7 @@
     (both_1,) = call(
         pack_kernel, (key_1, value_1), [VMEM] * 2, [shape((2 * toks, dim), bf16)], [], 0.01, 4, "pack"
     )
-    both_2 = moved(both_1, (-1, -1), 0)
+    over, beside = moved(both, (-2, 0), 0), moved(both_1, (-1, 1), 0)
 
     block = (toks // 2, rows // 2)
     kept_1, *sent = call(
@@ -454,26 +450,20 @@
         "join",
     )
     whole = [moved(part, (0, 0), away) for away, part in enumerate(sent, 1)]
-    pieces = 1
-    small = (2, toks // 2 // pieces, rows // 2)
-    kept_2, cut, last = [], [], sent[0]
-    for piece in range(pieces):
-        kept_piece, *sent = call(
-            functools.partial(far_kernel, heads, tile, scale, piece, pieces),
-            (span_ids, q, g, terms, both_2, last, *swapped),
-            [SMEM] + [VMEM] * 4 + [ANY] + [VMEM] * parts,
-            [shape(small, bf16)] + [shape((share // pieces, dim), bf16)] * parts,
-            [pltpu.VMEM((toks // pieces, dim), f32)] * 2 + [pltpu.VMEM(small, bf16)],
-            2 * heads / pieces,
-            18,
-            "far",
-        )
-        kept_2.append(kept_piece)
-        cut += [moved(part, (2, 2), away) for away, part in enumerate(sent)]
-        last = sent[0]
+    both_2, kept_2, *sent = call(
+        functools.partial(far_kernel, heads, tile, scale),
+        (span_ids, q, g, terms, over, beside, sent[0], *swapped),
+        [SMEM] + [VMEM] * 5 + [ANY] + [VMEM] * parts,
+        [shape((2 * toks, dim), bf16), shape((2,) + block, bf16)] + grads,
+        accs + [pltpu.VMEM((2,) + block, bf16)],
+        2 * heads,
+        18,
+        "far",
+    )
+    landed = whole + [moved(part, (2, 2), away) for away, part in enumerate(sent)]
     kept, _, _, total = call(
         functools.partial(last_kernel, heads, tile, scale, parts),
-        (span_ids, q, g, terms, both, kept, key_sum, value_sum, last),
+        (span_ids, q, g, terms, both, kept, key_sum, value_sum, sent[0]),
         [SMEM] + [VMEM] * 7 + [ANY],
         sums + [shape((share, dim), f32)],
         [probs],
@@ -483,9 +473,9 @@
         {5: 0, 6: 1, 7: 2},
     )
     (query_grad,) = call(
-        functools.partial(query_kernel, heads, tile, scale, pieces),
-        (span_ids, both, kept, key_1, both_2, kept_1, *kept_2),
-        [SMEM] + [VMEM] * (5 + pieces),
+        functools.partial(query_kernel, heads, tile, scale),
+        (span_ids, both, kept, key_1, both_2, kept_1, kept_2),
+        [SMEM] + [VMEM] * 6,
         [shape((rows, dim), bf16)],
         [pltpu.VMEM((dim, rows), f32), pltpu.VMEM((STEPS, dim, toks), bf16)],
         1.25 * heads,
@@ -493,9 +483,9 @@
         "queries",
     )
     key_grad, value_grad = call(
-        functools.partial(total_kernel, pieces),
-        (total, swapped[0], *whole, *cut),
-        [VMEM] * (2 + len(whole) + len(cut)),
+        total_kernel,
+        (total, swapped[0], *landed),
+        [VMEM] * (2 + len(landed)),
         [shape((share // 2, dim), bf16)] * 2,
         [],
         0.01,

time: 45.3 us -> 45.2 us (level)
  waiting for transfers between devices: 8.88 us -> 3.01 us
  starting transfers between devices: 8.84 us -> 14.1 us
    ppermute x8 -> x9, waiting for transfers between devices: 8.88 us -> 3.01 us  [moved(): return lax.ppermute(block, ('ctx', 'head'), route)]
    ppermute x8 -> x9, starting transfers between devices: 8.84 us -> 14.1 us  [moved(): return lax.ppermute(block, ('ctx', 'head'), route)]
  transfers between devices with their start and end apart: 8 -> 9, of which waited for: 6 -> 3; matrix products, arithmetic and copies ran while one was open for 0% -> 0% of each run, Pallas kernels for 57% -> 58%
where the time goes in v11:
time: 45.2 us; the launch traced here: 44.6 us
  Pallas kernels  26.7 us (59%)
  starting transfers between devices  14.1 us (31%)
  waiting for transfers between devices  3.01 us (7%)
  between operations  0.74 us (2%)
    pallas_call x8, Pallas kernels, call(): pl.pallas_call(kernel, out_shape=outs, in_specs=where, out_specs=[VMEM] *...  26.7 us
    ppermute x9, starting transfers between devices, moved(): return lax.ppermute(block, ('ctx', 'head'), route)  14.1 us
    ppermute x9, waiting for transfers between devices, moved(): return lax.ppermute(block, ('ctx', 'head'), route)  3.01 us
  transfers between devices with their start and end apart: 9, of which 3 were waited for; matrix products, arithmetic and copies ran while one was open for 0% of the time, Pallas kernels for 58%

profile of v11, /device:TPU:0, one launch (start us, length us, event | category | flops | bytes accessed | tf_op | source)
XLA Modules:
  0.0 44.6 jit_solution(13810587125174640224)
XLA Ops:
  0.6 0.5 %collective-permute-start.1 = (bf16[1024,128]{1,0:T(8,128)(2,1)}, bf16[1024,128]{1,0:T(8,128)(2,1)S(1)}, u32[]{:S(2)}, u32[]{:S(2)}) collective-permute-start(bf16[1024,128]{1,0:T(8,128)(2,1)} %refs_4_.1), channel_id=1, source_target_pairs={{0,2},{1,3},{2,4},{3,5},{4,6},{5,7},{6,8},{7,9},{8,10},{9,11},{10,... | collective-permute-start | bytes 786440 | tf_op jit(solution)/shard_map/ppermute | solution.py:389
  1.1 2.6 %collective-permute-start.2 = (bf16[1024,128]{1,0:T(8,128)(2,1)}, bf16[1024,128]{1,0:T(8,128)(2,1)S(1)}, u32[]{:S(2)}, u32[]{:S(2)}) collective-permute-start(bf16[1024,128]{1,0:T(8,128)(2,1)} %refs_5_.1), channel_id=1, source_target_pairs={{0,2},{1,3},{2,4},{3,5},{4,6},{5,7},{6,8},{7,9},{8,10},{9,11},{10,... | collective-permute-start | bytes 786440 | tf_op jit(solution)/shard_map/ppermute | solution.py:389
  3.8 0.0 copy-start
  3.8 0.0 copy-start.1
  3.8 0.0 copy-start.2
  3.8 6.1 %first.1 = (f32[8,4096]{1,0:T(8,128)S(1)}, bf16[2048,128]{1,0:T(8,128)(2,1)S(1)}, bf16[1024,4096]{1,0:T(8,128)(2,1)S(1)}, f32[1024,128]{1,0:T(8,128)S(1)}, f32[1024,128]{1,0:T(8,128)S(1)}) custom-call(bf16[4096,128]{1,0:T(8,128)(2,1)} %bitcast.4, bf16[4096,128]{1,0:T(8,128)(2,1)} %bitcast.12, bf16[4096,128]{1,0:T(8,128)(2,1)} %bitcast.8, f32[4,1024]{1,0:T(4,128)} %refs_3_.1, ...), custom_call_target="tpu_custom_call" | custom-call | flops 8724152320 | bytes 6815744 | tf_op jit(solution)/shard_map/first/pallas_call | solution.py:369
  9.9 3.6 %collective-permute-start = (bf16[2048,128]{1,0:T(8,128)(2,1)S(1)}, bf16[2048,128]{1,0:T(8,128)(2,1)S(1)}, u32[]{:S(2)}, u32[]{:S(2)}) collective-permute-start(bf16[2048,128]{1,0:T(8,128)(2,1)S(1)} %get-tuple-element.20.refs_3_.both_ref), channel_id=1, source_target_pairs={{0,4},{1,5},{2,2},{3,3},{4,8},{5,9},{6,6},{7,7},{8,12},{9,13},{10,... | collective-permute-start | bytes 1572872 | tf_op jit(solution)/shard_map/ppermute | solution.py:389
  13.5 0.0 collective-permute-done.1.key_ref.refs_3_.refs_0_
  13.5 0.0 collective-permute-done.2.value_ref.refs_4_
  13.6 0.1 collective-permute-start.3
  13.6 0.0 copy-done
  13.6 0.0 copy-done.1
  13.7 0.0 copy-done.2
  13.7 5.6 %near.1 = (bf16[2,512,2048]{2,1,0:T(8,128)(2,1)S(1)}, bf16[1024,128]{1,0:T(8,128)(2,1)S(1)}, bf16[1024,128]{1,0:T(8,128)(2,1)S(1)}, bf16[1024,128]{1,0:T(8,128)(2,1)S(1)}) custom-call(s32[32]{0:T(128)S(1)} %copy-done.2, bf16[4096,128]{1,0:T(8,128)(2,1)S(1)} %bitcast.9, bf16[4096,128]{1,0:T(8,128)(2,1)S(1)} %bitcast.5, ...), custom_call_target="tpu_custom_call" | custom-call | flops 10737418240 | bytes 8388608 | tf_op jit(solution)/shard_map/near/pallas_call | solution.py:369
  19.2 0.5 %collective-permute-start.4 = (bf16[1024,128]{1,0:T(8,128)(2,1)S(1)}, bf16[1024,128]{1,0:T(8,128)(2,1)S(1)}, u32[]{:S(2)}, u32[]{:S(2)}) collective-permute-start(bf16[1024,128]{1,0:T(8,128)(2,1)S(1)} %get-tuple-element.25), channel_id=1, source_target_pairs={{0,2},{1,3},{2,0},{3,1},{4,6},{5,7},{6,4},{7,5},{8,10},{9,11},{10,... | collective-permute-start | bytes 786440 | tf_op jit(solution)/shard_map/ppermute | solution.py:389
  19.8 0.1 collective-permute-start.5
  19.8 1.1 %collective-permute-done.4.refs_0_.refs_7_ = bf16[1024,128]{1,0:T(8,128)(2,1)S(1)} collective-permute-done((bf16[1024,128]{1,0:T(8,128)(2,1)S(1)}, bf16[1024,128]{1,0:T(8,128)(2,1)S(1)}, u32[]{:S(2)}, u32[]{:S(2)}) %collective-permute-start.4) | collective-permute-done | bytes 262176 | tf_op jit(solution)/shard_map/ppermute | solution.py:389
  20.9 0.1 join.1.refs_5_
  21.0 2.4 %collective-permute-start.6 = (bf16[1024,128]{1,0:T(8,128)(2,1)S(1)}, bf16[1024,128]{1,0:T(8,128)(2,1)S(1)}, u32[]{:S(2)}, u32[]{:S(2)}) collective-permute-start(bf16[1024,128]{1,0:T(8,128)(2,1)S(1)} %join.1.refs_5_), channel_id=1, source_target_pairs={{0,1},{1,0},{2,3},{3,2},{4,5},{5,4},{6,7},{7,6},{8,9},{9,8},{10,11... | collective-permute-start | bytes 786440 | tf_op jit(solution)/shard_map/ppermute | solution.py:389
  23.4 0.0 collective-permute-done.5.refs_6_.swapped_ref
  23.4 0.2 collective-permute-done.refs_3_
  23.6 0.0 collective-permute-done.3.refs_4_
  23.7 5.6 %far.1 = (bf16[2048,128]{1,0:T(8,128)(2,1)S(1)}, bf16[2,512,2048]{2,1,0:T(8,128)(2,1)S(1)}, bf16[1024,128]{1,0:T(8,128)(2,1)S(1)}, bf16[1024,128]{1,0:T(8,128)(2,1)S(1)}) custom-call(s32[32]{0:T(128)S(1)} %copy-done.2, bf16[4096,128]{1,0:T(8,128)(2,1)S(1)} %bitcast.10, bf16[4096,128]{1,0:T(8,128)(2,1)S(1)} %bitcast.6, ...), custom_call_target="tpu_custom_call" | custom-call | flops 10737418240 | bytes 8388608 | tf_op jit(solution)/shard_map/far/pallas_call | solution.py:369
  29.3 3.0 %collective-permute-start.7 = (bf16[1024,128]{1,0:T(8,128)(2,1)S(1)}, bf16[1024,128]{1,0:T(8,128)(2,1)S(1)}, u32[]{:S(2)}, u32[]{:S(2)}) collective-permute-start(bf16[1024,128]{1,0:T(8,128)(2,1)S(1)} %get-tuple-element.28.refs_7_), channel_id=1, source_target_pairs={{0,28},{1,29},{2,30},{3,31},{4,0},{5,1},{6,2},{7,3},{8,4},{9,5},{1... | collective-permute-start | bytes 786440 | tf_op jit(solution)/shard_map/ppermute | solution.py:389
  32.3 3.3 %last.1 = (bf16[1024,4096]{1,0:T(8,128)(2,1)S(1)}, f32[1024,128]{1,0:T(8,128)S(1)}, f32[1024,128]{1,0:T(8,128)S(1)}, f32[1024,128]{1,0:T(8,128)S(1)}) custom-call(s32[32]{0:T(128)S(1)} %copy-done.2, bf16[4096,128]{1,0:T(8,128)(2,1)S(1)} %bitcast.11, bf16[4096,128]{1,0:T(8,128)(2,1)S(1)} %bitcast.7, ...), custom_call_target="tpu_custom_call", output_to_operand_aliasing={{0}: (5, {}), {1}: (6, {}), {2}: (7, {})} | custom-call | flops 8724152320 | bytes 6815744 | tf_op jit(solution)/shard_map/last/pallas_call | solution.py:369
  35.6 1.3 %collective-permute-start.8 = (bf16[1024,128]{1,0:T(8,128)(2,1)S(1)}, bf16[1024,128]{1,0:T(8,128)(2,1)S(1)}, u32[]{:S(2)}, u32[]{:S(2)}) collective-permute-start(bf16[1024,128]{1,0:T(8,128)(2,1)S(1)} %get-tuple-element.34), channel_id=1, source_target_pairs={{0,29},{1,28},{2,31},{3,30},{4,1},{5,0},{6,3},{7,2},{8,5},{9,4},{1... | collective-permute-start | bytes 786440 | tf_op jit(solution)/shard_map/ppermute | solution.py:389
  36.9 5.2 %queries.1 = bf16[4096,128]{1,0:T(8,128)(2,1)} custom-call(s32[32]{0:T(128)S(1)} %copy-done.2, bf16[2048,128]{1,0:T(8,128)(2,1)S(1)} %get-tuple-element.20.refs_3_.both_ref, bf16[1024,4096]{1,0:T(8,128)(2,1)S(1)} %get-tuple-element.29.own_ref, bf16[1024,128]{1,0:T(8,128)(2,1)S(1)} %collective-permute-done.1.key_ref.refs_3_.refs_0_, ...), custom_call_target="tpu_custom_call" | custom-call | flops 6710886400 | bytes 5242880 | tf_op jit(solution)/shard_map/queries/pallas_call | solution.py:369
  42.1 0.0 collective-permute-done.6.refs_0_
  42.1 0.0 collective-permute-done.7.refs_1_
  42.1 1.7 %collective-permute-done.8.refs_2_ = bf16[1024,128]{1,0:T(8,128)(2,1)S(1)} collective-permute-done((bf16[1024,128]{1,0:T(8,128)(2,1)S(1)}, bf16[1024,128]{1,0:T(8,128)(2,1)S(1)}, u32[]{:S(2)}, u32[]{:S(2)}) %collective-permute-start.8) | collective-permute-done | bytes 262176 | tf_op jit(solution)/shard_map/ppermute | solution.py:389
  43.8 0.8 %total.1 = (bf16[512,128]{1,0:T(8,128)(2,1)}, bf16[512,128]{1,0:T(8,128)(2,1)}) custom-call(f32[1024,128]{1,0:T(8,128)S(1)} %get-tuple-element.33.total_ref, bf16[1024,128]{1,0:T(8,128)(2,1)S(1)} %collective-permute-done.5.refs_6_.swapped_ref, bf16[1024,128]{1,0:T(8,128)(2,1)S(1)} %collective-permute-done.6.refs_0_, ...), custom_call_target="tpu_custom_call" | custom-call | flops 13421772 | bytes 10485 | tf_op jit(solution)/shard_map/total/pallas_call | solution.py:369
  (1 shorter events, 0.0 us)
Async XLA Ops:
  0.6 12.9 %collective-permute-start.1 = (bf16[1024,128]{1,0:T(8,128)(2,1)}, bf16[1024,128]{1,0:T(8,128)(2,1)S(1)}, u32[]{:S(2)}, u32[]{:S(2)}) collective-permute-start(bf16[1024,128]{1,0:T(8,128)(2,1)} %refs_4_.1), channel_id=1, source_target_pairs={{0,2},{1,3},{2,4},{3,5},{4,6},{5,7},{6,8},{7,9},{8,10},{9,11},{10,... | collective-permute-start | bytes 786440 | tf_op jit(solution)/shard_map/ppermute | solution.py:389
  1.1 12.4 %collective-permute-start.2 = (bf16[1024,128]{1,0:T(8,128)(2,1)}, bf16[1024,128]{1,0:T(8,128)(2,1)S(1)}, u32[]{:S(2)}, u32[]{:S(2)}) collective-permute-start(bf16[1024,128]{1,0:T(8,128)(2,1)} %refs_5_.1), channel_id=1, source_target_pairs={{0,2},{1,3},{2,4},{3,5},{4,6},{5,7},{6,8},{7,9},{8,10},{9,11},{10,... | collective-permute-start | bytes 786440 | tf_op jit(solution)/shard_map/ppermute | solution.py:389
  3.8 9.9 %copy-start = (bf16[1024,4,128]{2,1,0:T(4,128)(2,1)S(1)}, bf16[1024,4,128]{2,1,0:T(4,128)(2,1)}, u32[]{:S(2)}) copy-start(bf16[1024,4,128]{2,1,0:T(4,128)(2,1)} %param.11) | copy-start | bytes 3145732
  3.8 9.9 %copy-start.1 = (bf16[1024,4,128]{2,1,0:T(4,128)(2,1)S(1)}, bf16[1024,4,128]{2,1,0:T(4,128)(2,1)}, u32[]{:S(2)}) copy-start(bf16[1024,4,128]{2,1,0:T(4,128)(2,1)} %param.7) | copy-start | bytes 3145732
  3.8 9.9 %copy-start.2 = (s32[32]{0:T(128)S(1)}, s32[32]{0:T(128)}, u32[]{:S(2)}) copy-start(s32[32]{0:T(128)} %span_ids.7) | copy-start | bytes 388
  9.9 13.8 %collective-permute-start = (bf16[2048,128]{1,0:T(8,128)(2,1)S(1)}, bf16[2048,128]{1,0:T(8,128)(2,1)S(1)}, u32[]{:S(2)}, u32[]{:S(2)}) collective-permute-start(bf16[2048,128]{1,0:T(8,128)(2,1)S(1)} %get-tuple-element.20.refs_3_.both_ref), channel_id=1, source_target_pairs={{0,4},{1,5},{2,2},{3,3},{4,8},{5,9},{6,6},{7,7},{8,12},{9,13},{10,... | collective-permute-start | bytes 1572872 | tf_op jit(solution)/shard_map/ppermute | solution.py:389
  13.6 10.1 %collective-permute-start.3 = (bf16[2048,128]{1,0:T(8,128)(2,1)S(1)}, bf16[2048,128]{1,0:T(8,128)(2,1)S(1)}, u32[]{:S(2)}, u32[]{:S(2)}) collective-permute-start(bf16[2048,128]{1,0:T(8,128)(2,1)S(1)} %pack.1.refs_7_), channel_id=1, source_target_pairs={{0,2},{1,3},{2,0},{3,1},{4,6},{5,7},{6,4},{7,5},{8,10},{9,11},{10,... | collective-permute-start | bytes 1572872 | tf_op jit(solution)/shard_map/ppermute | solution.py:389
  19.2 1.7 %collective-permute-start.4 = (bf16[1024,128]{1,0:T(8,128)(2,1)S(1)}, bf16[1024,128]{1,0:T(8,128)(2,1)S(1)}, u32[]{:S(2)}, u32[]{:S(2)}) collective-permute-start(bf16[1024,128]{1,0:T(8,128)(2,1)S(1)} %get-tuple-element.25), channel_id=1, source_target_pairs={{0,2},{1,3},{2,0},{3,1},{4,6},{5,7},{6,4},{7,5},{8,10},{9,11},{10,... | collective-permute-start | bytes 786440 | tf_op jit(solution)/shard_map/ppermute | solution.py:389
  19.8 3.6 %collective-permute-start.5 = (bf16[1024,128]{1,0:T(8,128)(2,1)S(1)}, bf16[1024,128]{1,0:T(8,128)(2,1)S(1)}, u32[]{:S(2)}, u32[]{:S(2)}) collective-permute-start(bf16[1024,128]{1,0:T(8,128)(2,1)S(1)} %get-tuple-element.27), channel_id=1, source_target_pairs={{0,2},{1,3},{2,0},{3,1},{4,6},{5,7},{6,4},{7,5},{8,10},{9,11},{10,... | collective-permute-start | bytes 786440 | tf_op jit(solution)/shard_map/ppermute | solution.py:389
  21.0 21.1 %collective-permute-start.6 = (bf16[1024,128]{1,0:T(8,128)(2,1)S(1)}, bf16[1024,128]{1,0:T(8,128)(2,1)S(1)}, u32[]{:S(2)}, u32[]{:S(2)}) collective-permute-start(bf16[1024,128]{1,0:T(8,128)(2,1)S(1)} %join.1.refs_5_), channel_id=1, source_target_pairs={{0,1},{1,0},{2,3},{3,2},{4,5},{5,4},{6,7},{7,6},{8,9},{9,8},{10,11... | collective-permute-start | bytes 786440 | tf_op jit(solution)/shard_map/ppermute | solution.py:389
  29.3 12.8 %collective-permute-start.7 = (bf16[1024,128]{1,0:T(8,128)(2,1)S(1)}, bf16[1024,128]{1,0:T(8,128)(2,1)S(1)}, u32[]{:S(2)}, u32[]{:S(2)}) collective-permute-start(bf16[1024,128]{1,0:T(8,128)(2,1)S(1)} %get-tuple-element.28.refs_7_), channel_id=1, source_target_pairs={{0,28},{1,29},{2,30},{3,31},{4,0},{5,1},{6,2},{7,3},{8,4},{9,5},{1... | collective-permute-start | bytes 786440 | tf_op jit(solution)/shard_map/ppermute | solution.py:389
  35.6 8.2 %collective-permute-start.8 = (bf16[1024,128]{1,0:T(8,128)(2,1)S(1)}, bf16[1024,128]{1,0:T(8,128)(2,1)S(1)}, u32[]{:S(2)}, u32[]{:S(2)}) collective-permute-start(bf16[1024,128]{1,0:T(8,128)(2,1)S(1)} %get-tuple-element.34), channel_id=1, source_target_pairs={{0,29},{1,28},{2,31},{3,30},{4,1},{5,0},{6,3},{7,2},{8,5},{9,4},{1... | collective-permute-start | bytes 786440 | tf_op jit(solution)/shard_map/ppermute | solution.py:389

commit v12 on v11

--- a/solution.py
+++ b/solution.py
@@ -241,8 +241,9 @@
     put_shares(outs, key_acc, value_acc, scale)
 
 
-def pack_kernel(key_ref, value_ref, out_ref):
+def pack_kernel(key_ref, value_ref, both_ref, out_ref, copy_ref):
     toks = key_ref.shape[0]
+    copy_ref[...] = both_ref[...]
     out_ref[0:toks, :] = key_ref[...]
     out_ref[toks : 2 * toks, :] = value_ref[...]
 
@@ -422,10 +423,11 @@
         20,
         "first",
     )
-    (both_1,) = call(
-        pack_kernel, (key_1, value_1), [VMEM] * 2, [shape((2 * toks, dim), bf16)], [], 0.01, 4, "pack"
-    )
-    over, beside = moved(both, (-2, 0), 0), moved(both_1, (-1, 1), 0)
+    packed = [shape((2 * toks, dim), bf16)] * 2
+    both_1, copied = call(
+        pack_kernel, (key_1, value_1, both), [VMEM] * 3, packed, [], 0.01, 4, "pack"
+    )
+    beside, over = moved(both_1, (-1, 1), 0), moved(copied, (-2, 0), 0)
 
     block = (toks // 2, rows // 2)
     kept_1, *sent = call(

time: 45.2 us -> 47.8 us (1.058); the launches traced: 44.6 us -> 48 us
  waiting for transfers between devices: 3.01 us -> 8.9 us
  starting transfers between devices: 14.1 us -> 11.6 us
    ppermute x9, waiting for transfers between devices: 3.01 us -> 8.9 us  [moved(): return lax.ppermute(block, ('ctx', 'head'), route)]
    ppermute x9, starting transfers between devices: 14.1 us -> 11.6 us  [moved(): return lax.ppermute(block, ('ctx', 'head'), route)]
  transfers between devices with their start and end apart: 9 -> 9, of which waited for: 3 -> 4; matrix products, arithmetic and copies ran while one was open for 0% -> 0% of each run, Pallas kernels for 58% -> 54%
where the time goes in v12:
time: 47.8 us; the launch traced here: 48 us
  Pallas kernels  26.8 us (56%)
  starting transfers between devices  11.6 us (24%)
  waiting for transfers between devices  8.9 us (19%)
  between operations  0.73 us (2%)
    pallas_call x8, Pallas kernels, call(): pl.pallas_call(kernel, out_shape=outs, in_specs=where, out_specs=[VMEM] *...  26.8 us
    ppermute x9, starting transfers between devices, moved(): return lax.ppermute(block, ('ctx', 'head'), route)  11.6 us
    ppermute x9, waiting for transfers between devices, moved(): return lax.ppermute(block, ('ctx', 'head'), route)  8.9 us
  transfers between devices with their start and end apart: 9, of which 4 were waited for; matrix products, arithmetic and copies ran while one was open for 0% of the time, Pallas kernels for 54%

profile of v12, /device:TPU:0, one launch (start us, length us, event | category | flops | bytes accessed | tf_op | source)
XLA Modules:
  0.0 48.0 jit_solution(146732487049326950)
XLA Ops:
  0.6 0.5 %collective-permute-start = (bf16[1024,128]{1,0:T(8,128)(2,1)}, bf16[1024,128]{1,0:T(8,128)(2,1)S(1)}, u32[]{:S(2)}, u32[]{:S(2)}) collective-permute-start(bf16[1024,128]{1,0:T(8,128)(2,1)} %refs_4_.1), channel_id=1, source_target_pairs={{0,2},{1,3},{2,4},{3,5},{4,6},{5,7},{6,8},{7,9},{8,10},{9,11},{10,... | collective-permute-start | bytes 786440 | tf_op jit(solution)/shard_map/ppermute | solution.py:390
  1.1 2.6 %collective-permute-start.1 = (bf16[1024,128]{1,0:T(8,128)(2,1)}, bf16[1024,128]{1,0:T(8,128)(2,1)S(1)}, u32[]{:S(2)}, u32[]{:S(2)}) collective-permute-start(bf16[1024,128]{1,0:T(8,128)(2,1)} %refs_5_.1), channel_id=1, source_target_pairs={{0,2},{1,3},{2,4},{3,5},{4,6},{5,7},{6,8},{7,9},{8,10},{9,11},{10,... | collective-permute-start | bytes 786440 | tf_op jit(solution)/shard_map/ppermute | solution.py:390
  3.8 0.0 copy-start
  3.8 0.0 copy-start.1
  3.8 0.0 copy-start.2
  3.8 6.9 %first.1 = (f32[8,4096]{1,0:T(8,128)S(1)}, bf16[2048,128]{1,0:T(8,128)(2,1)S(1)}, bf16[1024,4096]{1,0:T(8,128)(2,1)S(1)}, f32[1024,128]{1,0:T(8,128)S(1)}, f32[1024,128]{1,0:T(8,128)S(1)}) custom-call(bf16[4096,128]{1,0:T(8,128)(2,1)} %bitcast.4, bf16[4096,128]{1,0:T(8,128)(2,1)} %bitcast.12, bf16[4096,128]{1,0:T(8,128)(2,1)} %bitcast.8, f32[4,1024]{1,0:T(4,128)} %refs_3_.1, ...), custom_call_target="tpu_custom_call" | custom-call | flops 8724152320 | bytes 6815744 | tf_op jit(solution)/shard_map/first/pallas_call | solution.py:370
  10.7 0.0 collective-permute-done.key_ref.refs_3_.refs_0_
  10.7 2.5 %collective-permute-done.1.value_ref.refs_4_ = bf16[1024,128]{1,0:T(8,128)(2,1)S(1)} collective-permute-done((bf16[1024,128]{1,0:T(8,128)(2,1)}, bf16[1024,128]{1,0:T(8,128)(2,1)S(1)}, u32[]{:S(2)}, u32[]{:S(2)}) %collective-permute-start.1) | collective-permute-done | bytes 262176 | tf_op jit(solution)/shard_map/ppermute | solution.py:390
  13.2 0.1 pack.1
  13.3 0.1 collective-permute-start.3
  13.4 2.1 %collective-permute-start.2 = (bf16[2048,128]{1,0:T(8,128)(2,1)S(1)}, bf16[2048,128]{1,0:T(8,128)(2,1)S(1)}, u32[]{:S(2)}, u32[]{:S(2)}) collective-permute-start(bf16[2048,128]{1,0:T(8,128)(2,1)S(1)} %get-tuple-element.27), channel_id=1, source_target_pairs={{0,4},{1,5},{2,2},{3,3},{4,8},{5,9},{6,6},{7,7},{8,12},{9,13},{10,... | collective-permute-start | bytes 1572872 | tf_op jit(solution)/shard_map/ppermute | solution.py:390
  15.5 0.0 copy-done
  15.5 0.0 copy-done.1
  15.5 0.0 copy-done.2
  15.5 5.6 %near.1 = (bf16[2,512,2048]{2,1,0:T(8,128)(2,1)S(1)}, bf16[1024,128]{1,0:T(8,128)(2,1)S(1)}, bf16[1024,128]{1,0:T(8,128)(2,1)S(1)}, bf16[1024,128]{1,0:T(8,128)(2,1)S(1)}) custom-call(s32[32]{0:T(128)S(1)} %copy-done.2, bf16[4096,128]{1,0:T(8,128)(2,1)S(1)} %bitcast.9, bf16[4096,128]{1,0:T(8,128)(2,1)S(1)} %bitcast.5, ...), custom_call_target="tpu_custom_call" | custom-call | flops 10737418240 | bytes 8388608 | tf_op jit(solution)/shard_map/near/pallas_call | solution.py:370
  21.1 0.1 collective-permute-start.4
  21.2 0.5 %collective-permute-start.5 = (bf16[1024,128]{1,0:T(8,128)(2,1)S(1)}, bf16[1024,128]{1,0:T(8,128)(2,1)S(1)}, u32[]{:S(2)}, u32[]{:S(2)}) collective-permute-start(bf16[1024,128]{1,0:T(8,128)(2,1)S(1)} %get-tuple-element.31), channel_id=1, source_target_pairs={{0,2},{1,3},{2,0},{3,1},{4,6},{5,7},{6,4},{7,5},{8,10},{9,11},{10,... | collective-permute-start | bytes 786440 | tf_op jit(solution)/shard_map/ppermute | solution.py:390
  21.7 1.0 %collective-permute-done.4.refs_0_.refs_7_ = bf16[1024,128]{1,0:T(8,128)(2,1)S(1)} collective-permute-done((bf16[1024,128]{1,0:T(8,128)(2,1)S(1)}, bf16[1024,128]{1,0:T(8,128)(2,1)S(1)}, u32[]{:S(2)}, u32[]{:S(2)}) %collective-permute-start.4) | collective-permute-done | bytes 262176 | tf_op jit(solution)/shard_map/ppermute | solution.py:390
  22.7 0.1 join.1.refs_5_
  22.8 2.0 %collective-permute-start.6 = (bf16[1024,128]{1,0:T(8,128)(2,1)S(1)}, bf16[1024,128]{1,0:T(8,128)(2,1)S(1)}, u32[]{:S(2)}, u32[]{:S(2)}) collective-permute-start(bf16[1024,128]{1,0:T(8,128)(2,1)S(1)} %join.1.refs_5_), channel_id=1, source_target_pairs={{0,1},{1,0},{2,3},{3,2},{4,5},{5,4},{6,7},{7,6},{8,9},{9,8},{10,11... | collective-permute-start | bytes 786440 | tf_op jit(solution)/shard_map/ppermute | solution.py:390
  24.8 0.0 collective-permute-done.5.refs_6_.swapped_ref
  24.8 0.0 collective-permute-done.3.refs_4_
  24.8 2.4 %collective-permute-done.2.refs_3_ = bf16[2048,128]{1,0:T(8,128)(2,1)S(1)} collective-permute-done((bf16[2048,128]{1,0:T(8,128)(2,1)S(1)}, bf16[2048,128]{1,0:T(8,128)(2,1)S(1)}, u32[]{:S(2)}, u32[]{:S(2)}) %collective-permute-start.2) | collective-permute-done | bytes 524320 | tf_op jit(solution)/shard_map/ppermute | solution.py:390
  27.1 5.6 %far.1 = (bf16[2048,128]{1,0:T(8,128)(2,1)S(1)}, bf16[2,512,2048]{2,1,0:T(8,128)(2,1)S(1)}, bf16[1024,128]{1,0:T(8,128)(2,1)S(1)}, bf16[1024,128]{1,0:T(8,128)(2,1)S(1)}) custom-call(s32[32]{0:T(128)S(1)} %copy-done.2, bf16[4096,128]{1,0:T(8,128)(2,1)S(1)} %bitcast.10, bf16[4096,128]{1,0:T(8,128)(2,1)S(1)} %bitcast.6, ...), custom_call_target="tpu_custom_call" | custom-call | flops 10737418240 | bytes 8388608 | tf_op jit(solution)/shard_map/far/pallas_call | solution.py:370
  32.8 2.4 %collective-permute-start.7 = (bf16[1024,128]{1,0:T(8,128)(2,1)S(1)}, bf16[1024,128]{1,0:T(8,128)(2,1)S(1)}, u32[]{:S(2)}, u32[]{:S(2)}) collective-permute-start(bf16[1024,128]{1,0:T(8,128)(2,1)S(1)} %get-tuple-element.32.refs_7_), channel_id=1, source_target_pairs={{0,28},{1,29},{2,30},{3,31},{4,0},{5,1},{6,2},{7,3},{8,4},{9,5},{1... | collective-permute-start | bytes 786440 | tf_op jit(solution)/shard_map/ppermute | solution.py:390
  35.2 2.5 %last.1 = (bf16[1024,4096]{1,0:T(8,128)(2,1)S(1)}, f32[1024,128]{1,0:T(8,128)S(1)}, f32[1024,128]{1,0:T(8,128)S(1)}, f32[1024,128]{1,0:T(8,128)S(1)}) custom-call(s32[32]{0:T(128)S(1)} %copy-done.2, bf16[4096,128]{1,0:T(8,128)(2,1)S(1)} %bitcast.11, bf16[4096,128]{1,0:T(8,128)(2,1)S(1)} %bitcast.7, ...), custom_call_target="tpu_custom_call", output_to_operand_aliasing={{0}: (5, {}), {1}: (6, {}), {2}: (7, {})} | custom-call | flops 8724152320 | bytes 6815744 | tf_op jit(solution)/shard_map/last/pallas_call | solution.py:370
  37.6 1.3 %collective-permute-start.8 = (bf16[1024,128]{1,0:T(8,128)(2,1)S(1)}, bf16[1024,128]{1,0:T(8,128)(2,1)S(1)}, u32[]{:S(2)}, u32[]{:S(2)}) collective-permute-start(bf16[1024,128]{1,0:T(8,128)(2,1)S(1)} %get-tuple-element.38), channel_id=1, source_target_pairs={{0,29},{1,28},{2,31},{3,30},{4,1},{5,0},{6,3},{7,2},{8,5},{9,4},{1... | collective-permute-start | bytes 786440 | tf_op jit(solution)/shard_map/ppermute | solution.py:390
  39.0 5.2 %queries.1 = bf16[4096,128]{1,0:T(8,128)(2,1)} custom-call(s32[32]{0:T(128)S(1)} %copy-done.2, bf16[2048,128]{1,0:T(8,128)(2,1)S(1)} %get-tuple-element.22.both_ref.refs_3_, bf16[1024,4096]{1,0:T(8,128)(2,1)S(1)} %get-tuple-element.33.own_ref, bf16[1024,128]{1,0:T(8,128)(2,1)S(1)} %collective-permute-done.key_ref.refs_3_.refs_0_, ...), custom_call_target="tpu_custom_call" | custom-call | flops 6710886400 | bytes 5242880 | tf_op jit(solution)/shard_map/queries/pallas_call | solution.py:370
  44.2 0.0 collective-permute-done.6.refs_0_
  44.2 0.0 collective-permute-done.7.refs_1_
  44.2 3.0 %collective-permute-done.8.refs_2_ = bf16[1024,128]{1,0:T(8,128)(2,1)S(1)} collective-permute-done((bf16[1024,128]{1,0:T(8,128)(2,1)S(1)}, bf16[1024,128]{1,0:T(8,128)(2,1)S(1)}, u32[]{:S(2)}, u32[]{:S(2)}) %collective-permute-start.8) | collective-permute-done | bytes 262176 | tf_op jit(solution)/shard_map/ppermute | solution.py:390
  47.2 0.8 %total.1 = (bf16[512,128]{1,0:T(8,128)(2,1)}, bf16[512,128]{1,0:T(8,128)(2,1)}) custom-call(f32[1024,128]{1,0:T(8,128)S(1)} %get-tuple-element.37.total_ref, bf16[1024,128]{1,0:T(8,128)(2,1)S(1)} %collective-permute-done.5.refs_6_.swapped_ref, bf16[1024,128]{1,0:T(8,128)(2,1)S(1)} %collective-permute-done.6.refs_0_, ...), custom_call_target="tpu_custom_call" | custom-call | flops 13421772 | bytes 10485 | tf_op jit(solution)/shard_map/total/pallas_call | solution.py:370
Async XLA Ops:
  0.6 10.1 %collective-permute-start = (bf16[1024,128]{1,0:T(8,128)(2,1)}, bf16[1024,128]{1,0:T(8,128)(2,1)S(1)}, u32[]{:S(2)}, u32[]{:S(2)}) collective-permute-start(bf16[1024,128]{1,0:T(8,128)(2,1)} %refs_4_.1), channel_id=1, source_target_pairs={{0,2},{1,3},{2,4},{3,5},{4,6},{5,7},{6,8},{7,9},{8,10},{9,11},{10,... | collective-permute-start | bytes 786440 | tf_op jit(solution)/shard_map/ppermute | solution.py:390
  1.1 12.1 %collective-permute-start.1 = (bf16[1024,128]{1,0:T(8,128)(2,1)}, bf16[1024,128]{1,0:T(8,128)(2,1)S(1)}, u32[]{:S(2)}, u32[]{:S(2)}) collective-permute-start(bf16[1024,128]{1,0:T(8,128)(2,1)} %refs_5_.1), channel_id=1, source_target_pairs={{0,2},{1,3},{2,4},{3,5},{4,6},{5,7},{6,8},{7,9},{8,10},{9,11},{10,... | collective-permute-start | bytes 786440 | tf_op jit(solution)/shard_map/ppermute | solution.py:390
  3.8 11.7 %copy-start = (bf16[1024,4,128]{2,1,0:T(4,128)(2,1)S(1)}, bf16[1024,4,128]{2,1,0:T(4,128)(2,1)}, u32[]{:S(2)}) copy-start(bf16[1024,4,128]{2,1,0:T(4,128)(2,1)} %param.11) | copy-start | bytes 3145732
  3.8 11.7 %copy-start.1 = (bf16[1024,4,128]{2,1,0:T(4,128)(2,1)S(1)}, bf16[1024,4,128]{2,1,0:T(4,128)(2,1)}, u32[]{:S(2)}) copy-start(bf16[1024,4,128]{2,1,0:T(4,128)(2,1)} %param.7) | copy-start | bytes 3145732
  3.8 11.7 %copy-start.2 = (s32[32]{0:T(128)S(1)}, s32[32]{0:T(128)}, u32[]{:S(2)}) copy-start(s32[32]{0:T(128)} %span_ids.7) | copy-start | bytes 388
  13.3 11.5 %collective-permute-start.3 = (bf16[2048,128]{1,0:T(8,128)(2,1)S(1)}, bf16[2048,128]{1,0:T(8,128)(2,1)S(1)}, u32[]{:S(2)}, u32[]{:S(2)}) collective-permute-start(bf16[2048,128]{1,0:T(8,128)(2,1)S(1)} %get-tuple-element.28.refs_7_), channel_id=1, source_target_pairs={{0,2},{1,3},{2,0},{3,1},{4,6},{5,7},{6,4},{7,5},{8,10},{9,11},{10,... | collective-permute-start | bytes 1572872 | tf_op jit(solution)/shard_map/ppermute | solution.py:390
  13.4 13.8 %collective-permute-start.2 = (bf16[2048,128]{1,0:T(8,128)(2,1)S(1)}, bf16[2048,128]{1,0:T(8,128)(2,1)S(1)}, u32[]{:S(2)}, u32[]{:S(2)}) collective-permute-start(bf16[2048,128]{1,0:T(8,128)(2,1)S(1)} %get-tuple-element.27), channel_id=1, source_target_pairs={{0,4},{1,5},{2,2},{3,3},{4,8},{5,9},{6,6},{7,7},{8,12},{9,13},{10,... | collective-permute-start | bytes 1572872 | tf_op jit(solution)/shard_map/ppermute | solution.py:390
  21.1 1.6 %collective-permute-start.4 = (bf16[1024,128]{1,0:T(8,128)(2,1)S(1)}, bf16[1024,128]{1,0:T(8,128)(2,1)S(1)}, u32[]{:S(2)}, u32[]{:S(2)}) collective-permute-start(bf16[1024,128]{1,0:T(8,128)(2,1)S(1)} %get-tuple-element.29), channel_id=1, source_target_pairs={{0,2},{1,3},{2,0},{3,1},{4,6},{5,7},{6,4},{7,5},{8,10},{9,11},{10,... | collective-permute-start | bytes 786440 | tf_op jit(solution)/shard_map/ppermute | solution.py:390
  21.2 3.6 %collective-permute-start.5 = (bf16[1024,128]{1,0:T(8,128)(2,1)S(1)}, bf16[1024,128]{1,0:T(8,128)(2,1)S(1)}, u32[]{:S(2)}, u32[]{:S(2)}) collective-permute-start(bf16[1024,128]{1,0:T(8,128)(2,1)S(1)} %get-tuple-element.31), channel_id=1, source_target_pairs={{0,2},{1,3},{2,0},{3,1},{4,6},{5,7},{6,4},{7,5},{8,10},{9,11},{10,... | collective-permute-start | bytes 786440 | tf_op jit(solution)/shard_map/ppermute | solution.py:390
  22.8 21.4 %collective-permute-start.6 = (bf16[1024,128]{1,0:T(8,128)(2,1)S(1)}, bf16[1024,128]{1,0:T(8,128)(2,1)S(1)}, u32[]{:S(2)}, u32[]{:S(2)}) collective-permute-start(bf16[1024,128]{1,0:T(8,128)(2,1)S(1)} %join.1.refs_5_), channel_id=1, source_target_pairs={{0,1},{1,0},{2,3},{3,2},{4,5},{5,4},{6,7},{7,6},{8,9},{9,8},{10,11... | collective-permute-start | bytes 786440 | tf_op jit(solution)/shard_map/ppermute | solution.py:390
  32.8 11.4 %collective-permute-start.7 = (bf16[1024,128]{1,0:T(8,128)(2,1)S(1)}, bf16[1024,128]{1,0:T(8,128)(2,1)S(1)}, u32[]{:S(2)}, u32[]{:S(2)}) collective-permute-start(bf16[1024,128]{1,0:T(8,128)(2,1)S(1)} %get-tuple-element.32.refs_7_), channel_id=1, source_target_pairs={{0,28},{1,29},{2,30},{3,31},{4,0},{5,1},{6,2},{7,3},{8,4},{9,5},{1... | collective-permute-start | bytes 786440 | tf_op jit(solution)/shard_map/ppermute | solution.py:390
  37.6 9.5 %collective-permute-start.8 = (bf16[1024,128]{1,0:T(8,128)(2,1)S(1)}, bf16[1024,128]{1,0:T(8,128)(2,1)S(1)}, u32[]{:S(2)}, u32[]{:S(2)}) collective-permute-start(bf16[1024,128]{1,0:T(8,128)(2,1)S(1)} %get-tuple-element.38), channel_id=1, source_target_pairs={{0,29},{1,28},{2,31},{3,30},{4,1},{5,0},{6,3},{7,2},{8,5},{9,4},{1... | collective-permute-start | bytes 786440 | tf_op jit(solution)/shard_map/ppermute | solution.py:390

commit v13 on v11

--- a/solution.py
+++ b/solution.py
@@ -90,7 +90,8 @@
 
 
 def block_grads(group, accs, scale, rows, blocks):
-    query_ref, grad_ref, tile = group[0], group[1], group[-1]
+    query_ref, grad_ref, tile = group[0], group[1], 256
+    group = group[:-1] + (tile,)
     key_acc, value_acc = accs
     count = rows // tile
     tiles = [(block, p) for block in blocks for p in range(count)]
@@ -478,7 +479,7 @@
         [SMEM] + [VMEM] * 6,
         [shape((rows, dim), bf16)],
         [pltpu.VMEM((dim, rows), f32), pltpu.VMEM((STEPS, dim, toks), bf16)],
-        1.25 * heads,
+        0.02 * heads,
         28,
         "queries",
     )

time: 45.2 us -> 44.1 us (0.976); the launches traced: 44.6 us -> 44.3 us
  no operation moved by 1% of the time
where the time goes in v13:
time: 44.1 us; the launch traced here: 44.3 us
  Pallas kernels  26.4 us (60%)
  starting transfers between devices  14.1 us (32%)
  waiting for transfers between devices  2.99 us (7%)
  between operations  0.74 us (2%)
    pallas_call x8, Pallas kernels, call(): pl.pallas_call(kernel, out_shape=outs, in_specs=where, out_specs=[VMEM] *...  26.4 us
    ppermute x9, starting transfers between devices, moved(): return lax.ppermute(block, ('ctx', 'head'), route)  14.1 us
    ppermute x9, waiting for transfers between devices, moved(): return lax.ppermute(block, ('ctx', 'head'), route)  2.99 us
  transfers between devices with their start and end apart: 9, of which 3 were waited for; matrix products, arithmetic and copies ran while one was open for 0% of the time, Pallas kernels for 58%

profile of v13, /device:TPU:0, one launch (start us, length us, event | category | flops | bytes accessed | tf_op | source)
XLA Modules:
  0.0 44.3 jit_solution(12454123960130305801)
XLA Ops:
  0.6 0.5 %collective-permute-start.1 = (bf16[1024,128]{1,0:T(8,128)(2,1)}, bf16[1024,128]{1,0:T(8,128)(2,1)S(1)}, u32[]{:S(2)}, u32[]{:S(2)}) collective-permute-start(bf16[1024,128]{1,0:T(8,128)(2,1)} %refs_4_.1), channel_id=1, source_target_pairs={{0,2},{1,3},{2,4},{3,5},{4,6},{5,7},{6,8},{7,9},{8,10},{9,11},{10,... | collective-permute-start | bytes 786440 | tf_op jit(solution)/shard_map/ppermute | solution.py:390
  1.1 2.6 %collective-permute-start.2 = (bf16[1024,128]{1,0:T(8,128)(2,1)}, bf16[1024,128]{1,0:T(8,128)(2,1)S(1)}, u32[]{:S(2)}, u32[]{:S(2)}) collective-permute-start(bf16[1024,128]{1,0:T(8,128)(2,1)} %refs_5_.1), channel_id=1, source_target_pairs={{0,2},{1,3},{2,4},{3,5},{4,6},{5,7},{6,8},{7,9},{8,10},{9,11},{10,... | collective-permute-start | bytes 786440 | tf_op jit(solution)/shard_map/ppermute | solution.py:390
  3.8 0.0 copy-start
  3.8 0.0 copy-start.1
  3.8 0.0 copy-start.2
  3.8 6.1 %first.1 = (f32[8,4096]{1,0:T(8,128)S(1)}, bf16[2048,128]{1,0:T(8,128)(2,1)S(1)}, bf16[1024,4096]{1,0:T(8,128)(2,1)S(1)}, f32[1024,128]{1,0:T(8,128)S(1)}, f32[1024,128]{1,0:T(8,128)S(1)}) custom-call(bf16[4096,128]{1,0:T(8,128)(2,1)} %bitcast.4, bf16[4096,128]{1,0:T(8,128)(2,1)} %bitcast.13, bf16[4096,128]{1,0:T(8,128)(2,1)} %bitcast.8, f32[4,1024]{1,0:T(4,128)} %refs_3_.1, ...), custom_call_target="tpu_custom_call" | custom-call | flops 8724152320 | bytes 6815744 | tf_op jit(solution)/shard_map/first/pallas_call | solution.py:370
  9.9 4.4 %collective-permute-start = (bf16[2048,128]{1,0:T(8,128)(2,1)S(1)}, bf16[2048,128]{1,0:T(8,128)(2,1)S(1)}, u32[]{:S(2)}, u32[]{:S(2)}) collective-permute-start(bf16[2048,128]{1,0:T(8,128)(2,1)S(1)} %get-tuple-element.20.refs_3_.both_ref), channel_id=1, source_target_pairs={{0,4},{1,5},{2,2},{3,3},{4,8},{5,9},{6,6},{7,7},{8,12},{9,13},{10,... | collective-permute-start | bytes 1572872 | tf_op jit(solution)/shard_map/ppermute | solution.py:390
  14.3 0.0 collective-permute-done.1.key_ref.refs_3_.refs_0_
  14.3 0.0 collective-permute-done.2.value_ref.refs_4_
  14.3 0.1 collective-permute-start.3
  14.4 0.0 copy-done
  14.4 0.0 copy-done.1
  14.4 0.0 copy-done.2
  14.4 5.5 %near.1 = (bf16[2,512,2048]{2,1,0:T(8,128)(2,1)S(1)}, bf16[1024,128]{1,0:T(8,128)(2,1)S(1)}, bf16[1024,128]{1,0:T(8,128)(2,1)S(1)}, bf16[1024,128]{1,0:T(8,128)(2,1)S(1)}) custom-call(s32[32]{0:T(128)S(1)} %copy-done, bf16[4096,128]{1,0:T(8,128)(2,1)S(1)} %bitcast.9, bf16[4096,128]{1,0:T(8,128)(2,1)S(1)} %bitcast.5, ...), custom_call_target="tpu_custom_call" | custom-call | flops 10737418240 | bytes 8388608 | tf_op jit(solution)/shard_map/near/pallas_call | solution.py:370
  19.9 0.5 %collective-permute-start.4 = (bf16[1024,128]{1,0:T(8,128)(2,1)S(1)}, bf16[1024,128]{1,0:T(8,128)(2,1)S(1)}, u32[]{:S(2)}, u32[]{:S(2)}) collective-permute-start(bf16[1024,128]{1,0:T(8,128)(2,1)S(1)} %get-tuple-element.25), channel_id=1, source_target_pairs={{0,2},{1,3},{2,0},{3,1},{4,6},{5,7},{6,4},{7,5},{8,10},{9,11},{10,... | collective-permute-start | bytes 786440 | tf_op jit(solution)/shard_map/ppermute | solution.py:390
  20.4 0.1 collective-permute-start.5
  20.5 1.1 %collective-permute-done.4.refs_0_.refs_7_ = bf16[1024,128]{1,0:T(8,128)(2,1)S(1)} collective-permute-done((bf16[1024,128]{1,0:T(8,128)(2,1)S(1)}, bf16[1024,128]{1,0:T(8,128)(2,1)S(1)}, u32[]{:S(2)}, u32[]{:S(2)}) %collective-permute-start.4) | collective-permute-done | bytes 262176 | tf_op jit(solution)/shard_map/ppermute | solution.py:390
  21.6 0.1 join.1.refs_5_
  21.7 0.9 %collective-permute-start.6 = (bf16[1024,128]{1,0:T(8,128)(2,1)S(1)}, bf16[1024,128]{1,0:T(8,128)(2,1)S(1)}, u32[]{:S(2)}, u32[]{:S(2)}) collective-permute-start(bf16[1024,128]{1,0:T(8,128)(2,1)S(1)} %join.1.refs_5_), channel_id=1, source_target_pairs={{0,1},{1,0},{2,3},{3,2},{4,5},{5,4},{6,7},{7,6},{8,9},{9,8},{10,11... | collective-permute-start | bytes 786440 | tf_op jit(solution)/shard_map/ppermute | solution.py:390
  22.6 0.0 collective-permute-done.5.refs_6_.swapped_ref
  22.6 1.0 %collective-permute-done.refs_3_ = bf16[2048,128]{1,0:T(8,128)(2,1)S(1)} collective-permute-done((bf16[2048,128]{1,0:T(8,128)(2,1)S(1)}, bf16[2048,128]{1,0:T(8,128)(2,1)S(1)}, u32[]{:S(2)}, u32[]{:S(2)}) %collective-permute-start) | collective-permute-done | bytes 524320 | tf_op jit(solution)/shard_map/ppermute | solution.py:390
  23.7 0.0 collective-permute-done.3.refs_4_
  23.7 5.5 %far.1 = (bf16[2048,128]{1,0:T(8,128)(2,1)S(1)}, bf16[2,512,2048]{2,1,0:T(8,128)(2,1)S(1)}, bf16[1024,128]{1,0:T(8,128)(2,1)S(1)}, bf16[1024,128]{1,0:T(8,128)(2,1)S(1)}) custom-call(s32[32]{0:T(128)S(1)} %copy-done, bf16[4096,128]{1,0:T(8,128)(2,1)S(1)} %bitcast.10, bf16[4096,128]{1,0:T(8,128)(2,1)S(1)} %bitcast.6, ...), custom_call_target="tpu_custom_call" | custom-call | flops 10737418240 | bytes 8388608 | tf_op jit(solution)/shard_map/far/pallas_call | solution.py:370
  29.1 2.8 %collective-permute-start.7 = (bf16[1024,128]{1,0:T(8,128)(2,1)S(1)}, bf16[1024,128]{1,0:T(8,128)(2,1)S(1)}, u32[]{:S(2)}, u32[]{:S(2)}) collective-permute-start(bf16[1024,128]{1,0:T(8,128)(2,1)S(1)} %get-tuple-element.28.refs_7_), channel_id=1, source_target_pairs={{0,28},{1,29},{2,30},{3,31},{4,0},{5,1},{6,2},{7,3},{8,4},{9,5},{1... | collective-permute-start | bytes 786440 | tf_op jit(solution)/shard_map/ppermute | solution.py:390
  32.0 2.2 %collective-permute-start.8 = (bf16[1024,128]{1,0:T(8,128)(2,1)S(1)}, bf16[1024,128]{1,0:T(8,128)(2,1)S(1)}, u32[]{:S(2)}, u32[]{:S(2)}) collective-permute-start(bf16[1024,128]{1,0:T(8,128)(2,1)S(1)} %get-tuple-element.34), channel_id=1, source_target_pairs={{0,29},{1,28},{2,31},{3,30},{4,1},{5,0},{6,3},{7,2},{8,5},{9,4},{1... | collective-permute-start | bytes 786440 | tf_op jit(solution)/shard_map/ppermute | solution.py:390
  34.1 3.2 %last.1 = (bf16[1024,4096]{1,0:T(8,128)(2,1)S(1)}, f32[1024,128]{1,0:T(8,128)S(1)}, f32[1024,128]{1,0:T(8,128)S(1)}, f32[1024,128]{1,0:T(8,128)S(1)}) custom-call(s32[32]{0:T(128)S(1)} %copy-done, bf16[4096,128]{1,0:T(8,128)(2,1)S(1)} %bitcast.11, bf16[4096,128]{1,0:T(8,128)(2,1)S(1)} %bitcast.7, ...), custom_call_target="tpu_custom_call", output_to_operand_aliasing={{0}: (5, {}), {1}: (6, {}), {2}: (7, {})} | custom-call | flops 8724152320 | bytes 6815744 | tf_op jit(solution)/shard_map/last/pallas_call | solution.py:370
  37.4 5.2 %queries.1 = bf16[4096,128]{1,0:T(8,128)(2,1)} custom-call(s32[32]{0:T(128)S(1)} %copy-done, bf16[2048,128]{1,0:T(8,128)(2,1)S(1)} %get-tuple-element.20.refs_3_.both_ref, bf16[1024,4096]{1,0:T(8,128)(2,1)S(1)} %get-tuple-element.29.own_ref, bf16[1024,128]{1,0:T(8,128)(2,1)S(1)} %collective-permute-done.1.key_ref.refs_3_.refs_0_, ...), custom_call_target="tpu_custom_call" | custom-call | flops 107374184 | bytes 83886 | tf_op jit(solution)/shard_map/queries/pallas_call | solution.py:370
  42.6 0.0 collective-permute-done.6.refs_0_
  42.6 0.0 collective-permute-done.7.refs_1_
  42.6 0.8 %collective-permute-done.8.refs_2_ = bf16[1024,128]{1,0:T(8,128)(2,1)S(1)} collective-permute-done((bf16[1024,128]{1,0:T(8,128)(2,1)S(1)}, bf16[1024,128]{1,0:T(8,128)(2,1)S(1)}, u32[]{:S(2)}, u32[]{:S(2)}) %collective-permute-start.8) | collective-permute-done | bytes 262176 | tf_op jit(solution)/shard_map/ppermute | solution.py:390
  43.4 0.8 %total.1 = (bf16[512,128]{1,0:T(8,128)(2,1)}, bf16[512,128]{1,0:T(8,128)(2,1)}) custom-call(f32[1024,128]{1,0:T(8,128)S(1)} %get-tuple-element.33.total_ref, bf16[1024,128]{1,0:T(8,128)(2,1)S(1)} %collective-permute-done.5.refs_6_.swapped_ref, bf16[1024,128]{1,0:T(8,128)(2,1)S(1)} %collective-permute-done.6.refs_0_, ...), custom_call_target="tpu_custom_call" | custom-call | flops 13421772 | bytes 10485 | tf_op jit(solution)/shard_map/total/pallas_call | solution.py:370
  (1 shorter events, 0.0 us)
Async XLA Ops:
  0.6 13.6 %collective-permute-start.1 = (bf16[1024,128]{1,0:T(8,128)(2,1)}, bf16[1024,128]{1,0:T(8,128)(2,1)S(1)}, u32[]{:S(2)}, u32[]{:S(2)}) collective-permute-start(bf16[1024,128]{1,0:T(8,128)(2,1)} %refs_4_.1), channel_id=1, source_target_pairs={{0,2},{1,3},{2,4},{3,5},{4,6},{5,7},{6,8},{7,9},{8,10},{9,11},{10,... | collective-permute-start | bytes 786440 | tf_op jit(solution)/shard_map/ppermute | solution.py:390
  1.1 13.1 %collective-permute-start.2 = (bf16[1024,128]{1,0:T(8,128)(2,1)}, bf16[1024,128]{1,0:T(8,128)(2,1)S(1)}, u32[]{:S(2)}, u32[]{:S(2)}) collective-permute-start(bf16[1024,128]{1,0:T(8,128)(2,1)} %refs_5_.1), channel_id=1, source_target_pairs={{0,2},{1,3},{2,4},{3,5},{4,6},{5,7},{6,8},{7,9},{8,10},{9,11},{10,... | collective-permute-start | bytes 786440 | tf_op jit(solution)/shard_map/ppermute | solution.py:390
  3.8 10.6 %copy-start = (s32[32]{0:T(128)S(1)}, s32[32]{0:T(128)}, u32[]{:S(2)}) copy-start(s32[32]{0:T(128)} %span_ids.7) | copy-start | bytes 388
  3.8 10.6 %copy-start.1 = (bf16[1024,4,128]{2,1,0:T(4,128)(2,1)S(1)}, bf16[1024,4,128]{2,1,0:T(4,128)(2,1)}, u32[]{:S(2)}) copy-start(bf16[1024,4,128]{2,1,0:T(4,128)(2,1)} %param.11) | copy-start | bytes 3145732
  3.8 10.6 %copy-start.2 = (bf16[1024,4,128]{2,1,0:T(4,128)(2,1)S(1)}, bf16[1024,4,128]{2,1,0:T(4,128)(2,1)}, u32[]{:S(2)}) copy-start(bf16[1024,4,128]{2,1,0:T(4,128)(2,1)} %param.7) | copy-start | bytes 3145732
  9.9 13.8 %collective-permute-start = (bf16[2048,128]{1,0:T(8,128)(2,1)S(1)}, bf16[2048,128]{1,0:T(8,128)(2,1)S(1)}, u32[]{:S(2)}, u32[]{:S(2)}) collective-permute-start(bf16[2048,128]{1,0:T(8,128)(2,1)S(1)} %get-tuple-element.20.refs_3_.both_ref), channel_id=1, source_target_pairs={{0,4},{1,5},{2,2},{3,3},{4,8},{5,9},{6,6},{7,7},{8,12},{9,13},{10,... | collective-permute-start | bytes 1572872 | tf_op jit(solution)/shard_map/ppermute | solution.py:390
  14.3 9.3 %collective-permute-start.3 = (bf16[2048,128]{1,0:T(8,128)(2,1)S(1)}, bf16[2048,128]{1,0:T(8,128)(2,1)S(1)}, u32[]{:S(2)}, u32[]{:S(2)}) collective-permute-start(bf16[2048,128]{1,0:T(8,128)(2,1)S(1)} %pack.1.refs_7_), channel_id=1, source_target_pairs={{0,2},{1,3},{2,0},{3,1},{4,6},{5,7},{6,4},{7,5},{8,10},{9,11},{10,... | collective-permute-start | bytes 1572872 | tf_op jit(solution)/shard_map/ppermute | solution.py:390
  19.9 1.7 %collective-permute-start.4 = (bf16[1024,128]{1,0:T(8,128)(2,1)S(1)}, bf16[1024,128]{1,0:T(8,128)(2,1)S(1)}, u32[]{:S(2)}, u32[]{:S(2)}) collective-permute-start(bf16[1024,128]{1,0:T(8,128)(2,1)S(1)} %get-tuple-element.25), channel_id=1, source_target_pairs={{0,2},{1,3},{2,0},{3,1},{4,6},{5,7},{6,4},{7,5},{8,10},{9,11},{10,... | collective-permute-start | bytes 786440 | tf_op jit(solution)/shard_map/ppermute | solution.py:390
  20.4 2.2 %collective-permute-start.5 = (bf16[1024,128]{1,0:T(8,128)(2,1)S(1)}, bf16[1024,128]{1,0:T(8,128)(2,1)S(1)}, u32[]{:S(2)}, u32[]{:S(2)}) collective-permute-start(bf16[1024,128]{1,0:T(8,128)(2,1)S(1)} %get-tuple-element.27), channel_id=1, source_target_pairs={{0,2},{1,3},{2,0},{3,1},{4,6},{5,7},{6,4},{7,5},{8,10},{9,11},{10,... | collective-permute-start | bytes 786440 | tf_op jit(solution)/shard_map/ppermute | solution.py:390
  21.7 20.9 %collective-permute-start.6 = (bf16[1024,128]{1,0:T(8,128)(2,1)S(1)}, bf16[1024,128]{1,0:T(8,128)(2,1)S(1)}, u32[]{:S(2)}, u32[]{:S(2)}) collective-permute-start(bf16[1024,128]{1,0:T(8,128)(2,1)S(1)} %join.1.refs_5_), channel_id=1, source_target_pairs={{0,1},{1,0},{2,3},{3,2},{4,5},{5,4},{6,7},{7,6},{8,9},{9,8},{10,11... | collective-permute-start | bytes 786440 | tf_op jit(solution)/shard_map/ppermute | solution.py:390
  29.1 13.4 %collective-permute-start.7 = (bf16[1024,128]{1,0:T(8,128)(2,1)S(1)}, bf16[1024,128]{1,0:T(8,128)(2,1)S(1)}, u32[]{:S(2)}, u32[]{:S(2)}) collective-permute-start(bf16[1024,128]{1,0:T(8,128)(2,1)S(1)} %get-tuple-element.28.refs_7_), channel_id=1, source_target_pairs={{0,28},{1,29},{2,30},{3,31},{4,0},{5,1},{6,2},{7,3},{8,4},{9,5},{1... | collective-permute-start | bytes 786440 | tf_op jit(solution)/shard_map/ppermute | solution.py:390
  32.0 11.4 %collective-permute-start.8 = (bf16[1024,128]{1,0:T(8,128)(2,1)S(1)}, bf16[1024,128]{1,0:T(8,128)(2,1)S(1)}, u32[]{:S(2)}, u32[]{:S(2)}) collective-permute-start(bf16[1024,128]{1,0:T(8,128)(2,1)S(1)} %get-tuple-element.34), channel_id=1, source_target_pairs={{0,29},{1,28},{2,31},{3,30},{4,1},{5,0},{6,3},{7,2},{8,5},{9,4},{1... | collective-permute-start | bytes 786440 | tf_op jit(solution)/shard_map/ppermute | solution.py:390

commit v14 on v13

--- a/solution.py
+++ b/solution.py
@@ -210,24 +210,37 @@
     arrive(0)
     corner(order[0])
     arrive(1)
-    if parts == 2:
-        pl.when(low == order[0])(square)
-        pl.when(low == order[1])(lambda: corner(order[1]))
-    else:
+    if parts != 2:
         corner(order[1])
         square()
 
 
+def more_kernel(heads, tile, scale, span_ids, *refs):
+    kept_ref, key_acc, value_acc, probs_ref = refs[7:]
+    x = lax.axis_index("head")
+    _, low, corner, square = split_work(
+        heads, tile, scale, span_ids, refs[:4], kept_ref, key_acc, value_acc, probs_ref
+    )
+    pl.when(low != x)(square)
+    pl.when(low == x)(lambda: corner(x))
+
+
+def split_work(heads, tile, scale, span_ids, ins, kept_ref, key_acc, value_acc, probs_ref):
+    query_ref, grad_ref, terms_ref, both_ref = ins
+    toks = both_ref.shape[0] // 2
+    key_ref, value_ref = both_ref.at[pl.ds(0, toks)], both_ref.at[pl.ds(toks, toks)]
+    group = (query_ref, grad_ref, key_ref, value_ref, terms_ref, tile)
+    accs = (key_acc, value_acc)
+    return accs, *own_work(group, accs, scale, span_ids, kept_ref, probs_ref, heads)
+
+
 def last_kernel(heads, tile, scale, parts, span_ids, *refs):
-    query_ref, grad_ref, terms_ref, both_ref = refs[:4]
     kept_ref, key_acc, value_acc, total_ref, probs_ref = refs[8:]
     if parts == 2:
-        toks = both_ref.shape[0] // 2
-        key_ref, value_ref = both_ref.at[pl.ds(0, toks)], both_ref.at[pl.ds(toks, toks)]
-        group = (query_ref, grad_ref, key_ref, value_ref, terms_ref, tile)
-        accs = (key_acc, value_acc)
         x = lax.axis_index("head")
-        low, corner, square = own_work(group, accs, scale, span_ids, kept_ref, probs_ref, heads)
+        _, low, corner, square = split_work(
+            heads, tile, scale, span_ids, refs[:4], kept_ref, key_acc, value_acc, probs_ref
+        )
         pl.when(low == x)(square)
         pl.when(low != x)(lambda: corner(x))
     put_shares([total_ref], key_acc, value_acc, scale, 0, parts)
@@ -423,6 +436,18 @@
         20,
         "first",
     )
+    if parts == 2:
+        kept, key_sum, value_sum = call(
+            functools.partial(more_kernel, heads, tile, scale),
+            (span_ids, q, g, terms, both, kept, key_sum, value_sum),
+            [SMEM] + [VMEM] * 7,
+            sums,
+            [probs],
+            0.8 * heads,
+            20,
+            "more",
+            {5: 0, 6: 1, 7: 2},
+        )
     (both_1,) = call(
         pack_kernel, (key_1, value_1), [VMEM] * 2, [shape((2 * toks, dim), bf16)], [], 0.01, 4, "pack"
     )

time: 44.1 us -> 44.3 us (level)
  starting transfers between devices: 14.1 us -> 13.1 us
  Pallas kernels: 26.4 us -> 27.2 us
    ppermute x9, starting transfers between devices: 14.1 us -> 13.1 us  [moved(): return lax.ppermute(block, ('ctx', 'head'), route)]
    pallas_call x8 -> x9, Pallas kernels: 26.4 us -> 27.2 us  [call(): pl.pallas_call(kernel, out_shape=outs, in_specs=where, out_specs=[VMEM] *...]
  transfers between devices with their start and end apart: 9 -> 9, of which waited for: 3 -> 2; matrix products, arithmetic and copies ran while one was open for 0% -> 0% of each run, Pallas kernels for 58% -> 60%
where the time goes in v14:
time: 44.3 us; the launch traced here: 44.1 us
  Pallas kernels  27.2 us (61%)
  starting transfers between devices  13.1 us (30%)
  waiting for transfers between devices  3.04 us (7%)
  between operations  0.75 us (2%)
    pallas_call x9, Pallas kernels, call(): pl.pallas_call(kernel, out_shape=outs, in_specs=where, out_specs=[VMEM] *...  27.2 us
    ppermute x9, starting transfers between devices, moved(): return lax.ppermute(block, ('ctx', 'head'), route)  13.1 us
    ppermute x9, waiting for transfers between devices, moved(): return lax.ppermute(block, ('ctx', 'head'), route)  3.04 us
  transfers between devices with their start and end apart: 9, of which 2 were waited for; matrix products, arithmetic and copies ran while one was open for 0% of the time, Pallas kernels for 60%

profile of v14, /device:TPU:0, one launch (start us, length us, event | category | flops | bytes accessed | tf_op | source)
XLA Modules:
  0.0 44.1 jit_solution(11944594855932908486)
XLA Ops:
  0.6 0.5 %collective-permute-start.1 = (bf16[1024,128]{1,0:T(8,128)(2,1)}, bf16[1024,128]{1,0:T(8,128)(2,1)S(1)}, u32[]{:S(2)}, u32[]{:S(2)}) collective-permute-start(bf16[1024,128]{1,0:T(8,128)(2,1)} %refs_4_.1), channel_id=1, source_target_pairs={{0,2},{1,3},{2,4},{3,5},{4,6},{5,7},{6,8},{7,9},{8,10},{9,11},{10,... | collective-permute-start | bytes 786440 | tf_op jit(solution)/shard_map/ppermute | solution.py:403
  1.1 2.6 %collective-permute-start.2 = (bf16[1024,128]{1,0:T(8,128)(2,1)}, bf16[1024,128]{1,0:T(8,128)(2,1)S(1)}, u32[]{:S(2)}, u32[]{:S(2)}) collective-permute-start(bf16[1024,128]{1,0:T(8,128)(2,1)} %refs_5_.1), channel_id=1, source_target_pairs={{0,2},{1,3},{2,4},{3,5},{4,6},{5,7},{6,8},{7,9},{8,10},{9,11},{10,... | collective-permute-start | bytes 786440 | tf_op jit(solution)/shard_map/ppermute | solution.py:403
  3.8 0.0 copy-start
  3.8 0.0 copy-start.1
  3.8 0.0 copy-start.2
  3.8 4.5 %first.1 = (f32[8,4096]{1,0:T(8,128)S(1)}, bf16[2048,128]{1,0:T(8,128)(2,1)S(1)}, bf16[1024,4096]{1,0:T(8,128)(2,1)S(1)}, f32[1024,128]{1,0:T(8,128)S(1)}, f32[1024,128]{1,0:T(8,128)S(1)}) custom-call(bf16[4096,128]{1,0:T(8,128)(2,1)} %bitcast.4, bf16[4096,128]{1,0:T(8,128)(2,1)} %bitcast.15, bf16[4096,128]{1,0:T(8,128)(2,1)} %bitcast.9, f32[4,1024]{1,0:T(4,128)} %refs_3_.1, ...), custom_call_target="tpu_custom_call" | custom-call | flops 8724152320 | bytes 6815744 | tf_op jit(solution)/shard_map/first/pallas_call | solution.py:383
  8.3 3.4 %collective-permute-start = (bf16[2048,128]{1,0:T(8,128)(2,1)S(1)}, bf16[2048,128]{1,0:T(8,128)(2,1)S(1)}, u32[]{:S(2)}, u32[]{:S(2)}) collective-permute-start(bf16[2048,128]{1,0:T(8,128)(2,1)S(1)} %get-tuple-element.23.refs_3_.both_ref), channel_id=1, source_target_pairs={{0,4},{1,5},{2,2},{3,3},{4,8},{5,9},{6,6},{7,7},{8,12},{9,13},{10,... | collective-permute-start | bytes 1572872 | tf_op jit(solution)/shard_map/ppermute | solution.py:403
  11.7 0.0 copy-done
  11.7 0.0 copy-done.1
  11.7 0.0 copy-done.2
  11.7 2.4 %more.1 = (bf16[1024,4096]{1,0:T(8,128)(2,1)S(1)}, f32[1024,128]{1,0:T(8,128)S(1)}, f32[1024,128]{1,0:T(8,128)S(1)}) custom-call(s32[32]{0:T(128)S(1)} %copy-done, bf16[4096,128]{1,0:T(8,128)(2,1)S(1)} %bitcast.10, bf16[4096,128]{1,0:T(8,128)(2,1)S(1)} %bitcast.5, ...), custom_call_target="tpu_custom_call", output_to_operand_aliasing={{0}: (5, {}), {1}: (6, {}), {2}: (7, {})} | custom-call | flops 4294967296 | bytes 3355443 | tf_op jit(solution)/shard_map/more/pallas_call | solution.py:383
  14.1 0.0 collective-permute-done.1.key_ref.refs_3_.refs_0_
  14.2 0.0 collective-permute-done.2.value_ref.refs_4_
  14.2 0.1 collective-permute-start.3
  14.3 5.4 %near.1 = (bf16[2,512,2048]{2,1,0:T(8,128)(2,1)S(1)}, bf16[1024,128]{1,0:T(8,128)(2,1)S(1)}, bf16[1024,128]{1,0:T(8,128)(2,1)S(1)}, bf16[1024,128]{1,0:T(8,128)(2,1)S(1)}) custom-call(s32[32]{0:T(128)S(1)} %copy-done, bf16[4096,128]{1,0:T(8,128)(2,1)S(1)} %bitcast.11, bf16[4096,128]{1,0:T(8,128)(2,1)S(1)} %bitcast.6, ...), custom_call_target="tpu_custom_call" | custom-call | flops 10737418240 | bytes 8388608 | tf_op jit(solution)/shard_map/near/pallas_call | solution.py:383
  19.7 0.6 %collective-permute-start.4 = (bf16[1024,128]{1,0:T(8,128)(2,1)S(1)}, bf16[1024,128]{1,0:T(8,128)(2,1)S(1)}, u32[]{:S(2)}, u32[]{:S(2)}) collective-permute-start(bf16[1024,128]{1,0:T(8,128)(2,1)S(1)} %get-tuple-element.31), channel_id=1, source_target_pairs={{0,2},{1,3},{2,0},{3,1},{4,6},{5,7},{6,4},{7,5},{8,10},{9,11},{10,... | collective-permute-start | bytes 786440 | tf_op jit(solution)/shard_map/ppermute | solution.py:403
  20.3 0.1 collective-permute-start.5
  20.4 1.1 %collective-permute-done.4.refs_0_.refs_7_ = bf16[1024,128]{1,0:T(8,128)(2,1)S(1)} collective-permute-done((bf16[1024,128]{1,0:T(8,128)(2,1)S(1)}, bf16[1024,128]{1,0:T(8,128)(2,1)S(1)}, u32[]{:S(2)}, u32[]{:S(2)}) %collective-permute-start.4) | collective-permute-done | bytes 262176 | tf_op jit(solution)/shard_map/ppermute | solution.py:403
  21.5 0.1 join.1.refs_5_
  21.6 2.3 %collective-permute-start.6 = (bf16[1024,128]{1,0:T(8,128)(2,1)S(1)}, bf16[1024,128]{1,0:T(8,128)(2,1)S(1)}, u32[]{:S(2)}, u32[]{:S(2)}) collective-permute-start(bf16[1024,128]{1,0:T(8,128)(2,1)S(1)} %join.1.refs_5_), channel_id=1, source_target_pairs={{0,1},{1,0},{2,3},{3,2},{4,5},{5,4},{6,7},{7,6},{8,9},{9,8},{10,11... | collective-permute-start | bytes 786440 | tf_op jit(solution)/shard_map/ppermute | solution.py:403
  23.8 0.0 collective-permute-done.5.refs_6_.swapped_ref
  23.8 0.0 collective-permute-done.refs_3_
  23.9 0.0 collective-permute-done.3.refs_4_
  23.9 5.5 %far.1 = (bf16[2048,128]{1,0:T(8,128)(2,1)S(1)}, bf16[2,512,2048]{2,1,0:T(8,128)(2,1)S(1)}, bf16[1024,128]{1,0:T(8,128)(2,1)S(1)}, bf16[1024,128]{1,0:T(8,128)(2,1)S(1)}) custom-call(s32[32]{0:T(128)S(1)} %copy-done, bf16[4096,128]{1,0:T(8,128)(2,1)S(1)} %bitcast.12, bf16[4096,128]{1,0:T(8,128)(2,1)S(1)} %bitcast.7, ...), custom_call_target="tpu_custom_call" | custom-call | flops 10737418240 | bytes 8388608 | tf_op jit(solution)/shard_map/far/pallas_call | solution.py:383
  29.4 2.5 %collective-permute-start.7 = (bf16[1024,128]{1,0:T(8,128)(2,1)S(1)}, bf16[1024,128]{1,0:T(8,128)(2,1)S(1)}, u32[]{:S(2)}, u32[]{:S(2)}) collective-permute-start(bf16[1024,128]{1,0:T(8,128)(2,1)S(1)} %get-tuple-element.34.refs_7_), channel_id=1, source_target_pairs={{0,28},{1,29},{2,30},{3,31},{4,0},{5,1},{6,2},{7,3},{8,4},{9,5},{1... | collective-permute-start | bytes 786440 | tf_op jit(solution)/shard_map/ppermute | solution.py:403
  31.9 1.0 %collective-permute-start.8 = (bf16[1024,128]{1,0:T(8,128)(2,1)S(1)}, bf16[1024,128]{1,0:T(8,128)(2,1)S(1)}, u32[]{:S(2)}, u32[]{:S(2)}) collective-permute-start(bf16[1024,128]{1,0:T(8,128)(2,1)S(1)} %get-tuple-element.40), channel_id=1, source_target_pairs={{0,29},{1,28},{2,31},{3,30},{4,1},{5,0},{6,3},{7,2},{8,5},{9,4},{1... | collective-permute-start | bytes 786440 | tf_op jit(solution)/shard_map/ppermute | solution.py:403
  32.9 3.2 %last.1 = (bf16[1024,4096]{1,0:T(8,128)(2,1)S(1)}, f32[1024,128]{1,0:T(8,128)S(1)}, f32[1024,128]{1,0:T(8,128)S(1)}, f32[1024,128]{1,0:T(8,128)S(1)}) custom-call(s32[32]{0:T(128)S(1)} %copy-done, bf16[4096,128]{1,0:T(8,128)(2,1)S(1)} %bitcast.13, bf16[4096,128]{1,0:T(8,128)(2,1)S(1)} %bitcast.8, ...), custom_call_target="tpu_custom_call", output_to_operand_aliasing={{0}: (5, {}), {1}: (6, {}), {2}: (7, {})} | custom-call | flops 8724152320 | bytes 6815744 | tf_op jit(solution)/shard_map/last/pallas_call | solution.py:383
  36.1 5.2 %queries.1 = bf16[4096,128]{1,0:T(8,128)(2,1)} custom-call(s32[32]{0:T(128)S(1)} %copy-done, bf16[2048,128]{1,0:T(8,128)(2,1)S(1)} %get-tuple-element.23.refs_3_.both_ref, bf16[1024,4096]{1,0:T(8,128)(2,1)S(1)} %get-tuple-element.35.own_ref, bf16[1024,128]{1,0:T(8,128)(2,1)S(1)} %collective-permute-done.1.key_ref.refs_3_.refs_0_, ...), custom_call_target="tpu_custom_call" | custom-call | flops 107374184 | bytes 83886 | tf_op jit(solution)/shard_map/queries/pallas_call | solution.py:383
  41.4 0.0 collective-permute-done.6.refs_0_
  41.4 1.9 %collective-permute-done.7.refs_1_ = bf16[1024,128]{1,0:T(8,128)(2,1)S(1)} collective-permute-done((bf16[1024,128]{1,0:T(8,128)(2,1)S(1)}, bf16[1024,128]{1,0:T(8,128)(2,1)S(1)}, u32[]{:S(2)}, u32[]{:S(2)}) %collective-permute-start.7) | collective-permute-done | bytes 262176 | tf_op jit(solution)/shard_map/ppermute | solution.py:403
  43.3 0.0 collective-permute-done.8.refs_2_
  43.3 0.8 %total.1 = (bf16[512,128]{1,0:T(8,128)(2,1)}, bf16[512,128]{1,0:T(8,128)(2,1)}) custom-call(f32[1024,128]{1,0:T(8,128)S(1)} %get-tuple-element.39.total_ref, bf16[1024,128]{1,0:T(8,128)(2,1)S(1)} %collective-permute-done.5.refs_6_.swapped_ref, bf16[1024,128]{1,0:T(8,128)(2,1)S(1)} %collective-permute-done.6.refs_0_, ...), custom_call_target="tpu_custom_call" | custom-call | flops 13421772 | bytes 10485 | tf_op jit(solution)/shard_map/total/pallas_call | solution.py:383
  (1 shorter events, 0.0 us)
Async XLA Ops:
  0.6 13.5 %collective-permute-start.1 = (bf16[1024,128]{1,0:T(8,128)(2,1)}, bf16[1024,128]{1,0:T(8,128)(2,1)S(1)}, u32[]{:S(2)}, u32[]{:S(2)}) collective-permute-start(bf16[1024,128]{1,0:T(8,128)(2,1)} %refs_4_.1), channel_id=1, source_target_pairs={{0,2},{1,3},{2,4},{3,5},{4,6},{5,7},{6,8},{7,9},{8,10},{9,11},{10,... | collective-permute-start | bytes 786440 | tf_op jit(solution)/shard_map/ppermute | solution.py:403
  1.1 13.0 %collective-permute-start.2 = (bf16[1024,128]{1,0:T(8,128)(2,1)}, bf16[1024,128]{1,0:T(8,128)(2,1)S(1)}, u32[]{:S(2)}, u32[]{:S(2)}) collective-permute-start(bf16[1024,128]{1,0:T(8,128)(2,1)} %refs_5_.1), channel_id=1, source_target_pairs={{0,2},{1,3},{2,4},{3,5},{4,6},{5,7},{6,8},{7,9},{8,10},{9,11},{10,... | collective-permute-start | bytes 786440 | tf_op jit(solution)/shard_map/ppermute | solution.py:403
  3.8 7.9 %copy-start = (s32[32]{0:T(128)S(1)}, s32[32]{0:T(128)}, u32[]{:S(2)}) copy-start(s32[32]{0:T(128)} %span_ids.9) | copy-start | bytes 388
  3.8 7.9 %copy-start.1 = (bf16[1024,4,128]{2,1,0:T(4,128)(2,1)S(1)}, bf16[1024,4,128]{2,1,0:T(4,128)(2,1)}, u32[]{:S(2)}) copy-start(bf16[1024,4,128]{2,1,0:T(4,128)(2,1)} %param.11) | copy-start | bytes 3145732
  3.8 8.0 %copy-start.2 = (bf16[1024,4,128]{2,1,0:T(4,128)(2,1)S(1)}, bf16[1024,4,128]{2,1,0:T(4,128)(2,1)}, u32[]{:S(2)}) copy-start(bf16[1024,4,128]{2,1,0:T(4,128)(2,1)} %param.7) | copy-start | bytes 3145732
  8.3 15.6 %collective-permute-start = (bf16[2048,128]{1,0:T(8,128)(2,1)S(1)}, bf16[2048,128]{1,0:T(8,128)(2,1)S(1)}, u32[]{:S(2)}, u32[]{:S(2)}) collective-permute-start(bf16[2048,128]{1,0:T(8,128)(2,1)S(1)} %get-tuple-element.23.refs_3_.both_ref), channel_id=1, source_target_pairs={{0,4},{1,5},{2,2},{3,3},{4,8},{5,9},{6,6},{7,7},{8,12},{9,13},{10,... | collective-permute-start | bytes 1572872 | tf_op jit(solution)/shard_map/ppermute | solution.py:403
  14.2 9.6 %collective-permute-start.3 = (bf16[2048,128]{1,0:T(8,128)(2,1)S(1)}, bf16[2048,128]{1,0:T(8,128)(2,1)S(1)}, u32[]{:S(2)}, u32[]{:S(2)}) collective-permute-start(bf16[2048,128]{1,0:T(8,128)(2,1)S(1)} %pack.1.refs_7_), channel_id=1, source_target_pairs={{0,2},{1,3},{2,0},{3,1},{4,6},{5,7},{6,4},{7,5},{8,10},{9,11},{10,... | collective-permute-start | bytes 1572872 | tf_op jit(solution)/shard_map/ppermute | solution.py:403
  19.7 1.7 %collective-permute-start.4 = (bf16[1024,128]{1,0:T(8,128)(2,1)S(1)}, bf16[1024,128]{1,0:T(8,128)(2,1)S(1)}, u32[]{:S(2)}, u32[]{:S(2)}) collective-permute-start(bf16[1024,128]{1,0:T(8,128)(2,1)S(1)} %get-tuple-element.31), channel_id=1, source_target_pairs={{0,2},{1,3},{2,0},{3,1},{4,6},{5,7},{6,4},{7,5},{8,10},{9,11},{10,... | collective-permute-start | bytes 786440 | tf_op jit(solution)/shard_map/ppermute | solution.py:403
  20.3 3.5 %collective-permute-start.5 = (bf16[1024,128]{1,0:T(8,128)(2,1)S(1)}, bf16[1024,128]{1,0:T(8,128)(2,1)S(1)}, u32[]{:S(2)}, u32[]{:S(2)}) collective-permute-start(bf16[1024,128]{1,0:T(8,128)(2,1)S(1)} %get-tuple-element.33), channel_id=1, source_target_pairs={{0,2},{1,3},{2,0},{3,1},{4,6},{5,7},{6,4},{7,5},{8,10},{9,11},{10,... | collective-permute-start | bytes 786440 | tf_op jit(solution)/shard_map/ppermute | solution.py:403
  21.6 19.8 %collective-permute-start.6 = (bf16[1024,128]{1,0:T(8,128)(2,1)S(1)}, bf16[1024,128]{1,0:T(8,128)(2,1)S(1)}, u32[]{:S(2)}, u32[]{:S(2)}) collective-permute-start(bf16[1024,128]{1,0:T(8,128)(2,1)S(1)} %join.1.refs_5_), channel_id=1, source_target_pairs={{0,1},{1,0},{2,3},{3,2},{4,5},{5,4},{6,7},{7,6},{8,9},{9,8},{10,11... | collective-permute-start | bytes 786440 | tf_op jit(solution)/shard_map/ppermute | solution.py:403
  29.4 14.0 %collective-permute-start.7 = (bf16[1024,128]{1,0:T(8,128)(2,1)S(1)}, bf16[1024,128]{1,0:T(8,128)(2,1)S(1)}, u32[]{:S(2)}, u32[]{:S(2)}) collective-permute-start(bf16[1024,128]{1,0:T(8,128)(2,1)S(1)} %get-tuple-element.34.refs_7_), channel_id=1, source_target_pairs={{0,28},{1,29},{2,30},{3,31},{4,0},{5,1},{6,2},{7,3},{8,4},{9,5},{1... | collective-permute-start | bytes 786440 | tf_op jit(solution)/shard_map/ppermute | solution.py:403
  31.9 11.4 %collective-permute-start.8 = (bf16[1024,128]{1,0:T(8,128)(2,1)S(1)}, bf16[1024,128]{1,0:T(8,128)(2,1)S(1)}, u32[]{:S(2)}, u32[]{:S(2)}) collective-permute-start(bf16[1024,128]{1,0:T(8,128)(2,1)S(1)} %get-tuple-element.40), channel_id=1, source_target_pairs={{0,29},{1,28},{2,31},{3,30},{4,1},{5,0},{6,3},{7,2},{8,5},{9,4},{1... | collective-permute-start | bytes 786440 | tf_op jit(solution)/shard_map/ppermute | solution.py:403

commit v15 on v13

--- a/solution.py
+++ b/solution.py
@@ -93,23 +93,29 @@
     query_ref, grad_ref, tile = group[0], group[1], 256
     group = group[:-1] + (tile,)
     key_acc, value_acc = accs
-    count = rows // tile
-    tiles = [(block, p) for block in blocks for p in range(count)]
-
-    def start(block, p):
-        row, key, length = block[:3]
-        return opened(group, pl.multiple_of(row + p * tile, tile), key, length)
+    count, depth = rows // tile, 256
+    tiles = [
+        (block, p, low)
+        for block in blocks
+        for p in range(count)
+        for low in range(0, block[2], depth)
+    ]
+
+    def start(block, p, low):
+        row, key = block[:2]
+        row, key = pl.multiple_of(row + p * tile, tile), pl.multiple_of(key + low, depth)
+        return opened(group, row, key, depth)
 
     ahead = start(*tiles[0])
-    for index, (block, p) in enumerate(tiles):
+    for index, (block, p, low) in enumerate(tiles):
         now = ahead
         if index + 1 < len(tiles):
             ahead = start(*tiles[index + 1])
         row, key, length, kept, probs = block
         prob, dscore = closed(group, scale, pl.multiple_of(row + p * tile, tile), None, *now)
-        probs[:, p * tile : (p + 1) * tile] = prob
-        kept[:, p * tile : (p + 1) * tile] = dscore
-        if p == count - 1:
+        probs[low : low + depth, p * tile : (p + 1) * tile] = prob
+        kept[low : low + depth, p * tile : (p + 1) * tile] = dscore
+        if p == count - 1 and low == length - depth:
             value_acc[pl.ds(key, length), :] += dot(probs[...], grad_ref[pl.ds(row, rows), :], NN)
             key_acc[pl.ds(key, length), :] += dot(kept[...], query_ref[pl.ds(row, rows), :], NN)
 

time: 44.1 us -> 43.7 us (level)
  starting transfers between devices: 14.1 us -> 13.2 us
    ppermute x9, starting transfers between devices: 14.1 us -> 13.2 us  [moved(): return lax.ppermute(block, ('ctx', 'head'), route)]
  transfers between devices with their start and end apart: 9 -> 9, of which waited for: 3 -> 3; matrix products, arithmetic and copies ran while one was open for 0% -> 0% of each run, Pallas kernels for 58% -> 59%
where the time goes in v15:
time: 43.7 us; the launch traced here: 43.5 us
  Pallas kernels  26.4 us (60%)
  starting transfers between devices  13.2 us (30%)
  waiting for transfers between devices  3.1 us (7%)
  between operations  0.74 us (2%)
    pallas_call x8, Pallas kernels, call(): pl.pallas_call(kernel, out_shape=outs, in_specs=where, out_specs=[VMEM] *...  26.4 us
    ppermute x9, starting transfers between devices, moved(): return lax.ppermute(block, ('ctx', 'head'), route)  13.2 us
    ppermute x9, waiting for transfers between devices, moved(): return lax.ppermute(block, ('ctx', 'head'), route)  3.1 us
  transfers between devices with their start and end apart: 9, of which 3 were waited for; matrix products, arithmetic and copies ran while one was open for 0% of the time, Pallas kernels for 59%

profile of v15, /device:TPU:0, one launch (start us, length us, event | category | flops | bytes accessed | tf_op | source)
XLA Modules:
  0.0 43.5 jit_solution(3068808007253424854)
XLA Ops:
  0.6 0.5 %collective-permute-start.1 = (bf16[1024,128]{1,0:T(8,128)(2,1)}, bf16[1024,128]{1,0:T(8,128)(2,1)S(1)}, u32[]{:S(2)}, u32[]{:S(2)}) collective-permute-start(bf16[1024,128]{1,0:T(8,128)(2,1)} %refs_4_.1), channel_id=1, source_target_pairs={{0,2},{1,3},{2,4},{3,5},{4,6},{5,7},{6,8},{7,9},{8,10},{9,11},{10,... | collective-permute-start | bytes 786440 | tf_op jit(solution)/shard_map/ppermute | solution.py:396
  1.1 2.6 %collective-permute-start.2 = (bf16[1024,128]{1,0:T(8,128)(2,1)}, bf16[1024,128]{1,0:T(8,128)(2,1)S(1)}, u32[]{:S(2)}, u32[]{:S(2)}) collective-permute-start(bf16[1024,128]{1,0:T(8,128)(2,1)} %refs_5_.1), channel_id=1, source_target_pairs={{0,2},{1,3},{2,4},{3,5},{4,6},{5,7},{6,8},{7,9},{8,10},{9,11},{10,... | collective-permute-start | bytes 786440 | tf_op jit(solution)/shard_map/ppermute | solution.py:396
  3.8 0.0 copy-start
  3.8 0.0 copy-start.1
  3.8 0.0 copy-start.2
  3.8 6.9 %first.1 = (f32[8,4096]{1,0:T(8,128)S(1)}, bf16[2048,128]{1,0:T(8,128)(2,1)S(1)}, bf16[1024,4096]{1,0:T(8,128)(2,1)S(1)}, f32[1024,128]{1,0:T(8,128)S(1)}, f32[1024,128]{1,0:T(8,128)S(1)}) custom-call(bf16[4096,128]{1,0:T(8,128)(2,1)} %bitcast.4, bf16[4096,128]{1,0:T(8,128)(2,1)} %bitcast.13, bf16[4096,128]{1,0:T(8,128)(2,1)} %bitcast.8, f32[4,1024]{1,0:T(4,128)} %refs_3_.1, ...), custom_call_target="tpu_custom_call" | custom-call | flops 8724152320 | bytes 6815744 | tf_op jit(solution)/shard_map/first/pallas_call | solution.py:376
  10.6 2.8 %collective-permute-start = (bf16[2048,128]{1,0:T(8,128)(2,1)S(1)}, bf16[2048,128]{1,0:T(8,128)(2,1)S(1)}, u32[]{:S(2)}, u32[]{:S(2)}) collective-permute-start(bf16[2048,128]{1,0:T(8,128)(2,1)S(1)} %get-tuple-element.20.refs_3_.both_ref), channel_id=1, source_target_pairs={{0,4},{1,5},{2,2},{3,3},{4,8},{5,9},{6,6},{7,7},{8,12},{9,13},{10,... | collective-permute-start | bytes 1572872 | tf_op jit(solution)/shard_map/ppermute | solution.py:396
  13.5 0.0 collective-permute-done.1.key_ref.refs_3_.refs_0_
  13.5 0.0 collective-permute-done.2.value_ref.refs_4_
  13.6 0.1 collective-permute-start.3
  13.6 0.0 copy-done
  13.6 0.0 copy-done.1
  13.7 0.0 copy-done.2
  13.7 5.4 %near.1 = (bf16[2,512,2048]{2,1,0:T(8,128)(2,1)S(1)}, bf16[1024,128]{1,0:T(8,128)(2,1)S(1)}, bf16[1024,128]{1,0:T(8,128)(2,1)S(1)}, bf16[1024,128]{1,0:T(8,128)(2,1)S(1)}) custom-call(s32[32]{0:T(128)S(1)} %copy-done, bf16[4096,128]{1,0:T(8,128)(2,1)S(1)} %bitcast.9, bf16[4096,128]{1,0:T(8,128)(2,1)S(1)} %bitcast.5, ...), custom_call_target="tpu_custom_call" | custom-call | flops 10737418240 | bytes 8388608 | tf_op jit(solution)/shard_map/near/pallas_call | solution.py:376
  19.1 0.5 %collective-permute-start.4 = (bf16[1024,128]{1,0:T(8,128)(2,1)S(1)}, bf16[1024,128]{1,0:T(8,128)(2,1)S(1)}, u32[]{:S(2)}, u32[]{:S(2)}) collective-permute-start(bf16[1024,128]{1,0:T(8,128)(2,1)S(1)} %get-tuple-element.25), channel_id=1, source_target_pairs={{0,2},{1,3},{2,0},{3,1},{4,6},{5,7},{6,4},{7,5},{8,10},{9,11},{10,... | collective-permute-start | bytes 786440 | tf_op jit(solution)/shard_map/ppermute | solution.py:396
  19.7 0.1 collective-permute-start.5
  19.7 1.1 %collective-permute-done.4.refs_0_.refs_7_ = bf16[1024,128]{1,0:T(8,128)(2,1)S(1)} collective-permute-done((bf16[1024,128]{1,0:T(8,128)(2,1)S(1)}, bf16[1024,128]{1,0:T(8,128)(2,1)S(1)}, u32[]{:S(2)}, u32[]{:S(2)}) %collective-permute-start.4) | collective-permute-done | bytes 262176 | tf_op jit(solution)/shard_map/ppermute | solution.py:396
  20.8 0.1 join.1.refs_5_
  20.9 2.3 %collective-permute-start.6 = (bf16[1024,128]{1,0:T(8,128)(2,1)S(1)}, bf16[1024,128]{1,0:T(8,128)(2,1)S(1)}, u32[]{:S(2)}, u32[]{:S(2)}) collective-permute-start(bf16[1024,128]{1,0:T(8,128)(2,1)S(1)} %join.1.refs_5_), channel_id=1, source_target_pairs={{0,1},{1,0},{2,3},{3,2},{4,5},{5,4},{6,7},{7,6},{8,9},{9,8},{10,11... | collective-permute-start | bytes 786440 | tf_op jit(solution)/shard_map/ppermute | solution.py:396
  23.2 0.0 collective-permute-done.5.refs_6_.swapped_ref
  23.2 1.2 %collective-permute-done.refs_3_ = bf16[2048,128]{1,0:T(8,128)(2,1)S(1)} collective-permute-done((bf16[2048,128]{1,0:T(8,128)(2,1)S(1)}, bf16[2048,128]{1,0:T(8,128)(2,1)S(1)}, u32[]{:S(2)}, u32[]{:S(2)}) %collective-permute-start) | collective-permute-done | bytes 524320 | tf_op jit(solution)/shard_map/ppermute | solution.py:396
  24.4 0.0 collective-permute-done.3.refs_4_
  24.4 5.5 %far.1 = (bf16[2048,128]{1,0:T(8,128)(2,1)S(1)}, bf16[2,512,2048]{2,1,0:T(8,128)(2,1)S(1)}, bf16[1024,128]{1,0:T(8,128)(2,1)S(1)}, bf16[1024,128]{1,0:T(8,128)(2,1)S(1)}) custom-call(s32[32]{0:T(128)S(1)} %copy-done, bf16[4096,128]{1,0:T(8,128)(2,1)S(1)} %bitcast.10, bf16[4096,128]{1,0:T(8,128)(2,1)S(1)} %bitcast.6, ...), custom_call_target="tpu_custom_call" | custom-call | flops 10737418240 | bytes 8388608 | tf_op jit(solution)/shard_map/far/pallas_call | solution.py:376
  29.9 1.3 %collective-permute-start.7 = (bf16[1024,128]{1,0:T(8,128)(2,1)S(1)}, bf16[1024,128]{1,0:T(8,128)(2,1)S(1)}, u32[]{:S(2)}, u32[]{:S(2)}) collective-permute-start(bf16[1024,128]{1,0:T(8,128)(2,1)S(1)} %get-tuple-element.28.refs_7_), channel_id=1, source_target_pairs={{0,28},{1,29},{2,30},{3,31},{4,0},{5,1},{6,2},{7,3},{8,4},{9,5},{1... | collective-permute-start | bytes 786440 | tf_op jit(solution)/shard_map/ppermute | solution.py:396
  31.2 2.9 %collective-permute-start.8 = (bf16[1024,128]{1,0:T(8,128)(2,1)S(1)}, bf16[1024,128]{1,0:T(8,128)(2,1)S(1)}, u32[]{:S(2)}, u32[]{:S(2)}) collective-permute-start(bf16[1024,128]{1,0:T(8,128)(2,1)S(1)} %get-tuple-element.34), channel_id=1, source_target_pairs={{0,29},{1,28},{2,31},{3,30},{4,1},{5,0},{6,3},{7,2},{8,5},{9,4},{1... | collective-permute-start | bytes 786440 | tf_op jit(solution)/shard_map/ppermute | solution.py:396
  34.1 2.5 %last.1 = (bf16[1024,4096]{1,0:T(8,128)(2,1)S(1)}, f32[1024,128]{1,0:T(8,128)S(1)}, f32[1024,128]{1,0:T(8,128)S(1)}, f32[1024,128]{1,0:T(8,128)S(1)}) custom-call(s32[32]{0:T(128)S(1)} %copy-done, bf16[4096,128]{1,0:T(8,128)(2,1)S(1)} %bitcast.11, bf16[4096,128]{1,0:T(8,128)(2,1)S(1)} %bitcast.7, ...), custom_call_target="tpu_custom_call", output_to_operand_aliasing={{0}: (5, {}), {1}: (6, {}), {2}: (7, {})} | custom-call | flops 8724152320 | bytes 6815744 | tf_op jit(solution)/shard_map/last/pallas_call | solution.py:376
  36.6 5.2 %queries.1 = bf16[4096,128]{1,0:T(8,128)(2,1)} custom-call(s32[32]{0:T(128)S(1)} %copy-done, bf16[2048,128]{1,0:T(8,128)(2,1)S(1)} %get-tuple-element.20.refs_3_.both_ref, bf16[1024,4096]{1,0:T(8,128)(2,1)S(1)} %get-tuple-element.29.own_ref, bf16[1024,128]{1,0:T(8,128)(2,1)S(1)} %collective-permute-done.1.key_ref.refs_3_.refs_0_, ...), custom_call_target="tpu_custom_call" | custom-call | flops 107374184 | bytes 83886 | tf_op jit(solution)/shard_map/queries/pallas_call | solution.py:376
  41.9 0.0 collective-permute-done.6.refs_0_
  41.9 0.8 %collective-permute-done.7.refs_1_ = bf16[1024,128]{1,0:T(8,128)(2,1)S(1)} collective-permute-done((bf16[1024,128]{1,0:T(8,128)(2,1)S(1)}, bf16[1024,128]{1,0:T(8,128)(2,1)S(1)}, u32[]{:S(2)}, u32[]{:S(2)}) %collective-permute-start.7) | collective-permute-done | bytes 262176 | tf_op jit(solution)/shard_map/ppermute | solution.py:396
  42.7 0.0 collective-permute-done.8.refs_2_
  42.7 0.8 %total.1 = (bf16[512,128]{1,0:T(8,128)(2,1)}, bf16[512,128]{1,0:T(8,128)(2,1)}) custom-call(f32[1024,128]{1,0:T(8,128)S(1)} %get-tuple-element.33.total_ref, bf16[1024,128]{1,0:T(8,128)(2,1)S(1)} %collective-permute-done.5.refs_6_.swapped_ref, bf16[1024,128]{1,0:T(8,128)(2,1)S(1)} %collective-permute-done.6.refs_0_, ...), custom_call_target="tpu_custom_call" | custom-call | flops 13421772 | bytes 10485 | tf_op jit(solution)/shard_map/total/pallas_call | solution.py:376
  (1 shorter events, 0.0 us)
Async XLA Ops:
  0.6 12.9 %collective-permute-start.1 = (bf16[1024,128]{1,0:T(8,128)(2,1)}, bf16[1024,128]{1,0:T(8,128)(2,1)S(1)}, u32[]{:S(2)}, u32[]{:S(2)}) collective-permute-start(bf16[1024,128]{1,0:T(8,128)(2,1)} %refs_4_.1), channel_id=1, source_target_pairs={{0,2},{1,3},{2,4},{3,5},{4,6},{5,7},{6,8},{7,9},{8,10},{9,11},{10,... | collective-permute-start | bytes 786440 | tf_op jit(solution)/shard_map/ppermute | solution.py:396
  1.1 12.4 %collective-permute-start.2 = (bf16[1024,128]{1,0:T(8,128)(2,1)}, bf16[1024,128]{1,0:T(8,128)(2,1)S(1)}, u32[]{:S(2)}, u32[]{:S(2)}) collective-permute-start(bf16[1024,128]{1,0:T(8,128)(2,1)} %refs_5_.1), channel_id=1, source_target_pairs={{0,2},{1,3},{2,4},{3,5},{4,6},{5,7},{6,8},{7,9},{8,10},{9,11},{10,... | collective-permute-start | bytes 786440 | tf_op jit(solution)/shard_map/ppermute | solution.py:396
  3.8 9.9 %copy-start = (s32[32]{0:T(128)S(1)}, s32[32]{0:T(128)}, u32[]{:S(2)}) copy-start(s32[32]{0:T(128)} %span_ids.7) | copy-start | bytes 388
  3.8 9.9 %copy-start.1 = (bf16[1024,4,128]{2,1,0:T(4,128)(2,1)S(1)}, bf16[1024,4,128]{2,1,0:T(4,128)(2,1)}, u32[]{:S(2)}) copy-start(bf16[1024,4,128]{2,1,0:T(4,128)(2,1)} %param.11) | copy-start | bytes 3145732
  3.8 9.9 %copy-start.2 = (bf16[1024,4,128]{2,1,0:T(4,128)(2,1)S(1)}, bf16[1024,4,128]{2,1,0:T(4,128)(2,1)}, u32[]{:S(2)}) copy-start(bf16[1024,4,128]{2,1,0:T(4,128)(2,1)} %param.7) | copy-start | bytes 3145732
  10.6 13.8 %collective-permute-start = (bf16[2048,128]{1,0:T(8,128)(2,1)S(1)}, bf16[2048,128]{1,0:T(8,128)(2,1)S(1)}, u32[]{:S(2)}, u32[]{:S(2)}) collective-permute-start(bf16[2048,128]{1,0:T(8,128)(2,1)S(1)} %get-tuple-element.20.refs_3_.both_ref), channel_id=1, source_target_pairs={{0,4},{1,5},{2,2},{3,3},{4,8},{5,9},{6,6},{7,7},{8,12},{9,13},{10,... | collective-permute-start | bytes 1572872 | tf_op jit(solution)/shard_map/ppermute | solution.py:396
  13.6 10.9 %collective-permute-start.3 = (bf16[2048,128]{1,0:T(8,128)(2,1)S(1)}, bf16[2048,128]{1,0:T(8,128)(2,1)S(1)}, u32[]{:S(2)}, u32[]{:S(2)}) collective-permute-start(bf16[2048,128]{1,0:T(8,128)(2,1)S(1)} %pack.1.refs_7_), channel_id=1, source_target_pairs={{0,2},{1,3},{2,0},{3,1},{4,6},{5,7},{6,4},{7,5},{8,10},{9,11},{10,... | collective-permute-start | bytes 1572872 | tf_op jit(solution)/shard_map/ppermute | solution.py:396
  19.1 1.7 %collective-permute-start.4 = (bf16[1024,128]{1,0:T(8,128)(2,1)S(1)}, bf16[1024,128]{1,0:T(8,128)(2,1)S(1)}, u32[]{:S(2)}, u32[]{:S(2)}) collective-permute-start(bf16[1024,128]{1,0:T(8,128)(2,1)S(1)} %get-tuple-element.25), channel_id=1, source_target_pairs={{0,2},{1,3},{2,0},{3,1},{4,6},{5,7},{6,4},{7,5},{8,10},{9,11},{10,... | collective-permute-start | bytes 786440 | tf_op jit(solution)/shard_map/ppermute | solution.py:396
  19.7 3.6 %collective-permute-start.5 = (bf16[1024,128]{1,0:T(8,128)(2,1)S(1)}, bf16[1024,128]{1,0:T(8,128)(2,1)S(1)}, u32[]{:S(2)}, u32[]{:S(2)}) collective-permute-start(bf16[1024,128]{1,0:T(8,128)(2,1)S(1)} %get-tuple-element.27), channel_id=1, source_target_pairs={{0,2},{1,3},{2,0},{3,1},{4,6},{5,7},{6,4},{7,5},{8,10},{9,11},{10,... | collective-permute-start | bytes 786440 | tf_op jit(solution)/shard_map/ppermute | solution.py:396
  20.9 20.9 %collective-permute-start.6 = (bf16[1024,128]{1,0:T(8,128)(2,1)S(1)}, bf16[1024,128]{1,0:T(8,128)(2,1)S(1)}, u32[]{:S(2)}, u32[]{:S(2)}) collective-permute-start(bf16[1024,128]{1,0:T(8,128)(2,1)S(1)} %join.1.refs_5_), channel_id=1, source_target_pairs={{0,1},{1,0},{2,3},{3,2},{4,5},{5,4},{6,7},{7,6},{8,9},{9,8},{10,11... | collective-permute-start | bytes 786440 | tf_op jit(solution)/shard_map/ppermute | solution.py:396
  29.9 12.8 %collective-permute-start.7 = (bf16[1024,128]{1,0:T(8,128)(2,1)S(1)}, bf16[1024,128]{1,0:T(8,128)(2,1)S(1)}, u32[]{:S(2)}, u32[]{:S(2)}) collective-permute-start(bf16[1024,128]{1,0:T(8,128)(2,1)S(1)} %get-tuple-element.28.refs_7_), channel_id=1, source_target_pairs={{0,28},{1,29},{2,30},{3,31},{4,0},{5,1},{6,2},{7,3},{8,4},{9,5},{1... | collective-permute-start | bytes 786440 | tf_op jit(solution)/shard_map/ppermute | solution.py:396
  31.2 11.5 %collective-permute-start.8 = (bf16[1024,128]{1,0:T(8,128)(2,1)S(1)}, bf16[1024,128]{1,0:T(8,128)(2,1)S(1)}, u32[]{:S(2)}, u32[]{:S(2)}) collective-permute-start(bf16[1024,128]{1,0:T(8,128)(2,1)S(1)} %get-tuple-element.34), channel_id=1, source_target_pairs={{0,29},{1,28},{2,31},{3,30},{4,1},{5,0},{6,3},{7,2},{8,5},{9,4},{1... | collective-permute-start | bytes 786440 | tf_op jit(solution)/shard_map/ppermute | solution.py:396

commit v16 on v15

--- a/solution.py
+++ b/solution.py
@@ -273,10 +273,9 @@
     key_ref, value_ref = both_ref.at[pl.ds(0, toks)], both_ref.at[pl.ds(toks, toks)]
     group = (query_ref, grad_ref, key_ref, value_ref, terms_ref, tile)
     far_work(group, (key_acc, value_acc), scale, span_ids, kept_ref, probs_ref, heads, 2)
-    odd = is_odd.astype(jnp.float32)
 
     def more(away, low, share):
-        return swapped[away][low : low + share, :].astype(jnp.float32) * odd
+        return jnp.where(is_odd, swapped[away][low : low + share, :].astype(jnp.float32), 0.0)
 
     put_shares(outs, key_acc, value_acc, scale, more=more)
 
@@ -299,19 +298,19 @@
 
 def join_kernel(*refs):
     count = len(refs) // 3
-    even = 1.0 - lax.rem(lax.axis_index("ctx"), 2).astype(jnp.float32)
+    even = lax.rem(lax.axis_index("ctx"), 2) == 0
     for swapped, this, out in zip(refs, refs[count:], refs[2 * count :]):
-        more = swapped[...].astype(jnp.float32) * even
+        more = jnp.where(even, swapped[...].astype(jnp.float32), 0.0)
         out[...] = (this[...].astype(jnp.float32) + more).astype(out.dtype)
 
 
 def total_kernel(total_ref, swapped_ref, *refs):
     ins, (key_out, value_out) = refs[:-2], refs[-2:]
     share = key_out.shape[0]
-    even = 1.0 - lax.rem(lax.axis_index("ctx"), 2).astype(jnp.float32)
+    even = lax.rem(lax.axis_index("ctx"), 2) == 0
     for low, out in ((0, key_out), (share, value_out)):
         part = total_ref[low : low + share, :]
-        part = part + swapped_ref[low : low + share, :].astype(jnp.float32) * even
+        part = part + jnp.where(even, swapped_ref[low : low + share, :].astype(jnp.float32), 0.0)
         for ref in ins:
             part = part + ref[low : low + share, :].astype(jnp.float32)
         out[...] = part.astype(out.dtype)

time: 43.7 us -> 44.1 us (level)
  starting transfers between devices: 13.2 us -> 14.8 us
  waiting for transfers between devices: 3.1 us -> 2.35 us
    ppermute x9, starting transfers between devices: 13.2 us -> 14.8 us  [moved(): return lax.ppermute(block, ('ctx', 'head'), route)]
    ppermute x9, waiting for transfers between devices: 3.1 us -> 2.35 us  [moved(): return lax.ppermute(block, ('ctx', 'head'), route)]
  transfers between devices with their start and end apart: 9 -> 9, of which waited for: 3 -> 4; matrix products, arithmetic and copies ran while one was open for 0% -> 0% of each run, Pallas kernels for 59% -> 58%
where the time goes in v16:
time: 44.1 us; the launch traced here: 44.3 us
  Pallas kernels  26.4 us (60%)
  starting transfers between devices  14.8 us (34%)
  waiting for transfers between devices  2.35 us (5%)
  between operations  0.74 us (2%)
    pallas_call x8, Pallas kernels, call(): pl.pallas_call(kernel, out_shape=outs, in_specs=where, out_specs=[VMEM] *...  26.4 us
    ppermute x9, starting transfers between devices, moved(): return lax.ppermute(block, ('ctx', 'head'), route)  14.8 us
    ppermute x9, waiting for transfers between devices, moved(): return lax.ppermute(block, ('ctx', 'head'), route)  2.35 us
  transfers between devices with their start and end apart: 9, of which 4 were waited for; matrix products, arithmetic and copies ran while one was open for 0% of the time, Pallas kernels for 58%

profile of v16, /device:TPU:0, one launch (start us, length us, event | category | flops | bytes accessed | tf_op | source)
XLA Modules:
  0.0 44.3 jit_solution(13721194944088784326)
XLA Ops:
  0.6 0.5 %collective-permute-start.1 = (bf16[1024,128]{1,0:T(8,128)(2,1)}, bf16[1024,128]{1,0:T(8,128)(2,1)S(1)}, u32[]{:S(2)}, u32[]{:S(2)}) collective-permute-start(bf16[1024,128]{1,0:T(8,128)(2,1)} %refs_4_.1), channel_id=1, source_target_pairs={{0,2},{1,3},{2,4},{3,5},{4,6},{5,7},{6,8},{7,9},{8,10},{9,11},{10,... | collective-permute-start | bytes 786440 | tf_op jit(solution)/shard_map/ppermute | solution.py:395
  1.1 2.6 %collective-permute-start.2 = (bf16[1024,128]{1,0:T(8,128)(2,1)}, bf16[1024,128]{1,0:T(8,128)(2,1)S(1)}, u32[]{:S(2)}, u32[]{:S(2)}) collective-permute-start(bf16[1024,128]{1,0:T(8,128)(2,1)} %refs_5_.1), channel_id=1, source_target_pairs={{0,2},{1,3},{2,4},{3,5},{4,6},{5,7},{6,8},{7,9},{8,10},{9,11},{10,... | collective-permute-start | bytes 786440 | tf_op jit(solution)/shard_map/ppermute | solution.py:395
  3.8 0.0 copy-start
  3.8 0.0 copy-start.1
  3.8 0.0 copy-start.2
  3.8 6.1 %first.1 = (f32[8,4096]{1,0:T(8,128)S(1)}, bf16[2048,128]{1,0:T(8,128)(2,1)S(1)}, bf16[1024,4096]{1,0:T(8,128)(2,1)S(1)}, f32[1024,128]{1,0:T(8,128)S(1)}, f32[1024,128]{1,0:T(8,128)S(1)}) custom-call(bf16[4096,128]{1,0:T(8,128)(2,1)} %bitcast.4, bf16[4096,128]{1,0:T(8,128)(2,1)} %bitcast.13, bf16[4096,128]{1,0:T(8,128)(2,1)} %bitcast.8, f32[4,1024]{1,0:T(4,128)} %refs_3_.1, ...), custom_call_target="tpu_custom_call" | custom-call | flops 8724152320 | bytes 6815744 | tf_op jit(solution)/shard_map/first/pallas_call | solution.py:375
  9.9 3.6 %collective-permute-start = (bf16[2048,128]{1,0:T(8,128)(2,1)S(1)}, bf16[2048,128]{1,0:T(8,128)(2,1)S(1)}, u32[]{:S(2)}, u32[]{:S(2)}) collective-permute-start(bf16[2048,128]{1,0:T(8,128)(2,1)S(1)} %get-tuple-element.20.refs_3_.both_ref), channel_id=1, source_target_pairs={{0,4},{1,5},{2,2},{3,3},{4,8},{5,9},{6,6},{7,7},{8,12},{9,13},{10,... | collective-permute-start | bytes 1572872 | tf_op jit(solution)/shard_map/ppermute | solution.py:395
  13.5 0.0 collective-permute-done.1.key_ref.refs_3_.refs_0_
  13.5 0.0 collective-permute-done.2.value_ref.refs_4_
  13.6 0.1 collective-permute-start.3
  13.6 0.0 copy-done
  13.6 0.0 copy-done.1
  13.7 0.0 copy-done.2
  13.7 5.4 %near.1 = (bf16[2,512,2048]{2,1,0:T(8,128)(2,1)S(1)}, bf16[1024,128]{1,0:T(8,128)(2,1)S(1)}, bf16[1024,128]{1,0:T(8,128)(2,1)S(1)}, bf16[1024,128]{1,0:T(8,128)(2,1)S(1)}) custom-call(s32[32]{0:T(128)S(1)} %copy-done, bf16[4096,128]{1,0:T(8,128)(2,1)S(1)} %bitcast.9, bf16[4096,128]{1,0:T(8,128)(2,1)S(1)} %bitcast.5, ...), custom_call_target="tpu_custom_call" | custom-call | flops 10737418240 | bytes 8388608 | tf_op jit(solution)/shard_map/near/pallas_call | solution.py:375
  19.1 0.5 %collective-permute-start.4 = (bf16[1024,128]{1,0:T(8,128)(2,1)S(1)}, bf16[1024,128]{1,0:T(8,128)(2,1)S(1)}, u32[]{:S(2)}, u32[]{:S(2)}) collective-permute-start(bf16[1024,128]{1,0:T(8,128)(2,1)S(1)} %get-tuple-element.25), channel_id=1, source_target_pairs={{0,2},{1,3},{2,0},{3,1},{4,6},{5,7},{6,4},{7,5},{8,10},{9,11},{10,... | collective-permute-start | bytes 786440 | tf_op jit(solution)/shard_map/ppermute | solution.py:395
  19.7 0.1 collective-permute-start.5
  19.7 1.1 %collective-permute-done.4.refs_0_.refs_7_ = bf16[1024,128]{1,0:T(8,128)(2,1)S(1)} collective-permute-done((bf16[1024,128]{1,0:T(8,128)(2,1)S(1)}, bf16[1024,128]{1,0:T(8,128)(2,1)S(1)}, u32[]{:S(2)}, u32[]{:S(2)}) %collective-permute-start.4) | collective-permute-done | bytes 262176 | tf_op jit(solution)/shard_map/ppermute | solution.py:395
  20.8 0.1 join.1.refs_5_
  20.9 2.3 %collective-permute-start.6 = (bf16[1024,128]{1,0:T(8,128)(2,1)S(1)}, bf16[1024,128]{1,0:T(8,128)(2,1)S(1)}, u32[]{:S(2)}, u32[]{:S(2)}) collective-permute-start(bf16[1024,128]{1,0:T(8,128)(2,1)S(1)} %join.1.refs_5_), channel_id=1, source_target_pairs={{0,1},{1,0},{2,3},{3,2},{4,5},{5,4},{6,7},{7,6},{8,9},{9,8},{10,11... | collective-permute-start | bytes 786440 | tf_op jit(solution)/shard_map/ppermute | solution.py:395
  23.2 0.0 collective-permute-done.5.refs_6_.swapped_ref
  23.2 0.4 collective-permute-done.refs_3_
  23.7 0.0 collective-permute-done.3.refs_4_
  23.7 5.5 %far.1 = (bf16[2048,128]{1,0:T(8,128)(2,1)S(1)}, bf16[2,512,2048]{2,1,0:T(8,128)(2,1)S(1)}, bf16[1024,128]{1,0:T(8,128)(2,1)S(1)}, bf16[1024,128]{1,0:T(8,128)(2,1)S(1)}) custom-call(s32[32]{0:T(128)S(1)} %copy-done, bf16[4096,128]{1,0:T(8,128)(2,1)S(1)} %bitcast.10, bf16[4096,128]{1,0:T(8,128)(2,1)S(1)} %bitcast.6, ...), custom_call_target="tpu_custom_call" | custom-call | flops 10737418240 | bytes 8388608 | tf_op jit(solution)/shard_map/far/pallas_call | solution.py:375
  29.1 2.9 %collective-permute-start.7 = (bf16[1024,128]{1,0:T(8,128)(2,1)S(1)}, bf16[1024,128]{1,0:T(8,128)(2,1)S(1)}, u32[]{:S(2)}, u32[]{:S(2)}) collective-permute-start(bf16[1024,128]{1,0:T(8,128)(2,1)S(1)} %get-tuple-element.28.refs_7_), channel_id=1, source_target_pairs={{0,28},{1,29},{2,30},{3,31},{4,0},{5,1},{6,2},{7,3},{8,4},{9,5},{1... | collective-permute-start | bytes 786440 | tf_op jit(solution)/shard_map/ppermute | solution.py:395
  32.0 2.1 %collective-permute-start.8 = (bf16[1024,128]{1,0:T(8,128)(2,1)S(1)}, bf16[1024,128]{1,0:T(8,128)(2,1)S(1)}, u32[]{:S(2)}, u32[]{:S(2)}) collective-permute-start(bf16[1024,128]{1,0:T(8,128)(2,1)S(1)} %get-tuple-element.34), channel_id=1, source_target_pairs={{0,29},{1,28},{2,31},{3,30},{4,1},{5,0},{6,3},{7,2},{8,5},{9,4},{1... | collective-permute-start | bytes 786440 | tf_op jit(solution)/shard_map/ppermute | solution.py:395
  34.1 3.2 %last.1 = (bf16[1024,4096]{1,0:T(8,128)(2,1)S(1)}, f32[1024,128]{1,0:T(8,128)S(1)}, f32[1024,128]{1,0:T(8,128)S(1)}, f32[1024,128]{1,0:T(8,128)S(1)}) custom-call(s32[32]{0:T(128)S(1)} %copy-done, bf16[4096,128]{1,0:T(8,128)(2,1)S(1)} %bitcast.11, bf16[4096,128]{1,0:T(8,128)(2,1)S(1)} %bitcast.7, ...), custom_call_target="tpu_custom_call", output_to_operand_aliasing={{0}: (5, {}), {1}: (6, {}), {2}: (7, {})} | custom-call | flops 8724152320 | bytes 6815744 | tf_op jit(solution)/shard_map/last/pallas_call | solution.py:375
  37.4 5.2 %queries.1 = bf16[4096,128]{1,0:T(8,128)(2,1)} custom-call(s32[32]{0:T(128)S(1)} %copy-done, bf16[2048,128]{1,0:T(8,128)(2,1)S(1)} %get-tuple-element.20.refs_3_.both_ref, bf16[1024,4096]{1,0:T(8,128)(2,1)S(1)} %get-tuple-element.29.own_ref, bf16[1024,128]{1,0:T(8,128)(2,1)S(1)} %collective-permute-done.1.key_ref.refs_3_.refs_0_, ...), custom_call_target="tpu_custom_call" | custom-call | flops 107374184 | bytes 83886 | tf_op jit(solution)/shard_map/queries/pallas_call | solution.py:375
  42.6 0.0 collective-permute-done.6.refs_0_
  42.6 0.1 collective-permute-done.7.refs_1_
  42.7 0.7 %collective-permute-done.8.refs_2_ = bf16[1024,128]{1,0:T(8,128)(2,1)S(1)} collective-permute-done((bf16[1024,128]{1,0:T(8,128)(2,1)S(1)}, bf16[1024,128]{1,0:T(8,128)(2,1)S(1)}, u32[]{:S(2)}, u32[]{:S(2)}) %collective-permute-start.8) | collective-permute-done | bytes 262176 | tf_op jit(solution)/shard_map/ppermute | solution.py:395
  43.4 0.8 %total.1 = (bf16[512,128]{1,0:T(8,128)(2,1)}, bf16[512,128]{1,0:T(8,128)(2,1)}) custom-call(f32[1024,128]{1,0:T(8,128)S(1)} %get-tuple-element.33.total_ref, bf16[1024,128]{1,0:T(8,128)(2,1)S(1)} %collective-permute-done.5.refs_6_.swapped_ref, bf16[1024,128]{1,0:T(8,128)(2,1)S(1)} %collective-permute-done.6.refs_0_, ...), custom_call_target="tpu_custom_call" | custom-call | flops 13421772 | bytes 10485 | tf_op jit(solution)/shard_map/total/pallas_call | solution.py:375
  (1 shorter events, 0.0 us)
Async XLA Ops:
  0.6 12.9 %collective-permute-start.1 = (bf16[1024,128]{1,0:T(8,128)(2,1)}, bf16[1024,128]{1,0:T(8,128)(2,1)S(1)}, u32[]{:S(2)}, u32[]{:S(2)}) collective-permute-start(bf16[1024,128]{1,0:T(8,128)(2,1)} %refs_4_.1), channel_id=1, source_target_pairs={{0,2},{1,3},{2,4},{3,5},{4,6},{5,7},{6,8},{7,9},{8,10},{9,11},{10,... | collective-permute-start | bytes 786440 | tf_op jit(solution)/shard_map/ppermute | solution.py:395
  1.1 12.4 %collective-permute-start.2 = (bf16[1024,128]{1,0:T(8,128)(2,1)}, bf16[1024,128]{1,0:T(8,128)(2,1)S(1)}, u32[]{:S(2)}, u32[]{:S(2)}) collective-permute-start(bf16[1024,128]{1,0:T(8,128)(2,1)} %refs_5_.1), channel_id=1, source_target_pairs={{0,2},{1,3},{2,4},{3,5},{4,6},{5,7},{6,8},{7,9},{8,10},{9,11},{10,... | collective-permute-start | bytes 786440 | tf_op jit(solution)/shard_map/ppermute | solution.py:395
  3.8 9.9 %copy-start = (s32[32]{0:T(128)S(1)}, s32[32]{0:T(128)}, u32[]{:S(2)}) copy-start(s32[32]{0:T(128)} %span_ids.7) | copy-start | bytes 388
  3.8 9.9 %copy-start.1 = (bf16[1024,4,128]{2,1,0:T(4,128)(2,1)S(1)}, bf16[1024,4,128]{2,1,0:T(4,128)(2,1)}, u32[]{:S(2)}) copy-start(bf16[1024,4,128]{2,1,0:T(4,128)(2,1)} %param.11) | copy-start | bytes 3145732
  3.8 9.9 %copy-start.2 = (bf16[1024,4,128]{2,1,0:T(4,128)(2,1)S(1)}, bf16[1024,4,128]{2,1,0:T(4,128)(2,1)}, u32[]{:S(2)}) copy-start(bf16[1024,4,128]{2,1,0:T(4,128)(2,1)} %param.7) | copy-start | bytes 3145732
  9.9 13.8 %collective-permute-start = (bf16[2048,128]{1,0:T(8,128)(2,1)S(1)}, bf16[2048,128]{1,0:T(8,128)(2,1)S(1)}, u32[]{:S(2)}, u32[]{:S(2)}) collective-permute-start(bf16[2048,128]{1,0:T(8,128)(2,1)S(1)} %get-tuple-element.20.refs_3_.both_ref), channel_id=1, source_target_pairs={{0,4},{1,5},{2,2},{3,3},{4,8},{5,9},{6,6},{7,7},{8,12},{9,13},{10,... | collective-permute-start | bytes 1572872 | tf_op jit(solution)/shard_map/ppermute | solution.py:395
  13.6 10.1 %collective-permute-start.3 = (bf16[2048,128]{1,0:T(8,128)(2,1)S(1)}, bf16[2048,128]{1,0:T(8,128)(2,1)S(1)}, u32[]{:S(2)}, u32[]{:S(2)}) collective-permute-start(bf16[2048,128]{1,0:T(8,128)(2,1)S(1)} %pack.1.refs_7_), channel_id=1, source_target_pairs={{0,2},{1,3},{2,0},{3,1},{4,6},{5,7},{6,4},{7,5},{8,10},{9,11},{10,... | collective-permute-start | bytes 1572872 | tf_op jit(solution)/shard_map/ppermute | solution.py:395
  19.1 1.7 %collective-permute-start.4 = (bf16[1024,128]{1,0:T(8,128)(2,1)S(1)}, bf16[1024,128]{1,0:T(8,128)(2,1)S(1)}, u32[]{:S(2)}, u32[]{:S(2)}) collective-permute-start(bf16[1024,128]{1,0:T(8,128)(2,1)S(1)} %get-tuple-element.25), channel_id=1, source_target_pairs={{0,2},{1,3},{2,0},{3,1},{4,6},{5,7},{6,4},{7,5},{8,10},{9,11},{10,... | collective-permute-start | bytes 786440 | tf_op jit(solution)/shard_map/ppermute | solution.py:395
  19.7 3.6 %collective-permute-start.5 = (bf16[1024,128]{1,0:T(8,128)(2,1)S(1)}, bf16[1024,128]{1,0:T(8,128)(2,1)S(1)}, u32[]{:S(2)}, u32[]{:S(2)}) collective-permute-start(bf16[1024,128]{1,0:T(8,128)(2,1)S(1)} %get-tuple-element.27), channel_id=1, source_target_pairs={{0,2},{1,3},{2,0},{3,1},{4,6},{5,7},{6,4},{7,5},{8,10},{9,11},{10,... | collective-permute-start | bytes 786440 | tf_op jit(solution)/shard_map/ppermute | solution.py:395
  20.9 21.7 %collective-permute-start.6 = (bf16[1024,128]{1,0:T(8,128)(2,1)S(1)}, bf16[1024,128]{1,0:T(8,128)(2,1)S(1)}, u32[]{:S(2)}, u32[]{:S(2)}) collective-permute-start(bf16[1024,128]{1,0:T(8,128)(2,1)S(1)} %join.1.refs_5_), channel_id=1, source_target_pairs={{0,1},{1,0},{2,3},{3,2},{4,5},{5,4},{6,7},{7,6},{8,9},{9,8},{10,11... | collective-permute-start | bytes 786440 | tf_op jit(solution)/shard_map/ppermute | solution.py:395
  29.1 13.6 %collective-permute-start.7 = (bf16[1024,128]{1,0:T(8,128)(2,1)S(1)}, bf16[1024,128]{1,0:T(8,128)(2,1)S(1)}, u32[]{:S(2)}, u32[]{:S(2)}) collective-permute-start(bf16[1024,128]{1,0:T(8,128)(2,1)S(1)} %get-tuple-element.28.refs_7_), channel_id=1, source_target_pairs={{0,28},{1,29},{2,30},{3,31},{4,0},{5,1},{6,2},{7,3},{8,4},{9,5},{1... | collective-permute-start | bytes 786440 | tf_op jit(solution)/shard_map/ppermute | solution.py:395
  32.0 11.4 %collective-permute-start.8 = (bf16[1024,128]{1,0:T(8,128)(2,1)S(1)}, bf16[1024,128]{1,0:T(8,128)(2,1)S(1)}, u32[]{:S(2)}, u32[]{:S(2)}) collective-permute-start(bf16[1024,128]{1,0:T(8,128)(2,1)S(1)} %get-tuple-element.34), channel_id=1, source_target_pairs={{0,29},{1,28},{2,31},{3,30},{4,1},{5,0},{6,3},{7,2},{8,5},{9,4},{1... | collective-permute-start | bytes 786440 | tf_op jit(solution)/shard_map/ppermute | solution.py:395

commit v17 on v16

--- a/solution.py
+++ b/solution.py
@@ -198,12 +198,11 @@
 
     x = lax.axis_index("head")
     order = (1 - x, x) if parts == 2 else (0, 1)
-    for copy in whole + halves(0, order[0]) + halves(1, order[1]):
+    for copy in whole[:1] + halves(0, order[0]) + whole[1:] + halves(1, order[1]):
         copy.start()
     key_acc[...] = jnp.zeros_like(key_acc)
     value_acc[...] = jnp.zeros_like(value_acc)
-    for copy in whole:
-        copy.wait()
+    whole[0].wait()
 
     def arrive(slot):
         for copy in halves(slot, order[slot]):
@@ -212,8 +211,10 @@
 
     group = (query_ref, grad_ref, key_ref, value_ref, terms_ref, tile)
     accs = (key_acc, value_acc)
+    arrive(0)
+    for copy in whole[1:]:
+        copy.wait()
     low, corner, square = own_work(group, accs, scale, span_ids, kept_ref, probs_ref, heads)
-    arrive(0)
     corner(order[0])
     arrive(1)
     if parts == 2:

time: 44.1 us -> 44.4 us (level)
  waiting for transfers between devices: 2.35 us -> 2.96 us
  starting transfers between devices: 14.8 us -> 14.2 us
    ppermute x9, waiting for transfers between devices: 2.35 us -> 2.96 us  [moved(): return lax.ppermute(block, ('ctx', 'head'), route)]
    ppermute x9, starting transfers between devices: 14.8 us -> 14.2 us  [moved(): return lax.ppermute(block, ('ctx', 'head'), route)]
  transfers between devices with their start and end apart: 9 -> 9, of which waited for: 4 -> 3; matrix products, arithmetic and copies ran while one was open for 0% -> 0% of each run, Pallas kernels for 58% -> 58%
where the time goes in v17:
time: 44.4 us; the launch traced here: 44.2 us
  Pallas kernels  26.4 us (59%)
  starting transfers between devices  14.2 us (32%)
  waiting for transfers between devices  2.96 us (7%)
  between operations  0.74 us (2%)
    pallas_call x8, Pallas kernels, call(): pl.pallas_call(kernel, out_shape=outs, in_specs=where, out_specs=[VMEM] *...  26.4 us
    ppermute x9, starting transfers between devices, moved(): return lax.ppermute(block, ('ctx', 'head'), route)  14.2 us
    ppermute x9, waiting for transfers between devices, moved(): return lax.ppermute(block, ('ctx', 'head'), route)  2.96 us
  transfers between devices with their start and end apart: 9, of which 3 were waited for; matrix products, arithmetic and copies ran while one was open for 0% of the time, Pallas kernels for 58%

profile of v17, /device:TPU:0, one launch (start us, length us, event | category | flops | bytes accessed | tf_op | source)
XLA Modules:
  0.0 44.2 jit_solution(16508455666816957665)
XLA Ops:
  0.6 0.5 %collective-permute-start.1 = (bf16[1024,128]{1,0:T(8,128)(2,1)}, bf16[1024,128]{1,0:T(8,128)(2,1)S(1)}, u32[]{:S(2)}, u32[]{:S(2)}) collective-permute-start(bf16[1024,128]{1,0:T(8,128)(2,1)} %refs_4_.1), channel_id=1, source_target_pairs={{0,2},{1,3},{2,4},{3,5},{4,6},{5,7},{6,8},{7,9},{8,10},{9,11},{10,... | collective-permute-start | bytes 786440 | tf_op jit(solution)/shard_map/ppermute | solution.py:396
  1.1 2.6 %collective-permute-start.2 = (bf16[1024,128]{1,0:T(8,128)(2,1)}, bf16[1024,128]{1,0:T(8,128)(2,1)S(1)}, u32[]{:S(2)}, u32[]{:S(2)}) collective-permute-start(bf16[1024,128]{1,0:T(8,128)(2,1)} %refs_5_.1), channel_id=1, source_target_pairs={{0,2},{1,3},{2,4},{3,5},{4,6},{5,7},{6,8},{7,9},{8,10},{9,11},{10,... | collective-permute-start | bytes 786440 | tf_op jit(solution)/shard_map/ppermute | solution.py:396
  3.8 0.0 copy-start
  3.8 0.0 copy-start.1
  3.8 0.0 copy-start.2
  3.8 6.1 %first.1 = (f32[8,4096]{1,0:T(8,128)S(1)}, bf16[2048,128]{1,0:T(8,128)(2,1)S(1)}, bf16[1024,4096]{1,0:T(8,128)(2,1)S(1)}, f32[1024,128]{1,0:T(8,128)S(1)}, f32[1024,128]{1,0:T(8,128)S(1)}) custom-call(bf16[4096,128]{1,0:T(8,128)(2,1)} %bitcast.4, bf16[4096,128]{1,0:T(8,128)(2,1)} %bitcast.13, bf16[4096,128]{1,0:T(8,128)(2,1)} %bitcast.8, f32[4,1024]{1,0:T(4,128)} %refs_3_.1, ...), custom_call_target="tpu_custom_call" | custom-call | flops 8724152320 | bytes 6815744 | tf_op jit(solution)/shard_map/first/pallas_call | solution.py:376
  9.9 4.4 %collective-permute-start = (bf16[2048,128]{1,0:T(8,128)(2,1)S(1)}, bf16[2048,128]{1,0:T(8,128)(2,1)S(1)}, u32[]{:S(2)}, u32[]{:S(2)}) collective-permute-start(bf16[2048,128]{1,0:T(8,128)(2,1)S(1)} %get-tuple-element.20.refs_3_.both_ref), channel_id=1, source_target_pairs={{0,4},{1,5},{2,2},{3,3},{4,8},{5,9},{6,6},{7,7},{8,12},{9,13},{10,... | collective-permute-start | bytes 1572872 | tf_op jit(solution)/shard_map/ppermute | solution.py:396
  14.2 0.0 collective-permute-done.1.key_ref.refs_3_.refs_0_
  14.3 0.0 collective-permute-done.2.value_ref.refs_4_
  14.3 0.1 collective-permute-start.3
  14.4 0.0 copy-done
  14.4 0.0 copy-done.1
  14.4 0.0 copy-done.2
  14.4 5.4 %near.1 = (bf16[2,512,2048]{2,1,0:T(8,128)(2,1)S(1)}, bf16[1024,128]{1,0:T(8,128)(2,1)S(1)}, bf16[1024,128]{1,0:T(8,128)(2,1)S(1)}, bf16[1024,128]{1,0:T(8,128)(2,1)S(1)}) custom-call(s32[32]{0:T(128)S(1)} %copy-done, bf16[4096,128]{1,0:T(8,128)(2,1)S(1)} %bitcast.9, bf16[4096,128]{1,0:T(8,128)(2,1)S(1)} %bitcast.5, ...), custom_call_target="tpu_custom_call" | custom-call | flops 10737418240 | bytes 8388608 | tf_op jit(solution)/shard_map/near/pallas_call | solution.py:376
  19.9 0.5 %collective-permute-start.4 = (bf16[1024,128]{1,0:T(8,128)(2,1)S(1)}, bf16[1024,128]{1,0:T(8,128)(2,1)S(1)}, u32[]{:S(2)}, u32[]{:S(2)}) collective-permute-start(bf16[1024,128]{1,0:T(8,128)(2,1)S(1)} %get-tuple-element.25), channel_id=1, source_target_pairs={{0,2},{1,3},{2,0},{3,1},{4,6},{5,7},{6,4},{7,5},{8,10},{9,11},{10,... | collective-permute-start | bytes 786440 | tf_op jit(solution)/shard_map/ppermute | solution.py:396
  20.4 0.1 collective-permute-start.5
  20.5 1.1 %collective-permute-done.4.refs_0_.refs_7_ = bf16[1024,128]{1,0:T(8,128)(2,1)S(1)} collective-permute-done((bf16[1024,128]{1,0:T(8,128)(2,1)S(1)}, bf16[1024,128]{1,0:T(8,128)(2,1)S(1)}, u32[]{:S(2)}, u32[]{:S(2)}) %collective-permute-start.4) | collective-permute-done | bytes 262176 | tf_op jit(solution)/shard_map/ppermute | solution.py:396
  21.6 0.1 join.1.refs_5_
  21.7 0.9 %collective-permute-start.6 = (bf16[1024,128]{1,0:T(8,128)(2,1)S(1)}, bf16[1024,128]{1,0:T(8,128)(2,1)S(1)}, u32[]{:S(2)}, u32[]{:S(2)}) collective-permute-start(bf16[1024,128]{1,0:T(8,128)(2,1)S(1)} %join.1.refs_5_), channel_id=1, source_target_pairs={{0,1},{1,0},{2,3},{3,2},{4,5},{5,4},{6,7},{7,6},{8,9},{9,8},{10,11... | collective-permute-start | bytes 786440 | tf_op jit(solution)/shard_map/ppermute | solution.py:396
  22.6 0.0 collective-permute-done.5.refs_6_.swapped_ref
  22.6 1.0 %collective-permute-done.refs_3_ = bf16[2048,128]{1,0:T(8,128)(2,1)S(1)} collective-permute-done((bf16[2048,128]{1,0:T(8,128)(2,1)S(1)}, bf16[2048,128]{1,0:T(8,128)(2,1)S(1)}, u32[]{:S(2)}, u32[]{:S(2)}) %collective-permute-start) | collective-permute-done | bytes 524320 | tf_op jit(solution)/shard_map/ppermute | solution.py:396
  23.6 0.0 collective-permute-done.3.refs_4_
  23.6 5.5 %far.1 = (bf16[2048,128]{1,0:T(8,128)(2,1)S(1)}, bf16[2,512,2048]{2,1,0:T(8,128)(2,1)S(1)}, bf16[1024,128]{1,0:T(8,128)(2,1)S(1)}, bf16[1024,128]{1,0:T(8,128)(2,1)S(1)}) custom-call(s32[32]{0:T(128)S(1)} %copy-done, bf16[4096,128]{1,0:T(8,128)(2,1)S(1)} %bitcast.10, bf16[4096,128]{1,0:T(8,128)(2,1)S(1)} %bitcast.6, ...), custom_call_target="tpu_custom_call" | custom-call | flops 10737418240 | bytes 8388608 | tf_op jit(solution)/shard_map/far/pallas_call | solution.py:376
  29.1 2.9 %collective-permute-start.7 = (bf16[1024,128]{1,0:T(8,128)(2,1)S(1)}, bf16[1024,128]{1,0:T(8,128)(2,1)S(1)}, u32[]{:S(2)}, u32[]{:S(2)}) collective-permute-start(bf16[1024,128]{1,0:T(8,128)(2,1)S(1)} %get-tuple-element.28.refs_7_), channel_id=1, source_target_pairs={{0,28},{1,29},{2,30},{3,31},{4,0},{5,1},{6,2},{7,3},{8,4},{9,5},{1... | collective-permute-start | bytes 786440 | tf_op jit(solution)/shard_map/ppermute | solution.py:396
  32.0 2.1 %collective-permute-start.8 = (bf16[1024,128]{1,0:T(8,128)(2,1)S(1)}, bf16[1024,128]{1,0:T(8,128)(2,1)S(1)}, u32[]{:S(2)}, u32[]{:S(2)}) collective-permute-start(bf16[1024,128]{1,0:T(8,128)(2,1)S(1)} %get-tuple-element.34), channel_id=1, source_target_pairs={{0,29},{1,28},{2,31},{3,30},{4,1},{5,0},{6,3},{7,2},{8,5},{9,4},{1... | collective-permute-start | bytes 786440 | tf_op jit(solution)/shard_map/ppermute | solution.py:396
  34.1 3.2 %last.1 = (bf16[1024,4096]{1,0:T(8,128)(2,1)S(1)}, f32[1024,128]{1,0:T(8,128)S(1)}, f32[1024,128]{1,0:T(8,128)S(1)}, f32[1024,128]{1,0:T(8,128)S(1)}) custom-call(s32[32]{0:T(128)S(1)} %copy-done, bf16[4096,128]{1,0:T(8,128)(2,1)S(1)} %bitcast.11, bf16[4096,128]{1,0:T(8,128)(2,1)S(1)} %bitcast.7, ...), custom_call_target="tpu_custom_call", output_to_operand_aliasing={{0}: (5, {}), {1}: (6, {}), {2}: (7, {})} | custom-call | flops 8724152320 | bytes 6815744 | tf_op jit(solution)/shard_map/last/pallas_call | solution.py:376
  37.3 5.2 %queries.1 = bf16[4096,128]{1,0:T(8,128)(2,1)} custom-call(s32[32]{0:T(128)S(1)} %copy-done, bf16[2048,128]{1,0:T(8,128)(2,1)S(1)} %get-tuple-element.20.refs_3_.both_ref, bf16[1024,4096]{1,0:T(8,128)(2,1)S(1)} %get-tuple-element.29.own_ref, bf16[1024,128]{1,0:T(8,128)(2,1)S(1)} %collective-permute-done.1.key_ref.refs_3_.refs_0_, ...), custom_call_target="tpu_custom_call" | custom-call | flops 107374184 | bytes 83886 | tf_op jit(solution)/shard_map/queries/pallas_call | solution.py:376
  42.6 0.0 collective-permute-done.6.refs_0_
  42.6 0.0 collective-permute-done.7.refs_1_
  42.6 0.8 %collective-permute-done.8.refs_2_ = bf16[1024,128]{1,0:T(8,128)(2,1)S(1)} collective-permute-done((bf16[1024,128]{1,0:T(8,128)(2,1)S(1)}, bf16[1024,128]{1,0:T(8,128)(2,1)S(1)}, u32[]{:S(2)}, u32[]{:S(2)}) %collective-permute-start.8) | collective-permute-done | bytes 262176 | tf_op jit(solution)/shard_map/ppermute | solution.py:396
  43.4 0.8 %total.1 = (bf16[512,128]{1,0:T(8,128)(2,1)}, bf16[512,128]{1,0:T(8,128)(2,1)}) custom-call(f32[1024,128]{1,0:T(8,128)S(1)} %get-tuple-element.33.total_ref, bf16[1024,128]{1,0:T(8,128)(2,1)S(1)} %collective-permute-done.5.refs_6_.swapped_ref, bf16[1024,128]{1,0:T(8,128)(2,1)S(1)} %collective-permute-done.6.refs_0_, ...), custom_call_target="tpu_custom_call" | custom-call | flops 13421772 | bytes 10485 | tf_op jit(solution)/shard_map/total/pallas_call | solution.py:376
  (1 shorter events, 0.0 us)
Async XLA Ops:
  0.6 13.6 %collective-permute-start.1 = (bf16[1024,128]{1,0:T(8,128)(2,1)}, bf16[1024,128]{1,0:T(8,128)(2,1)S(1)}, u32[]{:S(2)}, u32[]{:S(2)}) collective-permute-start(bf16[1024,128]{1,0:T(8,128)(2,1)} %refs_4_.1), channel_id=1, source_target_pairs={{0,2},{1,3},{2,4},{3,5},{4,6},{5,7},{6,8},{7,9},{8,10},{9,11},{10,... | collective-permute-start | bytes 786440 | tf_op jit(solution)/shard_map/ppermute | solution.py:396
  1.1 13.1 %collective-permute-start.2 = (bf16[1024,128]{1,0:T(8,128)(2,1)}, bf16[1024,128]{1,0:T(8,128)(2,1)S(1)}, u32[]{:S(2)}, u32[]{:S(2)}) collective-permute-start(bf16[1024,128]{1,0:T(8,128)(2,1)} %refs_5_.1), channel_id=1, source_target_pairs={{0,2},{1,3},{2,4},{3,5},{4,6},{5,7},{6,8},{7,9},{8,10},{9,11},{10,... | collective-permute-start | bytes 786440 | tf_op jit(solution)/shard_map/ppermute | solution.py:396
  3.8 10.6 %copy-start = (s32[32]{0:T(128)S(1)}, s32[32]{0:T(128)}, u32[]{:S(2)}) copy-start(s32[32]{0:T(128)} %span_ids.7) | copy-start | bytes 388
  3.8 10.6 %copy-start.1 = (bf16[1024,4,128]{2,1,0:T(4,128)(2,1)S(1)}, bf16[1024,4,128]{2,1,0:T(4,128)(2,1)}, u32[]{:S(2)}) copy-start(bf16[1024,4,128]{2,1,0:T(4,128)(2,1)} %param.11) | copy-start | bytes 3145732
  3.8 10.6 %copy-start.2 = (bf16[1024,4,128]{2,1,0:T(4,128)(2,1)S(1)}, bf16[1024,4,128]{2,1,0:T(4,128)(2,1)}, u32[]{:S(2)}) copy-start(bf16[1024,4,128]{2,1,0:T(4,128)(2,1)} %param.7) | copy-start | bytes 3145732
  9.9 13.8 %collective-permute-start = (bf16[2048,128]{1,0:T(8,128)(2,1)S(1)}, bf16[2048,128]{1,0:T(8,128)(2,1)S(1)}, u32[]{:S(2)}, u32[]{:S(2)}) collective-permute-start(bf16[2048,128]{1,0:T(8,128)(2,1)S(1)} %get-tuple-element.20.refs_3_.both_ref), channel_id=1, source_target_pairs={{0,4},{1,5},{2,2},{3,3},{4,8},{5,9},{6,6},{7,7},{8,12},{9,13},{10,... | collective-permute-start | bytes 1572872 | tf_op jit(solution)/shard_map/ppermute | solution.py:396
  14.3 9.3 %collective-permute-start.3 = (bf16[2048,128]{1,0:T(8,128)(2,1)S(1)}, bf16[2048,128]{1,0:T(8,128)(2,1)S(1)}, u32[]{:S(2)}, u32[]{:S(2)}) collective-permute-start(bf16[2048,128]{1,0:T(8,128)(2,1)S(1)} %pack.1.refs_7_), channel_id=1, source_target_pairs={{0,2},{1,3},{2,0},{3,1},{4,6},{5,7},{6,4},{7,5},{8,10},{9,11},{10,... | collective-permute-start | bytes 1572872 | tf_op jit(solution)/shard_map/ppermute | solution.py:396
  19.9 1.7 %collective-permute-start.4 = (bf16[1024,128]{1,0:T(8,128)(2,1)S(1)}, bf16[1024,128]{1,0:T(8,128)(2,1)S(1)}, u32[]{:S(2)}, u32[]{:S(2)}) collective-permute-start(bf16[1024,128]{1,0:T(8,128)(2,1)S(1)} %get-tuple-element.25), channel_id=1, source_target_pairs={{0,2},{1,3},{2,0},{3,1},{4,6},{5,7},{6,4},{7,5},{8,10},{9,11},{10,... | collective-permute-start | bytes 786440 | tf_op jit(solution)/shard_map/ppermute | solution.py:396
  20.4 2.2 %collective-permute-start.5 = (bf16[1024,128]{1,0:T(8,128)(2,1)S(1)}, bf16[1024,128]{1,0:T(8,128)(2,1)S(1)}, u32[]{:S(2)}, u32[]{:S(2)}) collective-permute-start(bf16[1024,128]{1,0:T(8,128)(2,1)S(1)} %get-tuple-element.27), channel_id=1, source_target_pairs={{0,2},{1,3},{2,0},{3,1},{4,6},{5,7},{6,4},{7,5},{8,10},{9,11},{10,... | collective-permute-start | bytes 786440 | tf_op jit(solution)/shard_map/ppermute | solution.py:396
  21.7 20.9 %collective-permute-start.6 = (bf16[1024,128]{1,0:T(8,128)(2,1)S(1)}, bf16[1024,128]{1,0:T(8,128)(2,1)S(1)}, u32[]{:S(2)}, u32[]{:S(2)}) collective-permute-start(bf16[1024,128]{1,0:T(8,128)(2,1)S(1)} %join.1.refs_5_), channel_id=1, source_target_pairs={{0,1},{1,0},{2,3},{3,2},{4,5},{5,4},{6,7},{7,6},{8,9},{9,8},{10,11... | collective-permute-start | bytes 786440 | tf_op jit(solution)/shard_map/ppermute | solution.py:396
  29.1 13.5 %collective-permute-start.7 = (bf16[1024,128]{1,0:T(8,128)(2,1)S(1)}, bf16[1024,128]{1,0:T(8,128)(2,1)S(1)}, u32[]{:S(2)}, u32[]{:S(2)}) collective-permute-start(bf16[1024,128]{1,0:T(8,128)(2,1)S(1)} %get-tuple-element.28.refs_7_), channel_id=1, source_target_pairs={{0,28},{1,29},{2,30},{3,31},{4,0},{5,1},{6,2},{7,3},{8,4},{9,5},{1... | collective-permute-start | bytes 786440 | tf_op jit(solution)/shard_map/ppermute | solution.py:396
  32.0 11.4 %collective-permute-start.8 = (bf16[1024,128]{1,0:T(8,128)(2,1)S(1)}, bf16[1024,128]{1,0:T(8,128)(2,1)S(1)}, u32[]{:S(2)}, u32[]{:S(2)}) collective-permute-start(bf16[1024,128]{1,0:T(8,128)(2,1)S(1)} %get-tuple-element.34), channel_id=1, source_target_pairs={{0,29},{1,28},{2,31},{3,30},{4,1},{5,0},{6,3},{7,2},{8,5},{9,4},{1... | collective-permute-start | bytes 786440 | tf_op jit(solution)/shard_map/ppermute | solution.py:396
